TPU v7x, 32 devices: a whole 2x2x4 slice. The times are simulated.
32 devices in a mesh: lat: 4 (over y, x), lon: 8 (over z, core).
Axes of the slice: x: 2, y: 2, z: 4, core: 2. Of those that a mesh axis runs over, the one named last changes fastest.
Arguments:
- innovation: float32 [64, 2048], P(None, ('lat', 'lon')), may hold values from -6 to 6
- obs_weight: float32 [64, 2048], P(None, ('lat', 'lon')), may hold values from 0.5 to 4
- jacobian: float32 [6144, 64, 128], P(('lat', 'lon')), may hold values from -0.5 to 0.5
- block_list: int32 [2, 6144], P(None, ('lat', 'lon')), may hold values from 0 to 512, as said below
- pass_counts: int32 [2], replicated, may hold values from 3 to 6, as said below
- kappa_h: float32 [64, 256, 128], P('lat', 'lon'), may hold values from 0.03 to 0.24
- kappa_v: float32 [64, 256, 128], P('lat', 'lon'), may hold values from 0.05 to 0.45
Outputs:
- increment: float32 [64, 256, 128], P('lat', 'lon')
- residual: float32 [64, 256, 128], P('lat', 'lon')
Inputs may be any that keep to these rules, and one draw needn't show every extreme that they name: `pass_counts`: entry 0 counts lateral passes and entry 1 vertical passes; one of the two is 6 and the other is smaller. `block_list`: on each device the non-empty slots come first among its 192 slots, and in every latitude band some device has all 192 slots non-empty; an empty slot has block row 512.
All inputs are finite; a program needn't handle non-finite values.
Results may differ from a plain program's by a relative error of at most 0.0003.
Values sent between devices are 32-bit elements; how exact they have to be, the bound alone decides.
No kernel may reach another device: no remote copies, remote signals or barrier semaphores. Data moves between devices by JAX's collectives and lax.ppermute only.
A program may use at most 64 MiB of HBM per device.

v0:
```python
import functools

import jax
import jax.numpy as jnp
from jax import lax
from jax.experimental import pallas as pl
from jax.experimental.pallas import tpu as pltpu
from jax.sharding import PartitionSpec as P

LANES = 128
VMEM_LIMIT = 48 * 1024 * 1024
REACH = 6
FRAME = 2 * REACH


def split3(x):
    high = x.astype(jnp.bfloat16)
    rest = x - high.astype(jnp.float32)
    mid = rest.astype(jnp.bfloat16)
    low = (rest - mid.astype(jnp.float32)).astype(jnp.bfloat16)
    return high, mid, low


def fold_sum(x):
    total = None
    for i in range(x.shape[0] // 8):
        for j in range(x.shape[1] // LANES):
            tile = x[8 * i:8 * i + 8, LANES * j:LANES * j + LANES]
            total = tile if total is None else total + tile
    return total


def copies(pairs, sems):
    started = [pltpu.make_async_copy(src, dst, sems.at[i]) for i, (src, dst) in enumerate(pairs)]
    for copy in started:
        copy.start()
    return started


def lateral_pass(buf, face_lat, face_lon, first, last, left, right):
    cols = slice(left, right)
    width = right - left

    def body(step, carry):
        current, flux_above = carry
        row = first + 2 * step
        for k in range(2):
            below = buf[row + k + 1, cols]
            flux = face_lat[row + k, cols] * (below - current)
            side = face_lon[row + k, cols] * (pltpu.roll(current, width - 1, 0) - current)
            buf[row + k, cols] = current + ((flux - flux_above) + (side - pltpu.roll(side, 1, 0)))
            current, flux_above = below, flux
        return current, flux_above

    start = buf[first, cols]
    flux_start = face_lat[first - 1, cols] * (start - buf[first - 1, cols])
    lax.fori_loop(0, (last - first) // 2, body, (start, flux_start))


def lateral_passes(buf, face_lat, face_lon, nh, begin, end, left, right):
    rows, lost = buf.shape[0], FRAME - 2 * nh

    def body(p, c):
        lateral_pass(buf, face_lat, face_lon, lost + p, rows - lost - p, left, right)
        return c

    lax.fori_loop(begin + 1, end + 1, body, 0)


def last_lateral(buf, face_lat, face_lon, nh, lon_cells):
    close = jnp.minimum(nh, 4)
    lateral_passes(buf, face_lat, face_lon, nh, nh, 2 * nh - close, 0, buf.shape[1])
    left = (FRAME - 4) // 8 * 8
    right = -(-(FRAME + lon_cells + 4) // 8) * 8
    lateral_passes(buf, face_lat, face_lon, nh, 2 * nh - close, 2 * nh, left, right)


def vertical_passes(buf, keep, up, down, first, last, tile, offset, nv, left, right):
    cols = slice(left, right)

    def sweep(p, c):
        def rows(t, c):
            at = [first + t * tile + k for k in range(tile)]
            values = [buf[i, cols] for i in at]
            values = [
                keep[i - offset, cols] * w
                + (up[i - offset, cols] * pltpu.roll(w, LANES - 1, 1)
                   + down[i - offset, cols] * pltpu.roll(w, 1, 1))
                for i, w in zip(at, values)
            ]
            for i, w in zip(at, values):
                buf[i, cols] = w
            return c
        return lax.fori_loop(0, (last - first) // tile, rows, c)

    lax.fori_loop(0, nv, sweep, 0)


def place_halos(flags, buf, own, strips, sides, reach, dims):
    lat_cells, lon_cells = dims
    from_a, from_b = strips
    from_x, from_s = sides
    base = FRAME - reach
    lat_even, lon_even = flags[0] == 0, flags[1] == 0
    south = FRAME + lat_cells
    row_a = jnp.where(lat_even, south, base)
    row_b = jnp.where(lat_even, base, south)
    cols = slice(FRAME, FRAME + lon_cells)

    def put_own(i, c):
        buf[FRAME + i, cols] = own[pl.ds(pl.multiple_of(i * lon_cells, lon_cells), lon_cells)]
        return c

    def put_strips(i, c):
        buf[row_a + i, cols] = from_a(i)
        buf[row_b + i, cols] = from_b(i)
        return c

    lax.fori_loop(0, lat_cells, put_own, 0)
    lax.fori_loop(0, reach, put_strips, 0)
    west = slice(base, FRAME)
    east = slice(FRAME + lon_cells, FRAME + lon_cells + reach)

    def put_sides(first, second):
        def put(i, c):
            for k in range(2):
                buf[base + 2 * i + k, first] = from_x(i, k)
                buf[base + 2 * i + k, second] = from_s(i, k)
            return c
        lax.fori_loop(0, (lat_cells + 2 * reach) // 2, put, 0)

    pl.when(lon_even)(lambda: put_sides(east, west))
    pl.when(jnp.logical_not(lon_even))(lambda: put_sides(west, east))


def strip_of(ref, lon_cells, skip=0):
    return lambda i: ref[pl.ds(pl.multiple_of((skip + i) * lon_cells, lon_cells), lon_cells)]


def side_of(ref):
    return lambda i, k: ref[2 * i + k]


def folded_side_of(ref, skip, reach):
    return lambda i, k: ref[skip + i, k * reach:k * reach + reach]


def faces_kernel(dims, flags, root_h, root_v, from_a, from_b, from_x, from_s, *refs):
    lat_cells, lon_cells = dims
    out, (face_lat, face_lon, keep, up, down, buf, sems) = refs[:5], refs[5:]
    rows = lat_cells + 2 * FRAME
    width = buf.shape[1]
    place_halos(
        flags, buf, root_h, (strip_of(from_a, lon_cells), strip_of(from_b, lon_cells)),
        (side_of(from_x), side_of(from_s)), FRAME, dims,
    )

    def clear(first):
        def body(i, c):
            buf[first + i] = jnp.zeros((width, LANES), jnp.float32)
            return c
        lax.fori_loop(0, FRAME, body, 0)

    pl.when(flags[2] == 1)(lambda: clear(0))
    pl.when(flags[3] == 1)(lambda: clear(FRAME + lat_cells))

    def lateral(i, c):
        here = buf[i]
        face_lat[i] = here * buf[i + 1]
        face_lon[i] = here * pltpu.roll(here, width - 1, 0)
        return c

    lax.fori_loop(0, rows - 1, lateral, 0)
    here = buf[rows - 1]
    face_lat[rows - 1] = jnp.zeros((width, LANES), jnp.float32)
    face_lon[rows - 1] = here * pltpu.roll(here, width - 1, 0)
    side = copies([(face_lat, out[0]), (face_lon, out[1])], sems)
    place_halos(
        flags, buf, root_v, (strip_of(from_a, lon_cells, FRAME), strip_of(from_b, lon_cells, FRAME)),
        (folded_side_of(from_x, rows, REACH), folded_side_of(from_s, rows, REACH)), REACH, dims,
    )
    top = lax.broadcasted_iota(jnp.int32, (width, LANES), 1) == LANES - 1

    def vertical(i, c):
        here = buf[FRAME - REACH + i]
        face = jnp.where(top, 0.0, here * pltpu.roll(here, LANES - 1, 1))
        below = pltpu.roll(face, 1, 1)
        up[i] = face
        down[i] = below
        keep[i] = 1.0 - (face + below)
        return c

    lax.fori_loop(0, lat_cells + 2 * REACH, vertical, 0)
    level = copies([(keep, out[2]), (up, out[3]), (down, out[4])], sems.at[pl.ds(2, 3)])
    for copy in side + level:
        copy.wait()


def observe(cells, jac, field, out):
    slots, obs, _ = jac.shape
    lane = lax.broadcasted_iota(jnp.int32, (obs, LANES), 1)

    def part(first, count):
        def body(step, acc):
            for k in range(8):
                slot = first + step * 8 + k
                row = field[pl.ds(cells[slot], 1), :]
                value = jnp.sum(jac[slot] * row, axis=1, keepdims=True)
                acc = jnp.where(lane == step * 8 + k, value, acc)
            return acc
        return lax.fori_loop(0, count // 8, body, jnp.zeros((obs, LANES), jnp.float32))

    out[0:obs] = part(0, LANES)
    rest = part(LANES, slots - LANES)
    out[obs:obs + obs // 2] = rest[:obs // 2] + pltpu.roll(rest[obs // 2:], LANES // 2, 1)


def pack_kernel(innovation, obs_weight, rows, out):
    obs, own = innovation.shape
    weight = obs_weight[...]
    out[0:obs, 0:own] = weight * innovation[...]
    out[0:obs, own:2 * own] = weight
    out[obs:obs + 8] = rows[...]


def adjoint_kernel(first_call, parts, *refs):
    pieces, refs = refs[:2 * parts], refs[2 * parts:]
    if first_call:
        own_hot, cell_hot, jac_hbm, field, weight, band, jac, taken, contrib, sems = refs
    else:
        row_hot, weight, own_hot, cell_hot, jac_hbm, field, sums, jac, taken, contrib, sems = refs
    slots, obs, _ = jac.shape
    group = 32
    groups = slots // group

    def chunk(g):
        place = pl.ds(g * group, group)
        return pltpu.make_async_copy(jac_hbm.at[place], jac.at[place], sems.at[g])

    for g in range(groups):
        chunk(g).start()
    if first_call:
        own = weight.shape[1] // (2 * parts)
        for d, piece in enumerate(pieces):
            band[:, d * own:d * own + own] = piece[0:obs, 0:own]
            weight[:, d * own:d * own + own] = piece[0:obs, own:2 * own]
        weighted = band[...]
    else:
        total = None
        scal = None
        for d, piece in enumerate(pieces):
            fold = piece[obs:obs + obs // 2]
            rest = jnp.concatenate([fold, pltpu.roll(fold, LANES // 2, 1)], axis=0)
            values = jnp.concatenate([piece[0:obs], rest], axis=1)
            stack = jnp.concatenate(split3(values), axis=0)
            prod = jnp.dot(stack, row_hot[d], preferred_element_type=jnp.float32)
            total = prod if total is None else total + prod
            tail = piece[obs + obs // 2:obs + obs // 2 + 8]
            scal = tail if scal is None else scal + tail
        total = total[:obs] + (total[obs:2 * obs] + total[2 * obs:])
        weighted = weight[...] * total
        sums[0:8] = scal
        sums[8:16] = fold_sum(weighted * total)
    stack = jnp.concatenate(split3(weighted), axis=0)
    picked = jnp.dot(stack, own_hot[...], preferred_element_type=jnp.float32)
    picked = picked[:obs] + (picked[obs:2 * obs] + picked[2 * obs:])
    taken[0] = picked[:, :LANES]
    taken[1] = picked[:, LANES:]

    def body(g, c):
        chunk(g).wait()
        per = LANES // group
        values = pltpu.roll(taken[g // per], LANES - (g % per) * group, 1)
        for k in range(group):
            slot = g * group + k
            contrib[pl.ds(slot, 1), :] = jnp.sum(jac[slot] * values[:, k:k + 1], axis=0, keepdims=True)
        return c

    lax.fori_loop(0, groups, body, 0)
    out = None
    for piece in split3(contrib[...]):
        prod = jnp.dot(cell_hot[...], piece, preferred_element_type=jnp.float32)
        out = prod if out is None else out + prod
    field[...] = out


def spread_kernel(dims, first_call, *refs):
    lat_cells, lon_cells = dims
    flags, cells, own, from_a, from_b, from_x, from_s = refs[:7]
    refs = refs[7:]
    if not first_call:
        scal, refs = refs[0], refs[1:]
    faces_hbm, jac_hbm, refs = refs[:5], refs[5], refs[6:]
    if not first_call:
        grad_hbm, spread_hbm, refs = refs[0], refs[1], refs[2:]
    one_hbm, two_hbm, message = refs[:3]
    refs = refs[3:]
    face_lat, face_lon, keep, up, down, jac, one, two, grad, buf, mid, sems = refs
    loads = copies(
        list(zip(faces_hbm, (face_lat, face_lon, keep, up, down))) + [(jac_hbm, jac)], sems
    )
    if not first_call:
        old_loads = copies([(grad_hbm, grad), (spread_hbm, two)], sems.at[pl.ds(6, 2)])
    nh, nv = flags[4], flags[5]
    rows = lat_cells + 2 * FRAME
    width = buf.shape[1]
    place_halos(
        flags, buf, own, (strip_of(from_a, lon_cells), strip_of(from_b, lon_cells)),
        (side_of(from_x), side_of(from_s)), FRAME, dims,
    )
    for load in loads[:2]:
        load.wait()
    lateral_passes(buf, face_lat, face_lon, nh, 0, nh, 0, width)
    border = FRAME - REACH
    tall = lat_cells + 2 * REACH
    vertical = functools.partial(
        vertical_passes, buf, keep, up, down, border, border + tall, tall // 2, border, nv, 0, width
    )
    for load in loads[2:5]:
        load.wait()
    vertical()

    def save(i, c):
        mid[i] = buf[FRAME + i]
        return c

    lax.fori_loop(0, lat_cells, save, 0)
    vertical()
    last_lateral(buf, face_lat, face_lon, nh, lon_cells)
    cols = slice(FRAME, FRAME + lon_cells)
    if not first_call:
        rr = jnp.sum(scal[0:8])
        alpha = rr / (rr + jnp.sum(scal[8:16]))
        for load in old_loads:
            load.wait()

    def finish(i, acc):
        place = pl.ds(pl.multiple_of(i * lon_cells, lon_cells), lon_cells)
        vector = mid[i, cols]
        after = buf[FRAME + i, cols]
        if first_call:
            one[place] = vector
            two[place] = after
        else:
            old = two[place]
            base = grad[place]
            applied = base + vector
            one[place] = applied
            two[place] = old - alpha * (old + after)
            vector = base - alpha * applied
        square = vector * vector
        for j in range(lon_cells // 8):
            acc = acc + square[8 * j:8 * j + 8]
        return acc

    norm = lax.fori_loop(0, lat_cells, finish, jnp.zeros((8, LANES), jnp.float32))
    stores = copies([(one, one_hbm), (two, two_hbm)], sems.at[pl.ds(8, 2)])
    loads[5].wait()
    obs = jac.shape[1]
    observe(cells, jac, two, message)
    message[obs + obs // 2:] = norm
    for store in stores:
        store.wait()


def final_kernel(dims, *refs):
    lat_cells, lon_cells = dims
    flags, own, from_a, from_b, from_x, from_s, scal0, scal1 = refs[:8]
    hbm, (increment, residual), refs = refs[8:17], refs[17:19], refs[19:]
    face_lat, face_lon, keep, up, down, grad, spread, image, spread_next, buf, sems = refs
    loads = copies(list(zip(hbm, refs[:9])), sems)
    nh, nv = flags[4], flags[5]
    place_halos(
        flags, buf, own, (strip_of(from_a, lon_cells), strip_of(from_b, lon_cells)),
        (side_of(from_x), side_of(from_s)), REACH, dims,
    )
    for load in loads[:2]:
        load.wait()
    last_lateral(buf, face_lat, face_lon, nh, lon_cells)
    left = FRAME // 8 * 8
    right = -(-(FRAME + lon_cells) // 8) * 8
    for load in loads[2:]:
        load.wait()
    vertical_passes(
        buf, keep, up, down, FRAME, FRAME + lat_cells, lat_cells, FRAME - REACH, nv, left, right
    )
    rr0 = jnp.sum(scal0[0:8])
    alpha0 = rr0 / (rr0 + jnp.sum(scal0[8:16]))
    rr1 = jnp.sum(scal1[0:8])
    beta = rr1 / rr0
    alpha1 = rr1 / ((rr1 + jnp.sum(scal1[8:16])) - beta * (rr1 / alpha0))
    cols = slice(FRAME, FRAME + lon_cells)

    def finish(i, c):
        place = pl.ds(pl.multiple_of(i * lon_cells, lon_cells), lon_cells)
        applied = image[place]
        rest = grad[place] - alpha0 * applied
        residual[place] = rest - alpha1 * ((rest + buf[FRAME + i, cols]) + beta * applied)
        old = spread[place]
        increment[place] = alpha0 * old + alpha1 * (spread_next[place] + beta * old)
        return c

    lax.fori_loop(0, lat_cells, finish, 0)


def local(innovation, obs_weight, jacobian, block_list, pass_counts, kappa_h, kappa_v):
    lat_cells, lon_cells, levels = kappa_h.shape
    cells_n = lat_cells * lon_cells
    slots, obs, _ = jacobian.shape
    own_rows = innovation.shape[1]
    n_lat, n_lon = lax.axis_size("lat"), lax.axis_size("lon")
    parts = n_lon // 2
    lat, lon = lax.axis_index("lat"), lax.axis_index("lon")
    lat_even, lon_even = lat % 2 == 0, lon % 2 == 0
    f32 = jnp.float32

    def swap(n, k):
        return [(i, i ^ k) for i in range(n)]

    def odd_pairs(n):
        return [(i, (i + 1) % n if i % 2 else (i - 1) % n) for i in range(n)]

    def send(x, axis, pairs):
        return lax.ppermute(x, axis, pairs)

    def gather_band(x):
        near = [x] + [send(x, "lon", swap(n_lon, 2 * k)) for k in range(1, parts)]
        return near + [send(piece, "lon", swap(n_lon, 1)) for piece in near]

    def lat_strips(top, bottom, tail=None):
        to_a = jnp.where(lat_even, bottom, top)
        to_b = jnp.where(lat_even, top, bottom)
        if tail is not None:
            to_a = jnp.concatenate([to_a, tail], 0)
            to_b = jnp.concatenate([to_b, tail], 0)
        return send(to_a, "lat", swap(n_lat, 1)), send(to_b, "lat", odd_pairs(n_lat))

    def side_strips(ext, reach):
        west, east = ext[:, :reach], ext[:, lon_cells - reach:]
        return jnp.where(lon_even, east, west), jnp.where(lon_even, west, east)

    def lon_send(to_x, to_s):
        return send(to_x, "lon", swap(n_lon, 1)), send(to_s, "lon", odd_pairs(n_lon))

    def stacked(own, from_a, from_b, reach):
        shape = (reach, lon_cells, levels)
        from_a, from_b = from_a.reshape(shape), from_b.reshape(shape)
        north = jnp.where(lat_even, from_b, from_a)
        south = jnp.where(lat_even, from_a, from_b)
        return jnp.concatenate([north, own.reshape(lat_cells, lon_cells, levels), south], 0)

    def halo(own, reach, tail=None):
        count = reach * lon_cells
        from_a, from_b = lat_strips(own[:count], own[cells_n - count:], tail)
        sums = None
        if tail is not None:
            if n_lat == 4:
                sums = (tail + send(tail, "lat", swap(n_lat, 2))) + (from_a[count:] + from_b[count:])
            else:
                sums = lax.psum(tail, "lat")
            from_a, from_b = from_a[:count], from_b[:count]
        ext = stacked(own, from_a, from_b, reach)
        from_x, from_s = lon_send(*side_strips(ext, reach))
        return (from_a, from_b, from_x, from_s), sums

    vmem = pl.BlockSpec(memory_space=pltpu.VMEM)
    smem = pl.BlockSpec(memory_space=pltpu.SMEM)
    hbm = pl.BlockSpec(memory_space=pl.ANY)
    params = pltpu.CompilerParams(vmem_limit_bytes=VMEM_LIMIT)
    shape = lambda *dims: jax.ShapeDtypeStruct(dims, f32)
    scratch = lambda *dims: pltpu.VMEM(dims, f32)
    rows_h = lat_cells + 2 * FRAME
    rows_v = lat_cells + 2 * REACH
    width = lon_cells + 2 * FRAME
    band_rows = n_lon * own_rows
    dims = (lat_cells, lon_cells)
    field = shape(cells_n, levels)
    msg = shape(obs + obs // 2 + 8, LANES)
    wide, tall = shape(rows_h, width, levels), shape(rows_v, width, levels)
    wide_vmem, tall_vmem = scratch(rows_h, width, levels), scratch(rows_v, width, levels)
    field_vmem = scratch(cells_n, levels)
    jac_vmem = scratch(slots, obs, levels)
    faces_vmem = [wide_vmem] * 2 + [tall_vmem] * 3
    sems = lambda count: pltpu.SemaphoreType.DMA((count,))

    def call(kernel, name, outs, ins, scalars=0, far_in=(), far_out=False, scratches=()):
        out_specs = jax.tree.map(lambda _: vmem, outs)
        if far_out:
            out_specs = (hbm,) * far_out + out_specs[far_out:]
        specs = [smem] * scalars + [vmem] * (len(ins) - scalars) + [hbm] * len(far_in)
        return pl.pallas_call(
            kernel, out_shape=outs, in_specs=specs, out_specs=out_specs,
            scratch_shapes=list(scratches), compiler_params=params, name=name,
        )(*ins, *far_in)

    rows_own = jnp.pad(block_list[0].astype(f32), (0, 2 * LANES - slots), constant_values=-1.0)
    first = call(pack_kernel, "pack", shape(obs + 8, LANES),
                 (innovation, obs_weight, jnp.pad(rows_own.reshape(2, LANES), ((0, 6), (0, 0)))))
    band = gather_band(first)

    kh_lat = FRAME * lon_cells
    kv_lat = REACH * lon_cells
    kh2, kv2 = (jnp.sqrt(v).reshape(cells_n, levels) for v in (kappa_h, kappa_v))
    k_strips = lat_strips(
        jnp.concatenate([kh2[:kh_lat], kv2[:kv_lat]], 0),
        jnp.concatenate([kh2[cells_n - kh_lat:], kv2[cells_n - kv_lat:]], 0),
    )
    hx, hs = side_strips(stacked(kh2, k_strips[0][:kh_lat], k_strips[1][:kh_lat], FRAME), FRAME)
    vx, vs = side_strips(stacked(kv2, k_strips[0][kh_lat:], k_strips[1][kh_lat:], REACH), REACH)
    fold = lambda v: v.reshape(rows_v // 2, 2 * REACH, levels)
    k_messages = [jnp.concatenate([hx, fold(vx)], 0), jnp.concatenate([hs, fold(vs)], 0)]

    def place_of(row):
        row = row.astype(jnp.int32)
        key = (row // own_rows) ^ lon
        at = (key // 2 + parts * (key % 2)) * own_rows + row % own_rows
        return jnp.where((row >= 0) & (row < band_rows), at, -1)

    all_at = place_of(jnp.stack([piece[obs:obs + 2] for piece in band]).reshape(n_lon, 2 * LANES))
    row_iota = jnp.arange(band_rows, dtype=jnp.int32)
    row_hot = (all_at[:, :, None] == row_iota[None, None, :]).astype(jnp.bfloat16)
    own_at = place_of(rows_own)
    own_hot = (row_iota[:, None] == own_at[None, :]).astype(jnp.bfloat16)
    cells = jnp.clip(block_list[1], 0, cells_n - 1)
    cell_hot = (jnp.arange(cells_n, dtype=jnp.int32)[:, None] == cells[None, :]).astype(jnp.bfloat16)
    flags = jnp.stack([
        lat % 2, lon % 2, (lat == 0).astype(jnp.int32), (lat == n_lat - 1).astype(jnp.int32),
        pass_counts[0], pass_counts[1],
    ]).astype(jnp.int32)

    adj_scratch = [jac_vmem, scratch(2, obs, LANES), scratch(slots, levels), sems(slots // 32)]
    band[0], k_messages = lax.optimization_barrier((band[0], k_messages))
    k_sides = lon_send(*k_messages)
    own, weight = call(
        functools.partial(adjoint_kernel, True, parts), "adjoint_first",
        (field, shape(obs, band_rows)), (*band, own_hot, cell_hot), far_in=(jacobian,),
        scratches=[scratch(obs, band_rows)] + adj_scratch)
    faces = call(
        functools.partial(faces_kernel, dims), "faces", (wide, wide, tall, tall, tall),
        (flags, kh2, kv2, *k_strips, *k_sides), 1, far_out=5,
        scratches=faces_vmem + [wide_vmem, sems(5)])
    halos, _ = halo(own, FRAME)
    spread_scratch = faces_vmem + [jac_vmem] + [field_vmem] * 3 + [
        wide_vmem, scratch(lat_cells, width, levels), sems(10)]
    grad, spread, message = call(
        functools.partial(spread_kernel, dims, True), "spread_first", (field, field, msg),
        (flags, cells, own, *halos), 2, (*faces, jacobian), 2, spread_scratch)

    def adjoint(message):
        return call(
            functools.partial(adjoint_kernel, False, parts), "adjoint_next",
            (field, shape(16, LANES)), (*gather_band(message), row_hot, weight, own_hot, cell_hot),
            far_in=(jacobian,), scratches=adj_scratch)

    own, sums = adjoint(message)
    halos, scal0 = halo(own, FRAME, sums)
    image, spread_next, message = call(
        functools.partial(spread_kernel, dims, False), "spread_next", (field, field, msg),
        (flags, cells, own, *halos, scal0), 2, (*faces, jacobian, grad, spread), 2, spread_scratch)
    own, sums = adjoint(message)
    halos, scal1 = halo(own, REACH, sums)
    increment, residual = call(
        functools.partial(final_kernel, dims), "final", (field, field),
        (flags, own, *halos, scal0, scal1), 1,
        (*faces, grad, spread, image, spread_next), 0,
        faces_vmem + [field_vmem] * 4 + [wide_vmem, sems(9)])
    block = (lat_cells, lon_cells, levels)
    return increment.reshape(block), residual.reshape(block)


def solution(mesh):
    return jax.shard_map(
        local,
        mesh=mesh,
        in_specs=(
            P(None, ("lat", "lon")),
            P(None, ("lat", "lon")),
            P(("lat", "lon"), None, None),
            P(None, ("lat", "lon")),
            P(),
            P("lat", "lon", None),
            P("lat", "lon", None),
        ),
        out_specs=(P("lat", "lon", None), P("lat", "lon", None)),
        check_vma=False,
    )
```

profile of v0, /device:TPU:0, one launch (start us, length us, event | category | flops | bytes accessed | tf_op | source)
XLA Modules:
  0.0 162.9 jit_solution(4678678292326276583)
XLA Ops:
  0.6 0.8 slice_convert_fusion
  1.4 0.7 copy-done.2
  2.2 0.8 copy-done.3
  3.0 3.0 %collective-permute-start.2 = (f32[72,128]{1,0:T(8,128)S(1)}, f32[72,128]{1,0:T(8,128)S(1)}, u32[]{:S(2)}, u32[]{:S(2)}) collective-permute-start(f32[72,128]{1,0:T(8,128)S(1)} %pack.1.refs_0_), channel_id=1, source_target_pairs={{0,2},{1,3},{2,0},{3,1},{4,6},{5,7},{6,4},{7,5},{8,10},{9,11},{10,... | collective-permute-start | bytes 110600 | tf_op jit(solution)/shard_map/ppermute | solution.py:424
  6.0 2.6 %collective-permute-start.3 = (f32[72,128]{1,0:T(8,128)S(1)}, f32[72,128]{1,0:T(8,128)S(1)}, u32[]{:S(2)}, u32[]{:S(2)}) collective-permute-start(f32[72,128]{1,0:T(8,128)S(1)} %pack.1.refs_0_), channel_id=1, source_target_pairs={{0,4},{1,5},{2,6},{3,7},{4,0},{5,1},{6,2},{7,3},{8,12},{9,13},{10,... | collective-permute-start | bytes 110600 | tf_op jit(solution)/shard_map/ppermute | solution.py:424
  8.6 1.0 sqrt.6
  9.7 1.0 sqrt.7
  10.8 2.7 %collective-permute-start = (f32[576,128]{1,0:T(8,128)S(1)}, f32[576,128]{1,0:T(8,128)S(1)}, u32[]{:S(2)}, u32[]{:S(2)}) collective-permute-start(f32[576,128]{1,0:T(8,128)S(1)} %get-tuple-element.62), channel_id=1, source_target_pairs={{0,24},{8,16},{16,8},{24,0},{1,25},{9,17},{17,9},{25,1},{2,26},{10... | collective-permute-start | bytes 884744 | tf_op jit(solution)/shard_map/ppermute | solution.py:424
  14.9 6.8 %collective-permute-done.from_b = f32[576,128]{1,0:T(8,128)S(1)} collective-permute-done((f32[576,128]{1,0:T(8,128)S(1)}, f32[576,128]{1,0:T(8,128)S(1)}, u32[]{:S(2)}, u32[]{:S(2)}) %collective-permute-start) | collective-permute-done | bytes 294944 | tf_op jit(solution)/shard_map/ppermute | solution.py:424
  21.7 4.6 %collective-permute-done.1.from_a = f32[576,128]{1,0:T(8,128)S(1)} collective-permute-done((f32[576,128]{1,0:T(8,128)S(1)}, f32[576,128]{1,0:T(8,128)S(1)}, u32[]{:S(2)}, u32[]{:S(2)}) %collective-permute-start.1) | collective-permute-done | bytes 294944 | tf_op jit(solution)/shard_map/ppermute | solution.py:424
  26.4 0.8 slice_select_fusion.4
  27.3 0.9 copy-done.4
  28.2 1.0 pad_maximum_fusion.3
  29.2 4.6 %adjoint_first.1 = (f32[512,128]{1,0:T(8,128)S(1)}, f32[64,512]{1,0:T(8,128)S(1)}) custom-call(f32[72,128]{1,0:T(8,128)S(1)} %pack.1.refs_0_, f32[72,128]{1,0:T(8,128)S(1)} %collective-permute-done.2.refs_1_, f32[72,128]{1,0:T(8,128)S(1)} %collective-permute-done.3.refs_2_, f32[72,128]{1,0:T(8,128)S(1)} %collective-permute-done.4.refs_3_, ...), custom_call_target="tpu_custom_call" | custom-call | tf_op jit(solution)/shard_map/adjoint_first/pallas_call | solution.py:491
  33.9 1.5 collective-permute-start.10
  35.9 3.6 %collective-permute-start.14 = (f32[54,12,128]{2,1,0:T(8,128)}, f32[54,12,128]{2,1,0:T(8,128)S(1)}, u32[]{:S(2)}, u32[]{:S(2)}) collective-permute-start(f32[54,12,128]{2,1,0:T(8,128)} %get-tuple-element.27), channel_id=1, source_target_pairs={{0,7},{1,2},{2,1},{3,4},{4,3},{5,6},{6,5},{7,0},{8,15},{9,10},{10,... | collective-permute-start | bytes 995336 | tf_op jit(solution)/shard_map/ppermute | solution.py:424
  39.6 2.3 %collective-permute-done.10.refs_4_ = f32[384,128]{1,0:T(8,128)S(1)} collective-permute-done((f32[384,128]{1,0:T(8,128)S(1)}, f32[384,128]{1,0:T(8,128)S(1)}, u32[]{:S(2)}, u32[]{:S(2)}) %collective-permute-start.10) | collective-permute-done | bytes 196640 | tf_op jit(solution)/shard_map/ppermute | solution.py:424
  41.9 1.4 collective-permute-done.9.refs_3_
  43.4 0.9 slice_select_fusion.2
  44.3 3.4 %collective-permute-start.12 = (f32[40,12,128]{2,1,0:T(8,128)}, f32[40,12,128]{2,1,0:T(8,128)}, u32[]{:S(2)}, u32[]{:S(2)}) collective-permute-start(f32[40,12,128]{2,1,0:T(8,128)} %get-tuple-element.54), channel_id=1, source_target_pairs={{0,7},{1,2},{2,1},{3,4},{4,3},{5,6},{6,5},{7,0},{8,15},{9,10},{10,... | collective-permute-start | bytes 737288 | tf_op jit(solution)/shard_map/ppermute | solution.py:424
  47.8 2.5 %collective-permute-done.14.from_s = f32[54,12,128]{2,1,0:T(8,128)S(1)} collective-permute-done((f32[54,12,128]{2,1,0:T(8,128)}, f32[54,12,128]{2,1,0:T(8,128)S(1)}, u32[]{:S(2)}, u32[]{:S(2)}) %collective-permute-start.14) | collective-permute-done | bytes 331808 | tf_op jit(solution)/shard_map/ppermute | solution.py:424
  50.3 6.1 %faces.1 = (f32[40,56,128]{2,1,0:T(8,128)S(1)}, f32[40,56,128]{2,1,0:T(8,128)}, f32[28,56,128]{2,1,0:T(8,128)S(1)}, f32[28,56,128]{2,1,0:T(8,128)S(1)}, f32[28,56,128]{2,1,0:T(8,128)S(1)}) custom-call(s32[6]{0:T(128)S(1)} %stack.54.flags.refs_0_, f32[512,128]{1,0:T(8,128)S(1)} %bitcast.37, f32[512,128]{1,0:T(8,128)S(1)} %bitcast.38, ...), custom_call_target="tpu_custom_call" | custom-call | tf_op jit(solution)/shard_map/faces/pallas_call | solution.py:491
  56.4 1.0 collective-permute-done.12.refs_6_
  57.5 16.4 %spread_first.1 = (f32[512,128]{1,0:T(8,128)S(1)}, f32[512,128]{1,0:T(8,128)S(1)}, f32[104,128]{1,0:T(8,128)S(1)}) custom-call(s32[6]{0:T(128)S(1)} %stack.54.flags.refs_0_, s32[192]{0:T(256)S(1)} %bitcast.45, f32[512,128]{1,0:T(8,128)S(1)} %get-tuple-element.25.refs_2_, f32[384,128]{1,0:T(8,128)S(1)} %collective-permute-done.9.refs_3_, ...), custom_call_target="tpu_custom_call" | custom-call | tf_op jit(solution)/shard_map/spread_first/pallas_call | solution.py:491
  74.0 2.4 %collective-permute-start.16 = (f32[104,128]{1,0:T(8,128)S(1)}, f32[104,128]{1,0:T(8,128)S(1)}, u32[]{:S(2)}, u32[]{:S(2)}) collective-permute-start(f32[104,128]{1,0:T(8,128)S(1)} %get-tuple-element.33.refs_0_), channel_id=1, source_target_pairs={{0,4},{1,5},{2,6},{3,7},{4,0},{5,1},{6,2},{7,3},{8,12},{9,13},{10,... | collective-permute-start | bytes 159752 | tf_op jit(solution)/shard_map/ppermute | solution.py:424
  76.4 2.0 %collective-permute-start.17 = (f32[104,128]{1,0:T(8,128)S(1)}, f32[104,128]{1,0:T(8,128)S(1)}, u32[]{:S(2)}, u32[]{:S(2)}) collective-permute-start(f32[104,128]{1,0:T(8,128)S(1)} %get-tuple-element.33.refs_0_), channel_id=1, source_target_pairs={{0,6},{1,7},{2,4},{3,5},{4,2},{5,3},{6,0},{7,1},{8,14},{9,15},{10,... | collective-permute-start | bytes 159752 | tf_op jit(solution)/shard_map/ppermute | solution.py:424
  79.2 3.1 %collective-permute-done.17.refs_3_ = f32[104,128]{1,0:T(8,128)S(1)} collective-permute-done((f32[104,128]{1,0:T(8,128)S(1)}, f32[104,128]{1,0:T(8,128)S(1)}, u32[]{:S(2)}, u32[]{:S(2)}) %collective-permute-start.17) | collective-permute-done | bytes 53280 | tf_op jit(solution)/shard_map/ppermute | solution.py:424
  82.8 0.7 collective-permute-done.21.refs_7_
  83.5 5.2 %adjoint_next.2 = (f32[512,128]{1,0:T(8,128)S(1)}, f32[16,128]{1,0:T(8,128)S(1)}) custom-call(f32[104,128]{1,0:T(8,128)S(1)} %get-tuple-element.33.refs_0_, f32[104,128]{1,0:T(8,128)S(1)} %collective-permute-done.15.refs_1_, f32[104,128]{1,0:T(8,128)S(1)} %collective-permute-done.16.refs_2_, f32[104,128]{1,0:T(8,128)S(1)} %collective-permute-done.17.refs_3_, ...), custom_call_target="tpu_custom_call" | custom-call | tf_op jit(solution)/shard_map/adjoint_next/pallas_call | solution.py:491
  88.8 1.6 collective-permute-start.22
  90.4 1.5 collective-permute-start.23
  91.9 4.9 %collective-permute-done.22 = f32[400,128]{1,0:T(8,128)S(1)} collective-permute-done((f32[400,128]{1,0:T(8,128)S(1)}, f32[400,128]{1,0:T(8,128)S(1)}, u32[]{:S(2)}, u32[]{:S(2)}) %collective-permute-start.22) | collective-permute-done | bytes 204832 | tf_op jit(solution)/shard_map/ppermute | solution.py:424
  96.8 4.6 %collective-permute-done.23 = f32[400,128]{1,0:T(8,128)S(1)} collective-permute-done((f32[400,128]{1,0:T(8,128)S(1)}, f32[400,128]{1,0:T(8,128)S(1)}, u32[]{:S(2)}, u32[]{:S(2)}) %collective-permute-start.23) | collective-permute-done | bytes 204832 | tf_op jit(solution)/shard_map/ppermute | solution.py:424
  101.6 2.1 %collective-permute-start.25 = (f32[40,12,128]{2,1,0:T(8,128)S(1)}, f32[40,12,128]{2,1,0:T(8,128)S(1)}, u32[]{:S(2)}, u32[]{:S(2)}) collective-permute-start(f32[40,12,128]{2,1,0:T(8,128)S(1)} %get-tuple-element.52), channel_id=1, source_target_pairs={{0,7},{1,2},{2,1},{3,4},{4,3},{5,6},{6,5},{7,0},{8,15},{9,10},{10,... | collective-permute-start | bytes 737288 | tf_op jit(solution)/shard_map/ppermute | solution.py:424
  104.2 3.1 %collective-permute-done.26 = f32[16,128]{1,0:T(8,128)S(1)} collective-permute-done((f32[16,128]{1,0:T(8,128)S(1)}, f32[16,128]{1,0:T(8,128)S(1)}, u32[]{:S(2)}, u32[]{:S(2)}) %collective-permute-start.26) | collective-permute-done | bytes 8224 | tf_op jit(solution)/shard_map/ppermute | solution.py:424
  107.4 4.9 %collective-permute-done.25.refs_6_ = f32[40,12,128]{2,1,0:T(8,128)S(1)} collective-permute-done((f32[40,12,128]{2,1,0:T(8,128)S(1)}, f32[40,12,128]{2,1,0:T(8,128)S(1)}, u32[]{:S(2)}, u32[]{:S(2)}) %collective-permute-start.25) | collective-permute-done | bytes 245792 | tf_op jit(solution)/shard_map/ppermute | solution.py:424
  112.3 16.1 %spread_next.1 = (f32[512,128]{1,0:T(8,128)S(1)}, f32[512,128]{1,0:T(8,128)S(1)}, f32[104,128]{1,0:T(8,128)S(1)}) custom-call(s32[6]{0:T(128)S(1)} %stack.54.flags.refs_0_, s32[192]{0:T(256)S(1)} %bitcast.46, f32[512,128]{1,0:T(8,128)S(1)} %get-tuple-element.35.refs_2_, f32[384,128]{1,0:T(8,128)S(1)} %get-tuple-element.80.refs_3_, ...), custom_call_target="tpu_custom_call" | custom-call | tf_op jit(solution)/shard_map/spread_next/pallas_call | solution.py:491
  128.6 4.3 %collective-permute-start.29 = (f32[104,128]{1,0:T(8,128)S(1)}, f32[104,128]{1,0:T(8,128)S(1)}, u32[]{:S(2)}, u32[]{:S(2)}) collective-permute-start(f32[104,128]{1,0:T(8,128)S(1)} %get-tuple-element.39.refs_0_), channel_id=1, source_target_pairs={{0,6},{1,7},{2,4},{3,5},{4,2},{5,3},{6,0},{7,1},{8,14},{9,15},{10,... | collective-permute-start | bytes 159752 | tf_op jit(solution)/shard_map/ppermute | solution.py:424
  133.7 2.3 %collective-permute-done.29.refs_3_ = f32[104,128]{1,0:T(8,128)S(1)} collective-permute-done((f32[104,128]{1,0:T(8,128)S(1)}, f32[104,128]{1,0:T(8,128)S(1)}, u32[]{:S(2)}, u32[]{:S(2)}) %collective-permute-start.29) | collective-permute-done | bytes 53280 | tf_op jit(solution)/shard_map/ppermute | solution.py:424
  136.0 1.2 collective-permute-done.33.refs_7_
  137.3 5.2 %adjoint_next.3 = (f32[512,128]{1,0:T(8,128)S(1)}, f32[16,128]{1,0:T(8,128)S(1)}) custom-call(f32[104,128]{1,0:T(8,128)S(1)} %get-tuple-element.39.refs_0_, f32[104,128]{1,0:T(8,128)S(1)} %collective-permute-done.27.refs_1_, f32[104,128]{1,0:T(8,128)S(1)} %collective-permute-done.28.refs_2_, f32[104,128]{1,0:T(8,128)S(1)} %collective-permute-done.29.refs_3_, ...), custom_call_target="tpu_custom_call" | custom-call | tf_op jit(solution)/shard_map/adjoint_next/pallas_call | solution.py:491
  142.5 1.8 %collective-permute-start.34 = (f32[208,128]{1,0:T(8,128)S(1)}, f32[208,128]{1,0:T(8,128)S(1)}, u32[]{:S(2)}, u32[]{:S(2)}) collective-permute-start(f32[208,128]{1,0:T(8,128)S(1)} %get-tuple-element.85), channel_id=1, source_target_pairs={{0,8},{8,0},{16,24},{24,16},{1,9},{9,1},{17,25},{25,17},{2,10},{10... | collective-permute-start | bytes 319496 | tf_op jit(solution)/shard_map/ppermute | solution.py:424
  144.8 1.3 collective-permute-start.38
  146.1 2.3 %collective-permute-done.34 = f32[208,128]{1,0:T(8,128)S(1)} collective-permute-done((f32[208,128]{1,0:T(8,128)S(1)}, f32[208,128]{1,0:T(8,128)S(1)}, u32[]{:S(2)}, u32[]{:S(2)}) %collective-permute-start.34) | collective-permute-done | bytes 106528 | tf_op jit(solution)/shard_map/ppermute | solution.py:424
  148.4 2.0 %collective-permute-done.35 = f32[208,128]{1,0:T(8,128)S(1)} collective-permute-done((f32[208,128]{1,0:T(8,128)S(1)}, f32[208,128]{1,0:T(8,128)S(1)}, u32[]{:S(2)}, u32[]{:S(2)}) %collective-permute-start.35) | collective-permute-done | bytes 106528 | tf_op jit(solution)/shard_map/ppermute | solution.py:424
  150.5 2.4 %collective-permute-start.37 = (f32[28,6,128]{2,1,0:T(8,128)S(1)}, f32[28,6,128]{2,1,0:T(8,128)S(1)}, u32[]{:S(2)}, u32[]{:S(2)}) collective-permute-start(f32[28,6,128]{2,1,0:T(8,128)S(1)} %get-tuple-element.46), channel_id=1, source_target_pairs={{0,7},{1,2},{2,1},{3,4},{4,3},{5,6},{6,5},{7,0},{8,15},{9,10},{10,... | collective-permute-start | bytes 258056 | tf_op jit(solution)/shard_map/ppermute | solution.py:424
  153.0 4.0 %collective-permute-done.37.refs_5_ = f32[28,6,128]{2,1,0:T(8,128)S(1)} collective-permute-done((f32[28,6,128]{2,1,0:T(8,128)S(1)}, f32[28,6,128]{2,1,0:T(8,128)S(1)}, u32[]{:S(2)}, u32[]{:S(2)}) %collective-permute-start.37) | collective-permute-done | bytes 86048 | tf_op jit(solution)/shard_map/ppermute | solution.py:424
  156.9 5.9 %final.1 = (f32[512,128]{1,0:T(8,128)}, f32[512,128]{1,0:T(8,128)}) custom-call(s32[6]{0:T(128)S(1)} %stack.54.flags.refs_0_, f32[512,128]{1,0:T(8,128)S(1)} %get-tuple-element.40.refs_1_, f32[192,128]{1,0:T(8,128)S(1)} %get-tuple-element.82.refs_2_, f32[192,128]{1,0:T(8,128)S(1)} %get-tuple-element.83.refs_3_, ...), custom_call_target="tpu_custom_call" | custom-call | tf_op jit(solution)/shard_map/final/pallas_call | solution.py:491
  (100 shorter events, 6.4 us)
Async XLA Ops:
  1.4 0.8 copy-start.2
  2.2 0.8 copy-start.3
  3.0 11.2 %collective-permute-start.2 = (f32[72,128]{1,0:T(8,128)S(1)}, f32[72,128]{1,0:T(8,128)S(1)}, u32[]{:S(2)}, u32[]{:S(2)}) collective-permute-start(f32[72,128]{1,0:T(8,128)S(1)} %pack.1.refs_0_), channel_id=1, source_target_pairs={{0,2},{1,3},{2,0},{3,1},{4,6},{5,7},{6,4},{7,5},{8,10},{9,11},{10,... | collective-permute-start | bytes 110600 | tf_op jit(solution)/shard_map/ppermute | solution.py:424
  6.0 8.3 %collective-permute-start.3 = (f32[72,128]{1,0:T(8,128)S(1)}, f32[72,128]{1,0:T(8,128)S(1)}, u32[]{:S(2)}, u32[]{:S(2)}) collective-permute-start(f32[72,128]{1,0:T(8,128)S(1)} %pack.1.refs_0_), channel_id=1, source_target_pairs={{0,4},{1,5},{2,6},{3,7},{4,0},{5,1},{6,2},{7,3},{8,12},{9,13},{10,... | collective-permute-start | bytes 110600 | tf_op jit(solution)/shard_map/ppermute | solution.py:424
  8.6 6.2 %collective-permute-start.4 = (f32[72,128]{1,0:T(8,128)S(1)}, f32[72,128]{1,0:T(8,128)S(1)}, u32[]{:S(2)}, u32[]{:S(2)}) collective-permute-start(f32[72,128]{1,0:T(8,128)S(1)} %pack.1.refs_0_), channel_id=1, source_target_pairs={{0,6},{1,7},{2,4},{3,5},{4,2},{5,3},{6,0},{7,1},{8,14},{9,15},{10,... | collective-permute-start | bytes 110600 | tf_op jit(solution)/shard_map/ppermute | solution.py:424
  10.8 10.9 %collective-permute-start = (f32[576,128]{1,0:T(8,128)S(1)}, f32[576,128]{1,0:T(8,128)S(1)}, u32[]{:S(2)}, u32[]{:S(2)}) collective-permute-start(f32[576,128]{1,0:T(8,128)S(1)} %get-tuple-element.62), channel_id=1, source_target_pairs={{0,24},{8,16},{16,8},{24,0},{1,25},{9,17},{17,9},{25,1},{2,26},{10... | collective-permute-start | bytes 884744 | tf_op jit(solution)/shard_map/ppermute | solution.py:424
  13.5 12.8 %collective-permute-start.1 = (f32[576,128]{1,0:T(8,128)S(1)}, f32[576,128]{1,0:T(8,128)S(1)}, u32[]{:S(2)}, u32[]{:S(2)}) collective-permute-start(f32[576,128]{1,0:T(8,128)S(1)} %get-tuple-element.63), channel_id=1, source_target_pairs={{0,8},{8,0},{16,24},{24,16},{1,9},{9,1},{17,25},{25,17},{2,10},{10... | collective-permute-start | bytes 884744 | tf_op jit(solution)/shard_map/ppermute | solution.py:424
  14.3 14.9 %collective-permute-start.5 = (f32[72,128]{1,0:T(8,128)S(1)}, f32[72,128]{1,0:T(8,128)S(1)}, u32[]{:S(2)}, u32[]{:S(2)}) collective-permute-start(f32[72,128]{1,0:T(8,128)S(1)} %pack.1.refs_0_), channel_id=1, source_target_pairs={{0,1},{1,0},{2,3},{3,2},{4,5},{5,4},{6,7},{7,6},{8,9},{9,8},{10,11... | collective-permute-start | bytes 110600 | tf_op jit(solution)/shard_map/ppermute | solution.py:424
  14.3 14.9 %collective-permute-start.6 = (f32[72,128]{1,0:T(8,128)S(1)}, f32[72,128]{1,0:T(8,128)S(1)}, u32[]{:S(2)}, u32[]{:S(2)}) collective-permute-start(f32[72,128]{1,0:T(8,128)S(1)} %collective-permute-done.2.refs_1_), channel_id=1, source_target_pairs={{0,1},{1,0},{2,3},{3,2},{4,5},{5,4},{6,7},{7,6},{8,9},{9,8},{10,11... | collective-permute-start | bytes 110600 | tf_op jit(solution)/shard_map/ppermute | solution.py:424
  14.8 14.4 %collective-permute-start.7 = (f32[72,128]{1,0:T(8,128)S(1)}, f32[72,128]{1,0:T(8,128)S(1)}, u32[]{:S(2)}, u32[]{:S(2)}) collective-permute-start(f32[72,128]{1,0:T(8,128)S(1)} %collective-permute-done.3.refs_2_), channel_id=1, source_target_pairs={{0,1},{1,0},{2,3},{3,2},{4,5},{5,4},{6,7},{7,6},{8,9},{9,8},{10,11... | collective-permute-start | bytes 110600 | tf_op jit(solution)/shard_map/ppermute | solution.py:424
  21.7 7.5 %collective-permute-start.8 = (f32[72,128]{1,0:T(8,128)S(1)}, f32[72,128]{1,0:T(8,128)S(1)}, u32[]{:S(2)}, u32[]{:S(2)}) collective-permute-start(f32[72,128]{1,0:T(8,128)S(1)} %collective-permute-done.4.refs_3_), channel_id=1, source_target_pairs={{0,1},{1,0},{2,3},{3,2},{4,5},{5,4},{6,7},{7,6},{8,9},{9,8},{10,11... | collective-permute-start | bytes 110600 | tf_op jit(solution)/shard_map/ppermute | solution.py:424
  27.2 1.0 copy-start.4
  29.2 4.6 %copy-start = (f32[72,128]{1,0:T(8,128)}, f32[72,128]{1,0:T(8,128)S(1)}, u32[]{:S(2)}) copy-start(f32[72,128]{1,0:T(8,128)S(1)} %collective-permute-done.7.refs_6_) | copy-start | bytes 110596
  29.2 4.6 %copy-start.1 = (f32[72,128]{1,0:T(8,128)}, f32[72,128]{1,0:T(8,128)S(1)}, u32[]{:S(2)}) copy-start(f32[72,128]{1,0:T(8,128)S(1)} %collective-permute-done.8.refs_7_) | copy-start | bytes 110596
  33.8 13.8 %copy-start.5 = (s32[2]{0:T(128)S(1)}, s32[2]{0:T(128)}, u32[]{:S(2)}) copy-start(s32[2]{0:T(128)} %param.11) | copy-start | bytes 28
  33.8 13.9 %slice-start = ((f32[72,128]{1,0:T(8,128)}), f32[2,128]{1,0:T(2,128)S(1)}, s32[]{:S(2)}) async-start(f32[72,128]{1,0:T(8,128)} %copy-done), calls=%async_computation | async-start | bytes 2048 | tf_op jit(solution)/shard_map/slice | solution.py:519
  33.8 13.9 %slice-start.1 = ((f32[72,128]{1,0:T(8,128)}), f32[2,128]{1,0:T(2,128)S(1)}, s32[]{:S(2)}) async-start(f32[72,128]{1,0:T(8,128)} %copy-done.1), calls=%async_computation.1 | async-start | bytes 2048 | tf_op jit(solution)/shard_map/slice | solution.py:519
  33.9 8.0 %collective-permute-start.10 = (f32[384,128]{1,0:T(8,128)S(1)}, f32[384,128]{1,0:T(8,128)S(1)}, u32[]{:S(2)}, u32[]{:S(2)}) collective-permute-start(f32[384,128]{1,0:T(8,128)S(1)} %get-tuple-element.72), channel_id=1, source_target_pairs={{0,24},{8,16},{16,8},{24,0},{1,25},{9,17},{17,9},{25,1},{2,26},{10... | collective-permute-start | bytes 589832 | tf_op jit(solution)/shard_map/ppermute | solution.py:424
  35.4 7.9 %collective-permute-start.9 = (f32[384,128]{1,0:T(8,128)S(1)}, f32[384,128]{1,0:T(8,128)S(1)}, u32[]{:S(2)}, u32[]{:S(2)}) collective-permute-start(f32[384,128]{1,0:T(8,128)S(1)} %get-tuple-element.73), channel_id=1, source_target_pairs={{0,8},{8,0},{16,24},{24,16},{1,9},{9,1},{17,25},{25,17},{2,10},{10... | collective-permute-start | bytes 589832 | tf_op jit(solution)/shard_map/ppermute | solution.py:424
  35.9 11.9 %collective-permute-start.13 = (f32[54,12,128]{2,1,0:T(8,128)}, f32[54,12,128]{2,1,0:T(8,128)S(1)}, u32[]{:S(2)}, u32[]{:S(2)}) collective-permute-start(f32[54,12,128]{2,1,0:T(8,128)} %get-tuple-element.26), channel_id=1, source_target_pairs={{0,1},{1,0},{2,3},{3,2},{4,5},{5,4},{6,7},{7,6},{8,9},{9,8},{10,11... | collective-permute-start | bytes 995336 | tf_op jit(solution)/shard_map/ppermute | solution.py:424
  35.9 14.4 %collective-permute-start.14 = (f32[54,12,128]{2,1,0:T(8,128)}, f32[54,12,128]{2,1,0:T(8,128)S(1)}, u32[]{:S(2)}, u32[]{:S(2)}) collective-permute-start(f32[54,12,128]{2,1,0:T(8,128)} %get-tuple-element.27), channel_id=1, source_target_pairs={{0,7},{1,2},{2,1},{3,4},{4,3},{5,6},{6,5},{7,0},{8,15},{9,10},{10,... | collective-permute-start | bytes 995336 | tf_op jit(solution)/shard_map/ppermute | solution.py:424
  44.3 12.2 %collective-permute-start.11 = (f32[40,12,128]{2,1,0:T(8,128)}, f32[40,12,128]{2,1,0:T(8,128)}, u32[]{:S(2)}, u32[]{:S(2)}) collective-permute-start(f32[40,12,128]{2,1,0:T(8,128)} %get-tuple-element.55), channel_id=1, source_target_pairs={{0,1},{1,0},{2,3},{3,2},{4,5},{5,4},{6,7},{7,6},{8,9},{9,8},{10,11... | collective-permute-start | bytes 737288 | tf_op jit(solution)/shard_map/ppermute | solution.py:424
  44.3 13.2 %collective-permute-start.12 = (f32[40,12,128]{2,1,0:T(8,128)}, f32[40,12,128]{2,1,0:T(8,128)}, u32[]{:S(2)}, u32[]{:S(2)}) collective-permute-start(f32[40,12,128]{2,1,0:T(8,128)} %get-tuple-element.54), channel_id=1, source_target_pairs={{0,7},{1,2},{2,1},{3,4},{4,3},{5,6},{6,5},{7,0},{8,15},{9,10},{10,... | collective-permute-start | bytes 737288 | tf_op jit(solution)/shard_map/ppermute | solution.py:424
  73.9 4.6 %collective-permute-start.15 = (f32[104,128]{1,0:T(8,128)S(1)}, f32[104,128]{1,0:T(8,128)S(1)}, u32[]{:S(2)}, u32[]{:S(2)}) collective-permute-start(f32[104,128]{1,0:T(8,128)S(1)} %get-tuple-element.33.refs_0_), channel_id=1, source_target_pairs={{0,2},{1,3},{2,0},{3,1},{4,6},{5,7},{6,4},{7,5},{8,10},{9,11},{10,... | collective-permute-start | bytes 159752 | tf_op jit(solution)/shard_map/ppermute | solution.py:424
  74.0 5.2 %collective-permute-start.16 = (f32[104,128]{1,0:T(8,128)S(1)}, f32[104,128]{1,0:T(8,128)S(1)}, u32[]{:S(2)}, u32[]{:S(2)}) collective-permute-start(f32[104,128]{1,0:T(8,128)S(1)} %get-tuple-element.33.refs_0_), channel_id=1, source_target_pairs={{0,4},{1,5},{2,6},{3,7},{4,0},{5,1},{6,2},{7,3},{8,12},{9,13},{10,... | collective-permute-start | bytes 159752 | tf_op jit(solution)/shard_map/ppermute | solution.py:424
  76.4 5.9 %collective-permute-start.17 = (f32[104,128]{1,0:T(8,128)S(1)}, f32[104,128]{1,0:T(8,128)S(1)}, u32[]{:S(2)}, u32[]{:S(2)}) collective-permute-start(f32[104,128]{1,0:T(8,128)S(1)} %get-tuple-element.33.refs_0_), channel_id=1, source_target_pairs={{0,6},{1,7},{2,4},{3,5},{4,2},{5,3},{6,0},{7,1},{8,14},{9,15},{10,... | collective-permute-start | bytes 159752 | tf_op jit(solution)/shard_map/ppermute | solution.py:424
  78.4 4.4 %collective-permute-start.18 = (f32[104,128]{1,0:T(8,128)S(1)}, f32[104,128]{1,0:T(8,128)S(1)}, u32[]{:S(2)}, u32[]{:S(2)}) collective-permute-start(f32[104,128]{1,0:T(8,128)S(1)} %get-tuple-element.33.refs_0_), channel_id=1, source_target_pairs={{0,1},{1,0},{2,3},{3,2},{4,5},{5,4},{6,7},{7,6},{8,9},{9,8},{10,11... | collective-permute-start | bytes 159752 | tf_op jit(solution)/shard_map/ppermute | solution.py:424
  78.5 4.3 %collective-permute-start.19 = (f32[104,128]{1,0:T(8,128)S(1)}, f32[104,128]{1,0:T(8,128)S(1)}, u32[]{:S(2)}, u32[]{:S(2)}) collective-permute-start(f32[104,128]{1,0:T(8,128)S(1)} %collective-permute-done.15.refs_1_), channel_id=1, source_target_pairs={{0,1},{1,0},{2,3},{3,2},{4,5},{5,4},{6,7},{7,6},{8,9},{9,8},{10,11... | collective-permute-start | bytes 159752 | tf_op jit(solution)/shard_map/ppermute | solution.py:424
  79.2 3.6 %collective-permute-start.20 = (f32[104,128]{1,0:T(8,128)S(1)}, f32[104,128]{1,0:T(8,128)S(1)}, u32[]{:S(2)}, u32[]{:S(2)}) collective-permute-start(f32[104,128]{1,0:T(8,128)S(1)} %collective-permute-done.16.refs_2_), channel_id=1, source_target_pairs={{0,1},{1,0},{2,3},{3,2},{4,5},{5,4},{6,7},{7,6},{8,9},{9,8},{10,11... | collective-permute-start | bytes 159752 | tf_op jit(solution)/shard_map/ppermute | solution.py:424
  82.3 1.2 collective-permute-start.21
  88.8 8.0 %collective-permute-start.22 = (f32[400,128]{1,0:T(8,128)S(1)}, f32[400,128]{1,0:T(8,128)S(1)}, u32[]{:S(2)}, u32[]{:S(2)}) collective-permute-start(f32[400,128]{1,0:T(8,128)S(1)} %get-tuple-element.87), channel_id=1, source_target_pairs={{0,8},{8,0},{16,24},{24,16},{1,9},{9,1},{17,25},{25,17},{2,10},{10... | collective-permute-start | bytes 614408 | tf_op jit(solution)/shard_map/ppermute | solution.py:424
  90.4 11.0 %collective-permute-start.23 = (f32[400,128]{1,0:T(8,128)S(1)}, f32[400,128]{1,0:T(8,128)S(1)}, u32[]{:S(2)}, u32[]{:S(2)}) collective-permute-start(f32[400,128]{1,0:T(8,128)S(1)} %get-tuple-element.86), channel_id=1, source_target_pairs={{0,24},{8,16},{16,8},{24,0},{1,25},{9,17},{17,9},{25,1},{2,26},{10... | collective-permute-start | bytes 614408 | tf_op jit(solution)/shard_map/ppermute | solution.py:424
  101.5 5.8 %collective-permute-start.24 = (f32[40,12,128]{2,1,0:T(8,128)S(1)}, f32[40,12,128]{2,1,0:T(8,128)S(1)}, u32[]{:S(2)}, u32[]{:S(2)}) collective-permute-start(f32[40,12,128]{2,1,0:T(8,128)S(1)} %get-tuple-element.53), channel_id=1, source_target_pairs={{0,1},{1,0},{2,3},{3,2},{4,5},{5,4},{6,7},{7,6},{8,9},{9,8},{10,11... | collective-permute-start | bytes 737288 | tf_op jit(solution)/shard_map/ppermute | solution.py:424
  101.6 10.7 %collective-permute-start.25 = (f32[40,12,128]{2,1,0:T(8,128)S(1)}, f32[40,12,128]{2,1,0:T(8,128)S(1)}, u32[]{:S(2)}, u32[]{:S(2)}) collective-permute-start(f32[40,12,128]{2,1,0:T(8,128)S(1)} %get-tuple-element.52), channel_id=1, source_target_pairs={{0,7},{1,2},{2,1},{3,4},{4,3},{5,6},{6,5},{7,0},{8,15},{9,10},{10,... | collective-permute-start | bytes 737288 | tf_op jit(solution)/shard_map/ppermute | solution.py:424
  103.7 3.7 %collective-permute-start.26 = (f32[16,128]{1,0:T(8,128)S(1)}, f32[16,128]{1,0:T(8,128)S(1)}, u32[]{:S(2)}, u32[]{:S(2)}) collective-permute-start(f32[16,128]{1,0:T(8,128)S(1)} %get-tuple-element.36), channel_id=1, source_target_pairs={{0,16},{8,24},{16,0},{24,8},{1,17},{9,25},{17,1},{25,9},{2,18},{10... | collective-permute-start | bytes 24584 | tf_op jit(solution)/shard_map/ppermute | solution.py:424
  128.4 4.5 %collective-permute-start.27 = (f32[104,128]{1,0:T(8,128)S(1)}, f32[104,128]{1,0:T(8,128)S(1)}, u32[]{:S(2)}, u32[]{:S(2)}) collective-permute-start(f32[104,128]{1,0:T(8,128)S(1)} %get-tuple-element.39.refs_0_), channel_id=1, source_target_pairs={{0,2},{1,3},{2,0},{3,1},{4,6},{5,7},{6,4},{7,5},{8,10},{9,11},{10,... | collective-permute-start | bytes 159752 | tf_op jit(solution)/shard_map/ppermute | solution.py:424
  128.5 5.2 %collective-permute-start.28 = (f32[104,128]{1,0:T(8,128)S(1)}, f32[104,128]{1,0:T(8,128)S(1)}, u32[]{:S(2)}, u32[]{:S(2)}) collective-permute-start(f32[104,128]{1,0:T(8,128)S(1)} %get-tuple-element.39.refs_0_), channel_id=1, source_target_pairs={{0,4},{1,5},{2,6},{3,7},{4,0},{5,1},{6,2},{7,3},{8,12},{9,13},{10,... | collective-permute-start | bytes 159752 | tf_op jit(solution)/shard_map/ppermute | solution.py:424
  128.6 7.4 %collective-permute-start.29 = (f32[104,128]{1,0:T(8,128)S(1)}, f32[104,128]{1,0:T(8,128)S(1)}, u32[]{:S(2)}, u32[]{:S(2)}) collective-permute-start(f32[104,128]{1,0:T(8,128)S(1)} %get-tuple-element.39.refs_0_), channel_id=1, source_target_pairs={{0,6},{1,7},{2,4},{3,5},{4,2},{5,3},{6,0},{7,1},{8,14},{9,15},{10,... | collective-permute-start | bytes 159752 | tf_op jit(solution)/shard_map/ppermute | solution.py:424
  132.9 3.1 %collective-permute-start.30 = (f32[104,128]{1,0:T(8,128)S(1)}, f32[104,128]{1,0:T(8,128)S(1)}, u32[]{:S(2)}, u32[]{:S(2)}) collective-permute-start(f32[104,128]{1,0:T(8,128)S(1)} %get-tuple-element.39.refs_0_), channel_id=1, source_target_pairs={{0,1},{1,0},{2,3},{3,2},{4,5},{5,4},{6,7},{7,6},{8,9},{9,8},{10,11... | collective-permute-start | bytes 159752 | tf_op jit(solution)/shard_map/ppermute | solution.py:424
  132.9 3.1 %collective-permute-start.31 = (f32[104,128]{1,0:T(8,128)S(1)}, f32[104,128]{1,0:T(8,128)S(1)}, u32[]{:S(2)}, u32[]{:S(2)}) collective-permute-start(f32[104,128]{1,0:T(8,128)S(1)} %collective-permute-done.27.refs_1_), channel_id=1, source_target_pairs={{0,1},{1,0},{2,3},{3,2},{4,5},{5,4},{6,7},{7,6},{8,9},{9,8},{10,11... | collective-permute-start | bytes 159752 | tf_op jit(solution)/shard_map/ppermute | solution.py:424
  133.7 2.3 %collective-permute-start.32 = (f32[104,128]{1,0:T(8,128)S(1)}, f32[104,128]{1,0:T(8,128)S(1)}, u32[]{:S(2)}, u32[]{:S(2)}) collective-permute-start(f32[104,128]{1,0:T(8,128)S(1)} %collective-permute-done.28.refs_2_), channel_id=1, source_target_pairs={{0,1},{1,0},{2,3},{3,2},{4,5},{5,4},{6,7},{7,6},{8,9},{9,8},{10,11... | collective-permute-start | bytes 159752 | tf_op jit(solution)/shard_map/ppermute | solution.py:424
  136.0 1.2 collective-permute-start.33
  142.5 5.9 %collective-permute-start.34 = (f32[208,128]{1,0:T(8,128)S(1)}, f32[208,128]{1,0:T(8,128)S(1)}, u32[]{:S(2)}, u32[]{:S(2)}) collective-permute-start(f32[208,128]{1,0:T(8,128)S(1)} %get-tuple-element.85), channel_id=1, source_target_pairs={{0,8},{8,0},{16,24},{24,16},{1,9},{9,1},{17,25},{25,17},{2,10},{10... | collective-permute-start | bytes 319496 | tf_op jit(solution)/shard_map/ppermute | solution.py:424
  144.3 6.0 %collective-permute-start.35 = (f32[208,128]{1,0:T(8,128)S(1)}, f32[208,128]{1,0:T(8,128)S(1)}, u32[]{:S(2)}, u32[]{:S(2)}) collective-permute-start(f32[208,128]{1,0:T(8,128)S(1)} %get-tuple-element.84), channel_id=1, source_target_pairs={{0,24},{8,16},{16,8},{24,0},{1,25},{9,17},{17,9},{25,1},{2,26},{10... | collective-permute-start | bytes 319496 | tf_op jit(solution)/shard_map/ppermute | solution.py:424
  144.8 8.2 %collective-permute-start.38 = (f32[16,128]{1,0:T(8,128)S(1)}, f32[16,128]{1,0:T(8,128)S(1)}, u32[]{:S(2)}, u32[]{:S(2)}) collective-permute-start(f32[16,128]{1,0:T(8,128)S(1)} %get-tuple-element.41), channel_id=1, source_target_pairs={{0,16},{8,24},{16,0},{24,8},{1,17},{9,25},{17,1},{25,9},{2,18},{10... | collective-permute-start | bytes 24584 | tf_op jit(solution)/shard_map/ppermute | solution.py:424
  150.5 2.5 %collective-permute-start.36 = (f32[28,6,128]{2,1,0:T(8,128)S(1)}, f32[28,6,128]{2,1,0:T(8,128)S(1)}, u32[]{:S(2)}, u32[]{:S(2)}) collective-permute-start(f32[28,6,128]{2,1,0:T(8,128)S(1)} %broadcast_select_fusion.5), channel_id=1, source_target_pairs={{0,1},{1,0},{2,3},{3,2},{4,5},{5,4},{6,7},{7,6},{8,9},{9,8},{10,11... | collective-permute-start | bytes 258056 | tf_op jit(solution)/shard_map/ppermute | solution.py:424
  150.5 6.4 %collective-permute-start.37 = (f32[28,6,128]{2,1,0:T(8,128)S(1)}, f32[28,6,128]{2,1,0:T(8,128)S(1)}, u32[]{:S(2)}, u32[]{:S(2)}) collective-permute-start(f32[28,6,128]{2,1,0:T(8,128)S(1)} %get-tuple-element.46), channel_id=1, source_target_pairs={{0,7},{1,2},{2,1},{3,4},{4,3},{5,6},{6,5},{7,0},{8,15},{9,10},{10,... | collective-permute-start | bytes 258056 | tf_op jit(solution)/shard_map/ppermute | solution.py:424
where the time goes:
time: 162 us; the launch traced here: 163 us
  Pallas kernels  59.6 us (37%)
  waiting for transfers between devices  52.4 us (32%)
  starting transfers between devices  40.4 us (25%)
  other arithmetic  4.77 us (3%)
  local copies, waits for them, and re-layouts  4.63 us (3%)
    pallas_call x8, Pallas kernels, call(): pl.pallas_call(kernel, out_shape=outs, in_specs=specs, out_specs=out_spec...  59.6 us
    ppermute x39, waiting for transfers between devices, send(): return lax.ppermute(x, axis, pairs)  52.4 us
    ppermute x39, starting transfers between devices, send(): return lax.ppermute(x, axis, pairs)  40.4 us
  transfers between devices with their start and end apart: 39, of which 19 were waited for; matrix products, arithmetic and copies ran while one was open for 4% of the time, Pallas kernels for 4%

commit v1 on v0

--- a/solution.py
+++ b/solution.py
@@ -96,63 +96,152 @@
     lax.fori_loop(0, nv, sweep, 0)
 
 
-def place_halos(flags, buf, own, strips, sides, reach, dims):
+def side_rows(reach, lat_cells):
+    plan, first = [], 0
+    for i in range(lat_cells + 2 * reach):
+        outside = max(reach - i, i - (reach + lat_cells - 1), 0)
+        plan.append((first, reach - outside))
+        first += reach - outside
+    return plan, -(-first // 8) * 8
+
+
+def even(axis):
+    return lax.axis_index(axis) % 2 == 0
+
+
+def place_halos(buf, own, strips, sides, reach, dims):
     lat_cells, lon_cells = dims
-    from_a, from_b = strips
-    from_x, from_s = sides
+    (from_a, skip_a), (from_b, skip_b) = strips
+    (from_x, skip_x), (from_s, skip_s) = sides
     base = FRAME - reach
-    lat_even, lon_even = flags[0] == 0, flags[1] == 0
+    lat_even, lon_even = even("lat"), even("lon")
     south = FRAME + lat_cells
     row_a = jnp.where(lat_even, south, base)
     row_b = jnp.where(lat_even, base, south)
     cols = slice(FRAME, FRAME + lon_cells)
-
-    def put_own(i, c):
-        buf[FRAME + i, cols] = own[pl.ds(pl.multiple_of(i * lon_cells, lon_cells), lon_cells)]
-        return c
-
-    def put_strips(i, c):
-        buf[row_a + i, cols] = from_a(i)
-        buf[row_b + i, cols] = from_b(i)
-        return c
-
-    lax.fori_loop(0, lat_cells, put_own, 0)
-    lax.fori_loop(0, reach, put_strips, 0)
-    west = slice(base, FRAME)
-    east = slice(FRAME + lon_cells, FRAME + lon_cells + reach)
-
-    def put_sides(first, second):
-        def put(i, c):
-            for k in range(2):
-                buf[base + 2 * i + k, first] = from_x(i, k)
-                buf[base + 2 * i + k, second] = from_s(i, k)
-            return c
-        lax.fori_loop(0, (lat_cells + 2 * reach) // 2, put, 0)
-
-    pl.when(lon_even)(lambda: put_sides(east, west))
-    pl.when(jnp.logical_not(lon_even))(lambda: put_sides(west, east))
-
-
-def strip_of(ref, lon_cells, skip=0):
-    return lambda i: ref[pl.ds(pl.multiple_of((skip + i) * lon_cells, lon_cells), lon_cells)]
-
-
-def side_of(ref):
-    return lambda i, k: ref[2 * i + k]
-
-
-def folded_side_of(ref, skip, reach):
-    return lambda i, k: ref[skip + i, k * reach:k * reach + reach]
-
-
-def faces_kernel(dims, flags, root_h, root_v, from_a, from_b, from_x, from_s, *refs):
+    for i in range(lat_cells):
+        buf[FRAME + i, cols] = own[i * lon_cells:(i + 1) * lon_cells]
+    for i in range(reach):
+        place = i * lon_cells
+        buf[row_a + i, cols] = from_a[skip_a + place:skip_a + place + lon_cells]
+        buf[row_b + i, cols] = from_b[skip_b + place:skip_b + place + lon_cells]
+
+    def put_sides(west, skip_west, east, skip_east):
+        for i, (first, count) in enumerate(side_rows(reach, lat_cells)[0]):
+            if count:
+                buf[base + i, FRAME - count:FRAME] = west[skip_west + first:skip_west + first + count]
+                buf[base + i, FRAME + lon_cells:FRAME + lon_cells + count] = (
+                    east[skip_east + first:skip_east + first + count])
+
+    pl.when(lon_even)(lambda: put_sides(from_s, skip_s, from_x, skip_x))
+    pl.when(jnp.logical_not(lon_even))(lambda: put_sides(from_x, skip_x, from_s, skip_s))
+
+
+def pack_sides(own, strips, outs, reach, dims):
+    lat_cells, lon_cells = dims
+    (from_a, skip_a), (from_b, skip_b) = strips
+    (to_x, skip_x), (to_s, skip_s) = outs
+    plan, _ = side_rows(reach, lat_cells)
+
+    def write(north, skip_north, south, skip_south, west, skip_west, east, skip_east):
+        for i, (first, count) in enumerate(plan):
+            if not count:
+                continue
+            if i < reach:
+                ref, row = north, skip_north + i * lon_cells
+            elif i < reach + lat_cells:
+                ref, row = own, (i - reach) * lon_cells
+            else:
+                ref, row = south, skip_south + (i - reach - lat_cells) * lon_cells
+            west[skip_west + first:skip_west + first + count] = ref[row:row + count]
+            east[skip_east + first:skip_east + first + count] = (
+                ref[row + lon_cells - count:row + lon_cells])
+
+    lat_even, lon_even = even("lat"), even("lon")
+    for even_lat in (True, False):
+        for even_lon in (True, False):
+            poles = (from_b, skip_b, from_a, skip_a) if even_lat else (from_a, skip_a, from_b, skip_b)
+            edges = (to_s, skip_s, to_x, skip_x) if even_lon else (to_x, skip_x, to_s, skip_s)
+            pl.when((lat_even == even_lat) & (lon_even == even_lon))(
+                functools.partial(write, *poles, *edges))
+
+
+def cells_at(rows, slots):
+    return jnp.concatenate([rows[0:1], rows[1:2, :slots - LANES]], axis=1).astype(jnp.int32)
+
+
+def add_into(cells, parts, count):
+    hot = lax.broadcasted_iota(jnp.int32, (count, cells.shape[1]), 0) == cells
+    both = jnp.dot(hot.astype(jnp.bfloat16), jnp.concatenate(parts, axis=1),
+                   preferred_element_type=jnp.float32)
+    return both[:, :LANES] + (both[:, LANES:2 * LANES] + both[:, 2 * LANES:])
+
+
+def scatter_kernel(slots, cells_n, message, cells, own):
+    own[...] = add_into(cells[...], split3(message[0:slots]), cells_n)
+
+
+def sides_kernel(dims, slots, reach, own, from_a, from_b, cells_a, cells_b,
+                 strip_a, strip_b, to_x, to_s):
+    lat_cells, lon_cells = dims
+    skip = (lat_cells - reach) * lon_cells
+    for message, cells, strip, north in (
+        (from_a, cells_a, strip_a, jnp.logical_not(even("lat"))),
+        (from_b, cells_b, strip_b, even("lat")),
+    ):
+        at = cells_at(cells, slots) - jnp.where(north, skip, 0)
+        strip[...] = add_into(at, split3(message[0:slots]), reach * lon_cells)
+    pack_sides(own, ((strip_a, 0), (strip_b, 0)), ((to_x, 0), (to_s, 0)), reach, dims)
+
+
+def face_sides_kernel(dims, root_h, root_v, from_a, from_b, to_x, to_s):
+    skip = FRAME * dims[1]
+    rows = side_rows(FRAME, dims[0])[1]
+    pack_sides(root_h, ((from_a, 0), (from_b, 0)), ((to_x, 0), (to_s, 0)), FRAME, dims)
+    pack_sides(root_v, ((from_a, skip), (from_b, skip)), ((to_x, rows), (to_s, rows)), REACH, dims)
+
+
+def start_kernel(dims, *refs):
+    lat_cells, lon_cells = dims
+    sources, (first, root_h, root_v, to_a, to_b), refs = refs[:5], refs[5:10], refs[10:]
+    (innovation, obs_weight, block_list, kappa_h, kappa_v), sems = refs[:5], refs[5]
+    loads = copies(list(zip(sources, refs[:5])), sems)
+    obs, own = innovation.shape
+    slots = block_list.shape[1]
+    for load in loads:
+        load.wait()
+    weight = obs_weight[...]
+    first[0:obs, 0:own] = weight * innovation[...]
+    first[0:obs, own:2 * own] = weight
+    places = block_list[...].astype(jnp.float32)
+    tail = to_a.shape[0] - 8
+    cells = jnp.clip(places[1:2], 0.0, lat_cells * lon_cells - 1.0)
+    for ref, base, row in ((first, obs, places[0:1]), (to_a, tail, cells), (to_b, tail, cells)):
+        ref[base:base + 8] = jnp.full((8, LANES), -1.0, jnp.float32)
+        ref[base:base + 1] = row[:, :LANES]
+        ref[base + 1:base + 2, 0:slots - LANES] = row[:, LANES:]
+    root_h[...] = jnp.sqrt(kappa_h[...])
+    root_v[...] = jnp.sqrt(kappa_v[...])
+
+    def write(south, north):
+        skip = 0
+        for ref, reach in ((root_h, FRAME), (root_v, REACH)):
+            count = reach * lon_cells
+            north[skip:skip + count] = ref[0:count]
+            south[skip:skip + count] = ref[lat_cells * lon_cells - count:]
+            skip += count
+
+    pl.when(even("lat"))(lambda: write(to_a, to_b))
+    pl.when(jnp.logical_not(even("lat")))(lambda: write(to_b, to_a))
+
+
+def faces_kernel(dims, root_h, root_v, from_a, from_b, from_x, from_s, *refs):
     lat_cells, lon_cells = dims
     out, (face_lat, face_lon, keep, up, down, buf, sems) = refs[:5], refs[5:]
     rows = lat_cells + 2 * FRAME
     width = buf.shape[1]
     place_halos(
-        flags, buf, root_h, (strip_of(from_a, lon_cells), strip_of(from_b, lon_cells)),
-        (side_of(from_x), side_of(from_s)), FRAME, dims,
+        buf, root_h, ((from_a, 0), (from_b, 0)), ((from_x, 0), (from_s, 0)), FRAME, dims
     )
 
     def clear(first):
@@ -161,36 +250,41 @@
             return c
         lax.fori_loop(0, FRAME, body, 0)
 
-    pl.when(flags[2] == 1)(lambda: clear(0))
-    pl.when(flags[3] == 1)(lambda: clear(FRAME + lat_cells))
-
-    def lateral(i, c):
-        here = buf[i]
-        face_lat[i] = here * buf[i + 1]
-        face_lon[i] = here * pltpu.roll(here, width - 1, 0)
+    lat = lax.axis_index("lat")
+    pl.when(lat == 0)(lambda: clear(0))
+    pl.when(lat == lax.axis_size("lat") - 1)(lambda: clear(FRAME + lat_cells))
+
+    buf[rows] = jnp.zeros((width, LANES), jnp.float32)
+
+    def lateral(step, c):
+        for k in range(4):
+            i = 4 * step + k
+            here = buf[i]
+            face_lat[i] = here * buf[i + 1]
+            face_lon[i] = here * pltpu.roll(here, width - 1, 0)
         return c
 
-    lax.fori_loop(0, rows - 1, lateral, 0)
-    here = buf[rows - 1]
-    face_lat[rows - 1] = jnp.zeros((width, LANES), jnp.float32)
-    face_lon[rows - 1] = here * pltpu.roll(here, width - 1, 0)
+    lax.fori_loop(0, rows // 4, lateral, 0)
     side = copies([(face_lat, out[0]), (face_lon, out[1])], sems)
+    skip, skip_side = FRAME * lon_cells, side_rows(FRAME, lat_cells)[1]
     place_halos(
-        flags, buf, root_v, (strip_of(from_a, lon_cells, FRAME), strip_of(from_b, lon_cells, FRAME)),
-        (folded_side_of(from_x, rows, REACH), folded_side_of(from_s, rows, REACH)), REACH, dims,
+        buf, root_v, ((from_a, skip), (from_b, skip)),
+        ((from_x, skip_side), (from_s, skip_side)), REACH, dims,
     )
     top = lax.broadcasted_iota(jnp.int32, (width, LANES), 1) == LANES - 1
 
-    def vertical(i, c):
-        here = buf[FRAME - REACH + i]
-        face = jnp.where(top, 0.0, here * pltpu.roll(here, LANES - 1, 1))
-        below = pltpu.roll(face, 1, 1)
-        up[i] = face
-        down[i] = below
-        keep[i] = 1.0 - (face + below)
+    def vertical(step, c):
+        at = [4 * step + k for k in range(4)]
+        here = [buf[FRAME - REACH + i] for i in at]
+        face = [jnp.where(top, 0.0, v * pltpu.roll(v, LANES - 1, 1)) for v in here]
+        below = [pltpu.roll(v, 1, 1) for v in face]
+        for i, f, g in zip(at, face, below):
+            up[i] = f
+            down[i] = g
+            keep[i] = 1.0 - (f + g)
         return c
 
-    lax.fori_loop(0, lat_cells + 2 * REACH, vertical, 0)
+    lax.fori_loop(0, (lat_cells + 2 * REACH) // 4, vertical, 0)
     level = copies([(keep, out[2]), (up, out[3]), (down, out[4])], sems.at[pl.ds(2, 3)])
     for copy in side + level:
         copy.wait()
@@ -200,35 +294,37 @@
     slots, obs, _ = jac.shape
     lane = lax.broadcasted_iota(jnp.int32, (obs, LANES), 1)
 
+    ones = jnp.ones((2 * LANES, LANES), jnp.bfloat16)
+    group = 16
+
     def part(first, count):
         def body(step, acc):
-            for k in range(8):
-                slot = first + step * 8 + k
-                row = field[pl.ds(cells[slot], 1), :]
-                value = jnp.sum(jac[slot] * row, axis=1, keepdims=True)
-                acc = jnp.where(lane == step * 8 + k, value, acc)
+            at = [first + step * group + k for k in range(group)]
+            prods = [jac[slot] * field[pl.ds(cells[slot], 1), :] for slot in at]
+            half = jnp.concatenate(prods[:group // 2], axis=0)
+            high = half.astype(jnp.bfloat16)
+            low = (half - high.astype(jnp.float32)).astype(jnp.bfloat16)
+            sums = jnp.dot(jnp.concatenate([high, low], axis=1), ones, preferred_element_type=jnp.float32)
+            for k in range(group):
+                if k < group // 2:
+                    value = sums[obs * k:obs * k + obs]
+                else:
+                    value = jnp.sum(prods[k], axis=1, keepdims=True)
+                acc = jnp.where(lane == step * group + k, value, acc)
             return acc
-        return lax.fori_loop(0, count // 8, body, jnp.zeros((obs, LANES), jnp.float32))
+        return lax.fori_loop(0, count // group, body, jnp.zeros((obs, LANES), jnp.float32))
 
     out[0:obs] = part(0, LANES)
     rest = part(LANES, slots - LANES)
     out[obs:obs + obs // 2] = rest[:obs // 2] + pltpu.roll(rest[obs // 2:], LANES // 2, 1)
 
 
-def pack_kernel(innovation, obs_weight, rows, out):
-    obs, own = innovation.shape
-    weight = obs_weight[...]
-    out[0:obs, 0:own] = weight * innovation[...]
-    out[0:obs, own:2 * own] = weight
-    out[obs:obs + 8] = rows[...]
-
-
 def adjoint_kernel(first_call, parts, *refs):
     pieces, refs = refs[:2 * parts], refs[2 * parts:]
     if first_call:
-        own_hot, cell_hot, jac_hbm, field, weight, band, jac, taken, contrib, sems = refs
+        own_hot, jac_hbm, out, weight, band, jac, taken, sems = refs
     else:
-        row_hot, weight, own_hot, cell_hot, jac_hbm, field, sums, jac, taken, contrib, sems = refs
+        row_hot, weight, own_hot, jac_hbm, out, jac, taken, sems = refs
     slots, obs, _ = jac.shape
     group = 32
     groups = slots // group
@@ -259,34 +355,44 @@
             scal = tail if scal is None else scal + tail
         total = total[:obs] + (total[obs:2 * obs] + total[2 * obs:])
         weighted = weight[...] * total
-        sums[0:8] = scal
-        sums[8:16] = fold_sum(weighted * total)
+        out[slots:slots + 8] = scal
+        out[slots + 8:slots + 16] = fold_sum(weighted * total)
     stack = jnp.concatenate(split3(weighted), axis=0)
     picked = jnp.dot(stack, own_hot[...], preferred_element_type=jnp.float32)
     picked = picked[:obs] + (picked[obs:2 * obs] + picked[2 * obs:])
     taken[0] = picked[:, :LANES]
     taken[1] = picked[:, LANES:]
 
+    ones = jnp.ones((2 * LANES, LANES), jnp.bfloat16)
+    lane = lax.broadcasted_iota(jnp.int32, (obs, LANES), 1)
+
     def body(g, c):
         chunk(g).wait()
         per = LANES // group
-        values = pltpu.roll(taken[g // per], LANES - (g % per) * group, 1)
+        base = (g % per) * group
+        values = taken[g // per]
+        high = values.astype(jnp.bfloat16)
+        low = (values - high.astype(jnp.float32)).astype(jnp.bfloat16)
+        none = jnp.zeros_like(high)
+        stack = jnp.concatenate([
+            jnp.concatenate([jnp.where(lane == base + k, high, none),
+                             jnp.where(lane == base + k, low, none)], axis=1)
+            for k in range(group // 2)
+        ], axis=0)
+        spread = jnp.dot(stack, ones, preferred_element_type=jnp.float32)
+        values = pltpu.roll(values, LANES - base, 1)
         for k in range(group):
             slot = g * group + k
-            contrib[pl.ds(slot, 1), :] = jnp.sum(jac[slot] * values[:, k:k + 1], axis=0, keepdims=True)
+            wide = spread[obs * k:obs * k + obs] if k < group // 2 else values[:, k:k + 1]
+            out[pl.ds(slot, 1), :] = jnp.sum(jac[slot] * wide, axis=0, keepdims=True)
         return c
 
     lax.fori_loop(0, groups, body, 0)
-    out = None
-    for piece in split3(contrib[...]):
-        prod = jnp.dot(cell_hot[...], piece, preferred_element_type=jnp.float32)
-        out = prod if out is None else out + prod
-    field[...] = out
 
 
 def spread_kernel(dims, first_call, *refs):
     lat_cells, lon_cells = dims
-    flags, cells, own, from_a, from_b, from_x, from_s = refs[:7]
+    counts, cells, own, from_a, from_b, from_x, from_s = refs[:7]
     refs = refs[7:]
     if not first_call:
         scal, refs = refs[0], refs[1:]
@@ -301,12 +407,11 @@
     )
     if not first_call:
         old_loads = copies([(grad_hbm, grad), (spread_hbm, two)], sems.at[pl.ds(6, 2)])
-    nh, nv = flags[4], flags[5]
+    nh, nv = counts[0], counts[1]
     rows = lat_cells + 2 * FRAME
     width = buf.shape[1]
     place_halos(
-        flags, buf, own, (strip_of(from_a, lon_cells), strip_of(from_b, lon_cells)),
-        (side_of(from_x), side_of(from_s)), FRAME, dims,
+        buf, own, ((from_a, 0), (from_b, 0)), ((from_x, 0), (from_s, 0)), FRAME, dims
     )
     for load in loads[:2]:
         load.wait()
@@ -365,21 +470,25 @@
 
 def final_kernel(dims, *refs):
     lat_cells, lon_cells = dims
-    flags, own, from_a, from_b, from_x, from_s, scal0, scal1 = refs[:8]
+    counts, own, from_a, from_b, from_x, from_s, scal0, scal1 = refs[:8]
     hbm, (increment, residual), refs = refs[8:17], refs[17:19], refs[19:]
     face_lat, face_lon, keep, up, down, grad, spread, image, spread_next, buf, sems = refs
-    loads = copies(list(zip(hbm, refs[:9])), sems)
-    nh, nv = flags[4], flags[5]
+    inner = pl.ds(FRAME - REACH, lat_cells + 2 * REACH)
+    block = pl.ds(REACH, lat_cells)
+    loads = copies(
+        [(src.at[inner], dst.at[inner]) for src, dst in zip(hbm[:2], refs[:2])]
+        + [(src.at[block], dst.at[block]) for src, dst in zip(hbm[2:5], refs[2:5])]
+        + list(zip(hbm[5:], refs[5:9])), sems)
+    nh, nv = counts[0], counts[1]
     place_halos(
-        flags, buf, own, (strip_of(from_a, lon_cells), strip_of(from_b, lon_cells)),
-        (side_of(from_x), side_of(from_s)), REACH, dims,
+        buf, own, ((from_a, 0), (from_b, 0)), ((from_x, 0), (from_s, 0)), REACH, dims
     )
     for load in loads[:2]:
         load.wait()
     last_lateral(buf, face_lat, face_lon, nh, lon_cells)
     left = FRAME // 8 * 8
     right = -(-(FRAME + lon_cells) // 8) * 8
-    for load in loads[2:]:
+    for load in loads[2:5]:
         load.wait()
     vertical_passes(
         buf, keep, up, down, FRAME, FRAME + lat_cells, lat_cells, FRAME - REACH, nv, left, right
@@ -390,6 +499,8 @@
     beta = rr1 / rr0
     alpha1 = rr1 / ((rr1 + jnp.sum(scal1[8:16])) - beta * (rr1 / alpha0))
     cols = slice(FRAME, FRAME + lon_cells)
+    for load in loads[5:]:
+        load.wait()
 
     def finish(i, c):
         place = pl.ds(pl.multiple_of(i * lon_cells, lon_cells), lon_cells)
@@ -410,8 +521,7 @@
     own_rows = innovation.shape[1]
     n_lat, n_lon = lax.axis_size("lat"), lax.axis_size("lon")
     parts = n_lon // 2
-    lat, lon = lax.axis_index("lat"), lax.axis_index("lon")
-    lat_even, lon_even = lat % 2 == 0, lon % 2 == 0
+    lon = lax.axis_index("lon")
     f32 = jnp.float32
 
     def swap(n, k):
@@ -427,41 +537,34 @@
         near = [x] + [send(x, "lon", swap(n_lon, 2 * k)) for k in range(1, parts)]
         return near + [send(piece, "lon", swap(n_lon, 1)) for piece in near]
 
-    def lat_strips(top, bottom, tail=None):
-        to_a = jnp.where(lat_even, bottom, top)
-        to_b = jnp.where(lat_even, top, bottom)
-        if tail is not None:
-            to_a = jnp.concatenate([to_a, tail], 0)
-            to_b = jnp.concatenate([to_b, tail], 0)
-        return send(to_a, "lat", swap(n_lat, 1)), send(to_b, "lat", odd_pairs(n_lat))
-
-    def side_strips(ext, reach):
-        west, east = ext[:, :reach], ext[:, lon_cells - reach:]
-        return jnp.where(lon_even, east, west), jnp.where(lon_even, west, east)
-
     def lon_send(to_x, to_s):
         return send(to_x, "lon", swap(n_lon, 1)), send(to_s, "lon", odd_pairs(n_lon))
 
-    def stacked(own, from_a, from_b, reach):
-        shape = (reach, lon_cells, levels)
-        from_a, from_b = from_a.reshape(shape), from_b.reshape(shape)
-        north = jnp.where(lat_even, from_b, from_a)
-        south = jnp.where(lat_even, from_a, from_b)
-        return jnp.concatenate([north, own.reshape(lat_cells, lon_cells, levels), south], 0)
-
-    def halo(own, reach, tail=None):
-        count = reach * lon_cells
-        from_a, from_b = lat_strips(own[:count], own[cells_n - count:], tail)
-        sums = None
-        if tail is not None:
-            if n_lat == 4:
-                sums = (tail + send(tail, "lat", swap(n_lat, 2))) + (from_a[count:] + from_b[count:])
-            else:
-                sums = lax.psum(tail, "lat")
-            from_a, from_b = from_a[:count], from_b[:count]
-        ext = stacked(own, from_a, from_b, reach)
-        from_x, from_s = lon_send(*side_strips(ext, reach))
-        return (from_a, from_b, from_x, from_s), sums
+    def lat_send(to_a, to_b):
+        return send(to_a, "lat", swap(n_lat, 1)), send(to_b, "lat", odd_pairs(n_lat))
+
+    def lat_sum(message, from_a, from_b):
+        tail = message[slots:]
+        if n_lat != 4:
+            return lax.psum(tail, "lat")
+        return (tail + send(tail, "lat", swap(n_lat, 2))) + (from_a[slots:] + from_b[slots:])
+
+    def scatter(message):
+        return call(functools.partial(scatter_kernel, slots, cells_n), "scatter", field, (message, cells))
+
+    def sides_of(own, from_a, from_b, reach):
+        side = shape(side_rows(reach, lat_cells)[1], levels)
+        strip = shape(reach * lon_cells, levels)
+        strip_a, strip_b, to_x, to_s = call(
+            functools.partial(sides_kernel, dims, slots, reach), "sides", (strip, strip, side, side),
+            (own, from_a, from_b, *cells_near))
+        return (strip_a, strip_b), (to_x, to_s)
+
+    def halo(message, reach):
+        from_a, from_b = lat_send(message, message)
+        own = scatter(message)
+        strips, sides = sides_of(own, from_a, from_b, reach)
+        return (own, *strips, *lon_send(*sides)), lat_sum(message, from_a, from_b)
 
     vmem = pl.BlockSpec(memory_space=pltpu.VMEM)
     smem = pl.BlockSpec(memory_space=pltpu.SMEM)
@@ -493,22 +596,15 @@
             scratch_shapes=list(scratches), compiler_params=params, name=name,
         )(*ins, *far_in)
 
-    rows_own = jnp.pad(block_list[0].astype(f32), (0, 2 * LANES - slots), constant_values=-1.0)
-    first = call(pack_kernel, "pack", shape(obs + 8, LANES),
-                 (innovation, obs_weight, jnp.pad(rows_own.reshape(2, LANES), ((0, 6), (0, 0)))))
+    strip = shape((FRAME + REACH) * lon_cells + 8, levels)
+    start_in = (innovation, obs_weight, block_list,
+                kappa_h.reshape(cells_n, levels), kappa_v.reshape(cells_n, levels))
+    first, root_h, root_v, to_a, to_b = call(
+        functools.partial(start_kernel, dims), "start", (shape(obs + 8, LANES), field, field, strip, strip),
+        (), far_in=start_in, scratches=[pltpu.VMEM(v.shape, v.dtype) for v in start_in] + [sems(5)])
+    k_strips = lat_send(to_a, to_b)
     band = gather_band(first)
-
-    kh_lat = FRAME * lon_cells
-    kv_lat = REACH * lon_cells
-    kh2, kv2 = (jnp.sqrt(v).reshape(cells_n, levels) for v in (kappa_h, kappa_v))
-    k_strips = lat_strips(
-        jnp.concatenate([kh2[:kh_lat], kv2[:kv_lat]], 0),
-        jnp.concatenate([kh2[cells_n - kh_lat:], kv2[cells_n - kv_lat:]], 0),
-    )
-    hx, hs = side_strips(stacked(kh2, k_strips[0][:kh_lat], k_strips[1][:kh_lat], FRAME), FRAME)
-    vx, vs = side_strips(stacked(kv2, k_strips[0][kh_lat:], k_strips[1][kh_lat:], REACH), REACH)
-    fold = lambda v: v.reshape(rows_v // 2, 2 * REACH, levels)
-    k_messages = [jnp.concatenate([hx, fold(vx)], 0), jnp.concatenate([hs, fold(vs)], 0)]
+    cells_near = [v[(FRAME + REACH) * lon_cells:] for v in k_strips]
 
     def place_of(row):
         row = row.astype(jnp.int32)
@@ -519,49 +615,50 @@
     all_at = place_of(jnp.stack([piece[obs:obs + 2] for piece in band]).reshape(n_lon, 2 * LANES))
     row_iota = jnp.arange(band_rows, dtype=jnp.int32)
     row_hot = (all_at[:, :, None] == row_iota[None, None, :]).astype(jnp.bfloat16)
-    own_at = place_of(rows_own)
+    own_at = jnp.pad(place_of(block_list[0]), (0, 2 * LANES - slots), constant_values=-1)
     own_hot = (row_iota[:, None] == own_at[None, :]).astype(jnp.bfloat16)
-    cells = jnp.clip(block_list[1], 0, cells_n - 1)
-    cell_hot = (jnp.arange(cells_n, dtype=jnp.int32)[:, None] == cells[None, :]).astype(jnp.bfloat16)
-    flags = jnp.stack([
-        lat % 2, lon % 2, (lat == 0).astype(jnp.int32), (lat == n_lat - 1).astype(jnp.int32),
-        pass_counts[0], pass_counts[1],
-    ]).astype(jnp.int32)
-
-    adj_scratch = [jac_vmem, scratch(2, obs, LANES), scratch(slots, levels), sems(slots // 32)]
-    band[0], k_messages = lax.optimization_barrier((band[0], k_messages))
+    cells = jnp.clip(block_list[1:], 0, cells_n - 1)
+    cells_flat = cells.reshape(slots)
+
+    adj_scratch = [jac_vmem, scratch(2, obs, LANES), sems(slots // 32)]
+    message, weight = call(
+        functools.partial(adjoint_kernel, True, parts), "adjoint_first",
+        (shape(slots, levels), shape(obs, band_rows)), (*band, own_hot), far_in=(jacobian,),
+        scratches=[scratch(obs, band_rows)] + adj_scratch)
+
+    from_a, from_b = lat_send(message, message)
+    own = scatter(message)
+    side = shape(sum(side_rows(reach, lat_cells)[1] for reach in (FRAME, REACH)), levels)
+    k_messages = call(functools.partial(face_sides_kernel, dims), "face_sides", (side, side),
+                      (root_h, root_v, *k_strips))
     k_sides = lon_send(*k_messages)
-    own, weight = call(
-        functools.partial(adjoint_kernel, True, parts), "adjoint_first",
-        (field, shape(obs, band_rows)), (*band, own_hot, cell_hot), far_in=(jacobian,),
-        scratches=[scratch(obs, band_rows)] + adj_scratch)
+    k_messages, from_a, from_b = lax.optimization_barrier((k_messages, from_a, from_b))
+    strips, sides = sides_of(own, from_a, from_b, FRAME)
+    halos = (own, *strips, *lon_send(*sides))
     faces = call(
         functools.partial(faces_kernel, dims), "faces", (wide, wide, tall, tall, tall),
-        (flags, kh2, kv2, *k_strips, *k_sides), 1, far_out=5,
-        scratches=faces_vmem + [wide_vmem, sems(5)])
-    halos, _ = halo(own, FRAME)
+        (root_h, root_v, *k_strips, *k_sides), far_out=5,
+        scratches=faces_vmem + [scratch(rows_h + 1, width, levels), sems(5)])
     spread_scratch = faces_vmem + [jac_vmem] + [field_vmem] * 3 + [
         wide_vmem, scratch(lat_cells, width, levels), sems(10)]
     grad, spread, message = call(
         functools.partial(spread_kernel, dims, True), "spread_first", (field, field, msg),
-        (flags, cells, own, *halos), 2, (*faces, jacobian), 2, spread_scratch)
+        (pass_counts, cells_flat, *halos), 2, (*faces, jacobian), 2, spread_scratch)
 
     def adjoint(message):
         return call(
             functools.partial(adjoint_kernel, False, parts), "adjoint_next",
-            (field, shape(16, LANES)), (*gather_band(message), row_hot, weight, own_hot, cell_hot),
+            shape(slots + 16, levels), (*gather_band(message), row_hot, weight, own_hot),
             far_in=(jacobian,), scratches=adj_scratch)
 
-    own, sums = adjoint(message)
-    halos, scal0 = halo(own, FRAME, sums)
+    halos, scal0 = halo(adjoint(message), FRAME)
     image, spread_next, message = call(
         functools.partial(spread_kernel, dims, False), "spread_next", (field, field, msg),
-        (flags, cells, own, *halos, scal0), 2, (*faces, jacobian, grad, spread), 2, spread_scratch)
-    own, sums = adjoint(message)
-    halos, scal1 = halo(own, REACH, sums)
+        (pass_counts, cells_flat, *halos, scal0), 2, (*faces, jacobian, grad, spread), 2, spread_scratch)
+    halos, scal1 = halo(adjoint(message), REACH)
     increment, residual = call(
         functools.partial(final_kernel, dims), "final", (field, field),
-        (flags, own, *halos, scal0, scal1), 1,
+        (pass_counts, *halos, scal0, scal1), 1,
         (*faces, grad, spread, image, spread_next), 0,
         faces_vmem + [field_vmem] * 4 + [wide_vmem, sems(9)])
     block = (lat_cells, lon_cells, levels)

time: 162 us -> 131 us (0.81); the launches traced: 163 us -> 130 us
  waiting for transfers between devices: 52.4 us -> 34.6 us
  Pallas kernels: 59.6 us -> 48.9 us
  other arithmetic: 4.77 us -> 0.64 us
    ppermute x39, waiting for transfers between devices: 52.4 us -> 34.6 us  [send(): return lax.ppermute(x, axis, pairs)]
    pallas_call x8 -> x15, Pallas kernels: 59.6 us -> 48.9 us  [call(): pl.pallas_call(kernel, out_shape=outs, in_specs=specs, out_specs=out_spec...]
    select_n x16 -> x0, other arithmetic: 2.1 us -> none  [the longest x7 1.82 us: side_strips(): return (jnp.where(lon_even, east, west), jnp.where(lon_even, west, east))]
    sqrt x2 -> x0, local copies, waits for them, and re-layouts: 2.03 us -> none  [local(): jnp.sqrt(v).reshape(cells_n, levels)]
    unnamed x12, local copies, waits for them, and re-layouts: 2.38 us -> 4.09 us
  transfers between devices with their start and end apart: 39 -> 39, of which waited for: 19 -> 18; matrix products, arithmetic and copies ran while one was open for 4% -> 1% of each run, Pallas kernels for 4% -> 7%
where the time goes in v1:
time: 131 us; the launch traced here: 130 us
  Pallas kernels  48.9 us (37%)
  starting transfers between devices  40.8 us (31%)
  waiting for transfers between devices  34.6 us (26%)
  local copies, waits for them, and re-layouts  4.16 us (3%)
    pallas_call x15, Pallas kernels, call(): pl.pallas_call(kernel, out_shape=outs, in_specs=specs, out_specs=out_spec...  48.9 us
    ppermute x39, starting transfers between devices, send(): return lax.ppermute(x, axis, pairs)  40.8 us
    ppermute x39, waiting for transfers between devices, send(): return lax.ppermute(x, axis, pairs)  34.6 us
    unnamed x12, local copies, waits for them, and re-layouts  4.09 us
  transfers between devices with their start and end apart: 39, of which 18 were waited for; matrix products, arithmetic and copies ran while one was open for 1% of the time, Pallas kernels for 7%

profile of v1, /device:TPU:0, one launch (start us, length us, event | category | flops | bytes accessed | tf_op | source)
XLA Modules:
  0.0 130.1 jit_solution(8734828212100839914)
XLA Ops:
  0.6 0.9 copy-done
  1.6 0.9 copy-done.1
  2.5 0.8 copy-done.2
  3.3 0.8 copy-done.3
  4.1 0.7 copy-done.4
  5.0 3.1 %collective-permute-start = (f32[72,128]{1,0:T(8,128)S(1)}, f32[72,128]{1,0:T(8,128)S(1)}, u32[]{:S(2)}, u32[]{:S(2)}) collective-permute-start(f32[72,128]{1,0:T(8,128)S(1)} %get-tuple-element.38.refs_0_), channel_id=1, source_target_pairs={{0,2},{1,3},{2,0},{3,1},{4,6},{5,7},{6,4},{7,5},{8,10},{9,11},{10,... | collective-permute-start | bytes 110600 | tf_op jit(solution)/shard_map/ppermute | solution.py:534
  8.1 2.6 %collective-permute-start.1 = (f32[72,128]{1,0:T(8,128)S(1)}, f32[72,128]{1,0:T(8,128)S(1)}, u32[]{:S(2)}, u32[]{:S(2)}) collective-permute-start(f32[72,128]{1,0:T(8,128)S(1)} %get-tuple-element.38.refs_0_), channel_id=1, source_target_pairs={{0,4},{1,5},{2,6},{3,7},{4,0},{5,1},{6,2},{7,3},{8,12},{9,13},{10,... | collective-permute-start | bytes 110600 | tf_op jit(solution)/shard_map/ppermute | solution.py:534
  10.7 1.7 %collective-permute-start.7 = (f32[584,128]{1,0:T(8,128)S(1)}, f32[584,128]{1,0:T(8,128)S(1)}, u32[]{:S(2)}, u32[]{:S(2)}) collective-permute-start(f32[584,128]{1,0:T(8,128)S(1)} %get-tuple-element.42), channel_id=1, source_target_pairs={{0,8},{8,0},{16,24},{24,16},{1,9},{9,1},{17,25},{25,17},{2,10},{10... | collective-permute-start | bytes 897032 | tf_op jit(solution)/shard_map/ppermute | solution.py:534
  12.4 1.5 %collective-permute-start.8 = (f32[584,128]{1,0:T(8,128)S(1)}, f32[584,128]{1,0:T(8,128)S(1)}, u32[]{:S(2)}, u32[]{:S(2)}) collective-permute-start(f32[584,128]{1,0:T(8,128)S(1)} %get-tuple-element.43), channel_id=1, source_target_pairs={{0,24},{8,16},{16,8},{24,0},{1,25},{9,17},{17,9},{25,1},{2,26},{10... | collective-permute-start | bytes 897032 | tf_op jit(solution)/shard_map/ppermute | solution.py:534
  14.1 2.3 %collective-permute-done.2.refs_3_ = f32[72,128]{1,0:T(8,128)S(1)} collective-permute-done((f32[72,128]{1,0:T(8,128)S(1)}, f32[72,128]{1,0:T(8,128)S(1)}, u32[]{:S(2)}, u32[]{:S(2)}) %collective-permute-start.2) | collective-permute-done | bytes 36896 | tf_op jit(solution)/shard_map/ppermute | solution.py:534
  17.1 0.6 collective-permute-done.5.refs_6_
  17.9 3.5 %adjoint_first.1 = (f32[192,128]{1,0:T(8,128)S(1)}, f32[64,512]{1,0:T(8,128)S(1)}) custom-call(f32[72,128]{1,0:T(8,128)S(1)} %get-tuple-element.38.refs_0_, f32[72,128]{1,0:T(8,128)S(1)} %collective-permute-done.refs_1_, f32[72,128]{1,0:T(8,128)S(1)} %collective-permute-done.1.refs_2_, f32[72,128]{1,0:T(8,128)S(1)} %collective-permute-done.2.refs_3_, ...), custom_call_target="tpu_custom_call" | custom-call | tf_op jit(solution)/shard_map/adjoint_first/pallas_call | solution.py:594
  21.3 2.5 %collective-permute-start.10 = (f32[192,128]{1,0:T(8,128)S(1)}, f32[192,128]{1,0:T(8,128)S(1)}, u32[]{:S(2)}, u32[]{:S(2)}) collective-permute-start(f32[192,128]{1,0:T(8,128)S(1)} %get-tuple-element.39.message), channel_id=1, source_target_pairs={{0,24},{8,16},{16,8},{24,0},{1,25},{9,17},{17,9},{25,1},{2,26},{10... | collective-permute-start | bytes 294920 | tf_op jit(solution)/shard_map/ppermute | solution.py:534
  23.9 0.5 collective-permute-start.9
  24.4 3.8 %collective-permute-done.8.from_b = f32[584,128]{1,0:T(8,128)S(1)} collective-permute-done((f32[584,128]{1,0:T(8,128)S(1)}, f32[584,128]{1,0:T(8,128)S(1)}, u32[]{:S(2)}, u32[]{:S(2)}) %collective-permute-start.8) | collective-permute-done | bytes 299040 | tf_op jit(solution)/shard_map/ppermute | solution.py:534
  28.2 0.8 face_sides.1
  29.0 3.7 %collective-permute-start.14 = (f32[456,128]{1,0:T(8,128)S(1)}, f32[456,128]{1,0:T(8,128)S(1)}, u32[]{:S(2)}, u32[]{:S(2)}) collective-permute-start(f32[456,128]{1,0:T(8,128)S(1)} %get-tuple-element.45), channel_id=1, source_target_pairs={{0,7},{1,2},{2,1},{3,4},{4,3},{5,6},{6,5},{7,0},{8,15},{9,10},{10,... | collective-permute-start | bytes 700424 | tf_op jit(solution)/shard_map/ppermute | solution.py:534
  33.0 1.2 sides.3
  34.2 1.8 %collective-permute-start.12 = (f32[328,128]{1,0:T(8,128)}, f32[328,128]{1,0:T(8,128)S(1)}, u32[]{:S(2)}, u32[]{:S(2)}) collective-permute-start(f32[328,128]{1,0:T(8,128)} %get-tuple-element.51), channel_id=1, source_target_pairs={{0,7},{1,2},{2,1},{3,4},{4,3},{5,6},{6,5},{7,0},{8,15},{9,10},{10,... | collective-permute-start | bytes 503816 | tf_op jit(solution)/shard_map/ppermute | solution.py:534
  36.0 2.7 %collective-permute-done.14.from_s = f32[456,128]{1,0:T(8,128)S(1)} collective-permute-done((f32[456,128]{1,0:T(8,128)S(1)}, f32[456,128]{1,0:T(8,128)S(1)}, u32[]{:S(2)}, u32[]{:S(2)}) %collective-permute-start.14) | collective-permute-done | bytes 233504 | tf_op jit(solution)/shard_map/ppermute | solution.py:534
  38.8 2.1 %faces.1 = (f32[40,56,128]{2,1,0:T(8,128)S(1)}, f32[40,56,128]{2,1,0:T(8,128)}, f32[28,56,128]{2,1,0:T(8,128)S(1)}, f32[28,56,128]{2,1,0:T(8,128)S(1)}, f32[28,56,128]{2,1,0:T(8,128)S(1)}) custom-call(f32[512,128]{1,0:T(8,128)S(1)} %get-tuple-element.40.root_h, f32[512,128]{1,0:T(8,128)S(1)} %get-tuple-element.41.root_v, ...), custom_call_target="tpu_custom_call" | custom-call | tf_op jit(solution)/shard_map/faces/pallas_call | solution.py:594
  40.9 1.7 %collective-permute-done.12.refs_6_ = f32[328,128]{1,0:T(8,128)S(1)} collective-permute-done((f32[328,128]{1,0:T(8,128)}, f32[328,128]{1,0:T(8,128)S(1)}, u32[]{:S(2)}, u32[]{:S(2)}) %collective-permute-start.12) | collective-permute-done | bytes 167968 | tf_op jit(solution)/shard_map/ppermute | solution.py:534
  42.5 13.1 %spread_first.1 = (f32[512,128]{1,0:T(8,128)S(1)}, f32[512,128]{1,0:T(8,128)S(1)}, f32[104,128]{1,0:T(8,128)S(1)}) custom-call(s32[2]{0:T(128)S(1)} %copy-done.5, s32[192]{0:T(256)S(1)} %bitcast.16, f32[512,128]{1,0:T(8,128)S(1)} %scatter.3.own.refs_2_, f32[384,128]{1,0:T(8,128)S(1)} %get-tuple-element.48.refs_3_, f32[384,128]{1,0:T(8,128)S(1)} %get-tuple-element.49.refs_4_, ...), custom_call_target="tpu_custom_call" | custom-call | tf_op jit(solution)/shard_map/spread_first/pallas_call | solution.py:594
  55.7 1.3 collective-permute-start.16
  57.0 3.1 %collective-permute-start.17 = (f32[104,128]{1,0:T(8,128)S(1)}, f32[104,128]{1,0:T(8,128)S(1)}, u32[]{:S(2)}, u32[]{:S(2)}) collective-permute-start(f32[104,128]{1,0:T(8,128)S(1)} %get-tuple-element.57.refs_0_), channel_id=1, source_target_pairs={{0,6},{1,7},{2,4},{3,5},{4,2},{5,3},{6,0},{7,1},{8,14},{9,15},{10,... | collective-permute-start | bytes 159752 | tf_op jit(solution)/shard_map/ppermute | solution.py:534
  60.9 2.4 %collective-permute-done.17.refs_3_ = f32[104,128]{1,0:T(8,128)S(1)} collective-permute-done((f32[104,128]{1,0:T(8,128)S(1)}, f32[104,128]{1,0:T(8,128)S(1)}, u32[]{:S(2)}, u32[]{:S(2)}) %collective-permute-start.17) | collective-permute-done | bytes 53280 | tf_op jit(solution)/shard_map/ppermute | solution.py:534
  63.8 0.7 collective-permute-done.21.refs_7_
  64.5 3.9 %adjoint_next.2.message = f32[208,128]{1,0:T(8,128)S(1)} custom-call(f32[104,128]{1,0:T(8,128)S(1)} %get-tuple-element.57.refs_0_, f32[104,128]{1,0:T(8,128)S(1)} %collective-permute-done.15.refs_1_, f32[104,128]{1,0:T(8,128)S(1)} %collective-permute-done.16.refs_2_, f32[104,128]{1,0:T(8,128)S(1)} %collective-permute-done.17.refs_3_, ...), custom_call_target="tpu_custom_call" | custom-call | tf_op jit(solution)/shard_map/adjoint_next/pallas_call | solution.py:594
  68.4 1.5 %collective-permute-start.22 = (f32[208,128]{1,0:T(8,128)S(1)}, f32[208,128]{1,0:T(8,128)S(1)}, u32[]{:S(2)}, u32[]{:S(2)}) collective-permute-start(f32[208,128]{1,0:T(8,128)S(1)} %adjoint_next.2.message), channel_id=1, source_target_pairs={{0,8},{8,0},{16,24},{24,16},{1,9},{9,1},{17,25},{25,17},{2,10},{10... | collective-permute-start | bytes 319496 | tf_op jit(solution)/shard_map/ppermute | solution.py:534
  70.0 0.6 collective-permute-start.23
  70.5 1.5 %collective-permute-start.26 = (f32[16,128]{1,0:T(8,128)S(1)}, f32[16,128]{1,0:T(8,128)S(1)}, u32[]{:S(2)}, u32[]{:S(2)}) collective-permute-start(f32[16,128]{1,0:T(8,128)S(1)} %slice.81), channel_id=1, source_target_pairs={{0,16},{8,24},{16,0},{24,8},{1,17},{9,25},{17,1},{25,9},{2,18},{10... | collective-permute-start | bytes 24584 | tf_op jit(solution)/shard_map/ppermute | solution.py:534
  72.3 2.0 %collective-permute-done.22.from_a = f32[208,128]{1,0:T(8,128)S(1)} collective-permute-done((f32[208,128]{1,0:T(8,128)S(1)}, f32[208,128]{1,0:T(8,128)S(1)}, u32[]{:S(2)}, u32[]{:S(2)}) %collective-permute-start.22) | collective-permute-done | bytes 106528 | tf_op jit(solution)/shard_map/ppermute | solution.py:534
  74.3 1.6 %collective-permute-done.23.from_b = f32[208,128]{1,0:T(8,128)S(1)} collective-permute-done((f32[208,128]{1,0:T(8,128)S(1)}, f32[208,128]{1,0:T(8,128)S(1)}, u32[]{:S(2)}, u32[]{:S(2)}) %collective-permute-start.23) | collective-permute-done | bytes 106528 | tf_op jit(solution)/shard_map/ppermute | solution.py:534
  76.4 2.8 %collective-permute-start.25 = (f32[328,128]{1,0:T(8,128)S(1)}, f32[328,128]{1,0:T(8,128)S(1)}, u32[]{:S(2)}, u32[]{:S(2)}) collective-permute-start(f32[328,128]{1,0:T(8,128)S(1)} %get-tuple-element.62), channel_id=1, source_target_pairs={{0,7},{1,2},{2,1},{3,4},{4,3},{5,6},{6,5},{7,0},{8,15},{9,10},{10,... | collective-permute-start | bytes 503816 | tf_op jit(solution)/shard_map/ppermute | solution.py:534
  79.2 5.1 %collective-permute-done.25.refs_6_ = f32[328,128]{1,0:T(8,128)S(1)} collective-permute-done((f32[328,128]{1,0:T(8,128)S(1)}, f32[328,128]{1,0:T(8,128)S(1)}, u32[]{:S(2)}, u32[]{:S(2)}) %collective-permute-start.25) | collective-permute-done | bytes 167968 | tf_op jit(solution)/shard_map/ppermute | solution.py:534
  84.3 13.3 %spread_next.1 = (f32[512,128]{1,0:T(8,128)S(1)}, f32[512,128]{1,0:T(8,128)S(1)}, f32[104,128]{1,0:T(8,128)S(1)}) custom-call(s32[2]{0:T(128)S(1)} %copy-done.5, s32[192]{0:T(256)S(1)} %bitcast.17, f32[512,128]{1,0:T(8,128)S(1)} %scatter.4.own.refs_2_, f32[384,128]{1,0:T(8,128)S(1)} %get-tuple-element.59.refs_3_, f32[384,128]{1,0:T(8,128)S(1)} %get-tuple-element.60.refs_4_, ...), custom_call_target="tpu_custom_call" | custom-call | tf_op jit(solution)/shard_map/spread_next/pallas_call | solution.py:594
  97.9 4.2 %collective-permute-start.29 = (f32[104,128]{1,0:T(8,128)S(1)}, f32[104,128]{1,0:T(8,128)S(1)}, u32[]{:S(2)}, u32[]{:S(2)}) collective-permute-start(f32[104,128]{1,0:T(8,128)S(1)} %get-tuple-element.65.refs_0_), channel_id=1, source_target_pairs={{0,6},{1,7},{2,4},{3,5},{4,2},{5,3},{6,0},{7,1},{8,14},{9,15},{10,... | collective-permute-start | bytes 159752 | tf_op jit(solution)/shard_map/ppermute | solution.py:534
  103.1 2.3 %collective-permute-done.29.refs_3_ = f32[104,128]{1,0:T(8,128)S(1)} collective-permute-done((f32[104,128]{1,0:T(8,128)S(1)}, f32[104,128]{1,0:T(8,128)S(1)}, u32[]{:S(2)}, u32[]{:S(2)}) %collective-permute-start.29) | collective-permute-done | bytes 53280 | tf_op jit(solution)/shard_map/ppermute | solution.py:534
  105.4 1.2 collective-permute-done.33.refs_7_
  106.6 3.9 %adjoint_next.3.message = f32[208,128]{1,0:T(8,128)S(1)} custom-call(f32[104,128]{1,0:T(8,128)S(1)} %get-tuple-element.65.refs_0_, f32[104,128]{1,0:T(8,128)S(1)} %collective-permute-done.27.refs_1_, f32[104,128]{1,0:T(8,128)S(1)} %collective-permute-done.28.refs_2_, f32[104,128]{1,0:T(8,128)S(1)} %collective-permute-done.29.refs_3_, ...), custom_call_target="tpu_custom_call" | custom-call | tf_op jit(solution)/shard_map/adjoint_next/pallas_call | solution.py:594
  110.5 1.5 %collective-permute-start.34 = (f32[208,128]{1,0:T(8,128)S(1)}, f32[208,128]{1,0:T(8,128)S(1)}, u32[]{:S(2)}, u32[]{:S(2)}) collective-permute-start(f32[208,128]{1,0:T(8,128)S(1)} %adjoint_next.3.message), channel_id=1, source_target_pairs={{0,8},{8,0},{16,24},{24,16},{1,9},{9,1},{17,25},{25,17},{2,10},{10... | collective-permute-start | bytes 319496 | tf_op jit(solution)/shard_map/ppermute | solution.py:534
  112.0 1.5 %collective-permute-start.35 = (f32[208,128]{1,0:T(8,128)S(1)}, f32[208,128]{1,0:T(8,128)S(1)}, u32[]{:S(2)}, u32[]{:S(2)}) collective-permute-start(f32[208,128]{1,0:T(8,128)S(1)} %adjoint_next.3.message), channel_id=1, source_target_pairs={{0,24},{8,16},{16,8},{24,0},{1,25},{9,17},{17,9},{25,1},{2,26},{10... | collective-permute-start | bytes 319496 | tf_op jit(solution)/shard_map/ppermute | solution.py:534
  113.5 0.6 collective-permute-start.38
  114.4 1.4 %collective-permute-done.34.from_a = f32[208,128]{1,0:T(8,128)S(1)} collective-permute-done((f32[208,128]{1,0:T(8,128)S(1)}, f32[208,128]{1,0:T(8,128)S(1)}, u32[]{:S(2)}, u32[]{:S(2)}) %collective-permute-start.34) | collective-permute-done | bytes 106528 | tf_op jit(solution)/shard_map/ppermute | solution.py:534
  115.8 3.0 %collective-permute-done.35.from_b = f32[208,128]{1,0:T(8,128)S(1)} collective-permute-done((f32[208,128]{1,0:T(8,128)S(1)}, f32[208,128]{1,0:T(8,128)S(1)}, u32[]{:S(2)}, u32[]{:S(2)}) %collective-permute-start.35) | collective-permute-done | bytes 106528 | tf_op jit(solution)/shard_map/ppermute | solution.py:534
  119.2 2.7 %collective-permute-start.37 = (f32[128,128]{1,0:T(8,128)S(1)}, f32[128,128]{1,0:T(8,128)S(1)}, u32[]{:S(2)}, u32[]{:S(2)}) collective-permute-start(f32[128,128]{1,0:T(8,128)S(1)} %get-tuple-element.69), channel_id=1, source_target_pairs={{0,7},{1,2},{2,1},{3,4},{4,3},{5,6},{6,5},{7,0},{8,15},{9,10},{10,... | collective-permute-start | bytes 196616 | tf_op jit(solution)/shard_map/ppermute | solution.py:534
  121.9 2.9 %collective-permute-done.37.refs_5_ = f32[128,128]{1,0:T(8,128)S(1)} collective-permute-done((f32[128,128]{1,0:T(8,128)S(1)}, f32[128,128]{1,0:T(8,128)S(1)}, u32[]{:S(2)}, u32[]{:S(2)}) %collective-permute-start.37) | collective-permute-done | bytes 65568 | tf_op jit(solution)/shard_map/ppermute | solution.py:534
  124.8 5.3 %final.1 = (f32[512,128]{1,0:T(8,128)}, f32[512,128]{1,0:T(8,128)}) custom-call(s32[2]{0:T(128)S(1)} %copy-done.5, f32[512,128]{1,0:T(8,128)S(1)} %scatter.5.own.refs_1_, f32[192,128]{1,0:T(8,128)S(1)} %get-tuple-element.66.refs_2_, f32[192,128]{1,0:T(8,128)S(1)} %get-tuple-element.67.refs_3_, f32[128,128]{1,0:T(8,128)S(1)} %collective-permute-done.36.refs_4_, ...), custom_call_target="tpu_custom_call" | custom-call | tf_op jit(solution)/shard_map/final/pallas_call | solution.py:594
  (78 shorter events, 5.6 us)
Async XLA Ops:
  0.6 1.0 copy-start
  1.6 0.9 copy-start.1
  2.5 0.8 copy-start.2
  3.3 0.8 copy-start.3
  4.0 0.7 copy-start.4
  5.0 7.4 %collective-permute-start = (f32[72,128]{1,0:T(8,128)S(1)}, f32[72,128]{1,0:T(8,128)S(1)}, u32[]{:S(2)}, u32[]{:S(2)}) collective-permute-start(f32[72,128]{1,0:T(8,128)S(1)} %get-tuple-element.38.refs_0_), channel_id=1, source_target_pairs={{0,2},{1,3},{2,0},{3,1},{4,6},{5,7},{6,4},{7,5},{8,10},{9,11},{10,... | collective-permute-start | bytes 110600 | tf_op jit(solution)/shard_map/ppermute | solution.py:534
  8.1 5.9 %collective-permute-start.1 = (f32[72,128]{1,0:T(8,128)S(1)}, f32[72,128]{1,0:T(8,128)S(1)}, u32[]{:S(2)}, u32[]{:S(2)}) collective-permute-start(f32[72,128]{1,0:T(8,128)S(1)} %get-tuple-element.38.refs_0_), channel_id=1, source_target_pairs={{0,4},{1,5},{2,6},{3,7},{4,0},{5,1},{6,2},{7,3},{8,12},{9,13},{10,... | collective-permute-start | bytes 110600 | tf_op jit(solution)/shard_map/ppermute | solution.py:534
  10.7 5.8 %collective-permute-start.2 = (f32[72,128]{1,0:T(8,128)S(1)}, f32[72,128]{1,0:T(8,128)S(1)}, u32[]{:S(2)}, u32[]{:S(2)}) collective-permute-start(f32[72,128]{1,0:T(8,128)S(1)} %get-tuple-element.38.refs_0_), channel_id=1, source_target_pairs={{0,6},{1,7},{2,4},{3,5},{4,2},{5,3},{6,0},{7,1},{8,14},{9,15},{10,... | collective-permute-start | bytes 110600 | tf_op jit(solution)/shard_map/ppermute | solution.py:534
  10.7 5.8 %collective-permute-start.3 = (f32[72,128]{1,0:T(8,128)S(1)}, f32[72,128]{1,0:T(8,128)S(1)}, u32[]{:S(2)}, u32[]{:S(2)}) collective-permute-start(f32[72,128]{1,0:T(8,128)S(1)} %get-tuple-element.38.refs_0_), channel_id=1, source_target_pairs={{0,1},{1,0},{2,3},{3,2},{4,5},{5,4},{6,7},{7,6},{8,9},{9,8},{10,11... | collective-permute-start | bytes 110600 | tf_op jit(solution)/shard_map/ppermute | solution.py:534
  10.7 13.7 %collective-permute-start.7 = (f32[584,128]{1,0:T(8,128)S(1)}, f32[584,128]{1,0:T(8,128)S(1)}, u32[]{:S(2)}, u32[]{:S(2)}) collective-permute-start(f32[584,128]{1,0:T(8,128)S(1)} %get-tuple-element.42), channel_id=1, source_target_pairs={{0,8},{8,0},{16,24},{24,16},{1,9},{9,1},{17,25},{25,17},{2,10},{10... | collective-permute-start | bytes 897032 | tf_op jit(solution)/shard_map/ppermute | solution.py:534
  12.4 15.7 %collective-permute-start.8 = (f32[584,128]{1,0:T(8,128)S(1)}, f32[584,128]{1,0:T(8,128)S(1)}, u32[]{:S(2)}, u32[]{:S(2)}) collective-permute-start(f32[584,128]{1,0:T(8,128)S(1)} %get-tuple-element.43), channel_id=1, source_target_pairs={{0,24},{8,16},{16,8},{24,0},{1,25},{9,17},{17,9},{25,1},{2,26},{10... | collective-permute-start | bytes 897032 | tf_op jit(solution)/shard_map/ppermute | solution.py:534
  14.0 3.0 %collective-permute-start.4 = (f32[72,128]{1,0:T(8,128)S(1)}, f32[72,128]{1,0:T(8,128)S(1)}, u32[]{:S(2)}, u32[]{:S(2)}) collective-permute-start(f32[72,128]{1,0:T(8,128)S(1)} %collective-permute-done.refs_1_), channel_id=1, source_target_pairs={{0,1},{1,0},{2,3},{3,2},{4,5},{5,4},{6,7},{7,6},{8,9},{9,8},{10,11... | collective-permute-start | bytes 110600 | tf_op jit(solution)/shard_map/ppermute | solution.py:534
  16.5 1.2 collective-permute-start.5
  16.5 1.4 %collective-permute-start.6 = (f32[72,128]{1,0:T(8,128)S(1)}, f32[72,128]{1,0:T(8,128)S(1)}, u32[]{:S(2)}, u32[]{:S(2)}) collective-permute-start(f32[72,128]{1,0:T(8,128)S(1)} %collective-permute-done.2.refs_3_), channel_id=1, source_target_pairs={{0,1},{1,0},{2,3},{3,2},{4,5},{5,4},{6,7},{7,6},{8,9},{9,8},{10,11... | collective-permute-start | bytes 110600 | tf_op jit(solution)/shard_map/ppermute | solution.py:534
  21.3 21.2 %copy-start.5 = (s32[2]{0:T(128)S(1)}, s32[2]{0:T(128)}, u32[]{:S(2)}) copy-start(s32[2]{0:T(128)} %refs_0_.7) | copy-start | bytes 28
  21.3 11.6 %collective-permute-start.10 = (f32[192,128]{1,0:T(8,128)S(1)}, f32[192,128]{1,0:T(8,128)S(1)}, u32[]{:S(2)}, u32[]{:S(2)}) collective-permute-start(f32[192,128]{1,0:T(8,128)S(1)} %get-tuple-element.39.message), channel_id=1, source_target_pairs={{0,24},{8,16},{16,8},{24,0},{1,25},{9,17},{17,9},{25,1},{2,26},{10... | collective-permute-start | bytes 294920 | tf_op jit(solution)/shard_map/ppermute | solution.py:534
  23.9 9.1 %collective-permute-start.9 = (f32[192,128]{1,0:T(8,128)S(1)}, f32[192,128]{1,0:T(8,128)S(1)}, u32[]{:S(2)}, u32[]{:S(2)}) collective-permute-start(f32[192,128]{1,0:T(8,128)S(1)} %get-tuple-element.39.message), channel_id=1, source_target_pairs={{0,8},{8,0},{16,24},{24,16},{1,9},{9,1},{17,25},{25,17},{2,10},{10... | collective-permute-start | bytes 294920 | tf_op jit(solution)/shard_map/ppermute | solution.py:534
  29.0 7.1 %collective-permute-start.13 = (f32[456,128]{1,0:T(8,128)}, f32[456,128]{1,0:T(8,128)S(1)}, u32[]{:S(2)}, u32[]{:S(2)}) collective-permute-start(f32[456,128]{1,0:T(8,128)} %get-tuple-element.44), channel_id=1, source_target_pairs={{0,1},{1,0},{2,3},{3,2},{4,5},{5,4},{6,7},{7,6},{8,9},{9,8},{10,11... | collective-permute-start | bytes 700424 | tf_op jit(solution)/shard_map/ppermute | solution.py:534
  29.0 9.8 %collective-permute-start.14 = (f32[456,128]{1,0:T(8,128)S(1)}, f32[456,128]{1,0:T(8,128)S(1)}, u32[]{:S(2)}, u32[]{:S(2)}) collective-permute-start(f32[456,128]{1,0:T(8,128)S(1)} %get-tuple-element.45), channel_id=1, source_target_pairs={{0,7},{1,2},{2,1},{3,4},{4,3},{5,6},{6,5},{7,0},{8,15},{9,10},{10,... | collective-permute-start | bytes 700424 | tf_op jit(solution)/shard_map/ppermute | solution.py:534
  34.2 6.7 %collective-permute-start.11 = (f32[328,128]{1,0:T(8,128)}, f32[328,128]{1,0:T(8,128)S(1)}, u32[]{:S(2)}, u32[]{:S(2)}) collective-permute-start(f32[328,128]{1,0:T(8,128)} %get-tuple-element.50), channel_id=1, source_target_pairs={{0,1},{1,0},{2,3},{3,2},{4,5},{5,4},{6,7},{7,6},{8,9},{9,8},{10,11... | collective-permute-start | bytes 503816 | tf_op jit(solution)/shard_map/ppermute | solution.py:534
  34.2 8.3 %collective-permute-start.12 = (f32[328,128]{1,0:T(8,128)}, f32[328,128]{1,0:T(8,128)S(1)}, u32[]{:S(2)}, u32[]{:S(2)}) collective-permute-start(f32[328,128]{1,0:T(8,128)} %get-tuple-element.51), channel_id=1, source_target_pairs={{0,7},{1,2},{2,1},{3,4},{4,3},{5,6},{6,5},{7,0},{8,15},{9,10},{10,... | collective-permute-start | bytes 503816 | tf_op jit(solution)/shard_map/ppermute | solution.py:534
  55.6 4.6 %collective-permute-start.15 = (f32[104,128]{1,0:T(8,128)S(1)}, f32[104,128]{1,0:T(8,128)S(1)}, u32[]{:S(2)}, u32[]{:S(2)}) collective-permute-start(f32[104,128]{1,0:T(8,128)S(1)} %get-tuple-element.57.refs_0_), channel_id=1, source_target_pairs={{0,2},{1,3},{2,0},{3,1},{4,6},{5,7},{6,4},{7,5},{8,10},{9,11},{10,... | collective-permute-start | bytes 159752 | tf_op jit(solution)/shard_map/ppermute | solution.py:534
  55.7 5.1 %collective-permute-start.16 = (f32[104,128]{1,0:T(8,128)S(1)}, f32[104,128]{1,0:T(8,128)S(1)}, u32[]{:S(2)}, u32[]{:S(2)}) collective-permute-start(f32[104,128]{1,0:T(8,128)S(1)} %get-tuple-element.57.refs_0_), channel_id=1, source_target_pairs={{0,4},{1,5},{2,6},{3,7},{4,0},{5,1},{6,2},{7,3},{8,12},{9,13},{10,... | collective-permute-start | bytes 159752 | tf_op jit(solution)/shard_map/ppermute | solution.py:534
  57.0 6.3 %collective-permute-start.17 = (f32[104,128]{1,0:T(8,128)S(1)}, f32[104,128]{1,0:T(8,128)S(1)}, u32[]{:S(2)}, u32[]{:S(2)}) collective-permute-start(f32[104,128]{1,0:T(8,128)S(1)} %get-tuple-element.57.refs_0_), channel_id=1, source_target_pairs={{0,6},{1,7},{2,4},{3,5},{4,2},{5,3},{6,0},{7,1},{8,14},{9,15},{10,... | collective-permute-start | bytes 159752 | tf_op jit(solution)/shard_map/ppermute | solution.py:534
  60.1 3.7 %collective-permute-start.18 = (f32[104,128]{1,0:T(8,128)S(1)}, f32[104,128]{1,0:T(8,128)S(1)}, u32[]{:S(2)}, u32[]{:S(2)}) collective-permute-start(f32[104,128]{1,0:T(8,128)S(1)} %get-tuple-element.57.refs_0_), channel_id=1, source_target_pairs={{0,1},{1,0},{2,3},{3,2},{4,5},{5,4},{6,7},{7,6},{8,9},{9,8},{10,11... | collective-permute-start | bytes 159752 | tf_op jit(solution)/shard_map/ppermute | solution.py:534
  60.2 3.6 %collective-permute-start.19 = (f32[104,128]{1,0:T(8,128)S(1)}, f32[104,128]{1,0:T(8,128)S(1)}, u32[]{:S(2)}, u32[]{:S(2)}) collective-permute-start(f32[104,128]{1,0:T(8,128)S(1)} %collective-permute-done.15.refs_1_), channel_id=1, source_target_pairs={{0,1},{1,0},{2,3},{3,2},{4,5},{5,4},{6,7},{7,6},{8,9},{9,8},{10,11... | collective-permute-start | bytes 159752 | tf_op jit(solution)/shard_map/ppermute | solution.py:534
  60.8 2.9 %collective-permute-start.20 = (f32[104,128]{1,0:T(8,128)S(1)}, f32[104,128]{1,0:T(8,128)S(1)}, u32[]{:S(2)}, u32[]{:S(2)}) collective-permute-start(f32[104,128]{1,0:T(8,128)S(1)} %collective-permute-done.16.refs_2_), channel_id=1, source_target_pairs={{0,1},{1,0},{2,3},{3,2},{4,5},{5,4},{6,7},{7,6},{8,9},{9,8},{10,11... | collective-permute-start | bytes 159752 | tf_op jit(solution)/shard_map/ppermute | solution.py:534
  63.3 1.2 collective-permute-start.21
  68.4 5.9 %collective-permute-start.22 = (f32[208,128]{1,0:T(8,128)S(1)}, f32[208,128]{1,0:T(8,128)S(1)}, u32[]{:S(2)}, u32[]{:S(2)}) collective-permute-start(f32[208,128]{1,0:T(8,128)S(1)} %adjoint_next.2.message), channel_id=1, source_target_pairs={{0,8},{8,0},{16,24},{24,16},{1,9},{9,1},{17,25},{25,17},{2,10},{10... | collective-permute-start | bytes 319496 | tf_op jit(solution)/shard_map/ppermute | solution.py:534
  70.0 5.9 %collective-permute-start.23 = (f32[208,128]{1,0:T(8,128)S(1)}, f32[208,128]{1,0:T(8,128)S(1)}, u32[]{:S(2)}, u32[]{:S(2)}) collective-permute-start(f32[208,128]{1,0:T(8,128)S(1)} %adjoint_next.2.message), channel_id=1, source_target_pairs={{0,24},{8,16},{16,8},{24,0},{1,25},{9,17},{17,9},{25,1},{2,26},{10... | collective-permute-start | bytes 319496 | tf_op jit(solution)/shard_map/ppermute | solution.py:534
  70.5 8.7 %collective-permute-start.26 = (f32[16,128]{1,0:T(8,128)S(1)}, f32[16,128]{1,0:T(8,128)S(1)}, u32[]{:S(2)}, u32[]{:S(2)}) collective-permute-start(f32[16,128]{1,0:T(8,128)S(1)} %slice.81), channel_id=1, source_target_pairs={{0,16},{8,24},{16,0},{24,8},{1,17},{9,25},{17,1},{25,9},{2,18},{10... | collective-permute-start | bytes 24584 | tf_op jit(solution)/shard_map/ppermute | solution.py:534
  76.3 2.9 %collective-permute-start.24 = (f32[328,128]{1,0:T(8,128)S(1)}, f32[328,128]{1,0:T(8,128)S(1)}, u32[]{:S(2)}, u32[]{:S(2)}) collective-permute-start(f32[328,128]{1,0:T(8,128)S(1)} %get-tuple-element.61), channel_id=1, source_target_pairs={{0,1},{1,0},{2,3},{3,2},{4,5},{5,4},{6,7},{7,6},{8,9},{9,8},{10,11... | collective-permute-start | bytes 503816 | tf_op jit(solution)/shard_map/ppermute | solution.py:534
  76.4 7.9 %collective-permute-start.25 = (f32[328,128]{1,0:T(8,128)S(1)}, f32[328,128]{1,0:T(8,128)S(1)}, u32[]{:S(2)}, u32[]{:S(2)}) collective-permute-start(f32[328,128]{1,0:T(8,128)S(1)} %get-tuple-element.62), channel_id=1, source_target_pairs={{0,7},{1,2},{2,1},{3,4},{4,3},{5,6},{6,5},{7,0},{8,15},{9,10},{10,... | collective-permute-start | bytes 503816 | tf_op jit(solution)/shard_map/ppermute | solution.py:534
  97.6 4.5 %collective-permute-start.27 = (f32[104,128]{1,0:T(8,128)S(1)}, f32[104,128]{1,0:T(8,128)S(1)}, u32[]{:S(2)}, u32[]{:S(2)}) collective-permute-start(f32[104,128]{1,0:T(8,128)S(1)} %get-tuple-element.65.refs_0_), channel_id=1, source_target_pairs={{0,2},{1,3},{2,0},{3,1},{4,6},{5,7},{6,4},{7,5},{8,10},{9,11},{10,... | collective-permute-start | bytes 159752 | tf_op jit(solution)/shard_map/ppermute | solution.py:534
  97.7 5.4 %collective-permute-start.28 = (f32[104,128]{1,0:T(8,128)S(1)}, f32[104,128]{1,0:T(8,128)S(1)}, u32[]{:S(2)}, u32[]{:S(2)}) collective-permute-start(f32[104,128]{1,0:T(8,128)S(1)} %get-tuple-element.65.refs_0_), channel_id=1, source_target_pairs={{0,4},{1,5},{2,6},{3,7},{4,0},{5,1},{6,2},{7,3},{8,12},{9,13},{10,... | collective-permute-start | bytes 159752 | tf_op jit(solution)/shard_map/ppermute | solution.py:534
  97.9 7.5 %collective-permute-start.29 = (f32[104,128]{1,0:T(8,128)S(1)}, f32[104,128]{1,0:T(8,128)S(1)}, u32[]{:S(2)}, u32[]{:S(2)}) collective-permute-start(f32[104,128]{1,0:T(8,128)S(1)} %get-tuple-element.65.refs_0_), channel_id=1, source_target_pairs={{0,6},{1,7},{2,4},{3,5},{4,2},{5,3},{6,0},{7,1},{8,14},{9,15},{10,... | collective-permute-start | bytes 159752 | tf_op jit(solution)/shard_map/ppermute | solution.py:534
  102.1 3.3 %collective-permute-start.30 = (f32[104,128]{1,0:T(8,128)S(1)}, f32[104,128]{1,0:T(8,128)S(1)}, u32[]{:S(2)}, u32[]{:S(2)}) collective-permute-start(f32[104,128]{1,0:T(8,128)S(1)} %get-tuple-element.65.refs_0_), channel_id=1, source_target_pairs={{0,1},{1,0},{2,3},{3,2},{4,5},{5,4},{6,7},{7,6},{8,9},{9,8},{10,11... | collective-permute-start | bytes 159752 | tf_op jit(solution)/shard_map/ppermute | solution.py:534
  102.1 3.3 %collective-permute-start.31 = (f32[104,128]{1,0:T(8,128)S(1)}, f32[104,128]{1,0:T(8,128)S(1)}, u32[]{:S(2)}, u32[]{:S(2)}) collective-permute-start(f32[104,128]{1,0:T(8,128)S(1)} %collective-permute-done.27.refs_1_), channel_id=1, source_target_pairs={{0,1},{1,0},{2,3},{3,2},{4,5},{5,4},{6,7},{7,6},{8,9},{9,8},{10,11... | collective-permute-start | bytes 159752 | tf_op jit(solution)/shard_map/ppermute | solution.py:534
  103.1 2.3 %collective-permute-start.32 = (f32[104,128]{1,0:T(8,128)S(1)}, f32[104,128]{1,0:T(8,128)S(1)}, u32[]{:S(2)}, u32[]{:S(2)}) collective-permute-start(f32[104,128]{1,0:T(8,128)S(1)} %collective-permute-done.28.refs_2_), channel_id=1, source_target_pairs={{0,1},{1,0},{2,3},{3,2},{4,5},{5,4},{6,7},{7,6},{8,9},{9,8},{10,11... | collective-permute-start | bytes 159752 | tf_op jit(solution)/shard_map/ppermute | solution.py:534
  105.4 1.2 collective-permute-start.33
  110.5 5.2 %collective-permute-start.34 = (f32[208,128]{1,0:T(8,128)S(1)}, f32[208,128]{1,0:T(8,128)S(1)}, u32[]{:S(2)}, u32[]{:S(2)}) collective-permute-start(f32[208,128]{1,0:T(8,128)S(1)} %adjoint_next.3.message), channel_id=1, source_target_pairs={{0,8},{8,0},{16,24},{24,16},{1,9},{9,1},{17,25},{25,17},{2,10},{10... | collective-permute-start | bytes 319496 | tf_op jit(solution)/shard_map/ppermute | solution.py:534
  112.0 6.8 %collective-permute-start.35 = (f32[208,128]{1,0:T(8,128)S(1)}, f32[208,128]{1,0:T(8,128)S(1)}, u32[]{:S(2)}, u32[]{:S(2)}) collective-permute-start(f32[208,128]{1,0:T(8,128)S(1)} %adjoint_next.3.message), channel_id=1, source_target_pairs={{0,24},{8,16},{16,8},{24,0},{1,25},{9,17},{17,9},{25,1},{2,26},{10... | collective-permute-start | bytes 319496 | tf_op jit(solution)/shard_map/ppermute | solution.py:534
  113.5 8.4 %collective-permute-start.38 = (f32[16,128]{1,0:T(8,128)S(1)}, f32[16,128]{1,0:T(8,128)S(1)}, u32[]{:S(2)}, u32[]{:S(2)}) collective-permute-start(f32[16,128]{1,0:T(8,128)S(1)} %slice.84), channel_id=1, source_target_pairs={{0,16},{8,24},{16,0},{24,8},{1,17},{9,25},{17,1},{25,9},{2,18},{10... | collective-permute-start | bytes 24584 | tf_op jit(solution)/shard_map/ppermute | solution.py:534
  119.1 2.8 %collective-permute-start.36 = (f32[128,128]{1,0:T(8,128)S(1)}, f32[128,128]{1,0:T(8,128)S(1)}, u32[]{:S(2)}, u32[]{:S(2)}) collective-permute-start(f32[128,128]{1,0:T(8,128)S(1)} %get-tuple-element.68), channel_id=1, source_target_pairs={{0,1},{1,0},{2,3},{3,2},{4,5},{5,4},{6,7},{7,6},{8,9},{9,8},{10,11... | collective-permute-start | bytes 196616 | tf_op jit(solution)/shard_map/ppermute | solution.py:534
  119.2 5.6 %collective-permute-start.37 = (f32[128,128]{1,0:T(8,128)S(1)}, f32[128,128]{1,0:T(8,128)S(1)}, u32[]{:S(2)}, u32[]{:S(2)}) collective-permute-start(f32[128,128]{1,0:T(8,128)S(1)} %get-tuple-element.69), channel_id=1, source_target_pairs={{0,7},{1,2},{2,1},{3,4},{4,3},{5,6},{6,5},{7,0},{8,15},{9,10},{10,... | collective-permute-start | bytes 196616 | tf_op jit(solution)/shard_map/ppermute | solution.py:534

commit v2 on v1

--- a/solution.py
+++ b/solution.py
@@ -9,6 +9,7 @@
 
 LANES = 128
 VMEM_LIMIT = 48 * 1024 * 1024
+START_LIMIT = 60 * 1024 * 1024
 REACH = 6
 FRAME = 2 * REACH
 
@@ -75,23 +76,35 @@
     lateral_passes(buf, face_lat, face_lon, nh, 2 * nh - close, 2 * nh, left, right)
 
 
-def vertical_passes(buf, keep, up, down, first, last, tile, offset, nv, left, right):
+def shift_matrix():
+    source = lax.broadcasted_iota(jnp.int32, (2 * LANES, 2 * LANES), 0) % LANES
+    target = lax.broadcasted_iota(jnp.int32, (2 * LANES, 2 * LANES), 1)
+    wanted = jnp.where(target < LANES, target + 1, target - LANES - 1)
+    return (source == wanted).astype(jnp.bfloat16)
+
+
+def vertical_passes(buf, keep, up, down, first, last, offset, nv, left, right):
     cols = slice(left, right)
+    width = right - left
+    shifts = shift_matrix()
+    at = list(range(first, last))
+    half = (last - first) // 2
 
     def sweep(p, c):
-        def rows(t, c):
-            at = [first + t * tile + k for k in range(tile)]
-            values = [buf[i, cols] for i in at]
-            values = [
-                keep[i - offset, cols] * w
-                + (up[i - offset, cols] * pltpu.roll(w, LANES - 1, 1)
-                   + down[i - offset, cols] * pltpu.roll(w, 1, 1))
-                for i, w in zip(at, values)
-            ]
-            for i, w in zip(at, values):
-                buf[i, cols] = w
-            return c
-        return lax.fori_loop(0, (last - first) // tile, rows, c)
+        values = [buf[i, cols] for i in at]
+        stack = jnp.concatenate(values[:half], axis=0)
+        high = stack.astype(jnp.bfloat16)
+        low = (stack - high.astype(jnp.float32)).astype(jnp.bfloat16)
+        moved = jnp.dot(jnp.concatenate([high, low], axis=1), shifts, preferred_element_type=jnp.float32)
+        for n, (i, w) in enumerate(zip(at, values)):
+            if n < half:
+                here = moved[width * n:width * n + width]
+                above, below = here[:, :LANES], here[:, LANES:]
+            else:
+                above, below = pltpu.roll(w, LANES - 1, 1), pltpu.roll(w, 1, 1)
+            buf[i, cols] = keep[i - offset, cols] * w + (
+                up[i - offset, cols] * above + down[i - offset, cols] * below)
+        return c
 
     lax.fori_loop(0, nv, sweep, 0)
 
@@ -295,7 +308,7 @@
     lane = lax.broadcasted_iota(jnp.int32, (obs, LANES), 1)
 
     ones = jnp.ones((2 * LANES, LANES), jnp.bfloat16)
-    group = 16
+    group = 64
 
     def part(first, count):
         def body(step, acc):
@@ -326,7 +339,7 @@
     else:
         row_hot, weight, own_hot, jac_hbm, out, jac, taken, sems = refs
     slots, obs, _ = jac.shape
-    group = 32
+    group = 64
     groups = slots // group
 
     def chunk(g):
@@ -402,26 +415,27 @@
     one_hbm, two_hbm, message = refs[:3]
     refs = refs[3:]
     face_lat, face_lon, keep, up, down, jac, one, two, grad, buf, mid, sems = refs
-    loads = copies(
-        list(zip(faces_hbm, (face_lat, face_lon, keep, up, down))) + [(jac_hbm, jac)], sems
-    )
-    if not first_call:
-        old_loads = copies([(grad_hbm, grad), (spread_hbm, two)], sems.at[pl.ds(6, 2)])
+    loads = copies(list(zip(faces_hbm[:2], (face_lat, face_lon))), sems)
     nh, nv = counts[0], counts[1]
     rows = lat_cells + 2 * FRAME
     width = buf.shape[1]
     place_halos(
         buf, own, ((from_a, 0), (from_b, 0)), ((from_x, 0), (from_s, 0)), FRAME, dims
     )
-    for load in loads[:2]:
+    for load in loads:
         load.wait()
+    loads = copies(
+        list(zip(faces_hbm[2:], (keep, up, down))) + [(jac_hbm, jac)], sems.at[pl.ds(2, 4)]
+    )
+    if not first_call:
+        old_loads = copies([(grad_hbm, grad), (spread_hbm, two)], sems.at[pl.ds(6, 2)])
     lateral_passes(buf, face_lat, face_lon, nh, 0, nh, 0, width)
     border = FRAME - REACH
     tall = lat_cells + 2 * REACH
     vertical = functools.partial(
-        vertical_passes, buf, keep, up, down, border, border + tall, tall // 2, border, nv, 0, width
+        vertical_passes, buf, keep, up, down, border, border + tall, border, nv, 0, width
     )
-    for load in loads[2:5]:
+    for load in loads[:3]:
         load.wait()
     vertical()
 
@@ -460,7 +474,7 @@
 
     norm = lax.fori_loop(0, lat_cells, finish, jnp.zeros((8, LANES), jnp.float32))
     stores = copies([(one, one_hbm), (two, two_hbm)], sems.at[pl.ds(8, 2)])
-    loads[5].wait()
+    loads[3].wait()
     obs = jac.shape[1]
     observe(cells, jac, two, message)
     message[obs + obs // 2:] = norm
@@ -491,7 +505,7 @@
     for load in loads[2:5]:
         load.wait()
     vertical_passes(
-        buf, keep, up, down, FRAME, FRAME + lat_cells, lat_cells, FRAME - REACH, nv, left, right
+        buf, keep, up, down, FRAME, FRAME + lat_cells, FRAME - REACH, nv, left, right
     )
     rr0 = jnp.sum(scal0[0:8])
     alpha0 = rr0 / (rr0 + jnp.sum(scal0[8:16]))
@@ -530,6 +544,9 @@
     def odd_pairs(n):
         return [(i, (i + 1) % n if i % 2 else (i - 1) % n) for i in range(n)]
 
+    inner_pairs = [(0, 0), (n_lat - 1, n_lat - 1)] + [
+        pair for i in range(1, n_lat - 1, 2) for pair in ((i, i + 1), (i + 1, i))]
+
     def send(x, axis, pairs):
         return lax.ppermute(x, axis, pairs)
 
@@ -540,11 +557,10 @@
     def lon_send(to_x, to_s):
         return send(to_x, "lon", swap(n_lon, 1)), send(to_s, "lon", odd_pairs(n_lon))
 
-    def lat_send(to_a, to_b):
-        return send(to_a, "lat", swap(n_lat, 1)), send(to_b, "lat", odd_pairs(n_lat))
-
-    def lat_sum(message, from_a, from_b):
-        tail = message[slots:]
+    def lat_send(to_a, to_b, pairs):
+        return send(to_a, "lat", swap(n_lat, 1)), send(to_b, "lat", pairs)
+
+    def lat_sum(tail, from_a, from_b):
         if n_lat != 4:
             return lax.psum(tail, "lat")
         return (tail + send(tail, "lat", swap(n_lat, 2))) + (from_a[slots:] + from_b[slots:])
@@ -561,10 +577,10 @@
         return (strip_a, strip_b), (to_x, to_s)
 
     def halo(message, reach):
-        from_a, from_b = lat_send(message, message)
+        from_a, from_b = lat_send(message, message, odd_pairs(n_lat))
         own = scatter(message)
         strips, sides = sides_of(own, from_a, from_b, reach)
-        return (own, *strips, *lon_send(*sides)), lat_sum(message, from_a, from_b)
+        return (own, *strips, *lon_send(*sides)), lat_sum(message[slots:], from_a, from_b)
 
     vmem = pl.BlockSpec(memory_space=pltpu.VMEM)
     smem = pl.BlockSpec(memory_space=pltpu.SMEM)
@@ -586,7 +602,7 @@
     faces_vmem = [wide_vmem] * 2 + [tall_vmem] * 3
     sems = lambda count: pltpu.SemaphoreType.DMA((count,))
 
-    def call(kernel, name, outs, ins, scalars=0, far_in=(), far_out=False, scratches=()):
+    def call(kernel, name, outs, ins, scalars=0, far_in=(), far_out=False, scratches=(), params=params):
         out_specs = jax.tree.map(lambda _: vmem, outs)
         if far_out:
             out_specs = (hbm,) * far_out + out_specs[far_out:]
@@ -601,8 +617,9 @@
                 kappa_h.reshape(cells_n, levels), kappa_v.reshape(cells_n, levels))
     first, root_h, root_v, to_a, to_b = call(
         functools.partial(start_kernel, dims), "start", (shape(obs + 8, LANES), field, field, strip, strip),
-        (), far_in=start_in, scratches=[pltpu.VMEM(v.shape, v.dtype) for v in start_in] + [sems(5)])
-    k_strips = lat_send(to_a, to_b)
+        (), far_in=start_in, scratches=[pltpu.VMEM(v.shape, v.dtype) for v in start_in] + [sems(5)],
+        params=pltpu.CompilerParams(vmem_limit_bytes=START_LIMIT))
+    k_strips = lat_send(to_a, to_b, inner_pairs)
     band = gather_band(first)
     cells_near = [v[(FRAME + REACH) * lon_cells:] for v in k_strips]
 
@@ -620,13 +637,13 @@
     cells = jnp.clip(block_list[1:], 0, cells_n - 1)
     cells_flat = cells.reshape(slots)
 
-    adj_scratch = [jac_vmem, scratch(2, obs, LANES), sems(slots // 32)]
+    adj_scratch = [jac_vmem, scratch(2, obs, LANES), sems(slots // 64)]
     message, weight = call(
         functools.partial(adjoint_kernel, True, parts), "adjoint_first",
         (shape(slots, levels), shape(obs, band_rows)), (*band, own_hot), far_in=(jacobian,),
         scratches=[scratch(obs, band_rows)] + adj_scratch)
 
-    from_a, from_b = lat_send(message, message)
+    from_a, from_b = lat_send(message, message, inner_pairs)
     own = scatter(message)
     side = shape(sum(side_rows(reach, lat_cells)[1] for reach in (FRAME, REACH)), levels)
     k_messages = call(functools.partial(face_sides_kernel, dims), "face_sides", (side, side),

time: 131 us -> 123 us (0.939)
  Pallas kernels: 48.9 us -> 44 us
  waiting for transfers between devices: 34.6 us -> 30.1 us
  local copies, waits for them, and re-layouts: 4.16 us -> 0.85 us
  starting transfers between devices: 40.8 us -> 43.5 us
    pallas_call x15, Pallas kernels: 48.9 us -> 44 us  [call(): pl.pallas_call(kernel, out_shape=outs, in_specs=specs, out_specs=out_spec...]
    ppermute x39, waiting for transfers between devices: 34.6 us -> 30.1 us  [send(): return lax.ppermute(x, axis, pairs)]
    unnamed x12 -> x8, local copies, waits for them, and re-layouts: 4.09 us -> 0.79 us
    ppermute x39, starting transfers between devices: 40.8 us -> 43.5 us  [send(): return lax.ppermute(x, axis, pairs)]
where the time goes in v2:
time: 123 us; the launch traced here: 121 us
  Pallas kernels  44 us (36%)
  starting transfers between devices  43.5 us (35%)
  waiting for transfers between devices  30.1 us (24%)
  other arithmetic  1.39 us (1%)
    pallas_call x15, Pallas kernels, call(): pl.pallas_call(kernel, out_shape=outs, in_specs=specs, out_specs=out_spec...  44 us
    ppermute x39, starting transfers between devices, send(): return lax.ppermute(x, axis, pairs)  43.5 us
    ppermute x39, waiting for transfers between devices, send(): return lax.ppermute(x, axis, pairs)  30.1 us
  transfers between devices with their start and end apart: 39, of which 18 were waited for; matrix products, arithmetic and copies ran while one was open for 1% of the time, Pallas kernels for 7%

profile of v2, /device:TPU:0, one launch (start us, length us, event | category | flops | bytes accessed | tf_op | source)
XLA Modules:
  0.0 121.0 jit_solution(16723054049513689648)
XLA Ops:
  0.6 2.3 %start.1 = (f32[72,128]{1,0:T(8,128)}, f32[512,128]{1,0:T(8,128)}, f32[512,128]{1,0:T(8,128)}, f32[584,128]{1,0:T(8,128)}, f32[584,128]{1,0:T(8,128)}) custom-call(f32[64,64]{1,0:T(8,128)} %refs_0_.4, f32[64,64]{1,0:T(8,128)} %refs_1_.1, s32[2,192]{1,0:T(2,128)} %refs_2_.1, f32[512,128]{1,0:T(8,128)} %bitcast.16, f32[512,128]{1,0:T(8,128)} %bitcast.17), custom_call_target="tpu_custom_call" | custom-call | tf_op jit(solution)/shard_map/start/pallas_call | solution.py:610
  2.9 3.1 %collective-permute-start = (f32[72,128]{1,0:T(8,128)}, f32[72,128]{1,0:T(8,128)S(1)}, u32[]{:S(2)}, u32[]{:S(2)}) collective-permute-start(f32[72,128]{1,0:T(8,128)} %get-tuple-element.38.refs_0_), channel_id=1, source_target_pairs={{0,2},{1,3},{2,0},{3,1},{4,6},{5,7},{6,4},{7,5},{8,10},{9,11},{10,... | collective-permute-start | bytes 110600 | tf_op jit(solution)/shard_map/ppermute | solution.py:551
  6.0 2.6 %collective-permute-start.1 = (f32[72,128]{1,0:T(8,128)}, f32[72,128]{1,0:T(8,128)S(1)}, u32[]{:S(2)}, u32[]{:S(2)}) collective-permute-start(f32[72,128]{1,0:T(8,128)} %get-tuple-element.38.refs_0_), channel_id=1, source_target_pairs={{0,4},{1,5},{2,6},{3,7},{4,0},{5,1},{6,2},{7,3},{8,12},{9,13},{10,... | collective-permute-start | bytes 110600 | tf_op jit(solution)/shard_map/ppermute | solution.py:551
  8.6 1.7 %collective-permute-start.7 = (f32[584,128]{1,0:T(8,128)}, f32[584,128]{1,0:T(8,128)S(1)}, u32[]{:S(2)}, u32[]{:S(2)}) collective-permute-start(f32[584,128]{1,0:T(8,128)} %get-tuple-element.42), channel_id=1, source_target_pairs={{0,8},{8,0},{16,24},{24,16},{1,9},{9,1},{17,25},{25,17},{2,10},{10... | collective-permute-start | bytes 897032 | tf_op jit(solution)/shard_map/ppermute | solution.py:551
  10.3 0.8 fusion.20
  11.1 1.6 %collective-permute-start.8 = (f32[584,128]{1,0:T(8,128)}, f32[584,128]{1,0:T(8,128)S(1)}, u32[]{:S(2)}, u32[]{:S(2)}) collective-permute-start(f32[584,128]{1,0:T(8,128)} %get-tuple-element.43), channel_id=1, source_target_pairs={{0,0},{24,24},{8,16},{16,8},{1,1},{25,25},{9,17},{17,9},{2,2},{26,... | collective-permute-start | bytes 897032 | tf_op jit(solution)/shard_map/ppermute | solution.py:551
  13.1 1.5 %collective-permute-done.2.refs_3_ = f32[72,128]{1,0:T(8,128)S(1)} collective-permute-done((f32[72,128]{1,0:T(8,128)}, f32[72,128]{1,0:T(8,128)S(1)}, u32[]{:S(2)}, u32[]{:S(2)}) %collective-permute-start.2) | collective-permute-done | bytes 36896 | tf_op jit(solution)/shard_map/ppermute | solution.py:551
  14.6 0.5 collective-permute-start.6
  15.2 0.6 collective-permute-done.5.refs_6_
  16.0 0.8 copy-done.2
  16.7 3.4 %adjoint_first.1 = (f32[192,128]{1,0:T(8,128)S(1)}, f32[64,512]{1,0:T(8,128)S(1)}) custom-call(f32[72,128]{1,0:T(8,128)S(1)} %copy-done.2, f32[72,128]{1,0:T(8,128)S(1)} %collective-permute-done.refs_1_, f32[72,128]{1,0:T(8,128)S(1)} %collective-permute-done.1.refs_2_, f32[72,128]{1,0:T(8,128)S(1)} %collective-permute-done.2.refs_3_, ...), custom_call_target="tpu_custom_call" | custom-call | tf_op jit(solution)/shard_map/adjoint_first/pallas_call | solution.py:610
  20.2 0.7 collective-permute-start.10
  20.9 4.3 %collective-permute-start.9 = (f32[192,128]{1,0:T(8,128)S(1)}, f32[192,128]{1,0:T(8,128)S(1)}, u32[]{:S(2)}, u32[]{:S(2)}) collective-permute-start(f32[192,128]{1,0:T(8,128)S(1)} %get-tuple-element.39.message), channel_id=1, source_target_pairs={{0,8},{8,0},{16,24},{24,16},{1,9},{9,1},{17,25},{25,17},{2,10},{10... | collective-permute-start | bytes 294920 | tf_op jit(solution)/shard_map/ppermute | solution.py:551
  25.2 0.8 face_sides.1
  26.0 3.1 %collective-permute-start.14 = (f32[456,128]{1,0:T(8,128)S(1)}, f32[456,128]{1,0:T(8,128)S(1)}, u32[]{:S(2)}, u32[]{:S(2)}) collective-permute-start(f32[456,128]{1,0:T(8,128)S(1)} %get-tuple-element.45), channel_id=1, source_target_pairs={{0,7},{1,2},{2,1},{3,4},{4,3},{5,6},{6,5},{7,0},{8,15},{9,10},{10,... | collective-permute-start | bytes 700424 | tf_op jit(solution)/shard_map/ppermute | solution.py:551
  29.4 0.8 collective-permute-done.9.from_a
  30.2 1.1 sides.3
  31.3 2.9 %collective-permute-start.12 = (f32[328,128]{1,0:T(8,128)S(1)}, f32[328,128]{1,0:T(8,128)S(1)}, u32[]{:S(2)}, u32[]{:S(2)}) collective-permute-start(f32[328,128]{1,0:T(8,128)S(1)} %get-tuple-element.51), channel_id=1, source_target_pairs={{0,7},{1,2},{2,1},{3,4},{4,3},{5,6},{6,5},{7,0},{8,15},{9,10},{10,... | collective-permute-start | bytes 503816 | tf_op jit(solution)/shard_map/ppermute | solution.py:551
  34.3 1.3 %collective-permute-done.14.from_s = f32[456,128]{1,0:T(8,128)S(1)} collective-permute-done((f32[456,128]{1,0:T(8,128)S(1)}, f32[456,128]{1,0:T(8,128)S(1)}, u32[]{:S(2)}, u32[]{:S(2)}) %collective-permute-start.14) | collective-permute-done | bytes 233504 | tf_op jit(solution)/shard_map/ppermute | solution.py:551
  35.6 2.1 %faces.1 = (f32[40,56,128]{2,1,0:T(8,128)S(1)}, f32[40,56,128]{2,1,0:T(8,128)}, f32[28,56,128]{2,1,0:T(8,128)S(1)}, f32[28,56,128]{2,1,0:T(8,128)S(1)}, f32[28,56,128]{2,1,0:T(8,128)S(1)}) custom-call(f32[512,128]{1,0:T(8,128)S(1)} %copy-done, f32[512,128]{1,0:T(8,128)S(1)} %copy-done.1, f32[584,128]{1,0:T(8,128)S(1)} %collective-permute-done.7.from_a, ...), custom_call_target="tpu_custom_call" | custom-call | tf_op jit(solution)/shard_map/faces/pallas_call | solution.py:610
  37.7 1.5 %collective-permute-done.12.refs_6_ = f32[328,128]{1,0:T(8,128)S(1)} collective-permute-done((f32[328,128]{1,0:T(8,128)S(1)}, f32[328,128]{1,0:T(8,128)S(1)}, u32[]{:S(2)}, u32[]{:S(2)}) %collective-permute-start.12) | collective-permute-done | bytes 167968 | tf_op jit(solution)/shard_map/ppermute | solution.py:551
  39.2 9.7 %spread_first.1 = (f32[512,128]{1,0:T(8,128)S(1)}, f32[512,128]{1,0:T(8,128)S(1)}, f32[104,128]{1,0:T(8,128)S(1)}) custom-call(s32[2]{0:T(128)S(1)} %copy-done.3, s32[192]{0:T(256)S(1)} %bitcast.14, f32[512,128]{1,0:T(8,128)S(1)} %scatter.3.own.refs_2_, f32[384,128]{1,0:T(8,128)S(1)} %get-tuple-element.48.refs_3_, f32[384,128]{1,0:T(8,128)S(1)} %get-tuple-element.49.refs_4_, ...), custom_call_target="tpu_custom_call" | custom-call | tf_op jit(solution)/shard_map/spread_first/pallas_call | solution.py:610
  49.3 4.1 %collective-permute-start.17 = (f32[104,128]{1,0:T(8,128)S(1)}, f32[104,128]{1,0:T(8,128)S(1)}, u32[]{:S(2)}, u32[]{:S(2)}) collective-permute-start(f32[104,128]{1,0:T(8,128)S(1)} %get-tuple-element.57.refs_0_), channel_id=1, source_target_pairs={{0,6},{1,7},{2,4},{3,5},{4,2},{5,3},{6,0},{7,1},{8,14},{9,15},{10,... | collective-permute-start | bytes 159752 | tf_op jit(solution)/shard_map/ppermute | solution.py:551
  54.0 0.6 collective-permute-done.16.refs_2_
  54.6 2.1 %collective-permute-done.17.refs_3_ = f32[104,128]{1,0:T(8,128)S(1)} collective-permute-done((f32[104,128]{1,0:T(8,128)S(1)}, f32[104,128]{1,0:T(8,128)S(1)}, u32[]{:S(2)}, u32[]{:S(2)}) %collective-permute-start.17) | collective-permute-done | bytes 53280 | tf_op jit(solution)/shard_map/ppermute | solution.py:551
  56.7 0.5 fusion.refs_8_
  57.3 0.7 collective-permute-done.21.refs_7_
  58.0 4.0 %adjoint_next.2.message = f32[208,128]{1,0:T(8,128)S(1)} custom-call(f32[104,128]{1,0:T(8,128)S(1)} %get-tuple-element.57.refs_0_, f32[104,128]{1,0:T(8,128)S(1)} %collective-permute-done.15.refs_1_, f32[104,128]{1,0:T(8,128)S(1)} %collective-permute-done.16.refs_2_, f32[104,128]{1,0:T(8,128)S(1)} %collective-permute-done.17.refs_3_, ...), custom_call_target="tpu_custom_call" | custom-call | tf_op jit(solution)/shard_map/adjoint_next/pallas_call | solution.py:610
  62.0 2.5 %collective-permute-start.22 = (f32[208,128]{1,0:T(8,128)S(1)}, f32[208,128]{1,0:T(8,128)S(1)}, u32[]{:S(2)}, u32[]{:S(2)}) collective-permute-start(f32[208,128]{1,0:T(8,128)S(1)} %adjoint_next.2.message), channel_id=1, source_target_pairs={{0,8},{8,0},{16,24},{24,16},{1,9},{9,1},{17,25},{25,17},{2,10},{10... | collective-permute-start | bytes 319496 | tf_op jit(solution)/shard_map/ppermute | solution.py:551
  64.4 1.1 collective-permute-start.23
  66.3 1.9 %collective-permute-done.22.from_a = f32[208,128]{1,0:T(8,128)S(1)} collective-permute-done((f32[208,128]{1,0:T(8,128)S(1)}, f32[208,128]{1,0:T(8,128)S(1)}, u32[]{:S(2)}, u32[]{:S(2)}) %collective-permute-start.22) | collective-permute-done | bytes 106528 | tf_op jit(solution)/shard_map/ppermute | solution.py:551
  68.2 2.6 %collective-permute-done.23.from_b = f32[208,128]{1,0:T(8,128)S(1)} collective-permute-done((f32[208,128]{1,0:T(8,128)S(1)}, f32[208,128]{1,0:T(8,128)S(1)}, u32[]{:S(2)}, u32[]{:S(2)}) %collective-permute-start.23) | collective-permute-done | bytes 106528 | tf_op jit(solution)/shard_map/ppermute | solution.py:551
  71.3 2.3 %collective-permute-start.25 = (f32[328,128]{1,0:T(8,128)S(1)}, f32[328,128]{1,0:T(8,128)S(1)}, u32[]{:S(2)}, u32[]{:S(2)}) collective-permute-start(f32[328,128]{1,0:T(8,128)S(1)} %get-tuple-element.62), channel_id=1, source_target_pairs={{0,7},{1,2},{2,1},{3,4},{4,3},{5,6},{6,5},{7,0},{8,15},{9,10},{10,... | collective-permute-start | bytes 503816 | tf_op jit(solution)/shard_map/ppermute | solution.py:551
  73.6 5.1 %collective-permute-done.25.refs_6_ = f32[328,128]{1,0:T(8,128)S(1)} collective-permute-done((f32[328,128]{1,0:T(8,128)S(1)}, f32[328,128]{1,0:T(8,128)S(1)}, u32[]{:S(2)}, u32[]{:S(2)}) %collective-permute-start.25) | collective-permute-done | bytes 167968 | tf_op jit(solution)/shard_map/ppermute | solution.py:551
  78.7 10.1 %spread_next.1 = (f32[512,128]{1,0:T(8,128)S(1)}, f32[512,128]{1,0:T(8,128)S(1)}, f32[104,128]{1,0:T(8,128)S(1)}) custom-call(s32[2]{0:T(128)S(1)} %copy-done.3, s32[192]{0:T(256)S(1)} %bitcast.15, f32[512,128]{1,0:T(8,128)S(1)} %scatter.4.own.refs_2_, f32[384,128]{1,0:T(8,128)S(1)} %get-tuple-element.59.refs_3_, f32[384,128]{1,0:T(8,128)S(1)} %get-tuple-element.60.refs_4_, ...), custom_call_target="tpu_custom_call" | custom-call | tf_op jit(solution)/shard_map/spread_next/pallas_call | solution.py:610
  89.1 4.2 %collective-permute-start.29 = (f32[104,128]{1,0:T(8,128)S(1)}, f32[104,128]{1,0:T(8,128)S(1)}, u32[]{:S(2)}, u32[]{:S(2)}) collective-permute-start(f32[104,128]{1,0:T(8,128)S(1)} %get-tuple-element.65.refs_0_), channel_id=1, source_target_pairs={{0,6},{1,7},{2,4},{3,5},{4,2},{5,3},{6,0},{7,1},{8,14},{9,15},{10,... | collective-permute-start | bytes 159752 | tf_op jit(solution)/shard_map/ppermute | solution.py:551
  93.3 0.5 collective-permute-start.31
  94.3 2.3 %collective-permute-done.29.refs_3_ = f32[104,128]{1,0:T(8,128)S(1)} collective-permute-done((f32[104,128]{1,0:T(8,128)S(1)}, f32[104,128]{1,0:T(8,128)S(1)}, u32[]{:S(2)}, u32[]{:S(2)}) %collective-permute-start.29) | collective-permute-done | bytes 53280 | tf_op jit(solution)/shard_map/ppermute | solution.py:551
  96.6 1.2 %collective-permute-done.33.refs_7_ = f32[104,128]{1,0:T(8,128)S(1)} collective-permute-done((f32[104,128]{1,0:T(8,128)S(1)}, f32[104,128]{1,0:T(8,128)S(1)}, u32[]{:S(2)}, u32[]{:S(2)}) %collective-permute-start.33) | collective-permute-done | bytes 53280 | tf_op jit(solution)/shard_map/ppermute | solution.py:551
  97.8 4.0 %adjoint_next.3.message = f32[208,128]{1,0:T(8,128)S(1)} custom-call(f32[104,128]{1,0:T(8,128)S(1)} %get-tuple-element.65.refs_0_, f32[104,128]{1,0:T(8,128)S(1)} %collective-permute-done.27.refs_1_, f32[104,128]{1,0:T(8,128)S(1)} %collective-permute-done.28.refs_2_, f32[104,128]{1,0:T(8,128)S(1)} %collective-permute-done.29.refs_3_, ...), custom_call_target="tpu_custom_call" | custom-call | tf_op jit(solution)/shard_map/adjoint_next/pallas_call | solution.py:610
  101.8 1.2 %collective-permute-start.34 = (f32[208,128]{1,0:T(8,128)S(1)}, f32[208,128]{1,0:T(8,128)S(1)}, u32[]{:S(2)}, u32[]{:S(2)}) collective-permute-start(f32[208,128]{1,0:T(8,128)S(1)} %adjoint_next.3.message), channel_id=1, source_target_pairs={{0,8},{8,0},{16,24},{24,16},{1,9},{9,1},{17,25},{25,17},{2,10},{10... | collective-permute-start | bytes 319496 | tf_op jit(solution)/shard_map/ppermute | solution.py:551
  103.1 1.5 %collective-permute-start.35 = (f32[208,128]{1,0:T(8,128)S(1)}, f32[208,128]{1,0:T(8,128)S(1)}, u32[]{:S(2)}, u32[]{:S(2)}) collective-permute-start(f32[208,128]{1,0:T(8,128)S(1)} %adjoint_next.3.message), channel_id=1, source_target_pairs={{0,24},{8,16},{16,8},{24,0},{1,25},{9,17},{17,9},{25,1},{2,26},{10... | collective-permute-start | bytes 319496 | tf_op jit(solution)/shard_map/ppermute | solution.py:551
  104.5 0.8 collective-permute-start.38
  105.7 1.4 %collective-permute-done.34.from_a = f32[208,128]{1,0:T(8,128)S(1)} collective-permute-done((f32[208,128]{1,0:T(8,128)S(1)}, f32[208,128]{1,0:T(8,128)S(1)}, u32[]{:S(2)}, u32[]{:S(2)}) %collective-permute-start.34) | collective-permute-done | bytes 106528 | tf_op jit(solution)/shard_map/ppermute | solution.py:551
  107.1 2.7 %collective-permute-done.35.from_b = f32[208,128]{1,0:T(8,128)S(1)} collective-permute-done((f32[208,128]{1,0:T(8,128)S(1)}, f32[208,128]{1,0:T(8,128)S(1)}, u32[]{:S(2)}, u32[]{:S(2)}) %collective-permute-start.35) | collective-permute-done | bytes 106528 | tf_op jit(solution)/shard_map/ppermute | solution.py:551
  110.2 2.8 %collective-permute-start.37 = (f32[128,128]{1,0:T(8,128)S(1)}, f32[128,128]{1,0:T(8,128)S(1)}, u32[]{:S(2)}, u32[]{:S(2)}) collective-permute-start(f32[128,128]{1,0:T(8,128)S(1)} %get-tuple-element.69), channel_id=1, source_target_pairs={{0,7},{1,2},{2,1},{3,4},{4,3},{5,6},{6,5},{7,0},{8,15},{9,10},{10,... | collective-permute-start | bytes 196616 | tf_op jit(solution)/shard_map/ppermute | solution.py:551
  113.0 2.9 %collective-permute-done.37.refs_5_ = f32[128,128]{1,0:T(8,128)S(1)} collective-permute-done((f32[128,128]{1,0:T(8,128)S(1)}, f32[128,128]{1,0:T(8,128)S(1)}, u32[]{:S(2)}, u32[]{:S(2)}) %collective-permute-start.37) | collective-permute-done | bytes 65568 | tf_op jit(solution)/shard_map/ppermute | solution.py:551
  115.9 5.0 %final.1 = (f32[512,128]{1,0:T(8,128)}, f32[512,128]{1,0:T(8,128)}) custom-call(s32[2]{0:T(128)S(1)} %copy-done.3, f32[512,128]{1,0:T(8,128)S(1)} %scatter.5.own.refs_1_, f32[192,128]{1,0:T(8,128)S(1)} %get-tuple-element.66.refs_2_, f32[192,128]{1,0:T(8,128)S(1)} %get-tuple-element.67.refs_3_, f32[128,128]{1,0:T(8,128)S(1)} %collective-permute-done.36.refs_4_, ...), custom_call_target="tpu_custom_call" | custom-call | tf_op jit(solution)/shard_map/final/pallas_call | solution.py:610
  (74 shorter events, 4.6 us)
Async XLA Ops:
  2.9 8.2 %collective-permute-start = (f32[72,128]{1,0:T(8,128)}, f32[72,128]{1,0:T(8,128)S(1)}, u32[]{:S(2)}, u32[]{:S(2)}) collective-permute-start(f32[72,128]{1,0:T(8,128)} %get-tuple-element.38.refs_0_), channel_id=1, source_target_pairs={{0,2},{1,3},{2,0},{3,1},{4,6},{5,7},{6,4},{7,5},{8,10},{9,11},{10,... | collective-permute-start | bytes 110600 | tf_op jit(solution)/shard_map/ppermute | solution.py:551
  6.0 6.7 %collective-permute-start.1 = (f32[72,128]{1,0:T(8,128)}, f32[72,128]{1,0:T(8,128)S(1)}, u32[]{:S(2)}, u32[]{:S(2)}) collective-permute-start(f32[72,128]{1,0:T(8,128)} %get-tuple-element.38.refs_0_), channel_id=1, source_target_pairs={{0,4},{1,5},{2,6},{3,7},{4,0},{5,1},{6,2},{7,3},{8,12},{9,13},{10,... | collective-permute-start | bytes 110600 | tf_op jit(solution)/shard_map/ppermute | solution.py:551
  8.6 6.0 %collective-permute-start.2 = (f32[72,128]{1,0:T(8,128)}, f32[72,128]{1,0:T(8,128)S(1)}, u32[]{:S(2)}, u32[]{:S(2)}) collective-permute-start(f32[72,128]{1,0:T(8,128)} %get-tuple-element.38.refs_0_), channel_id=1, source_target_pairs={{0,6},{1,7},{2,4},{3,5},{4,2},{5,3},{6,0},{7,1},{8,14},{9,15},{10,... | collective-permute-start | bytes 110600 | tf_op jit(solution)/shard_map/ppermute | solution.py:551
  8.6 6.0 %collective-permute-start.3 = (f32[72,128]{1,0:T(8,128)}, f32[72,128]{1,0:T(8,128)S(1)}, u32[]{:S(2)}, u32[]{:S(2)}) collective-permute-start(f32[72,128]{1,0:T(8,128)} %get-tuple-element.38.refs_0_), channel_id=1, source_target_pairs={{0,1},{1,0},{2,3},{3,2},{4,5},{5,4},{6,7},{7,6},{8,9},{9,8},{10,11... | collective-permute-start | bytes 110600 | tf_op jit(solution)/shard_map/ppermute | solution.py:551
  8.6 16.6 %collective-permute-start.7 = (f32[584,128]{1,0:T(8,128)}, f32[584,128]{1,0:T(8,128)S(1)}, u32[]{:S(2)}, u32[]{:S(2)}) collective-permute-start(f32[584,128]{1,0:T(8,128)} %get-tuple-element.42), channel_id=1, source_target_pairs={{0,8},{8,0},{16,24},{24,16},{1,9},{9,1},{17,25},{25,17},{2,10},{10... | collective-permute-start | bytes 897032 | tf_op jit(solution)/shard_map/ppermute | solution.py:551
  11.1 14.1 %collective-permute-start.8 = (f32[584,128]{1,0:T(8,128)}, f32[584,128]{1,0:T(8,128)S(1)}, u32[]{:S(2)}, u32[]{:S(2)}) collective-permute-start(f32[584,128]{1,0:T(8,128)} %get-tuple-element.43), channel_id=1, source_target_pairs={{0,0},{24,24},{8,16},{16,8},{1,1},{25,25},{9,17},{17,9},{2,2},{26,... | collective-permute-start | bytes 897032 | tf_op jit(solution)/shard_map/ppermute | solution.py:551
  12.8 2.4 %collective-permute-start.4 = (f32[72,128]{1,0:T(8,128)S(1)}, f32[72,128]{1,0:T(8,128)S(1)}, u32[]{:S(2)}, u32[]{:S(2)}) collective-permute-start(f32[72,128]{1,0:T(8,128)S(1)} %collective-permute-done.refs_1_), channel_id=1, source_target_pairs={{0,1},{1,0},{2,3},{3,2},{4,5},{5,4},{6,7},{7,6},{8,9},{9,8},{10,11... | collective-permute-start | bytes 110600 | tf_op jit(solution)/shard_map/ppermute | solution.py:551
  14.6 1.2 %collective-permute-start.5 = (f32[72,128]{1,0:T(8,128)S(1)}, f32[72,128]{1,0:T(8,128)S(1)}, u32[]{:S(2)}, u32[]{:S(2)}) collective-permute-start(f32[72,128]{1,0:T(8,128)S(1)} %collective-permute-done.1.refs_2_), channel_id=1, source_target_pairs={{0,1},{1,0},{2,3},{3,2},{4,5},{5,4},{6,7},{7,6},{8,9},{9,8},{10,11... | collective-permute-start | bytes 110600 | tf_op jit(solution)/shard_map/ppermute | solution.py:551
  14.6 1.4 %collective-permute-start.6 = (f32[72,128]{1,0:T(8,128)S(1)}, f32[72,128]{1,0:T(8,128)S(1)}, u32[]{:S(2)}, u32[]{:S(2)}) collective-permute-start(f32[72,128]{1,0:T(8,128)S(1)} %collective-permute-done.2.refs_3_), channel_id=1, source_target_pairs={{0,1},{1,0},{2,3},{3,2},{4,5},{5,4},{6,7},{7,6},{8,9},{9,8},{10,11... | collective-permute-start | bytes 110600 | tf_op jit(solution)/shard_map/ppermute | solution.py:551
  15.2 10.0 %copy-start = (f32[512,128]{1,0:T(8,128)S(1)}, f32[512,128]{1,0:T(8,128)}, u32[]{:S(2)}) copy-start(f32[512,128]{1,0:T(8,128)} %get-tuple-element.40.root_h) | copy-start | bytes 786436
  15.2 10.0 %copy-start.1 = (f32[512,128]{1,0:T(8,128)S(1)}, f32[512,128]{1,0:T(8,128)}, u32[]{:S(2)}) copy-start(f32[512,128]{1,0:T(8,128)} %get-tuple-element.41.root_v) | copy-start | bytes 786436
  15.9 0.8 copy-start.2
  20.2 19.0 %copy-start.3 = (s32[2]{0:T(128)S(1)}, s32[2]{0:T(128)}, u32[]{:S(2)}) copy-start(s32[2]{0:T(128)} %refs_0_.7) | copy-start | bytes 28
  20.2 9.2 %collective-permute-start.10 = (f32[192,128]{1,0:T(8,128)S(1)}, f32[192,128]{1,0:T(8,128)S(1)}, u32[]{:S(2)}, u32[]{:S(2)}) collective-permute-start(f32[192,128]{1,0:T(8,128)S(1)} %get-tuple-element.39.message), channel_id=1, source_target_pairs={{0,0},{24,24},{8,16},{16,8},{1,1},{25,25},{9,17},{17,9},{2,2},{26,... | collective-permute-start | bytes 294920 | tf_op jit(solution)/shard_map/ppermute | solution.py:551
  20.9 9.3 %collective-permute-start.9 = (f32[192,128]{1,0:T(8,128)S(1)}, f32[192,128]{1,0:T(8,128)S(1)}, u32[]{:S(2)}, u32[]{:S(2)}) collective-permute-start(f32[192,128]{1,0:T(8,128)S(1)} %get-tuple-element.39.message), channel_id=1, source_target_pairs={{0,8},{8,0},{16,24},{24,16},{1,9},{9,1},{17,25},{25,17},{2,10},{10... | collective-permute-start | bytes 294920 | tf_op jit(solution)/shard_map/ppermute | solution.py:551
  26.0 8.3 %collective-permute-start.13 = (f32[456,128]{1,0:T(8,128)}, f32[456,128]{1,0:T(8,128)S(1)}, u32[]{:S(2)}, u32[]{:S(2)}) collective-permute-start(f32[456,128]{1,0:T(8,128)} %get-tuple-element.44), channel_id=1, source_target_pairs={{0,1},{1,0},{2,3},{3,2},{4,5},{5,4},{6,7},{7,6},{8,9},{9,8},{10,11... | collective-permute-start | bytes 700424 | tf_op jit(solution)/shard_map/ppermute | solution.py:551
  26.0 9.7 %collective-permute-start.14 = (f32[456,128]{1,0:T(8,128)S(1)}, f32[456,128]{1,0:T(8,128)S(1)}, u32[]{:S(2)}, u32[]{:S(2)}) collective-permute-start(f32[456,128]{1,0:T(8,128)S(1)} %get-tuple-element.45), channel_id=1, source_target_pairs={{0,7},{1,2},{2,1},{3,4},{4,3},{5,6},{6,5},{7,0},{8,15},{9,10},{10,... | collective-permute-start | bytes 700424 | tf_op jit(solution)/shard_map/ppermute | solution.py:551
  31.3 6.5 %collective-permute-start.11 = (f32[328,128]{1,0:T(8,128)}, f32[328,128]{1,0:T(8,128)S(1)}, u32[]{:S(2)}, u32[]{:S(2)}) collective-permute-start(f32[328,128]{1,0:T(8,128)} %get-tuple-element.50), channel_id=1, source_target_pairs={{0,1},{1,0},{2,3},{3,2},{4,5},{5,4},{6,7},{7,6},{8,9},{9,8},{10,11... | collective-permute-start | bytes 503816 | tf_op jit(solution)/shard_map/ppermute | solution.py:551
  31.3 7.9 %collective-permute-start.12 = (f32[328,128]{1,0:T(8,128)S(1)}, f32[328,128]{1,0:T(8,128)S(1)}, u32[]{:S(2)}, u32[]{:S(2)}) collective-permute-start(f32[328,128]{1,0:T(8,128)S(1)} %get-tuple-element.51), channel_id=1, source_target_pairs={{0,7},{1,2},{2,1},{3,4},{4,3},{5,6},{6,5},{7,0},{8,15},{9,10},{10,... | collective-permute-start | bytes 503816 | tf_op jit(solution)/shard_map/ppermute | solution.py:551
  48.9 4.6 %collective-permute-start.15 = (f32[104,128]{1,0:T(8,128)S(1)}, f32[104,128]{1,0:T(8,128)S(1)}, u32[]{:S(2)}, u32[]{:S(2)}) collective-permute-start(f32[104,128]{1,0:T(8,128)S(1)} %get-tuple-element.57.refs_0_), channel_id=1, source_target_pairs={{0,2},{1,3},{2,0},{3,1},{4,6},{5,7},{6,4},{7,5},{8,10},{9,11},{10,... | collective-permute-start | bytes 159752 | tf_op jit(solution)/shard_map/ppermute | solution.py:551
  49.0 5.6 %collective-permute-start.16 = (f32[104,128]{1,0:T(8,128)S(1)}, f32[104,128]{1,0:T(8,128)S(1)}, u32[]{:S(2)}, u32[]{:S(2)}) collective-permute-start(f32[104,128]{1,0:T(8,128)S(1)} %get-tuple-element.57.refs_0_), channel_id=1, source_target_pairs={{0,4},{1,5},{2,6},{3,7},{4,0},{5,1},{6,2},{7,3},{8,12},{9,13},{10,... | collective-permute-start | bytes 159752 | tf_op jit(solution)/shard_map/ppermute | solution.py:551
  49.3 7.4 %collective-permute-start.17 = (f32[104,128]{1,0:T(8,128)S(1)}, f32[104,128]{1,0:T(8,128)S(1)}, u32[]{:S(2)}, u32[]{:S(2)}) collective-permute-start(f32[104,128]{1,0:T(8,128)S(1)} %get-tuple-element.57.refs_0_), channel_id=1, source_target_pairs={{0,6},{1,7},{2,4},{3,5},{4,2},{5,3},{6,0},{7,1},{8,14},{9,15},{10,... | collective-permute-start | bytes 159752 | tf_op jit(solution)/shard_map/ppermute | solution.py:551
  53.4 3.8 %collective-permute-start.18 = (f32[104,128]{1,0:T(8,128)S(1)}, f32[104,128]{1,0:T(8,128)S(1)}, u32[]{:S(2)}, u32[]{:S(2)}) collective-permute-start(f32[104,128]{1,0:T(8,128)S(1)} %get-tuple-element.57.refs_0_), channel_id=1, source_target_pairs={{0,1},{1,0},{2,3},{3,2},{4,5},{5,4},{6,7},{7,6},{8,9},{9,8},{10,11... | collective-permute-start | bytes 159752 | tf_op jit(solution)/shard_map/ppermute | solution.py:551
  53.5 3.8 %collective-permute-start.19 = (f32[104,128]{1,0:T(8,128)S(1)}, f32[104,128]{1,0:T(8,128)S(1)}, u32[]{:S(2)}, u32[]{:S(2)}) collective-permute-start(f32[104,128]{1,0:T(8,128)S(1)} %collective-permute-done.15.refs_1_), channel_id=1, source_target_pairs={{0,1},{1,0},{2,3},{3,2},{4,5},{5,4},{6,7},{7,6},{8,9},{9,8},{10,11... | collective-permute-start | bytes 159752 | tf_op jit(solution)/shard_map/ppermute | solution.py:551
  54.6 2.7 %collective-permute-start.20 = (f32[104,128]{1,0:T(8,128)S(1)}, f32[104,128]{1,0:T(8,128)S(1)}, u32[]{:S(2)}, u32[]{:S(2)}) collective-permute-start(f32[104,128]{1,0:T(8,128)S(1)} %collective-permute-done.16.refs_2_), channel_id=1, source_target_pairs={{0,1},{1,0},{2,3},{3,2},{4,5},{5,4},{6,7},{7,6},{8,9},{9,8},{10,11... | collective-permute-start | bytes 159752 | tf_op jit(solution)/shard_map/ppermute | solution.py:551
  56.7 1.2 %collective-permute-start.21 = (f32[104,128]{1,0:T(8,128)S(1)}, f32[104,128]{1,0:T(8,128)S(1)}, u32[]{:S(2)}, u32[]{:S(2)}) collective-permute-start(f32[104,128]{1,0:T(8,128)S(1)} %collective-permute-done.17.refs_3_), channel_id=1, source_target_pairs={{0,1},{1,0},{2,3},{3,2},{4,5},{5,4},{6,7},{7,6},{8,9},{9,8},{10,11... | collective-permute-start | bytes 159752 | tf_op jit(solution)/shard_map/ppermute | solution.py:551
  62.0 6.2 %collective-permute-start.22 = (f32[208,128]{1,0:T(8,128)S(1)}, f32[208,128]{1,0:T(8,128)S(1)}, u32[]{:S(2)}, u32[]{:S(2)}) collective-permute-start(f32[208,128]{1,0:T(8,128)S(1)} %adjoint_next.2.message), channel_id=1, source_target_pairs={{0,8},{8,0},{16,24},{24,16},{1,9},{9,1},{17,25},{25,17},{2,10},{10... | collective-permute-start | bytes 319496 | tf_op jit(solution)/shard_map/ppermute | solution.py:551
  64.4 6.4 %collective-permute-start.23 = (f32[208,128]{1,0:T(8,128)S(1)}, f32[208,128]{1,0:T(8,128)S(1)}, u32[]{:S(2)}, u32[]{:S(2)}) collective-permute-start(f32[208,128]{1,0:T(8,128)S(1)} %adjoint_next.2.message), channel_id=1, source_target_pairs={{0,24},{8,16},{16,8},{24,0},{1,25},{9,17},{17,9},{25,1},{2,26},{10... | collective-permute-start | bytes 319496 | tf_op jit(solution)/shard_map/ppermute | solution.py:551
  65.5 8.1 %collective-permute-start.26 = (f32[16,128]{1,0:T(8,128)S(1)}, f32[16,128]{1,0:T(8,128)S(1)}, u32[]{:S(2)}, u32[]{:S(2)}) collective-permute-start(f32[16,128]{1,0:T(8,128)S(1)} %slice.81), channel_id=1, source_target_pairs={{0,16},{8,24},{16,0},{24,8},{1,17},{9,25},{17,1},{25,9},{2,18},{10... | collective-permute-start | bytes 24584 | tf_op jit(solution)/shard_map/ppermute | solution.py:551
  71.2 2.4 %collective-permute-start.24 = (f32[328,128]{1,0:T(8,128)S(1)}, f32[328,128]{1,0:T(8,128)S(1)}, u32[]{:S(2)}, u32[]{:S(2)}) collective-permute-start(f32[328,128]{1,0:T(8,128)S(1)} %get-tuple-element.61), channel_id=1, source_target_pairs={{0,1},{1,0},{2,3},{3,2},{4,5},{5,4},{6,7},{7,6},{8,9},{9,8},{10,11... | collective-permute-start | bytes 503816 | tf_op jit(solution)/shard_map/ppermute | solution.py:551
  71.3 7.4 %collective-permute-start.25 = (f32[328,128]{1,0:T(8,128)S(1)}, f32[328,128]{1,0:T(8,128)S(1)}, u32[]{:S(2)}, u32[]{:S(2)}) collective-permute-start(f32[328,128]{1,0:T(8,128)S(1)} %get-tuple-element.62), channel_id=1, source_target_pairs={{0,7},{1,2},{2,1},{3,4},{4,3},{5,6},{6,5},{7,0},{8,15},{9,10},{10,... | collective-permute-start | bytes 503816 | tf_op jit(solution)/shard_map/ppermute | solution.py:551
  88.9 4.5 %collective-permute-start.27 = (f32[104,128]{1,0:T(8,128)S(1)}, f32[104,128]{1,0:T(8,128)S(1)}, u32[]{:S(2)}, u32[]{:S(2)}) collective-permute-start(f32[104,128]{1,0:T(8,128)S(1)} %get-tuple-element.65.refs_0_), channel_id=1, source_target_pairs={{0,2},{1,3},{2,0},{3,1},{4,6},{5,7},{6,4},{7,5},{8,10},{9,11},{10,... | collective-permute-start | bytes 159752 | tf_op jit(solution)/shard_map/ppermute | solution.py:551
  88.9 5.4 %collective-permute-start.28 = (f32[104,128]{1,0:T(8,128)S(1)}, f32[104,128]{1,0:T(8,128)S(1)}, u32[]{:S(2)}, u32[]{:S(2)}) collective-permute-start(f32[104,128]{1,0:T(8,128)S(1)} %get-tuple-element.65.refs_0_), channel_id=1, source_target_pairs={{0,4},{1,5},{2,6},{3,7},{4,0},{5,1},{6,2},{7,3},{8,12},{9,13},{10,... | collective-permute-start | bytes 159752 | tf_op jit(solution)/shard_map/ppermute | solution.py:551
  89.1 7.5 %collective-permute-start.29 = (f32[104,128]{1,0:T(8,128)S(1)}, f32[104,128]{1,0:T(8,128)S(1)}, u32[]{:S(2)}, u32[]{:S(2)}) collective-permute-start(f32[104,128]{1,0:T(8,128)S(1)} %get-tuple-element.65.refs_0_), channel_id=1, source_target_pairs={{0,6},{1,7},{2,4},{3,5},{4,2},{5,3},{6,0},{7,1},{8,14},{9,15},{10,... | collective-permute-start | bytes 159752 | tf_op jit(solution)/shard_map/ppermute | solution.py:551
  93.3 3.3 %collective-permute-start.30 = (f32[104,128]{1,0:T(8,128)S(1)}, f32[104,128]{1,0:T(8,128)S(1)}, u32[]{:S(2)}, u32[]{:S(2)}) collective-permute-start(f32[104,128]{1,0:T(8,128)S(1)} %get-tuple-element.65.refs_0_), channel_id=1, source_target_pairs={{0,1},{1,0},{2,3},{3,2},{4,5},{5,4},{6,7},{7,6},{8,9},{9,8},{10,11... | collective-permute-start | bytes 159752 | tf_op jit(solution)/shard_map/ppermute | solution.py:551
  93.3 3.3 %collective-permute-start.31 = (f32[104,128]{1,0:T(8,128)S(1)}, f32[104,128]{1,0:T(8,128)S(1)}, u32[]{:S(2)}, u32[]{:S(2)}) collective-permute-start(f32[104,128]{1,0:T(8,128)S(1)} %collective-permute-done.27.refs_1_), channel_id=1, source_target_pairs={{0,1},{1,0},{2,3},{3,2},{4,5},{5,4},{6,7},{7,6},{8,9},{9,8},{10,11... | collective-permute-start | bytes 159752 | tf_op jit(solution)/shard_map/ppermute | solution.py:551
  94.3 2.3 %collective-permute-start.32 = (f32[104,128]{1,0:T(8,128)S(1)}, f32[104,128]{1,0:T(8,128)S(1)}, u32[]{:S(2)}, u32[]{:S(2)}) collective-permute-start(f32[104,128]{1,0:T(8,128)S(1)} %collective-permute-done.28.refs_2_), channel_id=1, source_target_pairs={{0,1},{1,0},{2,3},{3,2},{4,5},{5,4},{6,7},{7,6},{8,9},{9,8},{10,11... | collective-permute-start | bytes 159752 | tf_op jit(solution)/shard_map/ppermute | solution.py:551
  96.6 1.2 %collective-permute-start.33 = (f32[104,128]{1,0:T(8,128)S(1)}, f32[104,128]{1,0:T(8,128)S(1)}, u32[]{:S(2)}, u32[]{:S(2)}) collective-permute-start(f32[104,128]{1,0:T(8,128)S(1)} %collective-permute-done.29.refs_3_), channel_id=1, source_target_pairs={{0,1},{1,0},{2,3},{3,2},{4,5},{5,4},{6,7},{7,6},{8,9},{9,8},{10,11... | collective-permute-start | bytes 159752 | tf_op jit(solution)/shard_map/ppermute | solution.py:551
  101.8 5.3 %collective-permute-start.34 = (f32[208,128]{1,0:T(8,128)S(1)}, f32[208,128]{1,0:T(8,128)S(1)}, u32[]{:S(2)}, u32[]{:S(2)}) collective-permute-start(f32[208,128]{1,0:T(8,128)S(1)} %adjoint_next.3.message), channel_id=1, source_target_pairs={{0,8},{8,0},{16,24},{24,16},{1,9},{9,1},{17,25},{25,17},{2,10},{10... | collective-permute-start | bytes 319496 | tf_op jit(solution)/shard_map/ppermute | solution.py:551
  103.1 6.8 %collective-permute-start.35 = (f32[208,128]{1,0:T(8,128)S(1)}, f32[208,128]{1,0:T(8,128)S(1)}, u32[]{:S(2)}, u32[]{:S(2)}) collective-permute-start(f32[208,128]{1,0:T(8,128)S(1)} %adjoint_next.3.message), channel_id=1, source_target_pairs={{0,24},{8,16},{16,8},{24,0},{1,25},{9,17},{17,9},{25,1},{2,26},{10... | collective-permute-start | bytes 319496 | tf_op jit(solution)/shard_map/ppermute | solution.py:551
  104.5 8.4 %collective-permute-start.38 = (f32[16,128]{1,0:T(8,128)S(1)}, f32[16,128]{1,0:T(8,128)S(1)}, u32[]{:S(2)}, u32[]{:S(2)}) collective-permute-start(f32[16,128]{1,0:T(8,128)S(1)} %slice.84), channel_id=1, source_target_pairs={{0,16},{8,24},{16,0},{24,8},{1,17},{9,25},{17,1},{25,9},{2,18},{10... | collective-permute-start | bytes 24584 | tf_op jit(solution)/shard_map/ppermute | solution.py:551
  110.1 2.8 %collective-permute-start.36 = (f32[128,128]{1,0:T(8,128)S(1)}, f32[128,128]{1,0:T(8,128)S(1)}, u32[]{:S(2)}, u32[]{:S(2)}) collective-permute-start(f32[128,128]{1,0:T(8,128)S(1)} %get-tuple-element.68), channel_id=1, source_target_pairs={{0,1},{1,0},{2,3},{3,2},{4,5},{5,4},{6,7},{7,6},{8,9},{9,8},{10,11... | collective-permute-start | bytes 196616 | tf_op jit(solution)/shard_map/ppermute | solution.py:551
  110.2 5.7 %collective-permute-start.37 = (f32[128,128]{1,0:T(8,128)S(1)}, f32[128,128]{1,0:T(8,128)S(1)}, u32[]{:S(2)}, u32[]{:S(2)}) collective-permute-start(f32[128,128]{1,0:T(8,128)S(1)} %get-tuple-element.69), channel_id=1, source_target_pairs={{0,7},{1,2},{2,1},{3,4},{4,3},{5,6},{6,5},{7,0},{8,15},{9,10},{10,... | collective-permute-start | bytes 196616 | tf_op jit(solution)/shard_map/ppermute | solution.py:551

commit v3 on v2

--- a/solution.py
+++ b/solution.py
@@ -38,42 +38,66 @@
     return started
 
 
-def lateral_pass(buf, face_lat, face_lon, first, last, left, right):
-    cols = slice(left, right)
-    width = right - left
-
-    def body(step, carry):
+def to_strided(natural, buf, rows):
+    count = natural.shape[1] // 8
+    for i in rows:
+        for v in range(count):
+            buf[i, 8 * v:8 * v + 8] = natural[i, pl.ds(v, 8, stride=count)]
+
+
+def to_natural(buf, natural, rows, skip=0):
+    count = natural.shape[1] // 8
+    for i in rows:
+        for v in range(count):
+            natural[i - skip, pl.ds(v, 8, stride=count)] = buf[i, 8 * v:8 * v + 8]
+
+
+def eastern(tiles):
+    return tiles[1:] + [pltpu.roll(tiles[0], 7, 0)]
+
+
+def western(tiles):
+    return [pltpu.roll(tiles[-1], 1, 0)] + tiles[:-1]
+
+
+def lateral_pass(buf, face_lat, face_lon, first, last):
+    def tiles(ref, row):
+        return [ref[row, 8 * v:8 * v + 8] for v in range(buf.shape[1] // 8)]
+
+    def advance(row, carry):
         current, flux_above = carry
-        row = first + 2 * step
+        below = tiles(buf, row + 1)
+        flux = [f * (b - w) for f, b, w in zip(tiles(face_lat, row), below, current)]
+        side = [f * (e - w) for f, e, w in zip(tiles(face_lon, row), eastern(current), current)]
+        for v, (w, f, g, e, h) in enumerate(zip(current, flux, flux_above, side, western(side))):
+            buf[row, 8 * v:8 * v + 8] = w + ((f - g) + (e - h))
+        return below, flux
+
+    def four(step, carry):
+        for k in range(4):
+            carry = advance(first + 4 * step + k, carry)
+        return carry
+
+    def two(step, carry):
         for k in range(2):
-            below = buf[row + k + 1, cols]
-            flux = face_lat[row + k, cols] * (below - current)
-            side = face_lon[row + k, cols] * (pltpu.roll(current, width - 1, 0) - current)
-            buf[row + k, cols] = current + ((flux - flux_above) + (side - pltpu.roll(side, 1, 0)))
-            current, flux_above = below, flux
-        return current, flux_above
-
-    start = buf[first, cols]
-    flux_start = face_lat[first - 1, cols] * (start - buf[first - 1, cols])
-    lax.fori_loop(0, (last - first) // 2, body, (start, flux_start))
-
-
-def lateral_passes(buf, face_lat, face_lon, nh, begin, end, left, right):
+            carry = advance(last - 2 + k, carry)
+        return carry
+
+    start = tiles(buf, first)
+    flux = [f * (w - a) for f, w, a in zip(tiles(face_lat, first - 1), start, tiles(buf, first - 1))]
+    count = last - first
+    carry = lax.fori_loop(0, count // 4, four, (start, flux))
+    lax.fori_loop(0, (count % 4) // 2, two, carry)
+
+
+def lateral_passes(buf, face_lat, face_lon, nh, begin, end):
     rows, lost = buf.shape[0], FRAME - 2 * nh
 
     def body(p, c):
-        lateral_pass(buf, face_lat, face_lon, lost + p, rows - lost - p, left, right)
+        lateral_pass(buf, face_lat, face_lon, lost + p, rows - lost - p)
         return c
 
     lax.fori_loop(begin + 1, end + 1, body, 0)
-
-
-def last_lateral(buf, face_lat, face_lon, nh, lon_cells):
-    close = jnp.minimum(nh, 4)
-    lateral_passes(buf, face_lat, face_lon, nh, nh, 2 * nh - close, 0, buf.shape[1])
-    left = (FRAME - 4) // 8 * 8
-    right = -(-(FRAME + lon_cells + 4) // 8) * 8
-    lateral_passes(buf, face_lat, face_lon, nh, 2 * nh - close, 2 * nh, left, right)
 
 
 def shift_matrix():
@@ -83,15 +107,14 @@
     return (source == wanted).astype(jnp.bfloat16)
 
 
-def vertical_passes(buf, keep, up, down, first, last, offset, nv, left, right):
-    cols = slice(left, right)
-    width = right - left
+def vertical_passes(buf, keep, up, down, first, last, offset, nv):
+    width = buf.shape[1]
     shifts = shift_matrix()
     at = list(range(first, last))
     half = (last - first) // 2
 
     def sweep(p, c):
-        values = [buf[i, cols] for i in at]
+        values = [buf[i] for i in at]
         stack = jnp.concatenate(values[:half], axis=0)
         high = stack.astype(jnp.bfloat16)
         low = (stack - high.astype(jnp.float32)).astype(jnp.bfloat16)
@@ -102,8 +125,7 @@
                 above, below = here[:, :LANES], here[:, LANES:]
             else:
                 above, below = pltpu.roll(w, LANES - 1, 1), pltpu.roll(w, 1, 1)
-            buf[i, cols] = keep[i - offset, cols] * w + (
-                up[i - offset, cols] * above + down[i - offset, cols] * below)
+            buf[i] = keep[i - offset] * w + (up[i - offset] * above + down[i - offset] * below)
         return c
 
     lax.fori_loop(0, nv, sweep, 0)
@@ -113,9 +135,12 @@
     plan, first = [], 0
     for i in range(lat_cells + 2 * reach):
         outside = max(reach - i, i - (reach + lat_cells - 1), 0)
-        plan.append((first, reach - outside))
-        first += reach - outside
-    return plan, -(-first // 8) * 8
+        if outside:
+            plan.append((first, reach - outside))
+            first += reach - outside
+        else:
+            plan.append(((i - reach) * reach, reach))
+    return plan, (lat_cells * reach, -(-first // 8) * 8)
 
 
 def even(axis):
@@ -125,7 +150,7 @@
 def place_halos(buf, own, strips, sides, reach, dims):
     lat_cells, lon_cells = dims
     (from_a, skip_a), (from_b, skip_b) = strips
-    (from_x, skip_x), (from_s, skip_s) = sides
+    from_x, from_s = sides
     base = FRAME - reach
     lat_even, lon_even = even("lat"), even("lon")
     south = FRAME + lat_cells
@@ -139,43 +164,51 @@
         buf[row_a + i, cols] = from_a[skip_a + place:skip_a + place + lon_cells]
         buf[row_b + i, cols] = from_b[skip_b + place:skip_b + place + lon_cells]
 
-    def put_sides(west, skip_west, east, skip_east):
+    def put_sides(west, east):
         for i, (first, count) in enumerate(side_rows(reach, lat_cells)[0]):
-            if count:
-                buf[base + i, FRAME - count:FRAME] = west[skip_west + first:skip_west + first + count]
-                buf[base + i, FRAME + lon_cells:FRAME + lon_cells + count] = (
-                    east[skip_east + first:skip_east + first + count])
-
-    pl.when(lon_even)(lambda: put_sides(from_s, skip_s, from_x, skip_x))
-    pl.when(jnp.logical_not(lon_even))(lambda: put_sides(from_x, skip_x, from_s, skip_s))
-
-
-def pack_sides(own, strips, outs, reach, dims):
+            part = 0 if reach <= i < reach + lat_cells else 1
+            for (ref, skip), place in ((west[part], FRAME - count), (east[part], FRAME + lon_cells)):
+                if count:
+                    buf[base + i, place:place + count] = ref[skip + first:skip + first + count]
+
+    pl.when(lon_even)(lambda: put_sides(from_s, from_x))
+    pl.when(jnp.logical_not(lon_even))(lambda: put_sides(from_x, from_s))
+
+
+def pack_own_sides(own, outs, reach, dims):
     lat_cells, lon_cells = dims
-    (from_a, skip_a), (from_b, skip_b) = strips
-    (to_x, skip_x), (to_s, skip_s) = outs
+
+    def write(west, east):
+        for i in range(lat_cells):
+            row = i * lon_cells
+            for (ref, skip), place in ((west, row), (east, row + lon_cells - reach)):
+                ref[skip + i * reach:skip + (i + 1) * reach] = own[place:place + reach]
+
+    to_x, to_s = outs
+    pl.when(even("lon"))(lambda: write(to_s, to_x))
+    pl.when(jnp.logical_not(even("lon")))(lambda: write(to_x, to_s))
+
+
+def pack_corners(strips, outs, reach, dims):
+    lat_cells, lon_cells = dims
+    from_a, from_b = strips
+    to_x, to_s = outs
     plan, _ = side_rows(reach, lat_cells)
 
-    def write(north, skip_north, south, skip_south, west, skip_west, east, skip_east):
+    def write(north, south, west, east):
         for i, (first, count) in enumerate(plan):
-            if not count:
+            if reach <= i < reach + lat_cells or not count:
                 continue
-            if i < reach:
-                ref, row = north, skip_north + i * lon_cells
-            elif i < reach + lat_cells:
-                ref, row = own, (i - reach) * lon_cells
-            else:
-                ref, row = south, skip_south + (i - reach - lat_cells) * lon_cells
-            west[skip_west + first:skip_west + first + count] = ref[row:row + count]
-            east[skip_east + first:skip_east + first + count] = (
-                ref[row + lon_cells - count:row + lon_cells])
-
-    lat_even, lon_even = even("lat"), even("lon")
+            ref, skip = north if i < reach else south
+            row = skip + (i if i < reach else i - reach - lat_cells) * lon_cells
+            for (out, base), place in ((west, row), (east, row + lon_cells - count)):
+                out[base + first:base + first + count] = ref[place:place + count]
+
     for even_lat in (True, False):
         for even_lon in (True, False):
-            poles = (from_b, skip_b, from_a, skip_a) if even_lat else (from_a, skip_a, from_b, skip_b)
-            edges = (to_s, skip_s, to_x, skip_x) if even_lon else (to_x, skip_x, to_s, skip_s)
-            pl.when((lat_even == even_lat) & (lon_even == even_lon))(
+            poles = (from_b, from_a) if even_lat else (from_a, from_b)
+            edges = (to_s, to_x) if even_lon else (to_x, to_s)
+            pl.when((even("lat") == even_lat) & (even("lon") == even_lon))(
                 functools.partial(write, *poles, *edges))
 
 
@@ -190,13 +223,16 @@
     return both[:, :LANES] + (both[:, LANES:2 * LANES] + both[:, 2 * LANES:])
 
 
-def scatter_kernel(slots, cells_n, message, cells, own):
-    own[...] = add_into(cells[...], split3(message[0:slots]), cells_n)
-
-
-def sides_kernel(dims, slots, reach, own, from_a, from_b, cells_a, cells_b,
-                 strip_a, strip_b, to_x, to_s):
+def scatter_kernel(dims, slots, reach, message, cells, own, *outs):
+    own[...] = add_into(cells[...], split3(message[0:slots]), dims[0] * dims[1])
+    if outs:
+        pack_own_sides(own, [(out, 0) for out in outs], reach, dims)
+
+
+def sides_kernel(dims, slots, reach, joined, *refs):
     lat_cells, lon_cells = dims
+    own, refs = (refs[0], refs[1:]) if joined else (None, refs)
+    from_a, from_b, cells_a, cells_b, strip_a, strip_b, to_x, to_s = refs
     skip = (lat_cells - reach) * lon_cells
     for message, cells, strip, north in (
         (from_a, cells_a, strip_a, jnp.logical_not(even("lat"))),
@@ -204,14 +240,24 @@
     ):
         at = cells_at(cells, slots) - jnp.where(north, skip, 0)
         strip[...] = add_into(at, split3(message[0:slots]), reach * lon_cells)
-    pack_sides(own, ((strip_a, 0), (strip_b, 0)), ((to_x, 0), (to_s, 0)), reach, dims)
+    base = 0
+    if joined:
+        pack_own_sides(own, ((to_x, 0), (to_s, 0)), reach, dims)
+        base = side_rows(reach, lat_cells)[1][0]
+    pack_corners(((strip_a, 0), (strip_b, 0)), ((to_x, base), (to_s, base)), reach, dims)
+
+
+def face_places(lat_cells):
+    (own_h, corner_h), (own_v, _) = (side_rows(reach, lat_cells)[1] for reach in (FRAME, REACH))
+    return (0, own_h + own_v), (own_h, own_h + own_v + corner_h)
 
 
 def face_sides_kernel(dims, root_h, root_v, from_a, from_b, to_x, to_s):
-    skip = FRAME * dims[1]
-    rows = side_rows(FRAME, dims[0])[1]
-    pack_sides(root_h, ((from_a, 0), (from_b, 0)), ((to_x, 0), (to_s, 0)), FRAME, dims)
-    pack_sides(root_v, ((from_a, skip), (from_b, skip)), ((to_x, rows), (to_s, rows)), REACH, dims)
+    skip = 0
+    for root, reach, (own, corner) in zip((root_h, root_v), (FRAME, REACH), face_places(dims[0])):
+        pack_own_sides(root, ((to_x, own), (to_s, own)), reach, dims)
+        pack_corners(((from_a, skip), (from_b, skip)), ((to_x, corner), (to_s, corner)), reach, dims)
+        skip += reach * dims[1]
 
 
 def start_kernel(dims, *refs):
@@ -250,16 +296,18 @@
 
 def faces_kernel(dims, root_h, root_v, from_a, from_b, from_x, from_s, *refs):
     lat_cells, lon_cells = dims
-    out, (face_lat, face_lon, keep, up, down, buf, sems) = refs[:5], refs[5:]
+    out, (face_lat, face_lon, keep, up, down, natural, buf, sems) = refs[:5], refs[5:]
     rows = lat_cells + 2 * FRAME
     width = buf.shape[1]
+    places = face_places(lat_cells)
     place_halos(
-        buf, root_h, ((from_a, 0), (from_b, 0)), ((from_x, 0), (from_s, 0)), FRAME, dims
+        natural, root_h, ((from_a, 0), (from_b, 0)),
+        [[(ref, place) for place in places[0]] for ref in (from_x, from_s)], FRAME, dims,
     )
 
     def clear(first):
         def body(i, c):
-            buf[first + i] = jnp.zeros((width, LANES), jnp.float32)
+            natural[first + i] = jnp.zeros((width, LANES), jnp.float32)
             return c
         lax.fori_loop(0, FRAME, body, 0)
 
@@ -267,23 +315,26 @@
     pl.when(lat == 0)(lambda: clear(0))
     pl.when(lat == lax.axis_size("lat") - 1)(lambda: clear(FRAME + lat_cells))
 
+    to_strided(natural, buf, range(rows))
     buf[rows] = jnp.zeros((width, LANES), jnp.float32)
 
     def lateral(step, c):
         for k in range(4):
             i = 4 * step + k
-            here = buf[i]
-            face_lat[i] = here * buf[i + 1]
-            face_lon[i] = here * pltpu.roll(here, width - 1, 0)
+            here = [buf[i, 8 * v:8 * v + 8] for v in range(width // 8)]
+            face_lat[i] = buf[i] * buf[i + 1]
+            for v, (w, e) in enumerate(zip(here, eastern(here))):
+                face_lon[i, 8 * v:8 * v + 8] = w * e
         return c
 
     lax.fori_loop(0, rows // 4, lateral, 0)
     side = copies([(face_lat, out[0]), (face_lon, out[1])], sems)
-    skip, skip_side = FRAME * lon_cells, side_rows(FRAME, lat_cells)[1]
+    skip = FRAME * lon_cells
     place_halos(
-        buf, root_v, ((from_a, skip), (from_b, skip)),
-        ((from_x, skip_side), (from_s, skip_side)), REACH, dims,
+        natural, root_v, ((from_a, skip), (from_b, skip)),
+        [[(ref, place) for place in places[1]] for ref in (from_x, from_s)], REACH, dims,
     )
+    to_strided(natural, buf, range(FRAME - REACH, rows - FRAME + REACH))
     top = lax.broadcasted_iota(jnp.int32, (width, LANES), 1) == LANES - 1
 
     def vertical(step, c):
@@ -405,8 +456,14 @@
 
 def spread_kernel(dims, first_call, *refs):
     lat_cells, lon_cells = dims
-    counts, cells, own, from_a, from_b, from_x, from_s = refs[:7]
-    refs = refs[7:]
+    counts, cells, own, from_a, from_b = refs[:5]
+    if first_call:
+        (from_x, from_s), refs = refs[5:7], refs[7:]
+        corner = side_rows(FRAME, lat_cells)[1][0]
+        sides = [[(ref, 0), (ref, corner)] for ref in (from_x, from_s)]
+    else:
+        (own_x, own_s, corner_x, corner_s), refs = refs[5:9], refs[9:]
+        sides = [[(own_x, 0), (corner_x, 0)], [(own_s, 0), (corner_s, 0)]]
     if not first_call:
         scal, refs = refs[0], refs[1:]
     faces_hbm, jac_hbm, refs = refs[:5], refs[5], refs[6:]
@@ -414,14 +471,14 @@
         grad_hbm, spread_hbm, refs = refs[0], refs[1], refs[2:]
     one_hbm, two_hbm, message = refs[:3]
     refs = refs[3:]
-    face_lat, face_lon, keep, up, down, jac, one, two, grad, buf, mid, sems = refs
+    face_lat, face_lon, keep, up, down, jac, one, two, grad, natural, buf, mid, sems = refs
     loads = copies(list(zip(faces_hbm[:2], (face_lat, face_lon))), sems)
     nh, nv = counts[0], counts[1]
     rows = lat_cells + 2 * FRAME
-    width = buf.shape[1]
     place_halos(
-        buf, own, ((from_a, 0), (from_b, 0)), ((from_x, 0), (from_s, 0)), FRAME, dims
+        natural, own, ((from_a, 0), (from_b, 0)), sides, FRAME, dims
     )
+    to_strided(natural, buf, range(rows))
     for load in loads:
         load.wait()
     loads = copies(
@@ -429,23 +486,21 @@
     )
     if not first_call:
         old_loads = copies([(grad_hbm, grad), (spread_hbm, two)], sems.at[pl.ds(6, 2)])
-    lateral_passes(buf, face_lat, face_lon, nh, 0, nh, 0, width)
+    lateral_passes(buf, face_lat, face_lon, nh, 0, nh)
     border = FRAME - REACH
     tall = lat_cells + 2 * REACH
     vertical = functools.partial(
-        vertical_passes, buf, keep, up, down, border, border + tall, border, nv, 0, width
+        vertical_passes, buf, keep, up, down, border, border + tall, border, nv
     )
     for load in loads[:3]:
         load.wait()
     vertical()
 
-    def save(i, c):
-        mid[i] = buf[FRAME + i]
-        return c
-
-    lax.fori_loop(0, lat_cells, save, 0)
+    block = range(FRAME, FRAME + lat_cells)
+    to_natural(buf, mid, block, FRAME)
     vertical()
-    last_lateral(buf, face_lat, face_lon, nh, lon_cells)
+    lateral_passes(buf, face_lat, face_lon, nh, nh, 2 * nh)
+    to_natural(buf, natural, block)
     cols = slice(FRAME, FRAME + lon_cells)
     if not first_call:
         rr = jnp.sum(scal[0:8])
@@ -456,7 +511,7 @@
     def finish(i, acc):
         place = pl.ds(pl.multiple_of(i * lon_cells, lon_cells), lon_cells)
         vector = mid[i, cols]
-        after = buf[FRAME + i, cols]
+        after = natural[FRAME + i, cols]
         if first_call:
             one[place] = vector
             two[place] = after
@@ -484,9 +539,9 @@
 
 def final_kernel(dims, *refs):
     lat_cells, lon_cells = dims
-    counts, own, from_a, from_b, from_x, from_s, scal0, scal1 = refs[:8]
-    hbm, (increment, residual), refs = refs[8:17], refs[17:19], refs[19:]
-    face_lat, face_lon, keep, up, down, grad, spread, image, spread_next, buf, sems = refs
+    counts, own, from_a, from_b, own_x, own_s, corner_x, corner_s, scal0, scal1 = refs[:10]
+    hbm, (increment, residual), refs = refs[10:19], refs[19:21], refs[21:]
+    face_lat, face_lon, keep, up, down, grad, spread, image, spread_next, natural, buf, sems = refs
     inner = pl.ds(FRAME - REACH, lat_cells + 2 * REACH)
     block = pl.ds(REACH, lat_cells)
     loads = copies(
@@ -495,18 +550,19 @@
         + list(zip(hbm[5:], refs[5:9])), sems)
     nh, nv = counts[0], counts[1]
     place_halos(
-        buf, own, ((from_a, 0), (from_b, 0)), ((from_x, 0), (from_s, 0)), REACH, dims
+        natural, own, ((from_a, 0), (from_b, 0)),
+        (((own_x, 0), (corner_x, 0)), ((own_s, 0), (corner_s, 0))), REACH, dims,
     )
+    to_strided(natural, buf, range(FRAME - REACH, FRAME + lat_cells + REACH))
     for load in loads[:2]:
         load.wait()
-    last_lateral(buf, face_lat, face_lon, nh, lon_cells)
-    left = FRAME // 8 * 8
-    right = -(-(FRAME + lon_cells) // 8) * 8
+    lateral_passes(buf, face_lat, face_lon, nh, nh, 2 * nh)
     for load in loads[2:5]:
         load.wait()
     vertical_passes(
-        buf, keep, up, down, FRAME, FRAME + lat_cells, FRAME - REACH, nv, left, right
+        buf, keep, up, down, FRAME, FRAME + lat_cells, FRAME - REACH, nv
     )
+    to_natural(buf, natural, range(FRAME, FRAME + lat_cells))
     rr0 = jnp.sum(scal0[0:8])
     alpha0 = rr0 / (rr0 + jnp.sum(scal0[8:16]))
     rr1 = jnp.sum(scal1[0:8])
@@ -520,7 +576,7 @@
         place = pl.ds(pl.multiple_of(i * lon_cells, lon_cells), lon_cells)
         applied = image[place]
         rest = grad[place] - alpha0 * applied
-        residual[place] = rest - alpha1 * ((rest + buf[FRAME + i, cols]) + beta * applied)
+        residual[place] = rest - alpha1 * ((rest + natural[FRAME + i, cols]) + beta * applied)
         old = spread[place]
         increment[place] = alpha0 * old + alpha1 * (spread_next[place] + beta * old)
         return c
@@ -565,22 +621,34 @@
             return lax.psum(tail, "lat")
         return (tail + send(tail, "lat", swap(n_lat, 2))) + (from_a[slots:] + from_b[slots:])
 
-    def scatter(message):
-        return call(functools.partial(scatter_kernel, slots, cells_n), "scatter", field, (message, cells))
-
-    def sides_of(own, from_a, from_b, reach):
-        side = shape(side_rows(reach, lat_cells)[1], levels)
+    def side_shapes(reach):
+        return [shape(size, levels) for size in side_rows(reach, lat_cells)[1]]
+
+    def joined_shape(*reaches):
+        return shape(sum(sum(side_rows(reach, lat_cells)[1]) for reach in reaches), levels)
+
+    def scatter(message, reach):
+        side = side_shapes(reach)[0]
+        own, to_x, to_s = call(
+            functools.partial(scatter_kernel, dims, slots, reach), "scatter", (field, side, side),
+            (message, cells))
+        return own, lon_send(to_x, to_s)
+
+    def sides_of(from_a, from_b, reach, joined=()):
+        side = side_shapes(reach)[1]
+        if joined:
+            side = joined_shape(reach)
         strip = shape(reach * lon_cells, levels)
         strip_a, strip_b, to_x, to_s = call(
-            functools.partial(sides_kernel, dims, slots, reach), "sides", (strip, strip, side, side),
-            (own, from_a, from_b, *cells_near))
-        return (strip_a, strip_b), (to_x, to_s)
+            functools.partial(sides_kernel, dims, slots, reach, bool(joined)), "sides",
+            (strip, strip, side, side), (*joined, from_a, from_b, *cells_near))
+        return (strip_a, strip_b), lon_send(to_x, to_s)
 
     def halo(message, reach):
         from_a, from_b = lat_send(message, message, odd_pairs(n_lat))
-        own = scatter(message)
-        strips, sides = sides_of(own, from_a, from_b, reach)
-        return (own, *strips, *lon_send(*sides)), lat_sum(message[slots:], from_a, from_b)
+        own, own_sides = scatter(message, reach)
+        strips, corners = sides_of(from_a, from_b, reach)
+        return (own, *strips, *own_sides, *corners), lat_sum(message[slots:], from_a, from_b)
 
     vmem = pl.BlockSpec(memory_space=pltpu.VMEM)
     smem = pl.BlockSpec(memory_space=pltpu.SMEM)
@@ -644,20 +712,20 @@
         scratches=[scratch(obs, band_rows)] + adj_scratch)
 
     from_a, from_b = lat_send(message, message, inner_pairs)
-    own = scatter(message)
-    side = shape(sum(side_rows(reach, lat_cells)[1] for reach in (FRAME, REACH)), levels)
+    own = call(functools.partial(scatter_kernel, dims, slots, FRAME), "scatter", field, (message, cells))
+    side = joined_shape(FRAME, REACH)
     k_messages = call(functools.partial(face_sides_kernel, dims), "face_sides", (side, side),
                       (root_h, root_v, *k_strips))
     k_sides = lon_send(*k_messages)
     k_messages, from_a, from_b = lax.optimization_barrier((k_messages, from_a, from_b))
-    strips, sides = sides_of(own, from_a, from_b, FRAME)
-    halos = (own, *strips, *lon_send(*sides))
+    strips, sides = sides_of(from_a, from_b, FRAME, (own,))
+    halos = (own, *strips, *sides)
     faces = call(
         functools.partial(faces_kernel, dims), "faces", (wide, wide, tall, tall, tall),
         (root_h, root_v, *k_strips, *k_sides), far_out=5,
-        scratches=faces_vmem + [scratch(rows_h + 1, width, levels), sems(5)])
+        scratches=faces_vmem + [wide_vmem, scratch(rows_h + 1, width, levels), sems(5)])
     spread_scratch = faces_vmem + [jac_vmem] + [field_vmem] * 3 + [
-        wide_vmem, scratch(lat_cells, width, levels), sems(10)]
+        wide_vmem, wide_vmem, scratch(lat_cells, width, levels), sems(10)]
     grad, spread, message = call(
         functools.partial(spread_kernel, dims, True), "spread_first", (field, field, msg),
         (pass_counts, cells_flat, *halos), 2, (*faces, jacobian), 2, spread_scratch)
@@ -677,7 +745,7 @@
         functools.partial(final_kernel, dims), "final", (field, field),
         (pass_counts, *halos, scal0, scal1), 1,
         (*faces, grad, spread, image, spread_next), 0,
-        faces_vmem + [field_vmem] * 4 + [wide_vmem, sems(9)])
+        faces_vmem + [field_vmem] * 4 + [wide_vmem, wide_vmem, sems(9)])
     block = (lat_cells, lon_cells, levels)
     return increment.reshape(block), residual.reshape(block)
 

time: 123 us -> 119 us (0.967)
  waiting for transfers between devices: 30.1 us -> 20.4 us
  starting transfers between devices: 43.5 us -> 50.3 us
    ppermute x39 -> x43, waiting for transfers between devices: 30.1 us -> 20.4 us  [send(): return lax.ppermute(x, axis, pairs)]
    ppermute x39 -> x43, starting transfers between devices: 43.5 us -> 50.3 us  [send(): return lax.ppermute(x, axis, pairs)]
  transfers between devices with their start and end apart: 39 -> 43, of which waited for: 18 -> 17; matrix products, arithmetic and copies ran while one was open for 1% -> 1% of each run, Pallas kernels for 7% -> 8%
where the time goes in v3:
time: 119 us; the launch traced here: 118 us
  starting transfers between devices  50.3 us (42%)
  Pallas kernels  43.7 us (37%)
  waiting for transfers between devices  20.4 us (17%)
  other arithmetic  1.39 us (1%)
  between operations  1.19 us (1%)
    ppermute x43, starting transfers between devices, send(): return lax.ppermute(x, axis, pairs)  50.3 us
    pallas_call x15, Pallas kernels, call(): pl.pallas_call(kernel, out_shape=outs, in_specs=specs, out_specs=out_spec...  43.7 us
    ppermute x43, waiting for transfers between devices, send(): return lax.ppermute(x, axis, pairs)  20.4 us
  transfers between devices with their start and end apart: 43, of which 17 were waited for; matrix products, arithmetic and copies ran while one was open for 1% of the time, Pallas kernels for 8%

profile of v3, /device:TPU:0, one launch (start us, length us, event | category | flops | bytes accessed | tf_op | source)
XLA Modules:
  0.0 117.8 jit_solution(6033345345129118780)
XLA Ops:
  0.6 2.3 %start.1 = (f32[72,128]{1,0:T(8,128)}, f32[512,128]{1,0:T(8,128)}, f32[512,128]{1,0:T(8,128)}, f32[584,128]{1,0:T(8,128)}, f32[584,128]{1,0:T(8,128)}) custom-call(f32[64,64]{1,0:T(8,128)} %refs_0_.4, f32[64,64]{1,0:T(8,128)} %refs_1_.1, s32[2,192]{1,0:T(2,128)} %refs_2_.1, f32[512,128]{1,0:T(8,128)} %bitcast.16, f32[512,128]{1,0:T(8,128)} %bitcast.17), custom_call_target="tpu_custom_call" | custom-call | tf_op jit(solution)/shard_map/start/pallas_call | solution.py:678
  2.9 3.1 %collective-permute-start = (f32[72,128]{1,0:T(8,128)}, f32[72,128]{1,0:T(8,128)S(1)}, u32[]{:S(2)}, u32[]{:S(2)}) collective-permute-start(f32[72,128]{1,0:T(8,128)} %get-tuple-element.44.refs_0_), channel_id=1, source_target_pairs={{0,2},{1,3},{2,0},{3,1},{4,6},{5,7},{6,4},{7,5},{8,10},{9,11},{10,... | collective-permute-start | bytes 110600 | tf_op jit(solution)/shard_map/ppermute | solution.py:607
  6.0 2.6 %collective-permute-start.1 = (f32[72,128]{1,0:T(8,128)}, f32[72,128]{1,0:T(8,128)S(1)}, u32[]{:S(2)}, u32[]{:S(2)}) collective-permute-start(f32[72,128]{1,0:T(8,128)} %get-tuple-element.44.refs_0_), channel_id=1, source_target_pairs={{0,4},{1,5},{2,6},{3,7},{4,0},{5,1},{6,2},{7,3},{8,12},{9,13},{10,... | collective-permute-start | bytes 110600 | tf_op jit(solution)/shard_map/ppermute | solution.py:607
  8.6 1.7 %collective-permute-start.7 = (f32[584,128]{1,0:T(8,128)}, f32[584,128]{1,0:T(8,128)S(1)}, u32[]{:S(2)}, u32[]{:S(2)}) collective-permute-start(f32[584,128]{1,0:T(8,128)} %get-tuple-element.48), channel_id=1, source_target_pairs={{0,8},{8,0},{16,24},{24,16},{1,9},{9,1},{17,25},{25,17},{2,10},{10... | collective-permute-start | bytes 897032 | tf_op jit(solution)/shard_map/ppermute | solution.py:607
  10.3 0.8 fusion.20
  11.1 1.6 %collective-permute-start.8 = (f32[584,128]{1,0:T(8,128)}, f32[584,128]{1,0:T(8,128)S(1)}, u32[]{:S(2)}, u32[]{:S(2)}) collective-permute-start(f32[584,128]{1,0:T(8,128)} %get-tuple-element.49), channel_id=1, source_target_pairs={{0,0},{24,24},{8,16},{16,8},{1,1},{25,25},{9,17},{17,9},{2,2},{26,... | collective-permute-start | bytes 897032 | tf_op jit(solution)/shard_map/ppermute | solution.py:607
  13.1 1.5 %collective-permute-done.2.refs_3_ = f32[72,128]{1,0:T(8,128)S(1)} collective-permute-done((f32[72,128]{1,0:T(8,128)}, f32[72,128]{1,0:T(8,128)S(1)}, u32[]{:S(2)}, u32[]{:S(2)}) %collective-permute-start.2) | collective-permute-done | bytes 36896 | tf_op jit(solution)/shard_map/ppermute | solution.py:607
  14.6 0.5 collective-permute-start.6
  15.2 0.6 collective-permute-done.5.refs_6_
  16.0 0.8 copy-done.2
  16.7 3.4 %adjoint_first.1 = (f32[192,128]{1,0:T(8,128)S(1)}, f32[64,512]{1,0:T(8,128)S(1)}) custom-call(f32[72,128]{1,0:T(8,128)S(1)} %copy-done.2, f32[72,128]{1,0:T(8,128)S(1)} %collective-permute-done.refs_1_, f32[72,128]{1,0:T(8,128)S(1)} %collective-permute-done.1.refs_2_, f32[72,128]{1,0:T(8,128)S(1)} %collective-permute-done.2.refs_3_, ...), custom_call_target="tpu_custom_call" | custom-call | tf_op jit(solution)/shard_map/adjoint_first/pallas_call | solution.py:678
  20.2 0.7 collective-permute-start.10
  20.9 4.3 %collective-permute-start.9 = (f32[192,128]{1,0:T(8,128)S(1)}, f32[192,128]{1,0:T(8,128)S(1)}, u32[]{:S(2)}, u32[]{:S(2)}) collective-permute-start(f32[192,128]{1,0:T(8,128)S(1)} %get-tuple-element.45.message), channel_id=1, source_target_pairs={{0,8},{8,0},{16,24},{24,16},{1,9},{9,1},{17,25},{25,17},{2,10},{10... | collective-permute-start | bytes 294920 | tf_op jit(solution)/shard_map/ppermute | solution.py:607
  25.2 0.8 face_sides.1
  26.0 3.1 %collective-permute-start.14 = (f32[456,128]{1,0:T(8,128)S(1)}, f32[456,128]{1,0:T(8,128)S(1)}, u32[]{:S(2)}, u32[]{:S(2)}) collective-permute-start(f32[456,128]{1,0:T(8,128)S(1)} %get-tuple-element.51), channel_id=1, source_target_pairs={{0,7},{1,2},{2,1},{3,4},{4,3},{5,6},{6,5},{7,0},{8,15},{9,10},{10,... | collective-permute-start | bytes 700424 | tf_op jit(solution)/shard_map/ppermute | solution.py:607
  29.4 0.8 collective-permute-done.9.refs_1_
  30.2 1.1 sides.3
  31.3 2.9 %collective-permute-start.12 = (f32[328,128]{1,0:T(8,128)S(1)}, f32[328,128]{1,0:T(8,128)S(1)}, u32[]{:S(2)}, u32[]{:S(2)}) collective-permute-start(f32[328,128]{1,0:T(8,128)S(1)} %get-tuple-element.57), channel_id=1, source_target_pairs={{0,7},{1,2},{2,1},{3,4},{4,3},{5,6},{6,5},{7,0},{8,15},{9,10},{10,... | collective-permute-start | bytes 503816 | tf_op jit(solution)/shard_map/ppermute | solution.py:607
  34.3 1.3 %collective-permute-done.14.from_s = f32[456,128]{1,0:T(8,128)S(1)} collective-permute-done((f32[456,128]{1,0:T(8,128)S(1)}, f32[456,128]{1,0:T(8,128)S(1)}, u32[]{:S(2)}, u32[]{:S(2)}) %collective-permute-start.14) | collective-permute-done | bytes 233504 | tf_op jit(solution)/shard_map/ppermute | solution.py:607
  35.6 2.2 %faces.1 = (f32[40,56,128]{2,1,0:T(8,128)S(1)}, f32[40,56,128]{2,1,0:T(8,128)}, f32[28,56,128]{2,1,0:T(8,128)S(1)}, f32[28,56,128]{2,1,0:T(8,128)S(1)}, f32[28,56,128]{2,1,0:T(8,128)S(1)}) custom-call(f32[512,128]{1,0:T(8,128)S(1)} %copy-done, f32[512,128]{1,0:T(8,128)S(1)} %copy-done.1, f32[584,128]{1,0:T(8,128)S(1)} %collective-permute-done.7.from_a, ...), custom_call_target="tpu_custom_call" | custom-call | tf_op jit(solution)/shard_map/faces/pallas_call | solution.py:678
  37.9 1.3 %collective-permute-done.12.refs_6_ = f32[328,128]{1,0:T(8,128)S(1)} collective-permute-done((f32[328,128]{1,0:T(8,128)S(1)}, f32[328,128]{1,0:T(8,128)S(1)}, u32[]{:S(2)}, u32[]{:S(2)}) %collective-permute-start.12) | collective-permute-done | bytes 167968 | tf_op jit(solution)/shard_map/ppermute | solution.py:607
  39.2 9.4 %spread_first.1 = (f32[512,128]{1,0:T(8,128)S(1)}, f32[512,128]{1,0:T(8,128)S(1)}, f32[104,128]{1,0:T(8,128)S(1)}) custom-call(s32[2]{0:T(128)S(1)} %copy-done.3, s32[192]{0:T(256)S(1)} %bitcast.14, f32[512,128]{1,0:T(8,128)S(1)} %scatter.3.refs_0_.refs_2_, f32[384,128]{1,0:T(8,128)S(1)} %get-tuple-element.54.refs_3_, ...), custom_call_target="tpu_custom_call" | custom-call | tf_op jit(solution)/shard_map/spread_first/pallas_call | solution.py:678
  49.1 4.0 %collective-permute-start.17 = (f32[104,128]{1,0:T(8,128)S(1)}, f32[104,128]{1,0:T(8,128)S(1)}, u32[]{:S(2)}, u32[]{:S(2)}) collective-permute-start(f32[104,128]{1,0:T(8,128)S(1)} %get-tuple-element.63.refs_0_), channel_id=1, source_target_pairs={{0,6},{1,7},{2,4},{3,5},{4,2},{5,3},{6,0},{7,1},{8,14},{9,15},{10,... | collective-permute-start | bytes 159752 | tf_op jit(solution)/shard_map/ppermute | solution.py:607
  53.7 0.6 collective-permute-done.16.refs_2_
  54.3 2.1 %collective-permute-done.17.refs_3_ = f32[104,128]{1,0:T(8,128)S(1)} collective-permute-done((f32[104,128]{1,0:T(8,128)S(1)}, f32[104,128]{1,0:T(8,128)S(1)}, u32[]{:S(2)}, u32[]{:S(2)}) %collective-permute-start.17) | collective-permute-done | bytes 53280 | tf_op jit(solution)/shard_map/ppermute | solution.py:607
  57.0 0.7 collective-permute-done.21.refs_7_
  57.7 4.0 %adjoint_next.2.message = f32[208,128]{1,0:T(8,128)S(1)} custom-call(f32[104,128]{1,0:T(8,128)S(1)} %get-tuple-element.63.refs_0_, f32[104,128]{1,0:T(8,128)S(1)} %collective-permute-done.15.refs_1_, f32[104,128]{1,0:T(8,128)S(1)} %collective-permute-done.16.refs_2_, f32[104,128]{1,0:T(8,128)S(1)} %collective-permute-done.17.refs_3_, ...), custom_call_target="tpu_custom_call" | custom-call | tf_op jit(solution)/shard_map/adjoint_next/pallas_call | solution.py:678
  61.7 2.5 %collective-permute-start.22 = (f32[208,128]{1,0:T(8,128)S(1)}, f32[208,128]{1,0:T(8,128)S(1)}, u32[]{:S(2)}, u32[]{:S(2)}) collective-permute-start(f32[208,128]{1,0:T(8,128)S(1)} %adjoint_next.2.message), channel_id=1, source_target_pairs={{0,8},{8,0},{16,24},{24,16},{1,9},{9,1},{17,25},{25,17},{2,10},{10... | collective-permute-start | bytes 319496 | tf_op jit(solution)/shard_map/ppermute | solution.py:607
  64.1 1.1 collective-permute-start.23
  66.1 2.8 %collective-permute-start.25 = (f32[192,128]{1,0:T(8,128)S(1)}, f32[192,128]{1,0:T(8,128)S(1)}, u32[]{:S(2)}, u32[]{:S(2)}) collective-permute-start(f32[192,128]{1,0:T(8,128)S(1)} %get-tuple-element.69), channel_id=1, source_target_pairs={{0,7},{1,2},{2,1},{3,4},{4,3},{5,6},{6,5},{7,0},{8,15},{9,10},{10,... | collective-permute-start | bytes 294920 | tf_op jit(solution)/shard_map/ppermute | solution.py:607
  68.9 1.6 %collective-permute-done.23.refs_1_ = f32[208,128]{1,0:T(8,128)S(1)} collective-permute-done((f32[208,128]{1,0:T(8,128)S(1)}, f32[208,128]{1,0:T(8,128)S(1)}, u32[]{:S(2)}, u32[]{:S(2)}) %collective-permute-start.23) | collective-permute-done | bytes 106528 | tf_op jit(solution)/shard_map/ppermute | solution.py:607
  71.0 2.4 %collective-permute-start.27 = (f32[136,128]{1,0:T(8,128)S(1)}, f32[136,128]{1,0:T(8,128)S(1)}, u32[]{:S(2)}, u32[]{:S(2)}) collective-permute-start(f32[136,128]{1,0:T(8,128)S(1)} %get-tuple-element.71), channel_id=1, source_target_pairs={{0,7},{1,2},{2,1},{3,4},{4,3},{5,6},{6,5},{7,0},{8,15},{9,10},{10,... | collective-permute-start | bytes 208904 | tf_op jit(solution)/shard_map/ppermute | solution.py:607
  73.4 3.2 %collective-permute-done.27.refs_8_ = f32[136,128]{1,0:T(8,128)S(1)} collective-permute-done((f32[136,128]{1,0:T(8,128)S(1)}, f32[136,128]{1,0:T(8,128)S(1)}, u32[]{:S(2)}, u32[]{:S(2)}) %collective-permute-start.27) | collective-permute-done | bytes 69664 | tf_op jit(solution)/shard_map/ppermute | solution.py:607
  76.6 9.8 %spread_next.1 = (f32[512,128]{1,0:T(8,128)S(1)}, f32[512,128]{1,0:T(8,128)S(1)}, f32[104,128]{1,0:T(8,128)S(1)}) custom-call(s32[2]{0:T(128)S(1)} %copy-done.3, s32[192]{0:T(256)S(1)} %bitcast.15, f32[512,128]{1,0:T(8,128)S(1)} %get-tuple-element.65.refs_2_, f32[384,128]{1,0:T(8,128)S(1)} %get-tuple-element.66.refs_3_, ...), custom_call_target="tpu_custom_call" | custom-call | tf_op jit(solution)/shard_map/spread_next/pallas_call | solution.py:678
  86.5 1.0 collective-permute-start.30
  87.5 3.4 %collective-permute-start.31 = (f32[104,128]{1,0:T(8,128)S(1)}, f32[104,128]{1,0:T(8,128)S(1)}, u32[]{:S(2)}, u32[]{:S(2)}) collective-permute-start(f32[104,128]{1,0:T(8,128)S(1)} %get-tuple-element.74.refs_0_), channel_id=1, source_target_pairs={{0,6},{1,7},{2,4},{3,5},{4,2},{5,3},{6,0},{7,1},{8,14},{9,15},{10,... | collective-permute-start | bytes 159752 | tf_op jit(solution)/shard_map/ppermute | solution.py:607
  91.4 0.9 collective-permute-done.30.refs_2_
  92.3 1.4 %collective-permute-done.31.refs_3_ = f32[104,128]{1,0:T(8,128)S(1)} collective-permute-done((f32[104,128]{1,0:T(8,128)S(1)}, f32[104,128]{1,0:T(8,128)S(1)}, u32[]{:S(2)}, u32[]{:S(2)}) %collective-permute-start.31) | collective-permute-done | bytes 53280 | tf_op jit(solution)/shard_map/ppermute | solution.py:607
  94.1 0.9 collective-permute-done.35.refs_7_
  94.9 4.0 %adjoint_next.3.message = f32[208,128]{1,0:T(8,128)S(1)} custom-call(f32[104,128]{1,0:T(8,128)S(1)} %get-tuple-element.74.refs_0_, f32[104,128]{1,0:T(8,128)S(1)} %collective-permute-done.29.refs_1_, f32[104,128]{1,0:T(8,128)S(1)} %collective-permute-done.30.refs_2_, f32[104,128]{1,0:T(8,128)S(1)} %collective-permute-done.31.refs_3_, ...), custom_call_target="tpu_custom_call" | custom-call | tf_op jit(solution)/shard_map/adjoint_next/pallas_call | solution.py:678
  98.9 1.1 collective-permute-start.36
  100.0 1.6 %collective-permute-start.37 = (f32[208,128]{1,0:T(8,128)S(1)}, f32[208,128]{1,0:T(8,128)S(1)}, u32[]{:S(2)}, u32[]{:S(2)}) collective-permute-start(f32[208,128]{1,0:T(8,128)S(1)} %adjoint_next.3.message), channel_id=1, source_target_pairs={{0,24},{8,16},{16,8},{24,0},{1,25},{9,17},{17,9},{25,1},{2,26},{10... | collective-permute-start | bytes 319496 | tf_op jit(solution)/shard_map/ppermute | solution.py:607
  101.6 0.9 collective-permute-start.42
  102.9 3.3 %collective-permute-start.39 = (f32[96,128]{1,0:T(8,128)S(1)}, f32[96,128]{1,0:T(8,128)S(1)}, u32[]{:S(2)}, u32[]{:S(2)}) collective-permute-start(f32[96,128]{1,0:T(8,128)S(1)} %get-tuple-element.79), channel_id=1, source_target_pairs={{0,7},{1,2},{2,1},{3,4},{4,3},{5,6},{6,5},{7,0},{8,15},{9,10},{10,... | collective-permute-start | bytes 147464 | tf_op jit(solution)/shard_map/ppermute | solution.py:607
  106.2 0.9 collective-permute-done.37.refs_1_
  107.4 3.0 %collective-permute-start.41 = (f32[32,128]{1,0:T(8,128)S(1)}, f32[32,128]{1,0:T(8,128)S(1)}, u32[]{:S(2)}, u32[]{:S(2)}) collective-permute-start(f32[32,128]{1,0:T(8,128)S(1)} %get-tuple-element.81), channel_id=1, source_target_pairs={{0,7},{1,2},{2,1},{3,4},{4,3},{5,6},{6,5},{7,0},{8,15},{9,10},{10,... | collective-permute-start | bytes 49160 | tf_op jit(solution)/shard_map/ppermute | solution.py:607
  110.4 2.1 %collective-permute-done.41.refs_7_ = f32[32,128]{1,0:T(8,128)S(1)} collective-permute-done((f32[32,128]{1,0:T(8,128)S(1)}, f32[32,128]{1,0:T(8,128)S(1)}, u32[]{:S(2)}, u32[]{:S(2)}) %collective-permute-start.41) | collective-permute-done | bytes 16416 | tf_op jit(solution)/shard_map/ppermute | solution.py:607
  112.5 5.1 %final.1 = (f32[512,128]{1,0:T(8,128)}, f32[512,128]{1,0:T(8,128)}) custom-call(s32[2]{0:T(128)S(1)} %copy-done.3, f32[512,128]{1,0:T(8,128)S(1)} %get-tuple-element.75.refs_1_, f32[192,128]{1,0:T(8,128)S(1)} %get-tuple-element.76.refs_2_, f32[192,128]{1,0:T(8,128)S(1)} %get-tuple-element.77.refs_3_, f32[96,128]{1,0:T(8,128)S(1)} %collective-permute-done.38.refs_4_, ...), custom_call_target="tpu_custom_call" | custom-call | tf_op jit(solution)/shard_map/final/pallas_call | solution.py:678
  (82 shorter events, 5.5 us)
Async XLA Ops:
  2.9 8.2 %collective-permute-start = (f32[72,128]{1,0:T(8,128)}, f32[72,128]{1,0:T(8,128)S(1)}, u32[]{:S(2)}, u32[]{:S(2)}) collective-permute-start(f32[72,128]{1,0:T(8,128)} %get-tuple-element.44.refs_0_), channel_id=1, source_target_pairs={{0,2},{1,3},{2,0},{3,1},{4,6},{5,7},{6,4},{7,5},{8,10},{9,11},{10,... | collective-permute-start | bytes 110600 | tf_op jit(solution)/shard_map/ppermute | solution.py:607
  6.0 6.7 %collective-permute-start.1 = (f32[72,128]{1,0:T(8,128)}, f32[72,128]{1,0:T(8,128)S(1)}, u32[]{:S(2)}, u32[]{:S(2)}) collective-permute-start(f32[72,128]{1,0:T(8,128)} %get-tuple-element.44.refs_0_), channel_id=1, source_target_pairs={{0,4},{1,5},{2,6},{3,7},{4,0},{5,1},{6,2},{7,3},{8,12},{9,13},{10,... | collective-permute-start | bytes 110600 | tf_op jit(solution)/shard_map/ppermute | solution.py:607
  8.6 6.0 %collective-permute-start.2 = (f32[72,128]{1,0:T(8,128)}, f32[72,128]{1,0:T(8,128)S(1)}, u32[]{:S(2)}, u32[]{:S(2)}) collective-permute-start(f32[72,128]{1,0:T(8,128)} %get-tuple-element.44.refs_0_), channel_id=1, source_target_pairs={{0,6},{1,7},{2,4},{3,5},{4,2},{5,3},{6,0},{7,1},{8,14},{9,15},{10,... | collective-permute-start | bytes 110600 | tf_op jit(solution)/shard_map/ppermute | solution.py:607
  8.6 6.0 %collective-permute-start.3 = (f32[72,128]{1,0:T(8,128)}, f32[72,128]{1,0:T(8,128)S(1)}, u32[]{:S(2)}, u32[]{:S(2)}) collective-permute-start(f32[72,128]{1,0:T(8,128)} %get-tuple-element.44.refs_0_), channel_id=1, source_target_pairs={{0,1},{1,0},{2,3},{3,2},{4,5},{5,4},{6,7},{7,6},{8,9},{9,8},{10,11... | collective-permute-start | bytes 110600 | tf_op jit(solution)/shard_map/ppermute | solution.py:607
  8.6 16.5 %collective-permute-start.7 = (f32[584,128]{1,0:T(8,128)}, f32[584,128]{1,0:T(8,128)S(1)}, u32[]{:S(2)}, u32[]{:S(2)}) collective-permute-start(f32[584,128]{1,0:T(8,128)} %get-tuple-element.48), channel_id=1, source_target_pairs={{0,8},{8,0},{16,24},{24,16},{1,9},{9,1},{17,25},{25,17},{2,10},{10... | collective-permute-start | bytes 897032 | tf_op jit(solution)/shard_map/ppermute | solution.py:607
  11.1 14.1 %collective-permute-start.8 = (f32[584,128]{1,0:T(8,128)}, f32[584,128]{1,0:T(8,128)S(1)}, u32[]{:S(2)}, u32[]{:S(2)}) collective-permute-start(f32[584,128]{1,0:T(8,128)} %get-tuple-element.49), channel_id=1, source_target_pairs={{0,0},{24,24},{8,16},{16,8},{1,1},{25,25},{9,17},{17,9},{2,2},{26,... | collective-permute-start | bytes 897032 | tf_op jit(solution)/shard_map/ppermute | solution.py:607
  12.8 2.4 %collective-permute-start.4 = (f32[72,128]{1,0:T(8,128)S(1)}, f32[72,128]{1,0:T(8,128)S(1)}, u32[]{:S(2)}, u32[]{:S(2)}) collective-permute-start(f32[72,128]{1,0:T(8,128)S(1)} %collective-permute-done.refs_1_), channel_id=1, source_target_pairs={{0,1},{1,0},{2,3},{3,2},{4,5},{5,4},{6,7},{7,6},{8,9},{9,8},{10,11... | collective-permute-start | bytes 110600 | tf_op jit(solution)/shard_map/ppermute | solution.py:607
  14.6 1.2 %collective-permute-start.5 = (f32[72,128]{1,0:T(8,128)S(1)}, f32[72,128]{1,0:T(8,128)S(1)}, u32[]{:S(2)}, u32[]{:S(2)}) collective-permute-start(f32[72,128]{1,0:T(8,128)S(1)} %collective-permute-done.1.refs_2_), channel_id=1, source_target_pairs={{0,1},{1,0},{2,3},{3,2},{4,5},{5,4},{6,7},{7,6},{8,9},{9,8},{10,11... | collective-permute-start | bytes 110600 | tf_op jit(solution)/shard_map/ppermute | solution.py:607
  14.6 1.4 %collective-permute-start.6 = (f32[72,128]{1,0:T(8,128)S(1)}, f32[72,128]{1,0:T(8,128)S(1)}, u32[]{:S(2)}, u32[]{:S(2)}) collective-permute-start(f32[72,128]{1,0:T(8,128)S(1)} %collective-permute-done.2.refs_3_), channel_id=1, source_target_pairs={{0,1},{1,0},{2,3},{3,2},{4,5},{5,4},{6,7},{7,6},{8,9},{9,8},{10,11... | collective-permute-start | bytes 110600 | tf_op jit(solution)/shard_map/ppermute | solution.py:607
  15.2 10.0 %copy-start = (f32[512,128]{1,0:T(8,128)S(1)}, f32[512,128]{1,0:T(8,128)}, u32[]{:S(2)}) copy-start(f32[512,128]{1,0:T(8,128)} %get-tuple-element.46.root_h) | copy-start | bytes 786436
  15.2 10.0 %copy-start.1 = (f32[512,128]{1,0:T(8,128)S(1)}, f32[512,128]{1,0:T(8,128)}, u32[]{:S(2)}) copy-start(f32[512,128]{1,0:T(8,128)} %get-tuple-element.47.root_v) | copy-start | bytes 786436
  16.0 0.8 copy-start.2
  20.2 19.0 %copy-start.3 = (s32[2]{0:T(128)S(1)}, s32[2]{0:T(128)}, u32[]{:S(2)}) copy-start(s32[2]{0:T(128)} %refs_0_.7) | copy-start | bytes 28
  20.2 9.2 %collective-permute-start.10 = (f32[192,128]{1,0:T(8,128)S(1)}, f32[192,128]{1,0:T(8,128)S(1)}, u32[]{:S(2)}, u32[]{:S(2)}) collective-permute-start(f32[192,128]{1,0:T(8,128)S(1)} %get-tuple-element.45.message), channel_id=1, source_target_pairs={{0,0},{24,24},{8,16},{16,8},{1,1},{25,25},{9,17},{17,9},{2,2},{26,... | collective-permute-start | bytes 294920 | tf_op jit(solution)/shard_map/ppermute | solution.py:607
  20.9 9.3 %collective-permute-start.9 = (f32[192,128]{1,0:T(8,128)S(1)}, f32[192,128]{1,0:T(8,128)S(1)}, u32[]{:S(2)}, u32[]{:S(2)}) collective-permute-start(f32[192,128]{1,0:T(8,128)S(1)} %get-tuple-element.45.message), channel_id=1, source_target_pairs={{0,8},{8,0},{16,24},{24,16},{1,9},{9,1},{17,25},{25,17},{2,10},{10... | collective-permute-start | bytes 294920 | tf_op jit(solution)/shard_map/ppermute | solution.py:607
  26.0 8.3 %collective-permute-start.13 = (f32[456,128]{1,0:T(8,128)}, f32[456,128]{1,0:T(8,128)S(1)}, u32[]{:S(2)}, u32[]{:S(2)}) collective-permute-start(f32[456,128]{1,0:T(8,128)} %get-tuple-element.50), channel_id=1, source_target_pairs={{0,1},{1,0},{2,3},{3,2},{4,5},{5,4},{6,7},{7,6},{8,9},{9,8},{10,11... | collective-permute-start | bytes 700424 | tf_op jit(solution)/shard_map/ppermute | solution.py:607
  26.0 9.7 %collective-permute-start.14 = (f32[456,128]{1,0:T(8,128)S(1)}, f32[456,128]{1,0:T(8,128)S(1)}, u32[]{:S(2)}, u32[]{:S(2)}) collective-permute-start(f32[456,128]{1,0:T(8,128)S(1)} %get-tuple-element.51), channel_id=1, source_target_pairs={{0,7},{1,2},{2,1},{3,4},{4,3},{5,6},{6,5},{7,0},{8,15},{9,10},{10,... | collective-permute-start | bytes 700424 | tf_op jit(solution)/shard_map/ppermute | solution.py:607
  31.3 6.6 %collective-permute-start.11 = (f32[328,128]{1,0:T(8,128)}, f32[328,128]{1,0:T(8,128)S(1)}, u32[]{:S(2)}, u32[]{:S(2)}) collective-permute-start(f32[328,128]{1,0:T(8,128)} %get-tuple-element.56), channel_id=1, source_target_pairs={{0,1},{1,0},{2,3},{3,2},{4,5},{5,4},{6,7},{7,6},{8,9},{9,8},{10,11... | collective-permute-start | bytes 503816 | tf_op jit(solution)/shard_map/ppermute | solution.py:607
  31.3 7.9 %collective-permute-start.12 = (f32[328,128]{1,0:T(8,128)S(1)}, f32[328,128]{1,0:T(8,128)S(1)}, u32[]{:S(2)}, u32[]{:S(2)}) collective-permute-start(f32[328,128]{1,0:T(8,128)S(1)} %get-tuple-element.57), channel_id=1, source_target_pairs={{0,7},{1,2},{2,1},{3,4},{4,3},{5,6},{6,5},{7,0},{8,15},{9,10},{10,... | collective-permute-start | bytes 503816 | tf_op jit(solution)/shard_map/ppermute | solution.py:607
  48.7 4.6 %collective-permute-start.15 = (f32[104,128]{1,0:T(8,128)S(1)}, f32[104,128]{1,0:T(8,128)S(1)}, u32[]{:S(2)}, u32[]{:S(2)}) collective-permute-start(f32[104,128]{1,0:T(8,128)S(1)} %get-tuple-element.63.refs_0_), channel_id=1, source_target_pairs={{0,2},{1,3},{2,0},{3,1},{4,6},{5,7},{6,4},{7,5},{8,10},{9,11},{10,... | collective-permute-start | bytes 159752 | tf_op jit(solution)/shard_map/ppermute | solution.py:607
  48.7 5.6 %collective-permute-start.16 = (f32[104,128]{1,0:T(8,128)S(1)}, f32[104,128]{1,0:T(8,128)S(1)}, u32[]{:S(2)}, u32[]{:S(2)}) collective-permute-start(f32[104,128]{1,0:T(8,128)S(1)} %get-tuple-element.63.refs_0_), channel_id=1, source_target_pairs={{0,4},{1,5},{2,6},{3,7},{4,0},{5,1},{6,2},{7,3},{8,12},{9,13},{10,... | collective-permute-start | bytes 159752 | tf_op jit(solution)/shard_map/ppermute | solution.py:607
  49.1 7.4 %collective-permute-start.17 = (f32[104,128]{1,0:T(8,128)S(1)}, f32[104,128]{1,0:T(8,128)S(1)}, u32[]{:S(2)}, u32[]{:S(2)}) collective-permute-start(f32[104,128]{1,0:T(8,128)S(1)} %get-tuple-element.63.refs_0_), channel_id=1, source_target_pairs={{0,6},{1,7},{2,4},{3,5},{4,2},{5,3},{6,0},{7,1},{8,14},{9,15},{10,... | collective-permute-start | bytes 159752 | tf_op jit(solution)/shard_map/ppermute | solution.py:607
  53.1 3.8 %collective-permute-start.18 = (f32[104,128]{1,0:T(8,128)S(1)}, f32[104,128]{1,0:T(8,128)S(1)}, u32[]{:S(2)}, u32[]{:S(2)}) collective-permute-start(f32[104,128]{1,0:T(8,128)S(1)} %get-tuple-element.63.refs_0_), channel_id=1, source_target_pairs={{0,1},{1,0},{2,3},{3,2},{4,5},{5,4},{6,7},{7,6},{8,9},{9,8},{10,11... | collective-permute-start | bytes 159752 | tf_op jit(solution)/shard_map/ppermute | solution.py:607
  53.2 3.8 %collective-permute-start.19 = (f32[104,128]{1,0:T(8,128)S(1)}, f32[104,128]{1,0:T(8,128)S(1)}, u32[]{:S(2)}, u32[]{:S(2)}) collective-permute-start(f32[104,128]{1,0:T(8,128)S(1)} %collective-permute-done.15.refs_1_), channel_id=1, source_target_pairs={{0,1},{1,0},{2,3},{3,2},{4,5},{5,4},{6,7},{7,6},{8,9},{9,8},{10,11... | collective-permute-start | bytes 159752 | tf_op jit(solution)/shard_map/ppermute | solution.py:607
  54.3 2.7 %collective-permute-start.20 = (f32[104,128]{1,0:T(8,128)S(1)}, f32[104,128]{1,0:T(8,128)S(1)}, u32[]{:S(2)}, u32[]{:S(2)}) collective-permute-start(f32[104,128]{1,0:T(8,128)S(1)} %collective-permute-done.16.refs_2_), channel_id=1, source_target_pairs={{0,1},{1,0},{2,3},{3,2},{4,5},{5,4},{6,7},{7,6},{8,9},{9,8},{10,11... | collective-permute-start | bytes 159752 | tf_op jit(solution)/shard_map/ppermute | solution.py:607
  56.5 1.2 %collective-permute-start.21 = (f32[104,128]{1,0:T(8,128)S(1)}, f32[104,128]{1,0:T(8,128)S(1)}, u32[]{:S(2)}, u32[]{:S(2)}) collective-permute-start(f32[104,128]{1,0:T(8,128)S(1)} %collective-permute-done.17.refs_3_), channel_id=1, source_target_pairs={{0,1},{1,0},{2,3},{3,2},{4,5},{5,4},{6,7},{7,6},{8,9},{9,8},{10,11... | collective-permute-start | bytes 159752 | tf_op jit(solution)/shard_map/ppermute | solution.py:607
  61.7 7.2 %collective-permute-start.22 = (f32[208,128]{1,0:T(8,128)S(1)}, f32[208,128]{1,0:T(8,128)S(1)}, u32[]{:S(2)}, u32[]{:S(2)}) collective-permute-start(f32[208,128]{1,0:T(8,128)S(1)} %adjoint_next.2.message), channel_id=1, source_target_pairs={{0,8},{8,0},{16,24},{24,16},{1,9},{9,1},{17,25},{25,17},{2,10},{10... | collective-permute-start | bytes 319496 | tf_op jit(solution)/shard_map/ppermute | solution.py:607
  64.1 6.4 %collective-permute-start.23 = (f32[208,128]{1,0:T(8,128)S(1)}, f32[208,128]{1,0:T(8,128)S(1)}, u32[]{:S(2)}, u32[]{:S(2)}) collective-permute-start(f32[208,128]{1,0:T(8,128)S(1)} %adjoint_next.2.message), channel_id=1, source_target_pairs={{0,24},{8,16},{16,8},{24,0},{1,25},{9,17},{17,9},{25,1},{2,26},{10... | collective-permute-start | bytes 319496 | tf_op jit(solution)/shard_map/ppermute | solution.py:607
  65.2 8.1 %collective-permute-start.28 = (f32[16,128]{1,0:T(8,128)S(1)}, f32[16,128]{1,0:T(8,128)S(1)}, u32[]{:S(2)}, u32[]{:S(2)}) collective-permute-start(f32[16,128]{1,0:T(8,128)S(1)} %slice.81), channel_id=1, source_target_pairs={{0,16},{8,24},{16,0},{24,8},{1,17},{9,25},{17,1},{25,9},{2,18},{10... | collective-permute-start | bytes 24584 | tf_op jit(solution)/shard_map/ppermute | solution.py:607
  66.0 7.4 %collective-permute-start.24 = (f32[192,128]{1,0:T(8,128)S(1)}, f32[192,128]{1,0:T(8,128)S(1)}, u32[]{:S(2)}, u32[]{:S(2)}) collective-permute-start(f32[192,128]{1,0:T(8,128)S(1)} %get-tuple-element.68), channel_id=1, source_target_pairs={{0,1},{1,0},{2,3},{3,2},{4,5},{5,4},{6,7},{7,6},{8,9},{9,8},{10,11... | collective-permute-start | bytes 294920 | tf_op jit(solution)/shard_map/ppermute | solution.py:607
  66.1 7.3 %collective-permute-start.25 = (f32[192,128]{1,0:T(8,128)S(1)}, f32[192,128]{1,0:T(8,128)S(1)}, u32[]{:S(2)}, u32[]{:S(2)}) collective-permute-start(f32[192,128]{1,0:T(8,128)S(1)} %get-tuple-element.69), channel_id=1, source_target_pairs={{0,7},{1,2},{2,1},{3,4},{4,3},{5,6},{6,5},{7,0},{8,15},{9,10},{10,... | collective-permute-start | bytes 294920 | tf_op jit(solution)/shard_map/ppermute | solution.py:607
  70.9 2.5 %collective-permute-start.26 = (f32[136,128]{1,0:T(8,128)S(1)}, f32[136,128]{1,0:T(8,128)S(1)}, u32[]{:S(2)}, u32[]{:S(2)}) collective-permute-start(f32[136,128]{1,0:T(8,128)S(1)} %get-tuple-element.70), channel_id=1, source_target_pairs={{0,1},{1,0},{2,3},{3,2},{4,5},{5,4},{6,7},{7,6},{8,9},{9,8},{10,11... | collective-permute-start | bytes 208904 | tf_op jit(solution)/shard_map/ppermute | solution.py:607
  71.0 5.6 %collective-permute-start.27 = (f32[136,128]{1,0:T(8,128)S(1)}, f32[136,128]{1,0:T(8,128)S(1)}, u32[]{:S(2)}, u32[]{:S(2)}) collective-permute-start(f32[136,128]{1,0:T(8,128)S(1)} %get-tuple-element.71), channel_id=1, source_target_pairs={{0,7},{1,2},{2,1},{3,4},{4,3},{5,6},{6,5},{7,0},{8,15},{9,10},{10,... | collective-permute-start | bytes 208904 | tf_op jit(solution)/shard_map/ppermute | solution.py:607
  86.4 4.6 %collective-permute-start.29 = (f32[104,128]{1,0:T(8,128)S(1)}, f32[104,128]{1,0:T(8,128)S(1)}, u32[]{:S(2)}, u32[]{:S(2)}) collective-permute-start(f32[104,128]{1,0:T(8,128)S(1)} %get-tuple-element.74.refs_0_), channel_id=1, source_target_pairs={{0,2},{1,3},{2,0},{3,1},{4,6},{5,7},{6,4},{7,5},{8,10},{9,11},{10,... | collective-permute-start | bytes 159752 | tf_op jit(solution)/shard_map/ppermute | solution.py:607
  86.5 5.8 %collective-permute-start.30 = (f32[104,128]{1,0:T(8,128)S(1)}, f32[104,128]{1,0:T(8,128)S(1)}, u32[]{:S(2)}, u32[]{:S(2)}) collective-permute-start(f32[104,128]{1,0:T(8,128)S(1)} %get-tuple-element.74.refs_0_), channel_id=1, source_target_pairs={{0,4},{1,5},{2,6},{3,7},{4,0},{5,1},{6,2},{7,3},{8,12},{9,13},{10,... | collective-permute-start | bytes 159752 | tf_op jit(solution)/shard_map/ppermute | solution.py:607
  87.5 6.2 %collective-permute-start.31 = (f32[104,128]{1,0:T(8,128)S(1)}, f32[104,128]{1,0:T(8,128)S(1)}, u32[]{:S(2)}, u32[]{:S(2)}) collective-permute-start(f32[104,128]{1,0:T(8,128)S(1)} %get-tuple-element.74.refs_0_), channel_id=1, source_target_pairs={{0,6},{1,7},{2,4},{3,5},{4,2},{5,3},{6,0},{7,1},{8,14},{9,15},{10,... | collective-permute-start | bytes 159752 | tf_op jit(solution)/shard_map/ppermute | solution.py:607
  90.9 3.2 %collective-permute-start.32 = (f32[104,128]{1,0:T(8,128)S(1)}, f32[104,128]{1,0:T(8,128)S(1)}, u32[]{:S(2)}, u32[]{:S(2)}) collective-permute-start(f32[104,128]{1,0:T(8,128)S(1)} %get-tuple-element.74.refs_0_), channel_id=1, source_target_pairs={{0,1},{1,0},{2,3},{3,2},{4,5},{5,4},{6,7},{7,6},{8,9},{9,8},{10,11... | collective-permute-start | bytes 159752 | tf_op jit(solution)/shard_map/ppermute | solution.py:607
  91.0 3.0 %collective-permute-start.33 = (f32[104,128]{1,0:T(8,128)S(1)}, f32[104,128]{1,0:T(8,128)S(1)}, u32[]{:S(2)}, u32[]{:S(2)}) collective-permute-start(f32[104,128]{1,0:T(8,128)S(1)} %collective-permute-done.29.refs_1_), channel_id=1, source_target_pairs={{0,1},{1,0},{2,3},{3,2},{4,5},{5,4},{6,7},{7,6},{8,9},{9,8},{10,11... | collective-permute-start | bytes 159752 | tf_op jit(solution)/shard_map/ppermute | solution.py:607
  92.3 1.7 %collective-permute-start.34 = (f32[104,128]{1,0:T(8,128)S(1)}, f32[104,128]{1,0:T(8,128)S(1)}, u32[]{:S(2)}, u32[]{:S(2)}) collective-permute-start(f32[104,128]{1,0:T(8,128)S(1)} %collective-permute-done.30.refs_2_), channel_id=1, source_target_pairs={{0,1},{1,0},{2,3},{3,2},{4,5},{5,4},{6,7},{7,6},{8,9},{9,8},{10,11... | collective-permute-start | bytes 159752 | tf_op jit(solution)/shard_map/ppermute | solution.py:607
  93.7 1.2 %collective-permute-start.35 = (f32[104,128]{1,0:T(8,128)S(1)}, f32[104,128]{1,0:T(8,128)S(1)}, u32[]{:S(2)}, u32[]{:S(2)}) collective-permute-start(f32[104,128]{1,0:T(8,128)S(1)} %collective-permute-done.31.refs_3_), channel_id=1, source_target_pairs={{0,1},{1,0},{2,3},{3,2},{4,5},{5,4},{6,7},{7,6},{8,9},{9,8},{10,11... | collective-permute-start | bytes 159752 | tf_op jit(solution)/shard_map/ppermute | solution.py:607
  98.9 7.3 %collective-permute-start.36 = (f32[208,128]{1,0:T(8,128)S(1)}, f32[208,128]{1,0:T(8,128)S(1)}, u32[]{:S(2)}, u32[]{:S(2)}) collective-permute-start(f32[208,128]{1,0:T(8,128)S(1)} %adjoint_next.3.message), channel_id=1, source_target_pairs={{0,8},{8,0},{16,24},{24,16},{1,9},{9,1},{17,25},{25,17},{2,10},{10... | collective-permute-start | bytes 319496 | tf_op jit(solution)/shard_map/ppermute | solution.py:607
  100.0 7.1 %collective-permute-start.37 = (f32[208,128]{1,0:T(8,128)S(1)}, f32[208,128]{1,0:T(8,128)S(1)}, u32[]{:S(2)}, u32[]{:S(2)}) collective-permute-start(f32[208,128]{1,0:T(8,128)S(1)} %adjoint_next.3.message), channel_id=1, source_target_pairs={{0,24},{8,16},{16,8},{24,0},{1,25},{9,17},{17,9},{25,1},{2,26},{10... | collective-permute-start | bytes 319496 | tf_op jit(solution)/shard_map/ppermute | solution.py:607
  101.6 8.8 %collective-permute-start.42 = (f32[16,128]{1,0:T(8,128)S(1)}, f32[16,128]{1,0:T(8,128)S(1)}, u32[]{:S(2)}, u32[]{:S(2)}) collective-permute-start(f32[16,128]{1,0:T(8,128)S(1)} %slice.84), channel_id=1, source_target_pairs={{0,16},{8,24},{16,0},{24,8},{1,17},{9,25},{17,1},{25,9},{2,18},{10... | collective-permute-start | bytes 24584 | tf_op jit(solution)/shard_map/ppermute | solution.py:607
  102.8 7.6 %collective-permute-start.38 = (f32[96,128]{1,0:T(8,128)S(1)}, f32[96,128]{1,0:T(8,128)S(1)}, u32[]{:S(2)}, u32[]{:S(2)}) collective-permute-start(f32[96,128]{1,0:T(8,128)S(1)} %get-tuple-element.78), channel_id=1, source_target_pairs={{0,1},{1,0},{2,3},{3,2},{4,5},{5,4},{6,7},{7,6},{8,9},{9,8},{10,11... | collective-permute-start | bytes 147464 | tf_op jit(solution)/shard_map/ppermute | solution.py:607
  102.9 7.5 %collective-permute-start.39 = (f32[96,128]{1,0:T(8,128)S(1)}, f32[96,128]{1,0:T(8,128)S(1)}, u32[]{:S(2)}, u32[]{:S(2)}) collective-permute-start(f32[96,128]{1,0:T(8,128)S(1)} %get-tuple-element.79), channel_id=1, source_target_pairs={{0,7},{1,2},{2,1},{3,4},{4,3},{5,6},{6,5},{7,0},{8,15},{9,10},{10,... | collective-permute-start | bytes 147464 | tf_op jit(solution)/shard_map/ppermute | solution.py:607
  107.3 3.1 %collective-permute-start.40 = (f32[32,128]{1,0:T(8,128)S(1)}, f32[32,128]{1,0:T(8,128)S(1)}, u32[]{:S(2)}, u32[]{:S(2)}) collective-permute-start(f32[32,128]{1,0:T(8,128)S(1)} %get-tuple-element.80), channel_id=1, source_target_pairs={{0,1},{1,0},{2,3},{3,2},{4,5},{5,4},{6,7},{7,6},{8,9},{9,8},{10,11... | collective-permute-start | bytes 49160 | tf_op jit(solution)/shard_map/ppermute | solution.py:607
  107.4 5.1 %collective-permute-start.41 = (f32[32,128]{1,0:T(8,128)S(1)}, f32[32,128]{1,0:T(8,128)S(1)}, u32[]{:S(2)}, u32[]{:S(2)}) collective-permute-start(f32[32,128]{1,0:T(8,128)S(1)} %get-tuple-element.81), channel_id=1, source_target_pairs={{0,7},{1,2},{2,1},{3,4},{4,3},{5,6},{6,5},{7,0},{8,15},{9,10},{10,... | collective-permute-start | bytes 49160 | tf_op jit(solution)/shard_map/ppermute | solution.py:607

commit v4 on v3

--- a/solution.py
+++ b/solution.py
@@ -8,7 +8,8 @@
 from jax.sharding import PartitionSpec as P
 
 LANES = 128
-VMEM_LIMIT = 48 * 1024 * 1024
+VMEM_LIMIT = 40 * 1024 * 1024
+NEAR_LIMIT = 32 * 1024 * 1024
 START_LIMIT = 60 * 1024 * 1024
 REACH = 6
 FRAME = 2 * REACH
@@ -388,7 +389,7 @@
     if first_call:
         own_hot, jac_hbm, out, weight, band, jac, taken, sems = refs
     else:
-        row_hot, weight, own_hot, jac_hbm, out, jac, taken, sems = refs
+        row_hot, weight, own_hot, jac, out, taken = refs
     slots, obs, _ = jac.shape
     group = 64
     groups = slots // group
@@ -397,7 +398,7 @@
         place = pl.ds(g * group, group)
         return pltpu.make_async_copy(jac_hbm.at[place], jac.at[place], sems.at[g])
 
-    for g in range(groups):
+    for g in range(groups if first_call else 0):
         chunk(g).start()
     if first_call:
         own = weight.shape[1] // (2 * parts)
@@ -431,7 +432,8 @@
     lane = lax.broadcasted_iota(jnp.int32, (obs, LANES), 1)
 
     def body(g, c):
-        chunk(g).wait()
+        if first_call:
+            chunk(g).wait()
         per = LANES // group
         base = (g % per) * group
         values = taken[g // per]
@@ -466,12 +468,15 @@
         sides = [[(own_x, 0), (corner_x, 0)], [(own_s, 0), (corner_s, 0)]]
     if not first_call:
         scal, refs = refs[0], refs[1:]
-    faces_hbm, jac_hbm, refs = refs[:5], refs[5], refs[6:]
-    if not first_call:
-        grad_hbm, spread_hbm, refs = refs[0], refs[1], refs[2:]
-    one_hbm, two_hbm, message = refs[:3]
-    refs = refs[3:]
-    face_lat, face_lon, keep, up, down, jac, one, two, grad, natural, buf, mid, sems = refs
+    if first_call:
+        faces_hbm, jac_hbm, refs = refs[:5], refs[5], refs[6:]
+        one_hbm, two_hbm, message, jac = refs[:4]
+        refs = refs[4:]
+    else:
+        jac, faces_hbm, grad_hbm, spread_hbm = refs[0], refs[1:6], refs[6], refs[7]
+        one_hbm, two_hbm, message = refs[8:11]
+        refs = refs[11:]
+    face_lat, face_lon, keep, up, down, one, two, grad, natural, buf, mid, sems = refs
     loads = copies(list(zip(faces_hbm[:2], (face_lat, face_lon))), sems)
     nh, nv = counts[0], counts[1]
     rows = lat_cells + 2 * FRAME
@@ -482,8 +487,8 @@
     for load in loads:
         load.wait()
     loads = copies(
-        list(zip(faces_hbm[2:], (keep, up, down))) + [(jac_hbm, jac)], sems.at[pl.ds(2, 4)]
-    )
+        list(zip(faces_hbm[2:], (keep, up, down))) + ([(jac_hbm, jac)] if first_call else []),
+        sems.at[pl.ds(2, 4)])
     if not first_call:
         old_loads = copies([(grad_hbm, grad), (spread_hbm, two)], sems.at[pl.ds(6, 2)])
     lateral_passes(buf, face_lat, face_lon, nh, 0, nh)
@@ -529,7 +534,8 @@
 
     norm = lax.fori_loop(0, lat_cells, finish, jnp.zeros((8, LANES), jnp.float32))
     stores = copies([(one, one_hbm), (two, two_hbm)], sems.at[pl.ds(8, 2)])
-    loads[3].wait()
+    for load in loads[3:]:
+        load.wait()
     obs = jac.shape[1]
     observe(cells, jac, two, message)
     message[obs + obs // 2:] = norm
@@ -537,17 +543,30 @@
         store.wait()
 
 
+def combine_kernel(scal0, scal1, grad, spread, image, spread_next, increment, base, step):
+    rr0 = jnp.sum(scal0[0:8])
+    alpha0 = rr0 / (rr0 + jnp.sum(scal0[8:16]))
+    rr1 = jnp.sum(scal1[0:8])
+    beta = rr1 / rr0
+    alpha1 = rr1 / ((rr1 + jnp.sum(scal1[8:16])) - beta * (rr1 / alpha0))
+    step[...] = jnp.full(step.shape, 1.0, jnp.float32) * alpha1
+    applied = image[...]
+    rest = grad[...] - alpha0 * applied
+    base[...] = rest - alpha1 * (rest + beta * applied)
+    old = spread[...]
+    increment[...] = alpha0 * old + alpha1 * (spread_next[...] + beta * old)
+
+
 def final_kernel(dims, *refs):
     lat_cells, lon_cells = dims
-    counts, own, from_a, from_b, own_x, own_s, corner_x, corner_s, scal0, scal1 = refs[:10]
-    hbm, (increment, residual), refs = refs[10:19], refs[19:21], refs[21:]
-    face_lat, face_lon, keep, up, down, grad, spread, image, spread_next, natural, buf, sems = refs
+    counts, own, from_a, from_b, own_x, own_s, corner_x, corner_s, base, alpha = refs[:10]
+    hbm, residual, refs = refs[10:15], refs[15], refs[16:]
+    face_lat, face_lon, keep, up, down, natural, buf, sems = refs
     inner = pl.ds(FRAME - REACH, lat_cells + 2 * REACH)
     block = pl.ds(REACH, lat_cells)
     loads = copies(
         [(src.at[inner], dst.at[inner]) for src, dst in zip(hbm[:2], refs[:2])]
-        + [(src.at[block], dst.at[block]) for src, dst in zip(hbm[2:5], refs[2:5])]
-        + list(zip(hbm[5:], refs[5:9])), sems)
+        + [(src.at[block], dst.at[block]) for src, dst in zip(hbm[2:5], refs[2:5])], sems)
     nh, nv = counts[0], counts[1]
     place_halos(
         natural, own, ((from_a, 0), (from_b, 0)),
@@ -557,31 +576,17 @@
     for load in loads[:2]:
         load.wait()
     lateral_passes(buf, face_lat, face_lon, nh, nh, 2 * nh)
-    for load in loads[2:5]:
+    for load in loads[2:]:
         load.wait()
     vertical_passes(
         buf, keep, up, down, FRAME, FRAME + lat_cells, FRAME - REACH, nv
     )
     to_natural(buf, natural, range(FRAME, FRAME + lat_cells))
-    rr0 = jnp.sum(scal0[0:8])
-    alpha0 = rr0 / (rr0 + jnp.sum(scal0[8:16]))
-    rr1 = jnp.sum(scal1[0:8])
-    beta = rr1 / rr0
-    alpha1 = rr1 / ((rr1 + jnp.sum(scal1[8:16])) - beta * (rr1 / alpha0))
     cols = slice(FRAME, FRAME + lon_cells)
-    for load in loads[5:]:
-        load.wait()
-
-    def finish(i, c):
-        place = pl.ds(pl.multiple_of(i * lon_cells, lon_cells), lon_cells)
-        applied = image[place]
-        rest = grad[place] - alpha0 * applied
-        residual[place] = rest - alpha1 * ((rest + natural[FRAME + i, cols]) + beta * applied)
-        old = spread[place]
-        increment[place] = alpha0 * old + alpha1 * (spread_next[place] + beta * old)
-        return c
-
-    lax.fori_loop(0, lat_cells, finish, 0)
+    step = jnp.concatenate([alpha[...]] * (lon_cells // 8), axis=0)
+    for i in range(lat_cells):
+        place = slice(i * lon_cells, i * lon_cells + lon_cells)
+        residual[place] = base[place] - step * natural[FRAME + i, cols]
 
 
 def local(innovation, obs_weight, jacobian, block_list, pass_counts, kappa_h, kappa_v):
@@ -724,28 +729,33 @@
         functools.partial(faces_kernel, dims), "faces", (wide, wide, tall, tall, tall),
         (root_h, root_v, *k_strips, *k_sides), far_out=5,
         scratches=faces_vmem + [wide_vmem, scratch(rows_h + 1, width, levels), sems(5)])
-    spread_scratch = faces_vmem + [jac_vmem] + [field_vmem] * 3 + [
+    spread_scratch = faces_vmem + [field_vmem] * 3 + [
         wide_vmem, wide_vmem, scratch(lat_cells, width, levels), sems(10)]
-    grad, spread, message = call(
-        functools.partial(spread_kernel, dims, True), "spread_first", (field, field, msg),
+    near_params = pltpu.CompilerParams(vmem_limit_bytes=NEAR_LIMIT)
+    grad, spread, message, near_jac = call(
+        functools.partial(spread_kernel, dims, True), "spread_first",
+        (field, field, msg, shape(*jacobian.shape)),
         (pass_counts, cells_flat, *halos), 2, (*faces, jacobian), 2, spread_scratch)
 
     def adjoint(message):
         return call(
             functools.partial(adjoint_kernel, False, parts), "adjoint_next",
-            shape(slots + 16, levels), (*gather_band(message), row_hot, weight, own_hot),
-            far_in=(jacobian,), scratches=adj_scratch)
+            shape(slots + 16, levels), (*gather_band(message), row_hot, weight, own_hot, near_jac),
+            scratches=[scratch(2, obs, LANES)], params=near_params)
 
     halos, scal0 = halo(adjoint(message), FRAME)
     image, spread_next, message = call(
         functools.partial(spread_kernel, dims, False), "spread_next", (field, field, msg),
-        (pass_counts, cells_flat, *halos, scal0), 2, (*faces, jacobian, grad, spread), 2, spread_scratch)
+        (pass_counts, cells_flat, *halos, scal0, near_jac), 2, (*faces, grad, spread), 2, spread_scratch,
+        near_params)
     halos, scal1 = halo(adjoint(message), REACH)
-    increment, residual = call(
-        functools.partial(final_kernel, dims), "final", (field, field),
-        (pass_counts, *halos, scal0, scal1), 1,
-        (*faces, grad, spread, image, spread_next), 0,
-        faces_vmem + [field_vmem] * 4 + [wide_vmem, wide_vmem, sems(9)])
+    increment, base, step = call(
+        combine_kernel, "combine", (field, field, shape(8, LANES)),
+        (scal0, scal1, grad, spread, image, spread_next))
+    residual = call(
+        functools.partial(final_kernel, dims), "final", field,
+        (pass_counts, *halos, base, step), 1, faces, 0,
+        faces_vmem + [wide_vmem, wide_vmem, sems(5)])
     block = (lat_cells, lon_cells, levels)
     return increment.reshape(block), residual.reshape(block)
 

time: 119 us -> 115 us (0.966); the launches traced: 118 us -> 115 us
  local copies, waits for them, and re-layouts: 0.85 us -> 3.63 us
  Pallas kernels: 43.7 us -> 41.4 us
  waiting for transfers between devices: 20.4 us -> 18.1 us
    unnamed x8 -> x10, local copies, waits for them, and re-layouts: 0.79 us -> 3.57 us
    ppermute x43, waiting for transfers between devices: 20.4 us -> 18.1 us  [send(): return lax.ppermute(x, axis, pairs)]
    pallas_call x15 -> x16, Pallas kernels: 43.7 us -> 41.4 us  [call(): pl.pallas_call(kernel, out_shape=outs, in_specs=specs, out_specs=out_spec...]
  transfers between devices with their start and end apart: 43 -> 43, of which waited for: 17 -> 19; matrix products, arithmetic and copies ran while one was open for 1% -> 1% of each run, Pallas kernels for 8% -> 8%
where the time goes in v4:
time: 115 us
  starting transfers between devices  49.8 us (43%)
  Pallas kernels  41.4 us (36%)
  waiting for transfers between devices  18.1 us (16%)
  local copies, waits for them, and re-layouts  3.63 us (3%)
  other arithmetic  1.39 us (1%)
  between operations  1.16 us (1%)
    ppermute x43, starting transfers between devices, send(): return lax.ppermute(x, axis, pairs)  49.8 us
    pallas_call x16, Pallas kernels, call(): pl.pallas_call(kernel, out_shape=outs, in_specs=specs, out_specs=out_spec...  41.4 us
    ppermute x43, waiting for transfers between devices, send(): return lax.ppermute(x, axis, pairs)  18.1 us
    unnamed x10, local copies, waits for them, and re-layouts  3.57 us
  transfers between devices with their start and end apart: 43, of which 19 were waited for; matrix products, arithmetic and copies ran while one was open for 1% of the time, Pallas kernels for 8%

profile of v4, /device:TPU:0, one launch (start us, length us, event | category | flops | bytes accessed | tf_op | source)
XLA Modules:
  0.0 115.4 jit_solution(2257215038557896445)
XLA Ops:
  0.6 2.3 %start.1 = (f32[72,128]{1,0:T(8,128)}, f32[512,128]{1,0:T(8,128)}, f32[512,128]{1,0:T(8,128)}, f32[584,128]{1,0:T(8,128)}, f32[584,128]{1,0:T(8,128)}) custom-call(f32[64,64]{1,0:T(8,128)} %refs_0_.4, f32[64,64]{1,0:T(8,128)} %refs_1_.1, s32[2,192]{1,0:T(2,128)} %refs_2_.1, f32[512,128]{1,0:T(8,128)} %bitcast.16, f32[512,128]{1,0:T(8,128)} %bitcast.17), custom_call_target="tpu_custom_call" | custom-call | tf_op jit(solution)/shard_map/start/pallas_call | solution.py:683
  3.5 4.7 %collective-permute-start.2 = (f32[72,128]{1,0:T(8,128)}, f32[72,128]{1,0:T(8,128)S(1)}, u32[]{:S(2)}, u32[]{:S(2)}) collective-permute-start(f32[72,128]{1,0:T(8,128)} %get-tuple-element.46.refs_0_), channel_id=1, source_target_pairs={{0,6},{1,7},{2,4},{3,5},{4,2},{5,3},{6,0},{7,1},{8,14},{9,15},{10,... | collective-permute-start | bytes 110600 | tf_op jit(solution)/shard_map/ppermute | solution.py:612
  8.1 0.7 collective-permute-start
  8.8 1.6 %collective-permute-start.7 = (f32[584,128]{1,0:T(8,128)}, f32[584,128]{1,0:T(8,128)S(1)}, u32[]{:S(2)}, u32[]{:S(2)}) collective-permute-start(f32[584,128]{1,0:T(8,128)} %get-tuple-element.50), channel_id=1, source_target_pairs={{0,8},{8,0},{16,24},{24,16},{1,9},{9,1},{17,25},{25,17},{2,10},{10... | collective-permute-start | bytes 897032 | tf_op jit(solution)/shard_map/ppermute | solution.py:612
  10.4 0.8 fusion.20
  11.2 1.6 %collective-permute-start.8 = (f32[584,128]{1,0:T(8,128)}, f32[584,128]{1,0:T(8,128)S(1)}, u32[]{:S(2)}, u32[]{:S(2)}) collective-permute-start(f32[584,128]{1,0:T(8,128)} %get-tuple-element.51), channel_id=1, source_target_pairs={{0,0},{24,24},{8,16},{16,8},{1,1},{25,25},{9,17},{17,9},{2,2},{26,... | collective-permute-start | bytes 897032 | tf_op jit(solution)/shard_map/ppermute | solution.py:612
  14.7 2.8 %copy-done = f32[192,64,128]{2,1,0:T(8,128)S(1)} copy-done((f32[192,64,128]{2,1,0:T(8,128)S(1)}, f32[192,64,128]{2,1,0:T(8,128)}, u32[]{:S(2)}) %copy-start) | copy-done | bytes 6291480
  17.4 0.8 copy-done.3
  18.2 2.2 %adjoint_first.1 = (f32[192,128]{1,0:T(8,128)S(1)}, f32[64,512]{1,0:T(8,128)S(1)}) custom-call(f32[72,128]{1,0:T(8,128)S(1)} %copy-done.3, f32[72,128]{1,0:T(8,128)S(1)} %collective-permute-done.refs_1_, f32[72,128]{1,0:T(8,128)S(1)} %collective-permute-done.1.refs_2_, f32[72,128]{1,0:T(8,128)S(1)} %collective-permute-done.2.refs_3_, ...), custom_call_target="tpu_custom_call" | custom-call | tf_op jit(solution)/shard_map/adjoint_first/pallas_call | solution.py:683
  20.5 0.7 collective-permute-start.10
  21.1 4.9 %collective-permute-start.9 = (f32[192,128]{1,0:T(8,128)S(1)}, f32[192,128]{1,0:T(8,128)S(1)}, u32[]{:S(2)}, u32[]{:S(2)}) collective-permute-start(f32[192,128]{1,0:T(8,128)S(1)} %get-tuple-element.47.message), channel_id=1, source_target_pairs={{0,8},{8,0},{16,24},{24,16},{1,9},{9,1},{17,25},{25,17},{2,10},{10... | collective-permute-start | bytes 294920 | tf_op jit(solution)/shard_map/ppermute | solution.py:612
  26.1 0.8 face_sides.1
  26.9 3.8 %collective-permute-start.14 = (f32[456,128]{1,0:T(8,128)S(1)}, f32[456,128]{1,0:T(8,128)S(1)}, u32[]{:S(2)}, u32[]{:S(2)}) collective-permute-start(f32[456,128]{1,0:T(8,128)S(1)} %get-tuple-element.53), channel_id=1, source_target_pairs={{0,7},{1,2},{2,1},{3,4},{4,3},{5,6},{6,5},{7,0},{8,15},{9,10},{10,... | collective-permute-start | bytes 700424 | tf_op jit(solution)/shard_map/ppermute | solution.py:612
  31.1 1.1 sides.3
  32.2 3.7 %collective-permute-start.12 = (f32[328,128]{1,0:T(8,128)S(1)}, f32[328,128]{1,0:T(8,128)S(1)}, u32[]{:S(2)}, u32[]{:S(2)}) collective-permute-start(f32[328,128]{1,0:T(8,128)S(1)} %get-tuple-element.59), channel_id=1, source_target_pairs={{0,7},{1,2},{2,1},{3,4},{4,3},{5,6},{6,5},{7,0},{8,15},{9,10},{10,... | collective-permute-start | bytes 503816 | tf_op jit(solution)/shard_map/ppermute | solution.py:612
  36.0 0.7 collective-permute-done.14.from_s
  36.7 2.4 %faces.1 = (f32[40,56,128]{2,1,0:T(8,128)S(1)}, f32[40,56,128]{2,1,0:T(8,128)S(1)}, f32[28,56,128]{2,1,0:T(8,128)S(1)}, f32[28,56,128]{2,1,0:T(8,128)S(1)}, f32[28,56,128]{2,1,0:T(8,128)S(1)}) custom-call(f32[512,128]{1,0:T(8,128)S(1)} %copy-done.1, f32[512,128]{1,0:T(8,128)S(1)} %copy-done.2, f32[584,128]{1,0:T(8,128)S(1)} %collective-permute-done.7.from_a, ...), custom_call_target="tpu_custom_call" | custom-call | tf_op jit(solution)/shard_map/faces/pallas_call | solution.py:683
  39.1 1.3 %collective-permute-done.12.refs_6_ = f32[328,128]{1,0:T(8,128)S(1)} collective-permute-done((f32[328,128]{1,0:T(8,128)S(1)}, f32[328,128]{1,0:T(8,128)S(1)}, u32[]{:S(2)}, u32[]{:S(2)}) %collective-permute-start.12) | collective-permute-done | bytes 167968 | tf_op jit(solution)/shard_map/ppermute | solution.py:612
  40.4 9.9 %spread_first.1 = (f32[512,128]{1,0:T(8,128)S(1)}, f32[512,128]{1,0:T(8,128)S(1)}, f32[104,128]{1,0:T(8,128)S(1)}, f32[192,64,128]{2,1,0:T(8,128)S(1)}) custom-call(s32[2]{0:T(128)S(1)} %copy-done.4, s32[192]{0:T(256)S(1)} %bitcast.14, f32[512,128]{1,0:T(8,128)S(1)} %scatter.3.refs_0_.refs_2_, f32[384,128]{1,0:T(8,128)S(1)} %get-tuple-element.56.refs_3_, ...), custom_call_target="tpu_custom_call" | custom-call | tf_op jit(solution)/shard_map/spread_first/pallas_call | solution.py:683
  50.7 4.1 %collective-permute-start.15 = (f32[104,128]{1,0:T(8,128)S(1)}, f32[104,128]{1,0:T(8,128)S(1)}, u32[]{:S(2)}, u32[]{:S(2)}) collective-permute-start(f32[104,128]{1,0:T(8,128)S(1)} %get-tuple-element.65.refs_0_), channel_id=1, source_target_pairs={{0,2},{1,3},{2,0},{3,1},{4,6},{5,7},{6,4},{7,5},{8,10},{9,11},{10,... | collective-permute-start | bytes 159752 | tf_op jit(solution)/shard_map/ppermute | solution.py:612
  54.9 1.5 %collective-permute-done.17.refs_3_ = f32[104,128]{1,0:T(8,128)S(1)} collective-permute-done((f32[104,128]{1,0:T(8,128)S(1)}, f32[104,128]{1,0:T(8,128)S(1)}, u32[]{:S(2)}, u32[]{:S(2)}) %collective-permute-start.17) | collective-permute-done | bytes 53280 | tf_op jit(solution)/shard_map/ppermute | solution.py:612
  56.4 0.9 collective-permute-start.20
  57.4 0.6 collective-permute-done.15.refs_1_
  58.5 0.7 collective-permute-done.19.refs_5_
  59.2 2.3 %adjoint_next.2.message = f32[208,128]{1,0:T(8,128)S(1)} custom-call(f32[104,128]{1,0:T(8,128)S(1)} %get-tuple-element.65.refs_0_, f32[104,128]{1,0:T(8,128)S(1)} %collective-permute-done.15.refs_1_, f32[104,128]{1,0:T(8,128)S(1)} %collective-permute-done.16.refs_2_, f32[104,128]{1,0:T(8,128)S(1)} %collective-permute-done.17.refs_3_, ...), custom_call_target="tpu_custom_call" | custom-call | tf_op jit(solution)/shard_map/adjoint_next/pallas_call | solution.py:683
  61.6 2.5 %collective-permute-start.24 = (f32[208,128]{1,0:T(8,128)S(1)}, f32[208,128]{1,0:T(8,128)S(1)}, u32[]{:S(2)}, u32[]{:S(2)}) collective-permute-start(f32[208,128]{1,0:T(8,128)S(1)} %adjoint_next.2.message), channel_id=1, source_target_pairs={{0,24},{8,16},{16,8},{24,0},{1,25},{9,17},{17,9},{25,1},{2,26},{10... | collective-permute-start | bytes 319496 | tf_op jit(solution)/shard_map/ppermute | solution.py:612
  64.1 1.1 collective-permute-start.22
  65.5 2.1 %collective-permute-start.26 = (f32[192,128]{1,0:T(8,128)S(1)}, f32[192,128]{1,0:T(8,128)S(1)}, u32[]{:S(2)}, u32[]{:S(2)}) collective-permute-start(f32[192,128]{1,0:T(8,128)S(1)} %get-tuple-element.72), channel_id=1, source_target_pairs={{0,7},{1,2},{2,1},{3,4},{4,3},{5,6},{6,5},{7,0},{8,15},{9,10},{10,... | collective-permute-start | bytes 294920 | tf_op jit(solution)/shard_map/ppermute | solution.py:612
  67.6 0.7 collective-permute-done.24.refs_1_
  68.3 0.9 collective-permute-done.23.refs_0_
  69.7 2.3 %collective-permute-start.28 = (f32[136,128]{1,0:T(8,128)S(1)}, f32[136,128]{1,0:T(8,128)S(1)}, u32[]{:S(2)}, u32[]{:S(2)}) collective-permute-start(f32[136,128]{1,0:T(8,128)S(1)} %get-tuple-element.74), channel_id=1, source_target_pairs={{0,7},{1,2},{2,1},{3,4},{4,3},{5,6},{6,5},{7,0},{8,15},{9,10},{10,... | collective-permute-start | bytes 208904 | tf_op jit(solution)/shard_map/ppermute | solution.py:612
  72.0 3.4 %collective-permute-done.28.refs_8_ = f32[136,128]{1,0:T(8,128)S(1)} collective-permute-done((f32[136,128]{1,0:T(8,128)S(1)}, f32[136,128]{1,0:T(8,128)S(1)}, u32[]{:S(2)}, u32[]{:S(2)}) %collective-permute-start.28) | collective-permute-done | bytes 69664 | tf_op jit(solution)/shard_map/ppermute | solution.py:612
  75.4 10.3 %spread_next.1 = (f32[512,128]{1,0:T(8,128)S(1)}, f32[512,128]{1,0:T(8,128)S(1)}, f32[104,128]{1,0:T(8,128)S(1)}) custom-call(s32[2]{0:T(128)S(1)} %copy-done.4, s32[192]{0:T(256)S(1)} %bitcast.15, f32[512,128]{1,0:T(8,128)S(1)} %get-tuple-element.68.refs_2_, f32[384,128]{1,0:T(8,128)S(1)} %get-tuple-element.69.refs_3_, ...), custom_call_target="tpu_custom_call" | custom-call | tf_op jit(solution)/shard_map/spread_next/pallas_call | solution.py:683
  86.6 3.6 %collective-permute-start.29 = (f32[104,128]{1,0:T(8,128)S(1)}, f32[104,128]{1,0:T(8,128)S(1)}, u32[]{:S(2)}, u32[]{:S(2)}) collective-permute-start(f32[104,128]{1,0:T(8,128)S(1)} %get-tuple-element.77.refs_0_), channel_id=1, source_target_pairs={{0,2},{1,3},{2,0},{3,1},{4,6},{5,7},{6,4},{7,5},{8,10},{9,11},{10,... | collective-permute-start | bytes 159752 | tf_op jit(solution)/shard_map/ppermute | solution.py:612
  90.2 1.6 %collective-permute-done.31.refs_3_ = f32[104,128]{1,0:T(8,128)S(1)} collective-permute-done((f32[104,128]{1,0:T(8,128)S(1)}, f32[104,128]{1,0:T(8,128)S(1)}, u32[]{:S(2)}, u32[]{:S(2)}) %collective-permute-start.31) | collective-permute-done | bytes 53280 | tf_op jit(solution)/shard_map/ppermute | solution.py:612
  91.8 0.9 collective-permute-start.34
  92.7 0.7 collective-permute-done.29.refs_1_
  93.6 1.0 collective-permute-done.33.refs_5_
  94.6 2.3 %adjoint_next.3.message = f32[208,128]{1,0:T(8,128)S(1)} custom-call(f32[104,128]{1,0:T(8,128)S(1)} %get-tuple-element.77.refs_0_, f32[104,128]{1,0:T(8,128)S(1)} %collective-permute-done.29.refs_1_, f32[104,128]{1,0:T(8,128)S(1)} %collective-permute-done.30.refs_2_, f32[104,128]{1,0:T(8,128)S(1)} %collective-permute-done.31.refs_3_, ...), custom_call_target="tpu_custom_call" | custom-call | tf_op jit(solution)/shard_map/adjoint_next/pallas_call | solution.py:683
  97.0 1.7 %collective-permute-start.38 = (f32[208,128]{1,0:T(8,128)S(1)}, f32[208,128]{1,0:T(8,128)S(1)}, u32[]{:S(2)}, u32[]{:S(2)}) collective-permute-start(f32[208,128]{1,0:T(8,128)S(1)} %adjoint_next.3.message), channel_id=1, source_target_pairs={{0,24},{8,16},{16,8},{24,0},{1,25},{9,17},{17,9},{25,1},{2,26},{10... | collective-permute-start | bytes 319496 | tf_op jit(solution)/shard_map/ppermute | solution.py:612
  98.6 0.9 collective-permute-start.37
  99.5 1.0 collective-permute-start.36
  100.9 2.1 %collective-permute-start.40 = (f32[96,128]{1,0:T(8,128)S(1)}, f32[96,128]{1,0:T(8,128)S(1)}, u32[]{:S(2)}, u32[]{:S(2)}) collective-permute-start(f32[96,128]{1,0:T(8,128)S(1)} %get-tuple-element.85), channel_id=1, source_target_pairs={{0,7},{1,2},{2,1},{3,4},{4,3},{5,6},{6,5},{7,0},{8,15},{9,10},{10,... | collective-permute-start | bytes 147464 | tf_op jit(solution)/shard_map/ppermute | solution.py:612
  103.5 1.3 %collective-permute-done.37.refs_0_ = f32[208,128]{1,0:T(8,128)S(1)} collective-permute-done((f32[208,128]{1,0:T(8,128)S(1)}, f32[208,128]{1,0:T(8,128)S(1)}, u32[]{:S(2)}, u32[]{:S(2)}) %collective-permute-start.37) | collective-permute-done | bytes 106528 | tf_op jit(solution)/shard_map/ppermute | solution.py:612
  105.2 2.2 %collective-permute-start.42 = (f32[32,128]{1,0:T(8,128)S(1)}, f32[32,128]{1,0:T(8,128)S(1)}, u32[]{:S(2)}, u32[]{:S(2)}) collective-permute-start(f32[32,128]{1,0:T(8,128)S(1)} %get-tuple-element.87), channel_id=1, source_target_pairs={{0,7},{1,2},{2,1},{3,4},{4,3},{5,6},{6,5},{7,0},{8,15},{9,10},{10,... | collective-permute-start | bytes 49160 | tf_op jit(solution)/shard_map/ppermute | solution.py:612
  107.4 1.1 combine.1
  108.4 1.8 %collective-permute-done.42.refs_7_ = f32[32,128]{1,0:T(8,128)S(1)} collective-permute-done((f32[32,128]{1,0:T(8,128)S(1)}, f32[32,128]{1,0:T(8,128)S(1)}, u32[]{:S(2)}, u32[]{:S(2)}) %collective-permute-start.42) | collective-permute-done | bytes 16416 | tf_op jit(solution)/shard_map/ppermute | solution.py:612
  110.2 5.0 %final.1 = f32[512,128]{1,0:T(8,128)} custom-call(s32[2]{0:T(128)S(1)} %copy-done.4, f32[512,128]{1,0:T(8,128)S(1)} %get-tuple-element.81.refs_1_, f32[192,128]{1,0:T(8,128)S(1)} %get-tuple-element.82.refs_2_, f32[192,128]{1,0:T(8,128)S(1)} %get-tuple-element.83.refs_3_, f32[96,128]{1,0:T(8,128)S(1)} %collective-permute-done.39.refs_4_, ...), custom_call_target="tpu_custom_call" | custom-call | tf_op jit(solution)/shard_map/final/pallas_call | solution.py:683
  (85 shorter events, 6.8 us)
Async XLA Ops:
  2.9 23.1 %copy-start.1 = (f32[512,128]{1,0:T(8,128)S(1)}, f32[512,128]{1,0:T(8,128)}, u32[]{:S(2)}) copy-start(f32[512,128]{1,0:T(8,128)} %get-tuple-element.48.root_h) | copy-start | bytes 786436
  2.9 8.2 %collective-permute-start.3 = (f32[72,128]{1,0:T(8,128)}, f32[72,128]{1,0:T(8,128)S(1)}, u32[]{:S(2)}, u32[]{:S(2)}) collective-permute-start(f32[72,128]{1,0:T(8,128)} %get-tuple-element.46.refs_0_), channel_id=1, source_target_pairs={{0,1},{1,0},{2,3},{3,2},{4,5},{5,4},{6,7},{7,6},{8,9},{9,8},{10,11... | collective-permute-start | bytes 110600 | tf_op jit(solution)/shard_map/ppermute | solution.py:612
  3.5 9.4 %collective-permute-start.2 = (f32[72,128]{1,0:T(8,128)}, f32[72,128]{1,0:T(8,128)S(1)}, u32[]{:S(2)}, u32[]{:S(2)}) collective-permute-start(f32[72,128]{1,0:T(8,128)} %get-tuple-element.46.refs_0_), channel_id=1, source_target_pairs={{0,6},{1,7},{2,4},{3,5},{4,2},{5,3},{6,0},{7,1},{8,14},{9,15},{10,... | collective-permute-start | bytes 110600 | tf_op jit(solution)/shard_map/ppermute | solution.py:612
  8.1 5.1 %collective-permute-start.1 = (f32[72,128]{1,0:T(8,128)}, f32[72,128]{1,0:T(8,128)S(1)}, u32[]{:S(2)}, u32[]{:S(2)}) collective-permute-start(f32[72,128]{1,0:T(8,128)} %get-tuple-element.46.refs_0_), channel_id=1, source_target_pairs={{0,4},{1,5},{2,6},{3,7},{4,0},{5,1},{6,2},{7,3},{8,12},{9,13},{10,... | collective-permute-start | bytes 110600 | tf_op jit(solution)/shard_map/ppermute | solution.py:612
  8.1 5.3 %collective-permute-start = (f32[72,128]{1,0:T(8,128)}, f32[72,128]{1,0:T(8,128)S(1)}, u32[]{:S(2)}, u32[]{:S(2)}) collective-permute-start(f32[72,128]{1,0:T(8,128)} %get-tuple-element.46.refs_0_), channel_id=1, source_target_pairs={{0,2},{1,3},{2,0},{3,1},{4,6},{5,7},{6,4},{7,5},{8,10},{9,11},{10,... | collective-permute-start | bytes 110600 | tf_op jit(solution)/shard_map/ppermute | solution.py:612
  8.8 17.3 %collective-permute-start.7 = (f32[584,128]{1,0:T(8,128)}, f32[584,128]{1,0:T(8,128)S(1)}, u32[]{:S(2)}, u32[]{:S(2)}) collective-permute-start(f32[584,128]{1,0:T(8,128)} %get-tuple-element.50), channel_id=1, source_target_pairs={{0,8},{8,0},{16,24},{24,16},{1,9},{9,1},{17,25},{25,17},{2,10},{10... | collective-permute-start | bytes 897032 | tf_op jit(solution)/shard_map/ppermute | solution.py:612
  11.2 14.9 %collective-permute-start.8 = (f32[584,128]{1,0:T(8,128)}, f32[584,128]{1,0:T(8,128)S(1)}, u32[]{:S(2)}, u32[]{:S(2)}) collective-permute-start(f32[584,128]{1,0:T(8,128)} %get-tuple-element.51), channel_id=1, source_target_pairs={{0,0},{24,24},{8,16},{16,8},{1,1},{25,25},{9,17},{17,9},{2,2},{26,... | collective-permute-start | bytes 897032 | tf_op jit(solution)/shard_map/ppermute | solution.py:612
  12.9 1.3 %collective-permute-start.6 = (f32[72,128]{1,0:T(8,128)S(1)}, f32[72,128]{1,0:T(8,128)S(1)}, u32[]{:S(2)}, u32[]{:S(2)}) collective-permute-start(f32[72,128]{1,0:T(8,128)S(1)} %collective-permute-done.2.refs_3_), channel_id=1, source_target_pairs={{0,1},{1,0},{2,3},{3,2},{4,5},{5,4},{6,7},{7,6},{8,9},{9,8},{10,11... | collective-permute-start | bytes 110600 | tf_op jit(solution)/shard_map/ppermute | solution.py:612
  13.2 1.2 %collective-permute-start.5 = (f32[72,128]{1,0:T(8,128)S(1)}, f32[72,128]{1,0:T(8,128)S(1)}, u32[]{:S(2)}, u32[]{:S(2)}) collective-permute-start(f32[72,128]{1,0:T(8,128)S(1)} %collective-permute-done.1.refs_2_), channel_id=1, source_target_pairs={{0,1},{1,0},{2,3},{3,2},{4,5},{5,4},{6,7},{7,6},{8,9},{9,8},{10,11... | collective-permute-start | bytes 110600 | tf_op jit(solution)/shard_map/ppermute | solution.py:612
  13.4 1.2 %collective-permute-start.4 = (f32[72,128]{1,0:T(8,128)S(1)}, f32[72,128]{1,0:T(8,128)S(1)}, u32[]{:S(2)}, u32[]{:S(2)}) collective-permute-start(f32[72,128]{1,0:T(8,128)S(1)} %collective-permute-done.refs_1_), channel_id=1, source_target_pairs={{0,1},{1,0},{2,3},{3,2},{4,5},{5,4},{6,7},{7,6},{8,9},{9,8},{10,11... | collective-permute-start | bytes 110600 | tf_op jit(solution)/shard_map/ppermute | solution.py:612
  13.7 26.7 %copy-start.4 = (s32[2]{0:T(128)S(1)}, s32[2]{0:T(128)}, u32[]{:S(2)}) copy-start(s32[2]{0:T(128)} %refs_0_.7) | copy-start | bytes 28
  14.7 2.8 %copy-start = (f32[192,64,128]{2,1,0:T(8,128)S(1)}, f32[192,64,128]{2,1,0:T(8,128)}, u32[]{:S(2)}) copy-start(f32[192,64,128]{2,1,0:T(8,128)} %refs_12_.1) | copy-start | bytes 18874372
  17.4 0.8 copy-start.3
  18.2 7.9 %copy-start.2 = (f32[512,128]{1,0:T(8,128)S(1)}, f32[512,128]{1,0:T(8,128)}, u32[]{:S(2)}) copy-start(f32[512,128]{1,0:T(8,128)} %get-tuple-element.49.root_v) | copy-start | bytes 786436
  20.5 10.6 %collective-permute-start.10 = (f32[192,128]{1,0:T(8,128)S(1)}, f32[192,128]{1,0:T(8,128)S(1)}, u32[]{:S(2)}, u32[]{:S(2)}) collective-permute-start(f32[192,128]{1,0:T(8,128)S(1)} %get-tuple-element.47.message), channel_id=1, source_target_pairs={{0,0},{24,24},{8,16},{16,8},{1,1},{25,25},{9,17},{17,9},{2,2},{26,... | collective-permute-start | bytes 294920 | tf_op jit(solution)/shard_map/ppermute | solution.py:612
  21.1 9.9 %collective-permute-start.9 = (f32[192,128]{1,0:T(8,128)S(1)}, f32[192,128]{1,0:T(8,128)S(1)}, u32[]{:S(2)}, u32[]{:S(2)}) collective-permute-start(f32[192,128]{1,0:T(8,128)S(1)} %get-tuple-element.47.message), channel_id=1, source_target_pairs={{0,8},{8,0},{16,24},{24,16},{1,9},{9,1},{17,25},{25,17},{2,10},{10... | collective-permute-start | bytes 294920 | tf_op jit(solution)/shard_map/ppermute | solution.py:612
  26.9 9.1 %collective-permute-start.13 = (f32[456,128]{1,0:T(8,128)}, f32[456,128]{1,0:T(8,128)S(1)}, u32[]{:S(2)}, u32[]{:S(2)}) collective-permute-start(f32[456,128]{1,0:T(8,128)} %get-tuple-element.52), channel_id=1, source_target_pairs={{0,1},{1,0},{2,3},{3,2},{4,5},{5,4},{6,7},{7,6},{8,9},{9,8},{10,11... | collective-permute-start | bytes 700424 | tf_op jit(solution)/shard_map/ppermute | solution.py:612
  26.9 9.8 %collective-permute-start.14 = (f32[456,128]{1,0:T(8,128)S(1)}, f32[456,128]{1,0:T(8,128)S(1)}, u32[]{:S(2)}, u32[]{:S(2)}) collective-permute-start(f32[456,128]{1,0:T(8,128)S(1)} %get-tuple-element.53), channel_id=1, source_target_pairs={{0,7},{1,2},{2,1},{3,4},{4,3},{5,6},{6,5},{7,0},{8,15},{9,10},{10,... | collective-permute-start | bytes 700424 | tf_op jit(solution)/shard_map/ppermute | solution.py:612
  32.2 6.9 %collective-permute-start.11 = (f32[328,128]{1,0:T(8,128)}, f32[328,128]{1,0:T(8,128)S(1)}, u32[]{:S(2)}, u32[]{:S(2)}) collective-permute-start(f32[328,128]{1,0:T(8,128)} %get-tuple-element.58), channel_id=1, source_target_pairs={{0,1},{1,0},{2,3},{3,2},{4,5},{5,4},{6,7},{7,6},{8,9},{9,8},{10,11... | collective-permute-start | bytes 503816 | tf_op jit(solution)/shard_map/ppermute | solution.py:612
  32.2 8.3 %collective-permute-start.12 = (f32[328,128]{1,0:T(8,128)S(1)}, f32[328,128]{1,0:T(8,128)S(1)}, u32[]{:S(2)}, u32[]{:S(2)}) collective-permute-start(f32[328,128]{1,0:T(8,128)S(1)} %get-tuple-element.59), channel_id=1, source_target_pairs={{0,7},{1,2},{2,1},{3,4},{4,3},{5,6},{6,5},{7,0},{8,15},{9,10},{10,... | collective-permute-start | bytes 503816 | tf_op jit(solution)/shard_map/ppermute | solution.py:612
  50.3 6.1 %collective-permute-start.17 = (f32[104,128]{1,0:T(8,128)S(1)}, f32[104,128]{1,0:T(8,128)S(1)}, u32[]{:S(2)}, u32[]{:S(2)}) collective-permute-start(f32[104,128]{1,0:T(8,128)S(1)} %get-tuple-element.65.refs_0_), channel_id=1, source_target_pairs={{0,6},{1,7},{2,4},{3,5},{4,2},{5,3},{6,0},{7,1},{8,14},{9,15},{10,... | collective-permute-start | bytes 159752 | tf_op jit(solution)/shard_map/ppermute | solution.py:612
  50.7 5.8 %collective-permute-start.16 = (f32[104,128]{1,0:T(8,128)S(1)}, f32[104,128]{1,0:T(8,128)S(1)}, u32[]{:S(2)}, u32[]{:S(2)}) collective-permute-start(f32[104,128]{1,0:T(8,128)S(1)} %get-tuple-element.65.refs_0_), channel_id=1, source_target_pairs={{0,4},{1,5},{2,6},{3,7},{4,0},{5,1},{6,2},{7,3},{8,12},{9,13},{10,... | collective-permute-start | bytes 159752 | tf_op jit(solution)/shard_map/ppermute | solution.py:612
  50.7 7.3 %collective-permute-start.15 = (f32[104,128]{1,0:T(8,128)S(1)}, f32[104,128]{1,0:T(8,128)S(1)}, u32[]{:S(2)}, u32[]{:S(2)}) collective-permute-start(f32[104,128]{1,0:T(8,128)S(1)} %get-tuple-element.65.refs_0_), channel_id=1, source_target_pairs={{0,2},{1,3},{2,0},{3,1},{4,6},{5,7},{6,4},{7,5},{8,10},{9,11},{10,... | collective-permute-start | bytes 159752 | tf_op jit(solution)/shard_map/ppermute | solution.py:612
  54.8 3.7 %collective-permute-start.18 = (f32[104,128]{1,0:T(8,128)S(1)}, f32[104,128]{1,0:T(8,128)S(1)}, u32[]{:S(2)}, u32[]{:S(2)}) collective-permute-start(f32[104,128]{1,0:T(8,128)S(1)} %get-tuple-element.65.refs_0_), channel_id=1, source_target_pairs={{0,1},{1,0},{2,3},{3,2},{4,5},{5,4},{6,7},{7,6},{8,9},{9,8},{10,11... | collective-permute-start | bytes 159752 | tf_op jit(solution)/shard_map/ppermute | solution.py:612
  56.4 2.1 %collective-permute-start.21 = (f32[104,128]{1,0:T(8,128)S(1)}, f32[104,128]{1,0:T(8,128)S(1)}, u32[]{:S(2)}, u32[]{:S(2)}) collective-permute-start(f32[104,128]{1,0:T(8,128)S(1)} %collective-permute-done.17.refs_3_), channel_id=1, source_target_pairs={{0,1},{1,0},{2,3},{3,2},{4,5},{5,4},{6,7},{7,6},{8,9},{9,8},{10,11... | collective-permute-start | bytes 159752 | tf_op jit(solution)/shard_map/ppermute | solution.py:612
  56.4 2.1 %collective-permute-start.20 = (f32[104,128]{1,0:T(8,128)S(1)}, f32[104,128]{1,0:T(8,128)S(1)}, u32[]{:S(2)}, u32[]{:S(2)}) collective-permute-start(f32[104,128]{1,0:T(8,128)S(1)} %collective-permute-done.16.refs_2_), channel_id=1, source_target_pairs={{0,1},{1,0},{2,3},{3,2},{4,5},{5,4},{6,7},{7,6},{8,9},{9,8},{10,11... | collective-permute-start | bytes 159752 | tf_op jit(solution)/shard_map/ppermute | solution.py:612
  58.0 1.2 %collective-permute-start.19 = (f32[104,128]{1,0:T(8,128)S(1)}, f32[104,128]{1,0:T(8,128)S(1)}, u32[]{:S(2)}, u32[]{:S(2)}) collective-permute-start(f32[104,128]{1,0:T(8,128)S(1)} %collective-permute-done.15.refs_1_), channel_id=1, source_target_pairs={{0,1},{1,0},{2,3},{3,2},{4,5},{5,4},{6,7},{7,6},{8,9},{9,8},{10,11... | collective-permute-start | bytes 159752 | tf_op jit(solution)/shard_map/ppermute | solution.py:612
  61.6 6.8 %collective-permute-start.24 = (f32[208,128]{1,0:T(8,128)S(1)}, f32[208,128]{1,0:T(8,128)S(1)}, u32[]{:S(2)}, u32[]{:S(2)}) collective-permute-start(f32[208,128]{1,0:T(8,128)S(1)} %adjoint_next.2.message), channel_id=1, source_target_pairs={{0,24},{8,16},{16,8},{24,0},{1,25},{9,17},{17,9},{25,1},{2,26},{10... | collective-permute-start | bytes 319496 | tf_op jit(solution)/shard_map/ppermute | solution.py:612
  64.1 5.1 %collective-permute-start.23 = (f32[208,128]{1,0:T(8,128)S(1)}, f32[208,128]{1,0:T(8,128)S(1)}, u32[]{:S(2)}, u32[]{:S(2)}) collective-permute-start(f32[208,128]{1,0:T(8,128)S(1)} %adjoint_next.2.message), channel_id=1, source_target_pairs={{0,8},{8,0},{16,24},{24,16},{1,9},{9,1},{17,25},{25,17},{2,10},{10... | collective-permute-start | bytes 319496 | tf_op jit(solution)/shard_map/ppermute | solution.py:612
  64.1 7.9 %collective-permute-start.22 = (f32[16,128]{1,0:T(8,128)S(1)}, f32[16,128]{1,0:T(8,128)S(1)}, u32[]{:S(2)}, u32[]{:S(2)}) collective-permute-start(f32[16,128]{1,0:T(8,128)S(1)} %slice.81), channel_id=1, source_target_pairs={{0,16},{8,24},{16,0},{24,8},{1,17},{9,25},{17,1},{25,9},{2,18},{10... | collective-permute-start | bytes 24584 | tf_op jit(solution)/shard_map/ppermute | solution.py:612
  65.4 6.5 %collective-permute-start.25 = (f32[192,128]{1,0:T(8,128)S(1)}, f32[192,128]{1,0:T(8,128)S(1)}, u32[]{:S(2)}, u32[]{:S(2)}) collective-permute-start(f32[192,128]{1,0:T(8,128)S(1)} %get-tuple-element.71), channel_id=1, source_target_pairs={{0,1},{1,0},{2,3},{3,2},{4,5},{5,4},{6,7},{7,6},{8,9},{9,8},{10,11... | collective-permute-start | bytes 294920 | tf_op jit(solution)/shard_map/ppermute | solution.py:612
  65.5 6.5 %collective-permute-start.26 = (f32[192,128]{1,0:T(8,128)S(1)}, f32[192,128]{1,0:T(8,128)S(1)}, u32[]{:S(2)}, u32[]{:S(2)}) collective-permute-start(f32[192,128]{1,0:T(8,128)S(1)} %get-tuple-element.72), channel_id=1, source_target_pairs={{0,7},{1,2},{2,1},{3,4},{4,3},{5,6},{6,5},{7,0},{8,15},{9,10},{10,... | collective-permute-start | bytes 294920 | tf_op jit(solution)/shard_map/ppermute | solution.py:612
  69.6 2.4 %collective-permute-start.27 = (f32[136,128]{1,0:T(8,128)S(1)}, f32[136,128]{1,0:T(8,128)S(1)}, u32[]{:S(2)}, u32[]{:S(2)}) collective-permute-start(f32[136,128]{1,0:T(8,128)S(1)} %get-tuple-element.73), channel_id=1, source_target_pairs={{0,1},{1,0},{2,3},{3,2},{4,5},{5,4},{6,7},{7,6},{8,9},{9,8},{10,11... | collective-permute-start | bytes 208904 | tf_op jit(solution)/shard_map/ppermute | solution.py:612
  69.7 5.7 %collective-permute-start.28 = (f32[136,128]{1,0:T(8,128)S(1)}, f32[136,128]{1,0:T(8,128)S(1)}, u32[]{:S(2)}, u32[]{:S(2)}) collective-permute-start(f32[136,128]{1,0:T(8,128)S(1)} %get-tuple-element.74), channel_id=1, source_target_pairs={{0,7},{1,2},{2,1},{3,4},{4,3},{5,6},{6,5},{7,0},{8,15},{9,10},{10,... | collective-permute-start | bytes 208904 | tf_op jit(solution)/shard_map/ppermute | solution.py:612
  85.7 6.1 %collective-permute-start.31 = (f32[104,128]{1,0:T(8,128)S(1)}, f32[104,128]{1,0:T(8,128)S(1)}, u32[]{:S(2)}, u32[]{:S(2)}) collective-permute-start(f32[104,128]{1,0:T(8,128)S(1)} %get-tuple-element.77.refs_0_), channel_id=1, source_target_pairs={{0,6},{1,7},{2,4},{3,5},{4,2},{5,3},{6,0},{7,1},{8,14},{9,15},{10,... | collective-permute-start | bytes 159752 | tf_op jit(solution)/shard_map/ppermute | solution.py:612
  86.1 5.7 %collective-permute-start.30 = (f32[104,128]{1,0:T(8,128)S(1)}, f32[104,128]{1,0:T(8,128)S(1)}, u32[]{:S(2)}, u32[]{:S(2)}) collective-permute-start(f32[104,128]{1,0:T(8,128)S(1)} %get-tuple-element.77.refs_0_), channel_id=1, source_target_pairs={{0,4},{1,5},{2,6},{3,7},{4,0},{5,1},{6,2},{7,3},{8,12},{9,13},{10,... | collective-permute-start | bytes 159752 | tf_op jit(solution)/shard_map/ppermute | solution.py:612
  86.6 6.8 %collective-permute-start.29 = (f32[104,128]{1,0:T(8,128)S(1)}, f32[104,128]{1,0:T(8,128)S(1)}, u32[]{:S(2)}, u32[]{:S(2)}) collective-permute-start(f32[104,128]{1,0:T(8,128)S(1)} %get-tuple-element.77.refs_0_), channel_id=1, source_target_pairs={{0,2},{1,3},{2,0},{3,1},{4,6},{5,7},{6,4},{7,5},{8,10},{9,11},{10,... | collective-permute-start | bytes 159752 | tf_op jit(solution)/shard_map/ppermute | solution.py:612
  90.1 3.3 %collective-permute-start.32 = (f32[104,128]{1,0:T(8,128)S(1)}, f32[104,128]{1,0:T(8,128)S(1)}, u32[]{:S(2)}, u32[]{:S(2)}) collective-permute-start(f32[104,128]{1,0:T(8,128)S(1)} %get-tuple-element.77.refs_0_), channel_id=1, source_target_pairs={{0,1},{1,0},{2,3},{3,2},{4,5},{5,4},{6,7},{7,6},{8,9},{9,8},{10,11... | collective-permute-start | bytes 159752 | tf_op jit(solution)/shard_map/ppermute | solution.py:612
  91.8 1.6 %collective-permute-start.35 = (f32[104,128]{1,0:T(8,128)S(1)}, f32[104,128]{1,0:T(8,128)S(1)}, u32[]{:S(2)}, u32[]{:S(2)}) collective-permute-start(f32[104,128]{1,0:T(8,128)S(1)} %collective-permute-done.31.refs_3_), channel_id=1, source_target_pairs={{0,1},{1,0},{2,3},{3,2},{4,5},{5,4},{6,7},{7,6},{8,9},{9,8},{10,11... | collective-permute-start | bytes 159752 | tf_op jit(solution)/shard_map/ppermute | solution.py:612
  91.8 1.8 %collective-permute-start.34 = (f32[104,128]{1,0:T(8,128)S(1)}, f32[104,128]{1,0:T(8,128)S(1)}, u32[]{:S(2)}, u32[]{:S(2)}) collective-permute-start(f32[104,128]{1,0:T(8,128)S(1)} %collective-permute-done.30.refs_2_), channel_id=1, source_target_pairs={{0,1},{1,0},{2,3},{3,2},{4,5},{5,4},{6,7},{7,6},{8,9},{9,8},{10,11... | collective-permute-start | bytes 159752 | tf_op jit(solution)/shard_map/ppermute | solution.py:612
  93.4 1.2 %collective-permute-start.33 = (f32[104,128]{1,0:T(8,128)S(1)}, f32[104,128]{1,0:T(8,128)S(1)}, u32[]{:S(2)}, u32[]{:S(2)}) collective-permute-start(f32[104,128]{1,0:T(8,128)S(1)} %collective-permute-done.29.refs_1_), channel_id=1, source_target_pairs={{0,1},{1,0},{2,3},{3,2},{4,5},{5,4},{6,7},{7,6},{8,9},{9,8},{10,11... | collective-permute-start | bytes 159752 | tf_op jit(solution)/shard_map/ppermute | solution.py:612
  97.0 6.5 %collective-permute-start.38 = (f32[208,128]{1,0:T(8,128)S(1)}, f32[208,128]{1,0:T(8,128)S(1)}, u32[]{:S(2)}, u32[]{:S(2)}) collective-permute-start(f32[208,128]{1,0:T(8,128)S(1)} %adjoint_next.3.message), channel_id=1, source_target_pairs={{0,24},{8,16},{16,8},{24,0},{1,25},{9,17},{17,9},{25,1},{2,26},{10... | collective-permute-start | bytes 319496 | tf_op jit(solution)/shard_map/ppermute | solution.py:612
  98.6 6.2 %collective-permute-start.37 = (f32[208,128]{1,0:T(8,128)S(1)}, f32[208,128]{1,0:T(8,128)S(1)}, u32[]{:S(2)}, u32[]{:S(2)}) collective-permute-start(f32[208,128]{1,0:T(8,128)S(1)} %adjoint_next.3.message), channel_id=1, source_target_pairs={{0,8},{8,0},{16,24},{24,16},{1,9},{9,1},{17,25},{25,17},{2,10},{10... | collective-permute-start | bytes 319496 | tf_op jit(solution)/shard_map/ppermute | solution.py:612
  99.5 7.8 %collective-permute-start.36 = (f32[16,128]{1,0:T(8,128)S(1)}, f32[16,128]{1,0:T(8,128)S(1)}, u32[]{:S(2)}, u32[]{:S(2)}) collective-permute-start(f32[16,128]{1,0:T(8,128)S(1)} %slice.84), channel_id=1, source_target_pairs={{0,16},{8,24},{16,0},{24,8},{1,17},{9,25},{17,1},{25,9},{2,18},{10... | collective-permute-start | bytes 24584 | tf_op jit(solution)/shard_map/ppermute | solution.py:612
  100.9 7.6 %collective-permute-start.39 = (f32[96,128]{1,0:T(8,128)S(1)}, f32[96,128]{1,0:T(8,128)S(1)}, u32[]{:S(2)}, u32[]{:S(2)}) collective-permute-start(f32[96,128]{1,0:T(8,128)S(1)} %get-tuple-element.84), channel_id=1, source_target_pairs={{0,1},{1,0},{2,3},{3,2},{4,5},{5,4},{6,7},{7,6},{8,9},{9,8},{10,11... | collective-permute-start | bytes 147464 | tf_op jit(solution)/shard_map/ppermute | solution.py:612
  100.9 7.5 %collective-permute-start.40 = (f32[96,128]{1,0:T(8,128)S(1)}, f32[96,128]{1,0:T(8,128)S(1)}, u32[]{:S(2)}, u32[]{:S(2)}) collective-permute-start(f32[96,128]{1,0:T(8,128)S(1)} %get-tuple-element.85), channel_id=1, source_target_pairs={{0,7},{1,2},{2,1},{3,4},{4,3},{5,6},{6,5},{7,0},{8,15},{9,10},{10,... | collective-permute-start | bytes 147464 | tf_op jit(solution)/shard_map/ppermute | solution.py:612
  105.1 3.3 %collective-permute-start.41 = (f32[32,128]{1,0:T(8,128)S(1)}, f32[32,128]{1,0:T(8,128)S(1)}, u32[]{:S(2)}, u32[]{:S(2)}) collective-permute-start(f32[32,128]{1,0:T(8,128)S(1)} %get-tuple-element.86), channel_id=1, source_target_pairs={{0,1},{1,0},{2,3},{3,2},{4,5},{5,4},{6,7},{7,6},{8,9},{9,8},{10,11... | collective-permute-start | bytes 49160 | tf_op jit(solution)/shard_map/ppermute | solution.py:612
  105.2 5.0 %collective-permute-start.42 = (f32[32,128]{1,0:T(8,128)S(1)}, f32[32,128]{1,0:T(8,128)S(1)}, u32[]{:S(2)}, u32[]{:S(2)}) collective-permute-start(f32[32,128]{1,0:T(8,128)S(1)} %get-tuple-element.87), channel_id=1, source_target_pairs={{0,7},{1,2},{2,1},{3,4},{4,3},{5,6},{6,5},{7,0},{8,15},{9,10},{10,... | collective-permute-start | bytes 49160 | tf_op jit(solution)/shard_map/ppermute | solution.py:612

commit v5 on v4

--- a/solution.py
+++ b/solution.py
@@ -10,6 +10,7 @@
 LANES = 128
 VMEM_LIMIT = 40 * 1024 * 1024
 NEAR_LIMIT = 32 * 1024 * 1024
+FIRST_LIMIT = 48 * 1024 * 1024
 START_LIMIT = 60 * 1024 * 1024
 REACH = 6
 FRAME = 2 * REACH
@@ -297,7 +298,7 @@
 
 def faces_kernel(dims, root_h, root_v, from_a, from_b, from_x, from_s, *refs):
     lat_cells, lon_cells = dims
-    out, (face_lat, face_lon, keep, up, down, natural, buf, sems) = refs[:5], refs[5:]
+    face_lat, face_lon, keep, up, down, natural, buf = refs
     rows = lat_cells + 2 * FRAME
     width = buf.shape[1]
     places = face_places(lat_cells)
@@ -329,7 +330,6 @@
         return c
 
     lax.fori_loop(0, rows // 4, lateral, 0)
-    side = copies([(face_lat, out[0]), (face_lon, out[1])], sems)
     skip = FRAME * lon_cells
     place_halos(
         natural, root_v, ((from_a, skip), (from_b, skip)),
@@ -350,9 +350,6 @@
         return c
 
     lax.fori_loop(0, (lat_cells + 2 * REACH) // 4, vertical, 0)
-    level = copies([(keep, out[2]), (up, out[3]), (down, out[4])], sems.at[pl.ds(2, 3)])
-    for copy in side + level:
-        copy.wait()
 
 
 def observe(cells, jac, field, out):
@@ -469,36 +466,31 @@
     if not first_call:
         scal, refs = refs[0], refs[1:]
     if first_call:
-        faces_hbm, jac_hbm, refs = refs[:5], refs[5], refs[6:]
+        faces, jac_hbm, refs = refs[:5], refs[5], refs[6:]
         one_hbm, two_hbm, message, jac = refs[:4]
         refs = refs[4:]
     else:
-        jac, faces_hbm, grad_hbm, spread_hbm = refs[0], refs[1:6], refs[6], refs[7]
+        jac, faces, grad_hbm, spread_hbm = refs[0], refs[1:6], refs[6], refs[7]
         one_hbm, two_hbm, message = refs[8:11]
         refs = refs[11:]
-    face_lat, face_lon, keep, up, down, one, two, grad, natural, buf, mid, sems = refs
-    loads = copies(list(zip(faces_hbm[:2], (face_lat, face_lon))), sems)
+    face_lat, face_lon, keep, up, down = faces
+    one, two, grad, natural, buf, mid, sems = refs
+    if first_call:
+        loads = copies([(jac_hbm, jac)], sems)
+    else:
+        loads = copies([(grad_hbm, grad), (spread_hbm, two)], sems)
     nh, nv = counts[0], counts[1]
     rows = lat_cells + 2 * FRAME
     place_halos(
         natural, own, ((from_a, 0), (from_b, 0)), sides, FRAME, dims
     )
     to_strided(natural, buf, range(rows))
-    for load in loads:
-        load.wait()
-    loads = copies(
-        list(zip(faces_hbm[2:], (keep, up, down))) + ([(jac_hbm, jac)] if first_call else []),
-        sems.at[pl.ds(2, 4)])
-    if not first_call:
-        old_loads = copies([(grad_hbm, grad), (spread_hbm, two)], sems.at[pl.ds(6, 2)])
     lateral_passes(buf, face_lat, face_lon, nh, 0, nh)
     border = FRAME - REACH
     tall = lat_cells + 2 * REACH
     vertical = functools.partial(
         vertical_passes, buf, keep, up, down, border, border + tall, border, nv
     )
-    for load in loads[:3]:
-        load.wait()
     vertical()
 
     block = range(FRAME, FRAME + lat_cells)
@@ -510,7 +502,7 @@
     if not first_call:
         rr = jnp.sum(scal[0:8])
         alpha = rr / (rr + jnp.sum(scal[8:16]))
-        for load in old_loads:
+        for load in loads:
             load.wait()
 
     def finish(i, acc):
@@ -533,9 +525,9 @@
         return acc
 
     norm = lax.fori_loop(0, lat_cells, finish, jnp.zeros((8, LANES), jnp.float32))
-    stores = copies([(one, one_hbm), (two, two_hbm)], sems.at[pl.ds(8, 2)])
-    for load in loads[3:]:
-        load.wait()
+    stores = copies([(one, one_hbm), (two, two_hbm)], sems.at[pl.ds(2, 2)])
+    if first_call:
+        loads[0].wait()
     obs = jac.shape[1]
     observe(cells, jac, two, message)
     message[obs + obs // 2:] = norm
@@ -560,24 +552,14 @@
 def final_kernel(dims, *refs):
     lat_cells, lon_cells = dims
     counts, own, from_a, from_b, own_x, own_s, corner_x, corner_s, base, alpha = refs[:10]
-    hbm, residual, refs = refs[10:15], refs[15], refs[16:]
-    face_lat, face_lon, keep, up, down, natural, buf, sems = refs
-    inner = pl.ds(FRAME - REACH, lat_cells + 2 * REACH)
-    block = pl.ds(REACH, lat_cells)
-    loads = copies(
-        [(src.at[inner], dst.at[inner]) for src, dst in zip(hbm[:2], refs[:2])]
-        + [(src.at[block], dst.at[block]) for src, dst in zip(hbm[2:5], refs[2:5])], sems)
+    face_lat, face_lon, keep, up, down, residual, natural, buf = refs[10:]
     nh, nv = counts[0], counts[1]
     place_halos(
         natural, own, ((from_a, 0), (from_b, 0)),
         (((own_x, 0), (corner_x, 0)), ((own_s, 0), (corner_s, 0))), REACH, dims,
     )
     to_strided(natural, buf, range(FRAME - REACH, FRAME + lat_cells + REACH))
-    for load in loads[:2]:
-        load.wait()
     lateral_passes(buf, face_lat, face_lon, nh, nh, 2 * nh)
-    for load in loads[2:]:
-        load.wait()
     vertical_passes(
         buf, keep, up, down, FRAME, FRAME + lat_cells, FRAME - REACH, nv
     )
@@ -727,15 +709,15 @@
     halos = (own, *strips, *sides)
     faces = call(
         functools.partial(faces_kernel, dims), "faces", (wide, wide, tall, tall, tall),
-        (root_h, root_v, *k_strips, *k_sides), far_out=5,
-        scratches=faces_vmem + [wide_vmem, scratch(rows_h + 1, width, levels), sems(5)])
-    spread_scratch = faces_vmem + [field_vmem] * 3 + [
-        wide_vmem, wide_vmem, scratch(lat_cells, width, levels), sems(10)]
+        (root_h, root_v, *k_strips, *k_sides),
+        scratches=[wide_vmem, scratch(rows_h + 1, width, levels)])
+    spread_scratch = [field_vmem] * 3 + [
+        wide_vmem, wide_vmem, scratch(lat_cells, width, levels), sems(4)]
     near_params = pltpu.CompilerParams(vmem_limit_bytes=NEAR_LIMIT)
     grad, spread, message, near_jac = call(
         functools.partial(spread_kernel, dims, True), "spread_first",
         (field, field, msg, shape(*jacobian.shape)),
-        (pass_counts, cells_flat, *halos), 2, (*faces, jacobian), 2, spread_scratch)
+        (pass_counts, cells_flat, *halos, *faces), 2, (jacobian,), 2, spread_scratch)
 
     def adjoint(message):
         return call(
@@ -746,7 +728,7 @@
     halos, scal0 = halo(adjoint(message), FRAME)
     image, spread_next, message = call(
         functools.partial(spread_kernel, dims, False), "spread_next", (field, field, msg),
-        (pass_counts, cells_flat, *halos, scal0, near_jac), 2, (*faces, grad, spread), 2, spread_scratch,
+        (pass_counts, cells_flat, *halos, scal0, near_jac, *faces), 2, (grad, spread), 2, spread_scratch,
         near_params)
     halos, scal1 = halo(adjoint(message), REACH)
     increment, base, step = call(
@@ -754,8 +736,7 @@
         (scal0, scal1, grad, spread, image, spread_next))
     residual = call(
         functools.partial(final_kernel, dims), "final", field,
-        (pass_counts, *halos, base, step), 1, faces, 0,
-        faces_vmem + [wide_vmem, wide_vmem, sems(5)])
+        (pass_counts, *halos, base, step, *faces), 1, scratches=[wide_vmem, wide_vmem], params=near_params)
     block = (lat_cells, lon_cells, levels)
     return increment.reshape(block), residual.reshape(block)
 

time: 115 us -> 113 us (0.983)
  Pallas kernels: 41.4 us -> 37.9 us
    pallas_call x16, Pallas kernels: 41.4 us -> 37.9 us  [call(): pl.pallas_call(kernel, out_shape=outs, in_specs=specs, out_specs=out_spec...]
where the time goes in v5:
time: 113 us
  starting transfers between devices  49.9 us (44%)
  Pallas kernels  37.9 us (34%)
  waiting for transfers between devices  18.6 us (16%)
  local copies, waits for them, and re-layouts  3.63 us (3%)
  other arithmetic  1.39 us (1%)
    ppermute x43, starting transfers between devices, send(): return lax.ppermute(x, axis, pairs)  49.9 us
    pallas_call x16, Pallas kernels, call(): pl.pallas_call(kernel, out_shape=outs, in_specs=specs, out_specs=out_spec...  37.9 us
    ppermute x43, waiting for transfers between devices, send(): return lax.ppermute(x, axis, pairs)  18.6 us
    unnamed x10, local copies, waits for them, and re-layouts  3.57 us
  transfers between devices with their start and end apart: 43, of which 19 were waited for; matrix products, arithmetic and copies ran while one was open for 1% of the time, Pallas kernels for 8%

profile of v5, /device:TPU:0, one launch (start us, length us, event | category | flops | bytes accessed | tf_op | source)
XLA Modules:
  0.0 112.5 jit_solution(12050532755579603801)
XLA Ops:
  0.6 2.3 %start.1 = (f32[72,128]{1,0:T(8,128)}, f32[512,128]{1,0:T(8,128)}, f32[512,128]{1,0:T(8,128)}, f32[584,128]{1,0:T(8,128)}, f32[584,128]{1,0:T(8,128)}) custom-call(f32[64,64]{1,0:T(8,128)} %refs_0_.4, f32[64,64]{1,0:T(8,128)} %refs_1_.1, s32[2,192]{1,0:T(2,128)} %refs_2_.1, f32[512,128]{1,0:T(8,128)} %bitcast.16, f32[512,128]{1,0:T(8,128)} %bitcast.17), custom_call_target="tpu_custom_call" | custom-call | tf_op jit(solution)/shard_map/start/pallas_call | solution.py:665
  3.5 4.7 %collective-permute-start.2 = (f32[72,128]{1,0:T(8,128)}, f32[72,128]{1,0:T(8,128)S(1)}, u32[]{:S(2)}, u32[]{:S(2)}) collective-permute-start(f32[72,128]{1,0:T(8,128)} %get-tuple-element.46.refs_0_), channel_id=1, source_target_pairs={{0,6},{1,7},{2,4},{3,5},{4,2},{5,3},{6,0},{7,1},{8,14},{9,15},{10,... | collective-permute-start | bytes 110600 | tf_op jit(solution)/shard_map/ppermute | solution.py:594
  8.1 0.7 collective-permute-start
  8.8 1.6 %collective-permute-start.7 = (f32[584,128]{1,0:T(8,128)}, f32[584,128]{1,0:T(8,128)S(1)}, u32[]{:S(2)}, u32[]{:S(2)}) collective-permute-start(f32[584,128]{1,0:T(8,128)} %get-tuple-element.50), channel_id=1, source_target_pairs={{0,8},{8,0},{16,24},{24,16},{1,9},{9,1},{17,25},{25,17},{2,10},{10... | collective-permute-start | bytes 897032 | tf_op jit(solution)/shard_map/ppermute | solution.py:594
  10.4 0.8 fusion.20
  11.2 1.6 %collective-permute-start.8 = (f32[584,128]{1,0:T(8,128)}, f32[584,128]{1,0:T(8,128)S(1)}, u32[]{:S(2)}, u32[]{:S(2)}) collective-permute-start(f32[584,128]{1,0:T(8,128)} %get-tuple-element.51), channel_id=1, source_target_pairs={{0,0},{24,24},{8,16},{16,8},{1,1},{25,25},{9,17},{17,9},{2,2},{26,... | collective-permute-start | bytes 897032 | tf_op jit(solution)/shard_map/ppermute | solution.py:594
  14.7 2.8 %copy-done = f32[192,64,128]{2,1,0:T(8,128)S(1)} copy-done((f32[192,64,128]{2,1,0:T(8,128)S(1)}, f32[192,64,128]{2,1,0:T(8,128)}, u32[]{:S(2)}) %copy-start) | copy-done | bytes 6291480
  17.4 0.8 copy-done.3
  18.2 2.2 %adjoint_first.1 = (f32[192,128]{1,0:T(8,128)S(1)}, f32[64,512]{1,0:T(8,128)S(1)}) custom-call(f32[72,128]{1,0:T(8,128)S(1)} %copy-done.3, f32[72,128]{1,0:T(8,128)S(1)} %collective-permute-done.refs_1_, f32[72,128]{1,0:T(8,128)S(1)} %collective-permute-done.1.refs_2_, f32[72,128]{1,0:T(8,128)S(1)} %collective-permute-done.2.refs_3_, ...), custom_call_target="tpu_custom_call" | custom-call | tf_op jit(solution)/shard_map/adjoint_first/pallas_call | solution.py:665
  20.5 0.7 collective-permute-start.10
  21.1 4.9 %collective-permute-start.9 = (f32[192,128]{1,0:T(8,128)S(1)}, f32[192,128]{1,0:T(8,128)S(1)}, u32[]{:S(2)}, u32[]{:S(2)}) collective-permute-start(f32[192,128]{1,0:T(8,128)S(1)} %get-tuple-element.47.message), channel_id=1, source_target_pairs={{0,8},{8,0},{16,24},{24,16},{1,9},{9,1},{17,25},{25,17},{2,10},{10... | collective-permute-start | bytes 294920 | tf_op jit(solution)/shard_map/ppermute | solution.py:594
  26.1 0.8 face_sides.1
  26.9 3.8 %collective-permute-start.14 = (f32[456,128]{1,0:T(8,128)S(1)}, f32[456,128]{1,0:T(8,128)S(1)}, u32[]{:S(2)}, u32[]{:S(2)}) collective-permute-start(f32[456,128]{1,0:T(8,128)S(1)} %get-tuple-element.53), channel_id=1, source_target_pairs={{0,7},{1,2},{2,1},{3,4},{4,3},{5,6},{6,5},{7,0},{8,15},{9,10},{10,... | collective-permute-start | bytes 700424 | tf_op jit(solution)/shard_map/ppermute | solution.py:594
  31.1 1.1 sides.3
  32.2 3.7 %collective-permute-start.12 = (f32[328,128]{1,0:T(8,128)S(1)}, f32[328,128]{1,0:T(8,128)S(1)}, u32[]{:S(2)}, u32[]{:S(2)}) collective-permute-start(f32[328,128]{1,0:T(8,128)S(1)} %get-tuple-element.59), channel_id=1, source_target_pairs={{0,7},{1,2},{2,1},{3,4},{4,3},{5,6},{6,5},{7,0},{8,15},{9,10},{10,... | collective-permute-start | bytes 503816 | tf_op jit(solution)/shard_map/ppermute | solution.py:594
  36.0 0.7 collective-permute-done.14.from_s
  36.7 1.7 %faces.1 = (f32[40,56,128]{2,1,0:T(8,128)S(1)}, f32[40,56,128]{2,1,0:T(8,128)S(1)}, f32[28,56,128]{2,1,0:T(8,128)S(1)}, f32[28,56,128]{2,1,0:T(8,128)S(1)}, f32[28,56,128]{2,1,0:T(8,128)S(1)}) custom-call(f32[512,128]{1,0:T(8,128)S(1)} %copy-done.1, f32[512,128]{1,0:T(8,128)S(1)} %copy-done.2, f32[584,128]{1,0:T(8,128)S(1)} %collective-permute-done.7.from_a, ...), custom_call_target="tpu_custom_call" | custom-call | tf_op jit(solution)/shard_map/faces/pallas_call | solution.py:665
  38.4 2.0 %collective-permute-done.12.refs_6_ = f32[328,128]{1,0:T(8,128)S(1)} collective-permute-done((f32[328,128]{1,0:T(8,128)S(1)}, f32[328,128]{1,0:T(8,128)S(1)}, u32[]{:S(2)}, u32[]{:S(2)}) %collective-permute-start.12) | collective-permute-done | bytes 167968 | tf_op jit(solution)/shard_map/ppermute | solution.py:594
  40.4 9.1 %spread_first.1 = (f32[512,128]{1,0:T(8,128)S(1)}, f32[512,128]{1,0:T(8,128)S(1)}, f32[104,128]{1,0:T(8,128)S(1)}, f32[192,64,128]{2,1,0:T(8,128)S(1)}) custom-call(s32[2]{0:T(128)S(1)} %copy-done.4, s32[192]{0:T(256)S(1)} %bitcast.14, f32[512,128]{1,0:T(8,128)S(1)} %scatter.3.refs_0_.refs_2_, f32[384,128]{1,0:T(8,128)S(1)} %get-tuple-element.56.refs_3_, ...), custom_call_target="tpu_custom_call" | custom-call | tf_op jit(solution)/shard_map/spread_first/pallas_call | solution.py:665
  49.8 4.2 %collective-permute-start.15 = (f32[104,128]{1,0:T(8,128)S(1)}, f32[104,128]{1,0:T(8,128)S(1)}, u32[]{:S(2)}, u32[]{:S(2)}) collective-permute-start(f32[104,128]{1,0:T(8,128)S(1)} %get-tuple-element.65.refs_0_), channel_id=1, source_target_pairs={{0,2},{1,3},{2,0},{3,1},{4,6},{5,7},{6,4},{7,5},{8,10},{9,11},{10,... | collective-permute-start | bytes 159752 | tf_op jit(solution)/shard_map/ppermute | solution.py:594
  54.1 1.5 %collective-permute-done.17.refs_3_ = f32[104,128]{1,0:T(8,128)S(1)} collective-permute-done((f32[104,128]{1,0:T(8,128)S(1)}, f32[104,128]{1,0:T(8,128)S(1)}, u32[]{:S(2)}, u32[]{:S(2)}) %collective-permute-start.17) | collective-permute-done | bytes 53280 | tf_op jit(solution)/shard_map/ppermute | solution.py:594
  55.6 0.9 collective-permute-start.20
  56.5 0.6 collective-permute-done.15.refs_1_
  57.7 0.7 collective-permute-done.19.refs_5_
  58.4 2.3 %adjoint_next.2.message = f32[208,128]{1,0:T(8,128)S(1)} custom-call(f32[104,128]{1,0:T(8,128)S(1)} %get-tuple-element.65.refs_0_, f32[104,128]{1,0:T(8,128)S(1)} %collective-permute-done.15.refs_1_, f32[104,128]{1,0:T(8,128)S(1)} %collective-permute-done.16.refs_2_, f32[104,128]{1,0:T(8,128)S(1)} %collective-permute-done.17.refs_3_, ...), custom_call_target="tpu_custom_call" | custom-call | tf_op jit(solution)/shard_map/adjoint_next/pallas_call | solution.py:665
  60.7 2.6 %collective-permute-start.24 = (f32[208,128]{1,0:T(8,128)S(1)}, f32[208,128]{1,0:T(8,128)S(1)}, u32[]{:S(2)}, u32[]{:S(2)}) collective-permute-start(f32[208,128]{1,0:T(8,128)S(1)} %adjoint_next.2.message), channel_id=1, source_target_pairs={{0,24},{8,16},{16,8},{24,0},{1,25},{9,17},{17,9},{25,1},{2,26},{10... | collective-permute-start | bytes 319496 | tf_op jit(solution)/shard_map/ppermute | solution.py:594
  63.3 1.0 collective-permute-start.22
  64.7 2.1 %collective-permute-start.26 = (f32[192,128]{1,0:T(8,128)S(1)}, f32[192,128]{1,0:T(8,128)S(1)}, u32[]{:S(2)}, u32[]{:S(2)}) collective-permute-start(f32[192,128]{1,0:T(8,128)S(1)} %get-tuple-element.72), channel_id=1, source_target_pairs={{0,7},{1,2},{2,1},{3,4},{4,3},{5,6},{6,5},{7,0},{8,15},{9,10},{10,... | collective-permute-start | bytes 294920 | tf_op jit(solution)/shard_map/ppermute | solution.py:594
  66.8 0.7 collective-permute-done.24.refs_1_
  67.5 0.9 collective-permute-done.23.refs_0_
  68.8 2.3 %collective-permute-start.28 = (f32[136,128]{1,0:T(8,128)S(1)}, f32[136,128]{1,0:T(8,128)S(1)}, u32[]{:S(2)}, u32[]{:S(2)}) collective-permute-start(f32[136,128]{1,0:T(8,128)S(1)} %get-tuple-element.74), channel_id=1, source_target_pairs={{0,7},{1,2},{2,1},{3,4},{4,3},{5,6},{6,5},{7,0},{8,15},{9,10},{10,... | collective-permute-start | bytes 208904 | tf_op jit(solution)/shard_map/ppermute | solution.py:594
  71.1 3.4 %collective-permute-done.28.refs_8_ = f32[136,128]{1,0:T(8,128)S(1)} collective-permute-done((f32[136,128]{1,0:T(8,128)S(1)}, f32[136,128]{1,0:T(8,128)S(1)}, u32[]{:S(2)}, u32[]{:S(2)}) %collective-permute-start.28) | collective-permute-done | bytes 69664 | tf_op jit(solution)/shard_map/ppermute | solution.py:594
  74.6 9.5 %spread_next.1 = (f32[512,128]{1,0:T(8,128)S(1)}, f32[512,128]{1,0:T(8,128)S(1)}, f32[104,128]{1,0:T(8,128)S(1)}) custom-call(s32[2]{0:T(128)S(1)} %copy-done.4, s32[192]{0:T(256)S(1)} %bitcast.15, f32[512,128]{1,0:T(8,128)S(1)} %get-tuple-element.68.refs_2_, f32[384,128]{1,0:T(8,128)S(1)} %get-tuple-element.69.refs_3_, ...), custom_call_target="tpu_custom_call" | custom-call | tf_op jit(solution)/shard_map/spread_next/pallas_call | solution.py:665
  85.0 3.6 %collective-permute-start.29 = (f32[104,128]{1,0:T(8,128)S(1)}, f32[104,128]{1,0:T(8,128)S(1)}, u32[]{:S(2)}, u32[]{:S(2)}) collective-permute-start(f32[104,128]{1,0:T(8,128)S(1)} %get-tuple-element.77.refs_0_), channel_id=1, source_target_pairs={{0,2},{1,3},{2,0},{3,1},{4,6},{5,7},{6,4},{7,5},{8,10},{9,11},{10,... | collective-permute-start | bytes 159752 | tf_op jit(solution)/shard_map/ppermute | solution.py:594
  88.5 1.6 %collective-permute-done.31.refs_3_ = f32[104,128]{1,0:T(8,128)S(1)} collective-permute-done((f32[104,128]{1,0:T(8,128)S(1)}, f32[104,128]{1,0:T(8,128)S(1)}, u32[]{:S(2)}, u32[]{:S(2)}) %collective-permute-start.31) | collective-permute-done | bytes 53280 | tf_op jit(solution)/shard_map/ppermute | solution.py:594
  90.1 0.9 collective-permute-start.34
  91.1 0.6 collective-permute-done.29.refs_1_
  92.0 1.0 collective-permute-done.33.refs_5_
  92.9 2.3 %adjoint_next.3.message = f32[208,128]{1,0:T(8,128)S(1)} custom-call(f32[104,128]{1,0:T(8,128)S(1)} %get-tuple-element.77.refs_0_, f32[104,128]{1,0:T(8,128)S(1)} %collective-permute-done.29.refs_1_, f32[104,128]{1,0:T(8,128)S(1)} %collective-permute-done.30.refs_2_, f32[104,128]{1,0:T(8,128)S(1)} %collective-permute-done.31.refs_3_, ...), custom_call_target="tpu_custom_call" | custom-call | tf_op jit(solution)/shard_map/adjoint_next/pallas_call | solution.py:665
  95.3 1.8 %collective-permute-start.38 = (f32[208,128]{1,0:T(8,128)S(1)}, f32[208,128]{1,0:T(8,128)S(1)}, u32[]{:S(2)}, u32[]{:S(2)}) collective-permute-start(f32[208,128]{1,0:T(8,128)S(1)} %adjoint_next.3.message), channel_id=1, source_target_pairs={{0,24},{8,16},{16,8},{24,0},{1,25},{9,17},{17,9},{25,1},{2,26},{10... | collective-permute-start | bytes 319496 | tf_op jit(solution)/shard_map/ppermute | solution.py:594
  97.0 0.9 collective-permute-start.37
  97.9 1.1 collective-permute-start.36
  99.4 2.1 %collective-permute-start.40 = (f32[96,128]{1,0:T(8,128)S(1)}, f32[96,128]{1,0:T(8,128)S(1)}, u32[]{:S(2)}, u32[]{:S(2)}) collective-permute-start(f32[96,128]{1,0:T(8,128)S(1)} %get-tuple-element.85), channel_id=1, source_target_pairs={{0,7},{1,2},{2,1},{3,4},{4,3},{5,6},{6,5},{7,0},{8,15},{9,10},{10,... | collective-permute-start | bytes 147464 | tf_op jit(solution)/shard_map/ppermute | solution.py:594
  101.7 1.5 %collective-permute-done.37.refs_0_ = f32[208,128]{1,0:T(8,128)S(1)} collective-permute-done((f32[208,128]{1,0:T(8,128)S(1)}, f32[208,128]{1,0:T(8,128)S(1)}, u32[]{:S(2)}, u32[]{:S(2)}) %collective-permute-start.37) | collective-permute-done | bytes 106528 | tf_op jit(solution)/shard_map/ppermute | solution.py:594
  103.6 2.1 %collective-permute-start.42 = (f32[32,128]{1,0:T(8,128)S(1)}, f32[32,128]{1,0:T(8,128)S(1)}, u32[]{:S(2)}, u32[]{:S(2)}) collective-permute-start(f32[32,128]{1,0:T(8,128)S(1)} %get-tuple-element.87), channel_id=1, source_target_pairs={{0,7},{1,2},{2,1},{3,4},{4,3},{5,6},{6,5},{7,0},{8,15},{9,10},{10,... | collective-permute-start | bytes 49160 | tf_op jit(solution)/shard_map/ppermute | solution.py:594
  105.7 1.1 combine.1
  106.8 1.8 %collective-permute-done.42.refs_7_ = f32[32,128]{1,0:T(8,128)S(1)} collective-permute-done((f32[32,128]{1,0:T(8,128)S(1)}, f32[32,128]{1,0:T(8,128)S(1)}, u32[]{:S(2)}, u32[]{:S(2)}) %collective-permute-start.42) | collective-permute-done | bytes 16416 | tf_op jit(solution)/shard_map/ppermute | solution.py:594
  108.6 3.9 %final.1 = f32[512,128]{1,0:T(8,128)} custom-call(s32[2]{0:T(128)S(1)} %copy-done.4, f32[512,128]{1,0:T(8,128)S(1)} %get-tuple-element.81.refs_1_, f32[192,128]{1,0:T(8,128)S(1)} %get-tuple-element.82.refs_2_, f32[192,128]{1,0:T(8,128)S(1)} %get-tuple-element.83.refs_3_, f32[96,128]{1,0:T(8,128)S(1)} %collective-permute-done.39.refs_4_, ...), custom_call_target="tpu_custom_call" | custom-call | tf_op jit(solution)/shard_map/final/pallas_call | solution.py:665
  (85 shorter events, 6.6 us)
Async XLA Ops:
  2.9 23.1 %copy-start.1 = (f32[512,128]{1,0:T(8,128)S(1)}, f32[512,128]{1,0:T(8,128)}, u32[]{:S(2)}) copy-start(f32[512,128]{1,0:T(8,128)} %get-tuple-element.48.root_h) | copy-start | bytes 786436
  2.9 8.2 %collective-permute-start.3 = (f32[72,128]{1,0:T(8,128)}, f32[72,128]{1,0:T(8,128)S(1)}, u32[]{:S(2)}, u32[]{:S(2)}) collective-permute-start(f32[72,128]{1,0:T(8,128)} %get-tuple-element.46.refs_0_), channel_id=1, source_target_pairs={{0,1},{1,0},{2,3},{3,2},{4,5},{5,4},{6,7},{7,6},{8,9},{9,8},{10,11... | collective-permute-start | bytes 110600 | tf_op jit(solution)/shard_map/ppermute | solution.py:594
  3.5 9.4 %collective-permute-start.2 = (f32[72,128]{1,0:T(8,128)}, f32[72,128]{1,0:T(8,128)S(1)}, u32[]{:S(2)}, u32[]{:S(2)}) collective-permute-start(f32[72,128]{1,0:T(8,128)} %get-tuple-element.46.refs_0_), channel_id=1, source_target_pairs={{0,6},{1,7},{2,4},{3,5},{4,2},{5,3},{6,0},{7,1},{8,14},{9,15},{10,... | collective-permute-start | bytes 110600 | tf_op jit(solution)/shard_map/ppermute | solution.py:594
  8.1 5.1 %collective-permute-start.1 = (f32[72,128]{1,0:T(8,128)}, f32[72,128]{1,0:T(8,128)S(1)}, u32[]{:S(2)}, u32[]{:S(2)}) collective-permute-start(f32[72,128]{1,0:T(8,128)} %get-tuple-element.46.refs_0_), channel_id=1, source_target_pairs={{0,4},{1,5},{2,6},{3,7},{4,0},{5,1},{6,2},{7,3},{8,12},{9,13},{10,... | collective-permute-start | bytes 110600 | tf_op jit(solution)/shard_map/ppermute | solution.py:594
  8.1 5.3 %collective-permute-start = (f32[72,128]{1,0:T(8,128)}, f32[72,128]{1,0:T(8,128)S(1)}, u32[]{:S(2)}, u32[]{:S(2)}) collective-permute-start(f32[72,128]{1,0:T(8,128)} %get-tuple-element.46.refs_0_), channel_id=1, source_target_pairs={{0,2},{1,3},{2,0},{3,1},{4,6},{5,7},{6,4},{7,5},{8,10},{9,11},{10,... | collective-permute-start | bytes 110600 | tf_op jit(solution)/shard_map/ppermute | solution.py:594
  8.8 17.3 %collective-permute-start.7 = (f32[584,128]{1,0:T(8,128)}, f32[584,128]{1,0:T(8,128)S(1)}, u32[]{:S(2)}, u32[]{:S(2)}) collective-permute-start(f32[584,128]{1,0:T(8,128)} %get-tuple-element.50), channel_id=1, source_target_pairs={{0,8},{8,0},{16,24},{24,16},{1,9},{9,1},{17,25},{25,17},{2,10},{10... | collective-permute-start | bytes 897032 | tf_op jit(solution)/shard_map/ppermute | solution.py:594
  11.2 14.9 %collective-permute-start.8 = (f32[584,128]{1,0:T(8,128)}, f32[584,128]{1,0:T(8,128)S(1)}, u32[]{:S(2)}, u32[]{:S(2)}) collective-permute-start(f32[584,128]{1,0:T(8,128)} %get-tuple-element.51), channel_id=1, source_target_pairs={{0,0},{24,24},{8,16},{16,8},{1,1},{25,25},{9,17},{17,9},{2,2},{26,... | collective-permute-start | bytes 897032 | tf_op jit(solution)/shard_map/ppermute | solution.py:594
  12.9 1.3 %collective-permute-start.6 = (f32[72,128]{1,0:T(8,128)S(1)}, f32[72,128]{1,0:T(8,128)S(1)}, u32[]{:S(2)}, u32[]{:S(2)}) collective-permute-start(f32[72,128]{1,0:T(8,128)S(1)} %collective-permute-done.2.refs_3_), channel_id=1, source_target_pairs={{0,1},{1,0},{2,3},{3,2},{4,5},{5,4},{6,7},{7,6},{8,9},{9,8},{10,11... | collective-permute-start | bytes 110600 | tf_op jit(solution)/shard_map/ppermute | solution.py:594
  13.2 1.2 %collective-permute-start.5 = (f32[72,128]{1,0:T(8,128)S(1)}, f32[72,128]{1,0:T(8,128)S(1)}, u32[]{:S(2)}, u32[]{:S(2)}) collective-permute-start(f32[72,128]{1,0:T(8,128)S(1)} %collective-permute-done.1.refs_2_), channel_id=1, source_target_pairs={{0,1},{1,0},{2,3},{3,2},{4,5},{5,4},{6,7},{7,6},{8,9},{9,8},{10,11... | collective-permute-start | bytes 110600 | tf_op jit(solution)/shard_map/ppermute | solution.py:594
  13.4 1.2 %collective-permute-start.4 = (f32[72,128]{1,0:T(8,128)S(1)}, f32[72,128]{1,0:T(8,128)S(1)}, u32[]{:S(2)}, u32[]{:S(2)}) collective-permute-start(f32[72,128]{1,0:T(8,128)S(1)} %collective-permute-done.refs_1_), channel_id=1, source_target_pairs={{0,1},{1,0},{2,3},{3,2},{4,5},{5,4},{6,7},{7,6},{8,9},{9,8},{10,11... | collective-permute-start | bytes 110600 | tf_op jit(solution)/shard_map/ppermute | solution.py:594
  13.7 26.7 %copy-start.4 = (s32[2]{0:T(128)S(1)}, s32[2]{0:T(128)}, u32[]{:S(2)}) copy-start(s32[2]{0:T(128)} %refs_0_.7) | copy-start | bytes 28
  14.7 2.8 %copy-start = (f32[192,64,128]{2,1,0:T(8,128)S(1)}, f32[192,64,128]{2,1,0:T(8,128)}, u32[]{:S(2)}) copy-start(f32[192,64,128]{2,1,0:T(8,128)} %refs_12_.1) | copy-start | bytes 18874372
  17.4 0.8 copy-start.3
  18.2 7.9 %copy-start.2 = (f32[512,128]{1,0:T(8,128)S(1)}, f32[512,128]{1,0:T(8,128)}, u32[]{:S(2)}) copy-start(f32[512,128]{1,0:T(8,128)} %get-tuple-element.49.root_v) | copy-start | bytes 786436
  20.5 10.6 %collective-permute-start.10 = (f32[192,128]{1,0:T(8,128)S(1)}, f32[192,128]{1,0:T(8,128)S(1)}, u32[]{:S(2)}, u32[]{:S(2)}) collective-permute-start(f32[192,128]{1,0:T(8,128)S(1)} %get-tuple-element.47.message), channel_id=1, source_target_pairs={{0,0},{24,24},{8,16},{16,8},{1,1},{25,25},{9,17},{17,9},{2,2},{26,... | collective-permute-start | bytes 294920 | tf_op jit(solution)/shard_map/ppermute | solution.py:594
  21.1 9.9 %collective-permute-start.9 = (f32[192,128]{1,0:T(8,128)S(1)}, f32[192,128]{1,0:T(8,128)S(1)}, u32[]{:S(2)}, u32[]{:S(2)}) collective-permute-start(f32[192,128]{1,0:T(8,128)S(1)} %get-tuple-element.47.message), channel_id=1, source_target_pairs={{0,8},{8,0},{16,24},{24,16},{1,9},{9,1},{17,25},{25,17},{2,10},{10... | collective-permute-start | bytes 294920 | tf_op jit(solution)/shard_map/ppermute | solution.py:594
  26.9 9.1 %collective-permute-start.13 = (f32[456,128]{1,0:T(8,128)}, f32[456,128]{1,0:T(8,128)S(1)}, u32[]{:S(2)}, u32[]{:S(2)}) collective-permute-start(f32[456,128]{1,0:T(8,128)} %get-tuple-element.52), channel_id=1, source_target_pairs={{0,1},{1,0},{2,3},{3,2},{4,5},{5,4},{6,7},{7,6},{8,9},{9,8},{10,11... | collective-permute-start | bytes 700424 | tf_op jit(solution)/shard_map/ppermute | solution.py:594
  26.9 9.8 %collective-permute-start.14 = (f32[456,128]{1,0:T(8,128)S(1)}, f32[456,128]{1,0:T(8,128)S(1)}, u32[]{:S(2)}, u32[]{:S(2)}) collective-permute-start(f32[456,128]{1,0:T(8,128)S(1)} %get-tuple-element.53), channel_id=1, source_target_pairs={{0,7},{1,2},{2,1},{3,4},{4,3},{5,6},{6,5},{7,0},{8,15},{9,10},{10,... | collective-permute-start | bytes 700424 | tf_op jit(solution)/shard_map/ppermute | solution.py:594
  32.2 6.2 %collective-permute-start.11 = (f32[328,128]{1,0:T(8,128)}, f32[328,128]{1,0:T(8,128)S(1)}, u32[]{:S(2)}, u32[]{:S(2)}) collective-permute-start(f32[328,128]{1,0:T(8,128)} %get-tuple-element.58), channel_id=1, source_target_pairs={{0,1},{1,0},{2,3},{3,2},{4,5},{5,4},{6,7},{7,6},{8,9},{9,8},{10,11... | collective-permute-start | bytes 503816 | tf_op jit(solution)/shard_map/ppermute | solution.py:594
  32.2 8.3 %collective-permute-start.12 = (f32[328,128]{1,0:T(8,128)S(1)}, f32[328,128]{1,0:T(8,128)S(1)}, u32[]{:S(2)}, u32[]{:S(2)}) collective-permute-start(f32[328,128]{1,0:T(8,128)S(1)} %get-tuple-element.59), channel_id=1, source_target_pairs={{0,7},{1,2},{2,1},{3,4},{4,3},{5,6},{6,5},{7,0},{8,15},{9,10},{10,... | collective-permute-start | bytes 503816 | tf_op jit(solution)/shard_map/ppermute | solution.py:594
  49.5 6.1 %collective-permute-start.17 = (f32[104,128]{1,0:T(8,128)S(1)}, f32[104,128]{1,0:T(8,128)S(1)}, u32[]{:S(2)}, u32[]{:S(2)}) collective-permute-start(f32[104,128]{1,0:T(8,128)S(1)} %get-tuple-element.65.refs_0_), channel_id=1, source_target_pairs={{0,6},{1,7},{2,4},{3,5},{4,2},{5,3},{6,0},{7,1},{8,14},{9,15},{10,... | collective-permute-start | bytes 159752 | tf_op jit(solution)/shard_map/ppermute | solution.py:594
  49.8 5.8 %collective-permute-start.16 = (f32[104,128]{1,0:T(8,128)S(1)}, f32[104,128]{1,0:T(8,128)S(1)}, u32[]{:S(2)}, u32[]{:S(2)}) collective-permute-start(f32[104,128]{1,0:T(8,128)S(1)} %get-tuple-element.65.refs_0_), channel_id=1, source_target_pairs={{0,4},{1,5},{2,6},{3,7},{4,0},{5,1},{6,2},{7,3},{8,12},{9,13},{10,... | collective-permute-start | bytes 159752 | tf_op jit(solution)/shard_map/ppermute | solution.py:594
  49.8 7.3 %collective-permute-start.15 = (f32[104,128]{1,0:T(8,128)S(1)}, f32[104,128]{1,0:T(8,128)S(1)}, u32[]{:S(2)}, u32[]{:S(2)}) collective-permute-start(f32[104,128]{1,0:T(8,128)S(1)} %get-tuple-element.65.refs_0_), channel_id=1, source_target_pairs={{0,2},{1,3},{2,0},{3,1},{4,6},{5,7},{6,4},{7,5},{8,10},{9,11},{10,... | collective-permute-start | bytes 159752 | tf_op jit(solution)/shard_map/ppermute | solution.py:594
  54.0 3.6 %collective-permute-start.18 = (f32[104,128]{1,0:T(8,128)S(1)}, f32[104,128]{1,0:T(8,128)S(1)}, u32[]{:S(2)}, u32[]{:S(2)}) collective-permute-start(f32[104,128]{1,0:T(8,128)S(1)} %get-tuple-element.65.refs_0_), channel_id=1, source_target_pairs={{0,1},{1,0},{2,3},{3,2},{4,5},{5,4},{6,7},{7,6},{8,9},{9,8},{10,11... | collective-permute-start | bytes 159752 | tf_op jit(solution)/shard_map/ppermute | solution.py:594
  55.6 2.1 %collective-permute-start.21 = (f32[104,128]{1,0:T(8,128)S(1)}, f32[104,128]{1,0:T(8,128)S(1)}, u32[]{:S(2)}, u32[]{:S(2)}) collective-permute-start(f32[104,128]{1,0:T(8,128)S(1)} %collective-permute-done.17.refs_3_), channel_id=1, source_target_pairs={{0,1},{1,0},{2,3},{3,2},{4,5},{5,4},{6,7},{7,6},{8,9},{9,8},{10,11... | collective-permute-start | bytes 159752 | tf_op jit(solution)/shard_map/ppermute | solution.py:594
  55.6 2.1 %collective-permute-start.20 = (f32[104,128]{1,0:T(8,128)S(1)}, f32[104,128]{1,0:T(8,128)S(1)}, u32[]{:S(2)}, u32[]{:S(2)}) collective-permute-start(f32[104,128]{1,0:T(8,128)S(1)} %collective-permute-done.16.refs_2_), channel_id=1, source_target_pairs={{0,1},{1,0},{2,3},{3,2},{4,5},{5,4},{6,7},{7,6},{8,9},{9,8},{10,11... | collective-permute-start | bytes 159752 | tf_op jit(solution)/shard_map/ppermute | solution.py:594
  57.1 1.2 %collective-permute-start.19 = (f32[104,128]{1,0:T(8,128)S(1)}, f32[104,128]{1,0:T(8,128)S(1)}, u32[]{:S(2)}, u32[]{:S(2)}) collective-permute-start(f32[104,128]{1,0:T(8,128)S(1)} %collective-permute-done.15.refs_1_), channel_id=1, source_target_pairs={{0,1},{1,0},{2,3},{3,2},{4,5},{5,4},{6,7},{7,6},{8,9},{9,8},{10,11... | collective-permute-start | bytes 159752 | tf_op jit(solution)/shard_map/ppermute | solution.py:594
  60.7 6.8 %collective-permute-start.24 = (f32[208,128]{1,0:T(8,128)S(1)}, f32[208,128]{1,0:T(8,128)S(1)}, u32[]{:S(2)}, u32[]{:S(2)}) collective-permute-start(f32[208,128]{1,0:T(8,128)S(1)} %adjoint_next.2.message), channel_id=1, source_target_pairs={{0,24},{8,16},{16,8},{24,0},{1,25},{9,17},{17,9},{25,1},{2,26},{10... | collective-permute-start | bytes 319496 | tf_op jit(solution)/shard_map/ppermute | solution.py:594
  63.3 5.1 %collective-permute-start.23 = (f32[208,128]{1,0:T(8,128)S(1)}, f32[208,128]{1,0:T(8,128)S(1)}, u32[]{:S(2)}, u32[]{:S(2)}) collective-permute-start(f32[208,128]{1,0:T(8,128)S(1)} %adjoint_next.2.message), channel_id=1, source_target_pairs={{0,8},{8,0},{16,24},{24,16},{1,9},{9,1},{17,25},{25,17},{2,10},{10... | collective-permute-start | bytes 319496 | tf_op jit(solution)/shard_map/ppermute | solution.py:594
  63.3 7.8 %collective-permute-start.22 = (f32[16,128]{1,0:T(8,128)S(1)}, f32[16,128]{1,0:T(8,128)S(1)}, u32[]{:S(2)}, u32[]{:S(2)}) collective-permute-start(f32[16,128]{1,0:T(8,128)S(1)} %slice.81), channel_id=1, source_target_pairs={{0,16},{8,24},{16,0},{24,8},{1,17},{9,25},{17,1},{25,9},{2,18},{10... | collective-permute-start | bytes 24584 | tf_op jit(solution)/shard_map/ppermute | solution.py:594
  64.6 6.5 %collective-permute-start.25 = (f32[192,128]{1,0:T(8,128)S(1)}, f32[192,128]{1,0:T(8,128)S(1)}, u32[]{:S(2)}, u32[]{:S(2)}) collective-permute-start(f32[192,128]{1,0:T(8,128)S(1)} %get-tuple-element.71), channel_id=1, source_target_pairs={{0,1},{1,0},{2,3},{3,2},{4,5},{5,4},{6,7},{7,6},{8,9},{9,8},{10,11... | collective-permute-start | bytes 294920 | tf_op jit(solution)/shard_map/ppermute | solution.py:594
  64.7 6.5 %collective-permute-start.26 = (f32[192,128]{1,0:T(8,128)S(1)}, f32[192,128]{1,0:T(8,128)S(1)}, u32[]{:S(2)}, u32[]{:S(2)}) collective-permute-start(f32[192,128]{1,0:T(8,128)S(1)} %get-tuple-element.72), channel_id=1, source_target_pairs={{0,7},{1,2},{2,1},{3,4},{4,3},{5,6},{6,5},{7,0},{8,15},{9,10},{10,... | collective-permute-start | bytes 294920 | tf_op jit(solution)/shard_map/ppermute | solution.py:594
  68.8 2.4 %collective-permute-start.27 = (f32[136,128]{1,0:T(8,128)S(1)}, f32[136,128]{1,0:T(8,128)S(1)}, u32[]{:S(2)}, u32[]{:S(2)}) collective-permute-start(f32[136,128]{1,0:T(8,128)S(1)} %get-tuple-element.73), channel_id=1, source_target_pairs={{0,1},{1,0},{2,3},{3,2},{4,5},{5,4},{6,7},{7,6},{8,9},{9,8},{10,11... | collective-permute-start | bytes 208904 | tf_op jit(solution)/shard_map/ppermute | solution.py:594
  68.8 5.7 %collective-permute-start.28 = (f32[136,128]{1,0:T(8,128)S(1)}, f32[136,128]{1,0:T(8,128)S(1)}, u32[]{:S(2)}, u32[]{:S(2)}) collective-permute-start(f32[136,128]{1,0:T(8,128)S(1)} %get-tuple-element.74), channel_id=1, source_target_pairs={{0,7},{1,2},{2,1},{3,4},{4,3},{5,6},{6,5},{7,0},{8,15},{9,10},{10,... | collective-permute-start | bytes 208904 | tf_op jit(solution)/shard_map/ppermute | solution.py:594
  84.1 6.1 %collective-permute-start.31 = (f32[104,128]{1,0:T(8,128)S(1)}, f32[104,128]{1,0:T(8,128)S(1)}, u32[]{:S(2)}, u32[]{:S(2)}) collective-permute-start(f32[104,128]{1,0:T(8,128)S(1)} %get-tuple-element.77.refs_0_), channel_id=1, source_target_pairs={{0,6},{1,7},{2,4},{3,5},{4,2},{5,3},{6,0},{7,1},{8,14},{9,15},{10,... | collective-permute-start | bytes 159752 | tf_op jit(solution)/shard_map/ppermute | solution.py:594
  84.4 5.8 %collective-permute-start.30 = (f32[104,128]{1,0:T(8,128)S(1)}, f32[104,128]{1,0:T(8,128)S(1)}, u32[]{:S(2)}, u32[]{:S(2)}) collective-permute-start(f32[104,128]{1,0:T(8,128)S(1)} %get-tuple-element.77.refs_0_), channel_id=1, source_target_pairs={{0,4},{1,5},{2,6},{3,7},{4,0},{5,1},{6,2},{7,3},{8,12},{9,13},{10,... | collective-permute-start | bytes 159752 | tf_op jit(solution)/shard_map/ppermute | solution.py:594
  85.0 6.7 %collective-permute-start.29 = (f32[104,128]{1,0:T(8,128)S(1)}, f32[104,128]{1,0:T(8,128)S(1)}, u32[]{:S(2)}, u32[]{:S(2)}) collective-permute-start(f32[104,128]{1,0:T(8,128)S(1)} %get-tuple-element.77.refs_0_), channel_id=1, source_target_pairs={{0,2},{1,3},{2,0},{3,1},{4,6},{5,7},{6,4},{7,5},{8,10},{9,11},{10,... | collective-permute-start | bytes 159752 | tf_op jit(solution)/shard_map/ppermute | solution.py:594
  88.5 3.2 %collective-permute-start.32 = (f32[104,128]{1,0:T(8,128)S(1)}, f32[104,128]{1,0:T(8,128)S(1)}, u32[]{:S(2)}, u32[]{:S(2)}) collective-permute-start(f32[104,128]{1,0:T(8,128)S(1)} %get-tuple-element.77.refs_0_), channel_id=1, source_target_pairs={{0,1},{1,0},{2,3},{3,2},{4,5},{5,4},{6,7},{7,6},{8,9},{9,8},{10,11... | collective-permute-start | bytes 159752 | tf_op jit(solution)/shard_map/ppermute | solution.py:594
  90.1 1.6 %collective-permute-start.35 = (f32[104,128]{1,0:T(8,128)S(1)}, f32[104,128]{1,0:T(8,128)S(1)}, u32[]{:S(2)}, u32[]{:S(2)}) collective-permute-start(f32[104,128]{1,0:T(8,128)S(1)} %collective-permute-done.31.refs_3_), channel_id=1, source_target_pairs={{0,1},{1,0},{2,3},{3,2},{4,5},{5,4},{6,7},{7,6},{8,9},{9,8},{10,11... | collective-permute-start | bytes 159752 | tf_op jit(solution)/shard_map/ppermute | solution.py:594
  90.1 1.8 %collective-permute-start.34 = (f32[104,128]{1,0:T(8,128)S(1)}, f32[104,128]{1,0:T(8,128)S(1)}, u32[]{:S(2)}, u32[]{:S(2)}) collective-permute-start(f32[104,128]{1,0:T(8,128)S(1)} %collective-permute-done.30.refs_2_), channel_id=1, source_target_pairs={{0,1},{1,0},{2,3},{3,2},{4,5},{5,4},{6,7},{7,6},{8,9},{9,8},{10,11... | collective-permute-start | bytes 159752 | tf_op jit(solution)/shard_map/ppermute | solution.py:594
  91.7 1.2 %collective-permute-start.33 = (f32[104,128]{1,0:T(8,128)S(1)}, f32[104,128]{1,0:T(8,128)S(1)}, u32[]{:S(2)}, u32[]{:S(2)}) collective-permute-start(f32[104,128]{1,0:T(8,128)S(1)} %collective-permute-done.29.refs_1_), channel_id=1, source_target_pairs={{0,1},{1,0},{2,3},{3,2},{4,5},{5,4},{6,7},{7,6},{8,9},{9,8},{10,11... | collective-permute-start | bytes 159752 | tf_op jit(solution)/shard_map/ppermute | solution.py:594
  95.3 6.4 %collective-permute-start.38 = (f32[208,128]{1,0:T(8,128)S(1)}, f32[208,128]{1,0:T(8,128)S(1)}, u32[]{:S(2)}, u32[]{:S(2)}) collective-permute-start(f32[208,128]{1,0:T(8,128)S(1)} %adjoint_next.3.message), channel_id=1, source_target_pairs={{0,24},{8,16},{16,8},{24,0},{1,25},{9,17},{17,9},{25,1},{2,26},{10... | collective-permute-start | bytes 319496 | tf_op jit(solution)/shard_map/ppermute | solution.py:594
  97.0 6.2 %collective-permute-start.37 = (f32[208,128]{1,0:T(8,128)S(1)}, f32[208,128]{1,0:T(8,128)S(1)}, u32[]{:S(2)}, u32[]{:S(2)}) collective-permute-start(f32[208,128]{1,0:T(8,128)S(1)} %adjoint_next.3.message), channel_id=1, source_target_pairs={{0,8},{8,0},{16,24},{24,16},{1,9},{9,1},{17,25},{25,17},{2,10},{10... | collective-permute-start | bytes 319496 | tf_op jit(solution)/shard_map/ppermute | solution.py:594
  97.9 7.8 %collective-permute-start.36 = (f32[16,128]{1,0:T(8,128)S(1)}, f32[16,128]{1,0:T(8,128)S(1)}, u32[]{:S(2)}, u32[]{:S(2)}) collective-permute-start(f32[16,128]{1,0:T(8,128)S(1)} %slice.84), channel_id=1, source_target_pairs={{0,16},{8,24},{16,0},{24,8},{1,17},{9,25},{17,1},{25,9},{2,18},{10... | collective-permute-start | bytes 24584 | tf_op jit(solution)/shard_map/ppermute | solution.py:594
  99.3 7.5 %collective-permute-start.39 = (f32[96,128]{1,0:T(8,128)S(1)}, f32[96,128]{1,0:T(8,128)S(1)}, u32[]{:S(2)}, u32[]{:S(2)}) collective-permute-start(f32[96,128]{1,0:T(8,128)S(1)} %get-tuple-element.84), channel_id=1, source_target_pairs={{0,1},{1,0},{2,3},{3,2},{4,5},{5,4},{6,7},{7,6},{8,9},{9,8},{10,11... | collective-permute-start | bytes 147464 | tf_op jit(solution)/shard_map/ppermute | solution.py:594
  99.4 7.4 %collective-permute-start.40 = (f32[96,128]{1,0:T(8,128)S(1)}, f32[96,128]{1,0:T(8,128)S(1)}, u32[]{:S(2)}, u32[]{:S(2)}) collective-permute-start(f32[96,128]{1,0:T(8,128)S(1)} %get-tuple-element.85), channel_id=1, source_target_pairs={{0,7},{1,2},{2,1},{3,4},{4,3},{5,6},{6,5},{7,0},{8,15},{9,10},{10,... | collective-permute-start | bytes 147464 | tf_op jit(solution)/shard_map/ppermute | solution.py:594
  103.5 3.3 %collective-permute-start.41 = (f32[32,128]{1,0:T(8,128)S(1)}, f32[32,128]{1,0:T(8,128)S(1)}, u32[]{:S(2)}, u32[]{:S(2)}) collective-permute-start(f32[32,128]{1,0:T(8,128)S(1)} %get-tuple-element.86), channel_id=1, source_target_pairs={{0,1},{1,0},{2,3},{3,2},{4,5},{5,4},{6,7},{7,6},{8,9},{9,8},{10,11... | collective-permute-start | bytes 49160 | tf_op jit(solution)/shard_map/ppermute | solution.py:594
  103.6 5.0 %collective-permute-start.42 = (f32[32,128]{1,0:T(8,128)S(1)}, f32[32,128]{1,0:T(8,128)S(1)}, u32[]{:S(2)}, u32[]{:S(2)}) collective-permute-start(f32[32,128]{1,0:T(8,128)S(1)} %get-tuple-element.87), channel_id=1, source_target_pairs={{0,7},{1,2},{2,1},{3,4},{4,3},{5,6},{6,5},{7,0},{8,15},{9,10},{10,... | collective-permute-start | bytes 49160 | tf_op jit(solution)/shard_map/ppermute | solution.py:594

commit v6 on v5

--- a/solution.py
+++ b/solution.py
@@ -75,21 +75,21 @@
             buf[row, 8 * v:8 * v + 8] = w + ((f - g) + (e - h))
         return below, flux
 
-    def four(step, carry):
-        for k in range(4):
-            carry = advance(first + 4 * step + k, carry)
+    def six(step, carry):
+        for k in range(6):
+            carry = advance(first + 6 * step + k, carry)
         return carry
 
     def two(step, carry):
         for k in range(2):
-            carry = advance(last - 2 + k, carry)
+            carry = advance(first + count // 6 * 6 + 2 * step + k, carry)
         return carry
 
     start = tiles(buf, first)
     flux = [f * (w - a) for f, w, a in zip(tiles(face_lat, first - 1), start, tiles(buf, first - 1))]
     count = last - first
-    carry = lax.fori_loop(0, count // 4, four, (start, flux))
-    lax.fori_loop(0, (count % 4) // 2, two, carry)
+    carry = lax.fori_loop(0, count // 6, six, (start, flux))
+    lax.fori_loop(0, (count % 6) // 2, two, carry)
 
 
 def lateral_passes(buf, face_lat, face_lon, nh, begin, end):
@@ -505,8 +505,9 @@
         for load in loads:
             load.wait()
 
-    def finish(i, acc):
-        place = pl.ds(pl.multiple_of(i * lon_cells, lon_cells), lon_cells)
+    norm = jnp.zeros((8, LANES), jnp.float32)
+    for i in range(lat_cells):
+        place = slice(i * lon_cells, (i + 1) * lon_cells)
         vector = mid[i, cols]
         after = natural[FRAME + i, cols]
         if first_call:
@@ -521,10 +522,7 @@
             vector = base - alpha * applied
         square = vector * vector
         for j in range(lon_cells // 8):
-            acc = acc + square[8 * j:8 * j + 8]
-        return acc
-
-    norm = lax.fori_loop(0, lat_cells, finish, jnp.zeros((8, LANES), jnp.float32))
+            norm = norm + square[8 * j:8 * j + 8]
     stores = copies([(one, one_hbm), (two, two_hbm)], sems.at[pl.ds(2, 2)])
     if first_call:
         loads[0].wait()

time: 113 us -> 113 us (level)
  Pallas kernels: 37.9 us -> 39.1 us
    pallas_call x16, Pallas kernels: 37.9 us -> 39.1 us  [call(): pl.pallas_call(kernel, out_shape=outs, in_specs=specs, out_specs=out_spec...]
  transfers between devices with their start and end apart: 43 -> 43, of which waited for: 19 -> 19; matrix products, arithmetic and copies ran while one was open for 1% -> 1% of each run, Pallas kernels for 8% -> 7%
where the time goes in v6:
time: 113 us; the launch traced here: 114 us
  starting transfers between devices  49.8 us (44%)
  Pallas kernels  39.1 us (35%)
  waiting for transfers between devices  18.6 us (16%)
  local copies, waits for them, and re-layouts  3.63 us (3%)
  other arithmetic  1.39 us (1%)
    ppermute x43, starting transfers between devices, send(): return lax.ppermute(x, axis, pairs)  49.8 us
    pallas_call x16, Pallas kernels, call(): pl.pallas_call(kernel, out_shape=outs, in_specs=specs, out_specs=out_spec...  39.1 us
    ppermute x43, waiting for transfers between devices, send(): return lax.ppermute(x, axis, pairs)  18.6 us
    unnamed x10, local copies, waits for them, and re-layouts  3.57 us
  transfers between devices with their start and end apart: 43, of which 19 were waited for; matrix products, arithmetic and copies ran while one was open for 1% of the time, Pallas kernels for 7%

profile of v6, /device:TPU:0, one launch (start us, length us, event | category | flops | bytes accessed | tf_op | source)
XLA Modules:
  0.0 113.6 jit_solution(9877378233452494855)
XLA Ops:
  0.6 2.3 %start.1 = (f32[72,128]{1,0:T(8,128)}, f32[512,128]{1,0:T(8,128)}, f32[512,128]{1,0:T(8,128)}, f32[584,128]{1,0:T(8,128)}, f32[584,128]{1,0:T(8,128)}) custom-call(f32[64,64]{1,0:T(8,128)} %refs_0_.4, f32[64,64]{1,0:T(8,128)} %refs_1_.1, s32[2,192]{1,0:T(2,128)} %refs_2_.1, f32[512,128]{1,0:T(8,128)} %bitcast.16, f32[512,128]{1,0:T(8,128)} %bitcast.17), custom_call_target="tpu_custom_call" | custom-call | tf_op jit(solution)/shard_map/start/pallas_call | solution.py:663
  3.5 4.7 %collective-permute-start.2 = (f32[72,128]{1,0:T(8,128)}, f32[72,128]{1,0:T(8,128)S(1)}, u32[]{:S(2)}, u32[]{:S(2)}) collective-permute-start(f32[72,128]{1,0:T(8,128)} %get-tuple-element.46.refs_0_), channel_id=1, source_target_pairs={{0,6},{1,7},{2,4},{3,5},{4,2},{5,3},{6,0},{7,1},{8,14},{9,15},{10,... | collective-permute-start | bytes 110600 | tf_op jit(solution)/shard_map/ppermute | solution.py:592
  8.1 0.7 collective-permute-start
  8.8 1.6 %collective-permute-start.7 = (f32[584,128]{1,0:T(8,128)}, f32[584,128]{1,0:T(8,128)S(1)}, u32[]{:S(2)}, u32[]{:S(2)}) collective-permute-start(f32[584,128]{1,0:T(8,128)} %get-tuple-element.50), channel_id=1, source_target_pairs={{0,8},{8,0},{16,24},{24,16},{1,9},{9,1},{17,25},{25,17},{2,10},{10... | collective-permute-start | bytes 897032 | tf_op jit(solution)/shard_map/ppermute | solution.py:592
  10.4 0.8 fusion.20
  11.2 1.6 %collective-permute-start.8 = (f32[584,128]{1,0:T(8,128)}, f32[584,128]{1,0:T(8,128)S(1)}, u32[]{:S(2)}, u32[]{:S(2)}) collective-permute-start(f32[584,128]{1,0:T(8,128)} %get-tuple-element.51), channel_id=1, source_target_pairs={{0,0},{24,24},{8,16},{16,8},{1,1},{25,25},{9,17},{17,9},{2,2},{26,... | collective-permute-start | bytes 897032 | tf_op jit(solution)/shard_map/ppermute | solution.py:592
  14.7 2.8 %copy-done = f32[192,64,128]{2,1,0:T(8,128)S(1)} copy-done((f32[192,64,128]{2,1,0:T(8,128)S(1)}, f32[192,64,128]{2,1,0:T(8,128)}, u32[]{:S(2)}) %copy-start) | copy-done | bytes 6291480
  17.4 0.8 copy-done.3
  18.2 2.2 %adjoint_first.1 = (f32[192,128]{1,0:T(8,128)S(1)}, f32[64,512]{1,0:T(8,128)S(1)}) custom-call(f32[72,128]{1,0:T(8,128)S(1)} %copy-done.3, f32[72,128]{1,0:T(8,128)S(1)} %collective-permute-done.refs_1_, f32[72,128]{1,0:T(8,128)S(1)} %collective-permute-done.1.refs_2_, f32[72,128]{1,0:T(8,128)S(1)} %collective-permute-done.2.refs_3_, ...), custom_call_target="tpu_custom_call" | custom-call | tf_op jit(solution)/shard_map/adjoint_first/pallas_call | solution.py:663
  20.5 0.7 collective-permute-start.10
  21.1 4.9 %collective-permute-start.9 = (f32[192,128]{1,0:T(8,128)S(1)}, f32[192,128]{1,0:T(8,128)S(1)}, u32[]{:S(2)}, u32[]{:S(2)}) collective-permute-start(f32[192,128]{1,0:T(8,128)S(1)} %get-tuple-element.47.message), channel_id=1, source_target_pairs={{0,8},{8,0},{16,24},{24,16},{1,9},{9,1},{17,25},{25,17},{2,10},{10... | collective-permute-start | bytes 294920 | tf_op jit(solution)/shard_map/ppermute | solution.py:592
  26.1 0.8 face_sides.1
  26.9 3.8 %collective-permute-start.14 = (f32[456,128]{1,0:T(8,128)S(1)}, f32[456,128]{1,0:T(8,128)S(1)}, u32[]{:S(2)}, u32[]{:S(2)}) collective-permute-start(f32[456,128]{1,0:T(8,128)S(1)} %get-tuple-element.53), channel_id=1, source_target_pairs={{0,7},{1,2},{2,1},{3,4},{4,3},{5,6},{6,5},{7,0},{8,15},{9,10},{10,... | collective-permute-start | bytes 700424 | tf_op jit(solution)/shard_map/ppermute | solution.py:592
  31.1 1.1 sides.3
  32.2 3.7 %collective-permute-start.12 = (f32[328,128]{1,0:T(8,128)S(1)}, f32[328,128]{1,0:T(8,128)S(1)}, u32[]{:S(2)}, u32[]{:S(2)}) collective-permute-start(f32[328,128]{1,0:T(8,128)S(1)} %get-tuple-element.59), channel_id=1, source_target_pairs={{0,7},{1,2},{2,1},{3,4},{4,3},{5,6},{6,5},{7,0},{8,15},{9,10},{10,... | collective-permute-start | bytes 503816 | tf_op jit(solution)/shard_map/ppermute | solution.py:592
  36.0 0.7 collective-permute-done.14.from_s
  36.7 1.7 %faces.1 = (f32[40,56,128]{2,1,0:T(8,128)S(1)}, f32[40,56,128]{2,1,0:T(8,128)S(1)}, f32[28,56,128]{2,1,0:T(8,128)S(1)}, f32[28,56,128]{2,1,0:T(8,128)S(1)}, f32[28,56,128]{2,1,0:T(8,128)S(1)}) custom-call(f32[512,128]{1,0:T(8,128)S(1)} %copy-done.1, f32[512,128]{1,0:T(8,128)S(1)} %copy-done.2, f32[584,128]{1,0:T(8,128)S(1)} %collective-permute-done.7.from_a, ...), custom_call_target="tpu_custom_call" | custom-call | tf_op jit(solution)/shard_map/faces/pallas_call | solution.py:663
  38.4 2.0 %collective-permute-done.12.refs_6_ = f32[328,128]{1,0:T(8,128)S(1)} collective-permute-done((f32[328,128]{1,0:T(8,128)S(1)}, f32[328,128]{1,0:T(8,128)S(1)}, u32[]{:S(2)}, u32[]{:S(2)}) %collective-permute-start.12) | collective-permute-done | bytes 167968 | tf_op jit(solution)/shard_map/ppermute | solution.py:592
  40.4 9.6 %spread_first.1 = (f32[512,128]{1,0:T(8,128)S(1)}, f32[512,128]{1,0:T(8,128)S(1)}, f32[104,128]{1,0:T(8,128)S(1)}, f32[192,64,128]{2,1,0:T(8,128)S(1)}) custom-call(s32[2]{0:T(128)S(1)} %copy-done.4, s32[192]{0:T(256)S(1)} %bitcast.14, f32[512,128]{1,0:T(8,128)S(1)} %scatter.3.refs_0_.refs_2_, f32[384,128]{1,0:T(8,128)S(1)} %get-tuple-element.56.refs_3_, ...), custom_call_target="tpu_custom_call" | custom-call | tf_op jit(solution)/shard_map/spread_first/pallas_call | solution.py:663
  50.3 4.2 %collective-permute-start.15 = (f32[104,128]{1,0:T(8,128)S(1)}, f32[104,128]{1,0:T(8,128)S(1)}, u32[]{:S(2)}, u32[]{:S(2)}) collective-permute-start(f32[104,128]{1,0:T(8,128)S(1)} %get-tuple-element.65.refs_0_), channel_id=1, source_target_pairs={{0,2},{1,3},{2,0},{3,1},{4,6},{5,7},{6,4},{7,5},{8,10},{9,11},{10,... | collective-permute-start | bytes 159752 | tf_op jit(solution)/shard_map/ppermute | solution.py:592
  54.6 1.5 %collective-permute-done.17.refs_3_ = f32[104,128]{1,0:T(8,128)S(1)} collective-permute-done((f32[104,128]{1,0:T(8,128)S(1)}, f32[104,128]{1,0:T(8,128)S(1)}, u32[]{:S(2)}, u32[]{:S(2)}) %collective-permute-start.17) | collective-permute-done | bytes 53280 | tf_op jit(solution)/shard_map/ppermute | solution.py:592
  56.1 0.9 collective-permute-start.20
  57.1 0.6 collective-permute-done.15.refs_1_
  58.1 0.7 collective-permute-done.19.refs_5_
  58.8 2.3 %adjoint_next.2.message = f32[208,128]{1,0:T(8,128)S(1)} custom-call(f32[104,128]{1,0:T(8,128)S(1)} %get-tuple-element.65.refs_0_, f32[104,128]{1,0:T(8,128)S(1)} %collective-permute-done.15.refs_1_, f32[104,128]{1,0:T(8,128)S(1)} %collective-permute-done.16.refs_2_, f32[104,128]{1,0:T(8,128)S(1)} %collective-permute-done.17.refs_3_, ...), custom_call_target="tpu_custom_call" | custom-call | tf_op jit(solution)/shard_map/adjoint_next/pallas_call | solution.py:663
  61.2 2.6 %collective-permute-start.24 = (f32[208,128]{1,0:T(8,128)S(1)}, f32[208,128]{1,0:T(8,128)S(1)}, u32[]{:S(2)}, u32[]{:S(2)}) collective-permute-start(f32[208,128]{1,0:T(8,128)S(1)} %adjoint_next.2.message), channel_id=1, source_target_pairs={{0,24},{8,16},{16,8},{24,0},{1,25},{9,17},{17,9},{25,1},{2,26},{10... | collective-permute-start | bytes 319496 | tf_op jit(solution)/shard_map/ppermute | solution.py:592
  63.7 1.0 collective-permute-start.22
  65.1 2.2 %collective-permute-start.26 = (f32[192,128]{1,0:T(8,128)S(1)}, f32[192,128]{1,0:T(8,128)S(1)}, u32[]{:S(2)}, u32[]{:S(2)}) collective-permute-start(f32[192,128]{1,0:T(8,128)S(1)} %get-tuple-element.72), channel_id=1, source_target_pairs={{0,7},{1,2},{2,1},{3,4},{4,3},{5,6},{6,5},{7,0},{8,15},{9,10},{10,... | collective-permute-start | bytes 294920 | tf_op jit(solution)/shard_map/ppermute | solution.py:592
  67.3 0.7 collective-permute-done.24.refs_1_
  68.0 0.9 collective-permute-done.23.refs_0_
  69.3 2.3 %collective-permute-start.28 = (f32[136,128]{1,0:T(8,128)S(1)}, f32[136,128]{1,0:T(8,128)S(1)}, u32[]{:S(2)}, u32[]{:S(2)}) collective-permute-start(f32[136,128]{1,0:T(8,128)S(1)} %get-tuple-element.74), channel_id=1, source_target_pairs={{0,7},{1,2},{2,1},{3,4},{4,3},{5,6},{6,5},{7,0},{8,15},{9,10},{10,... | collective-permute-start | bytes 208904 | tf_op jit(solution)/shard_map/ppermute | solution.py:592
  71.6 3.4 %collective-permute-done.28.refs_8_ = f32[136,128]{1,0:T(8,128)S(1)} collective-permute-done((f32[136,128]{1,0:T(8,128)S(1)}, f32[136,128]{1,0:T(8,128)S(1)}, u32[]{:S(2)}, u32[]{:S(2)}) %collective-permute-start.28) | collective-permute-done | bytes 69664 | tf_op jit(solution)/shard_map/ppermute | solution.py:592
  75.0 10.0 %spread_next.1 = (f32[512,128]{1,0:T(8,128)S(1)}, f32[512,128]{1,0:T(8,128)S(1)}, f32[104,128]{1,0:T(8,128)S(1)}) custom-call(s32[2]{0:T(128)S(1)} %copy-done.4, s32[192]{0:T(256)S(1)} %bitcast.15, f32[512,128]{1,0:T(8,128)S(1)} %get-tuple-element.68.refs_2_, f32[384,128]{1,0:T(8,128)S(1)} %get-tuple-element.69.refs_3_, ...), custom_call_target="tpu_custom_call" | custom-call | tf_op jit(solution)/shard_map/spread_next/pallas_call | solution.py:663
  85.8 3.6 %collective-permute-start.29 = (f32[104,128]{1,0:T(8,128)S(1)}, f32[104,128]{1,0:T(8,128)S(1)}, u32[]{:S(2)}, u32[]{:S(2)}) collective-permute-start(f32[104,128]{1,0:T(8,128)S(1)} %get-tuple-element.77.refs_0_), channel_id=1, source_target_pairs={{0,2},{1,3},{2,0},{3,1},{4,6},{5,7},{6,4},{7,5},{8,10},{9,11},{10,... | collective-permute-start | bytes 159752 | tf_op jit(solution)/shard_map/ppermute | solution.py:592
  89.5 1.6 %collective-permute-done.31.refs_3_ = f32[104,128]{1,0:T(8,128)S(1)} collective-permute-done((f32[104,128]{1,0:T(8,128)S(1)}, f32[104,128]{1,0:T(8,128)S(1)}, u32[]{:S(2)}, u32[]{:S(2)}) %collective-permute-start.31) | collective-permute-done | bytes 53280 | tf_op jit(solution)/shard_map/ppermute | solution.py:592
  91.1 0.9 collective-permute-start.34
  92.0 0.6 collective-permute-done.29.refs_1_
  92.9 0.9 collective-permute-done.33.refs_5_
  93.8 2.3 %adjoint_next.3.message = f32[208,128]{1,0:T(8,128)S(1)} custom-call(f32[104,128]{1,0:T(8,128)S(1)} %get-tuple-element.77.refs_0_, f32[104,128]{1,0:T(8,128)S(1)} %collective-permute-done.29.refs_1_, f32[104,128]{1,0:T(8,128)S(1)} %collective-permute-done.30.refs_2_, f32[104,128]{1,0:T(8,128)S(1)} %collective-permute-done.31.refs_3_, ...), custom_call_target="tpu_custom_call" | custom-call | tf_op jit(solution)/shard_map/adjoint_next/pallas_call | solution.py:663
  96.2 1.7 %collective-permute-start.38 = (f32[208,128]{1,0:T(8,128)S(1)}, f32[208,128]{1,0:T(8,128)S(1)}, u32[]{:S(2)}, u32[]{:S(2)}) collective-permute-start(f32[208,128]{1,0:T(8,128)S(1)} %adjoint_next.3.message), channel_id=1, source_target_pairs={{0,24},{8,16},{16,8},{24,0},{1,25},{9,17},{17,9},{25,1},{2,26},{10... | collective-permute-start | bytes 319496 | tf_op jit(solution)/shard_map/ppermute | solution.py:592
  97.9 0.9 collective-permute-start.37
  98.8 1.0 collective-permute-start.36
  100.2 2.1 %collective-permute-start.40 = (f32[96,128]{1,0:T(8,128)S(1)}, f32[96,128]{1,0:T(8,128)S(1)}, u32[]{:S(2)}, u32[]{:S(2)}) collective-permute-start(f32[96,128]{1,0:T(8,128)S(1)} %get-tuple-element.85), channel_id=1, source_target_pairs={{0,7},{1,2},{2,1},{3,4},{4,3},{5,6},{6,5},{7,0},{8,15},{9,10},{10,... | collective-permute-start | bytes 147464 | tf_op jit(solution)/shard_map/ppermute | solution.py:592
  102.6 1.5 %collective-permute-done.37.refs_0_ = f32[208,128]{1,0:T(8,128)S(1)} collective-permute-done((f32[208,128]{1,0:T(8,128)S(1)}, f32[208,128]{1,0:T(8,128)S(1)}, u32[]{:S(2)}, u32[]{:S(2)}) %collective-permute-start.37) | collective-permute-done | bytes 106528 | tf_op jit(solution)/shard_map/ppermute | solution.py:592
  104.5 2.2 %collective-permute-start.42 = (f32[32,128]{1,0:T(8,128)S(1)}, f32[32,128]{1,0:T(8,128)S(1)}, u32[]{:S(2)}, u32[]{:S(2)}) collective-permute-start(f32[32,128]{1,0:T(8,128)S(1)} %get-tuple-element.87), channel_id=1, source_target_pairs={{0,7},{1,2},{2,1},{3,4},{4,3},{5,6},{6,5},{7,0},{8,15},{9,10},{10,... | collective-permute-start | bytes 49160 | tf_op jit(solution)/shard_map/ppermute | solution.py:592
  106.7 1.1 combine.1
  107.7 1.8 %collective-permute-done.42.refs_7_ = f32[32,128]{1,0:T(8,128)S(1)} collective-permute-done((f32[32,128]{1,0:T(8,128)S(1)}, f32[32,128]{1,0:T(8,128)S(1)}, u32[]{:S(2)}, u32[]{:S(2)}) %collective-permute-start.42) | collective-permute-done | bytes 16416 | tf_op jit(solution)/shard_map/ppermute | solution.py:592
  109.5 4.1 %final.1 = f32[512,128]{1,0:T(8,128)} custom-call(s32[2]{0:T(128)S(1)} %copy-done.4, f32[512,128]{1,0:T(8,128)S(1)} %get-tuple-element.81.refs_1_, f32[192,128]{1,0:T(8,128)S(1)} %get-tuple-element.82.refs_2_, f32[192,128]{1,0:T(8,128)S(1)} %get-tuple-element.83.refs_3_, f32[96,128]{1,0:T(8,128)S(1)} %collective-permute-done.39.refs_4_, ...), custom_call_target="tpu_custom_call" | custom-call | tf_op jit(solution)/shard_map/final/pallas_call | solution.py:663
  (85 shorter events, 6.5 us)
Async XLA Ops:
  2.9 23.1 %copy-start.1 = (f32[512,128]{1,0:T(8,128)S(1)}, f32[512,128]{1,0:T(8,128)}, u32[]{:S(2)}) copy-start(f32[512,128]{1,0:T(8,128)} %get-tuple-element.48.root_h) | copy-start | bytes 786436
  2.9 8.2 %collective-permute-start.3 = (f32[72,128]{1,0:T(8,128)}, f32[72,128]{1,0:T(8,128)S(1)}, u32[]{:S(2)}, u32[]{:S(2)}) collective-permute-start(f32[72,128]{1,0:T(8,128)} %get-tuple-element.46.refs_0_), channel_id=1, source_target_pairs={{0,1},{1,0},{2,3},{3,2},{4,5},{5,4},{6,7},{7,6},{8,9},{9,8},{10,11... | collective-permute-start | bytes 110600 | tf_op jit(solution)/shard_map/ppermute | solution.py:592
  3.5 9.4 %collective-permute-start.2 = (f32[72,128]{1,0:T(8,128)}, f32[72,128]{1,0:T(8,128)S(1)}, u32[]{:S(2)}, u32[]{:S(2)}) collective-permute-start(f32[72,128]{1,0:T(8,128)} %get-tuple-element.46.refs_0_), channel_id=1, source_target_pairs={{0,6},{1,7},{2,4},{3,5},{4,2},{5,3},{6,0},{7,1},{8,14},{9,15},{10,... | collective-permute-start | bytes 110600 | tf_op jit(solution)/shard_map/ppermute | solution.py:592
  8.1 5.1 %collective-permute-start.1 = (f32[72,128]{1,0:T(8,128)}, f32[72,128]{1,0:T(8,128)S(1)}, u32[]{:S(2)}, u32[]{:S(2)}) collective-permute-start(f32[72,128]{1,0:T(8,128)} %get-tuple-element.46.refs_0_), channel_id=1, source_target_pairs={{0,4},{1,5},{2,6},{3,7},{4,0},{5,1},{6,2},{7,3},{8,12},{9,13},{10,... | collective-permute-start | bytes 110600 | tf_op jit(solution)/shard_map/ppermute | solution.py:592
  8.1 5.3 %collective-permute-start = (f32[72,128]{1,0:T(8,128)}, f32[72,128]{1,0:T(8,128)S(1)}, u32[]{:S(2)}, u32[]{:S(2)}) collective-permute-start(f32[72,128]{1,0:T(8,128)} %get-tuple-element.46.refs_0_), channel_id=1, source_target_pairs={{0,2},{1,3},{2,0},{3,1},{4,6},{5,7},{6,4},{7,5},{8,10},{9,11},{10,... | collective-permute-start | bytes 110600 | tf_op jit(solution)/shard_map/ppermute | solution.py:592
  8.8 17.3 %collective-permute-start.7 = (f32[584,128]{1,0:T(8,128)}, f32[584,128]{1,0:T(8,128)S(1)}, u32[]{:S(2)}, u32[]{:S(2)}) collective-permute-start(f32[584,128]{1,0:T(8,128)} %get-tuple-element.50), channel_id=1, source_target_pairs={{0,8},{8,0},{16,24},{24,16},{1,9},{9,1},{17,25},{25,17},{2,10},{10... | collective-permute-start | bytes 897032 | tf_op jit(solution)/shard_map/ppermute | solution.py:592
  11.2 14.9 %collective-permute-start.8 = (f32[584,128]{1,0:T(8,128)}, f32[584,128]{1,0:T(8,128)S(1)}, u32[]{:S(2)}, u32[]{:S(2)}) collective-permute-start(f32[584,128]{1,0:T(8,128)} %get-tuple-element.51), channel_id=1, source_target_pairs={{0,0},{24,24},{8,16},{16,8},{1,1},{25,25},{9,17},{17,9},{2,2},{26,... | collective-permute-start | bytes 897032 | tf_op jit(solution)/shard_map/ppermute | solution.py:592
  12.9 1.3 %collective-permute-start.6 = (f32[72,128]{1,0:T(8,128)S(1)}, f32[72,128]{1,0:T(8,128)S(1)}, u32[]{:S(2)}, u32[]{:S(2)}) collective-permute-start(f32[72,128]{1,0:T(8,128)S(1)} %collective-permute-done.2.refs_3_), channel_id=1, source_target_pairs={{0,1},{1,0},{2,3},{3,2},{4,5},{5,4},{6,7},{7,6},{8,9},{9,8},{10,11... | collective-permute-start | bytes 110600 | tf_op jit(solution)/shard_map/ppermute | solution.py:592
  13.2 1.2 %collective-permute-start.5 = (f32[72,128]{1,0:T(8,128)S(1)}, f32[72,128]{1,0:T(8,128)S(1)}, u32[]{:S(2)}, u32[]{:S(2)}) collective-permute-start(f32[72,128]{1,0:T(8,128)S(1)} %collective-permute-done.1.refs_2_), channel_id=1, source_target_pairs={{0,1},{1,0},{2,3},{3,2},{4,5},{5,4},{6,7},{7,6},{8,9},{9,8},{10,11... | collective-permute-start | bytes 110600 | tf_op jit(solution)/shard_map/ppermute | solution.py:592
  13.4 1.2 %collective-permute-start.4 = (f32[72,128]{1,0:T(8,128)S(1)}, f32[72,128]{1,0:T(8,128)S(1)}, u32[]{:S(2)}, u32[]{:S(2)}) collective-permute-start(f32[72,128]{1,0:T(8,128)S(1)} %collective-permute-done.refs_1_), channel_id=1, source_target_pairs={{0,1},{1,0},{2,3},{3,2},{4,5},{5,4},{6,7},{7,6},{8,9},{9,8},{10,11... | collective-permute-start | bytes 110600 | tf_op jit(solution)/shard_map/ppermute | solution.py:592
  13.7 26.7 %copy-start.4 = (s32[2]{0:T(128)S(1)}, s32[2]{0:T(128)}, u32[]{:S(2)}) copy-start(s32[2]{0:T(128)} %refs_0_.7) | copy-start | bytes 28
  14.7 2.8 %copy-start = (f32[192,64,128]{2,1,0:T(8,128)S(1)}, f32[192,64,128]{2,1,0:T(8,128)}, u32[]{:S(2)}) copy-start(f32[192,64,128]{2,1,0:T(8,128)} %refs_12_.1) | copy-start | bytes 18874372
  17.4 0.8 copy-start.3
  18.2 7.9 %copy-start.2 = (f32[512,128]{1,0:T(8,128)S(1)}, f32[512,128]{1,0:T(8,128)}, u32[]{:S(2)}) copy-start(f32[512,128]{1,0:T(8,128)} %get-tuple-element.49.root_v) | copy-start | bytes 786436
  20.5 10.6 %collective-permute-start.10 = (f32[192,128]{1,0:T(8,128)S(1)}, f32[192,128]{1,0:T(8,128)S(1)}, u32[]{:S(2)}, u32[]{:S(2)}) collective-permute-start(f32[192,128]{1,0:T(8,128)S(1)} %get-tuple-element.47.message), channel_id=1, source_target_pairs={{0,0},{24,24},{8,16},{16,8},{1,1},{25,25},{9,17},{17,9},{2,2},{26,... | collective-permute-start | bytes 294920 | tf_op jit(solution)/shard_map/ppermute | solution.py:592
  21.1 9.9 %collective-permute-start.9 = (f32[192,128]{1,0:T(8,128)S(1)}, f32[192,128]{1,0:T(8,128)S(1)}, u32[]{:S(2)}, u32[]{:S(2)}) collective-permute-start(f32[192,128]{1,0:T(8,128)S(1)} %get-tuple-element.47.message), channel_id=1, source_target_pairs={{0,8},{8,0},{16,24},{24,16},{1,9},{9,1},{17,25},{25,17},{2,10},{10... | collective-permute-start | bytes 294920 | tf_op jit(solution)/shard_map/ppermute | solution.py:592
  26.9 9.1 %collective-permute-start.13 = (f32[456,128]{1,0:T(8,128)}, f32[456,128]{1,0:T(8,128)S(1)}, u32[]{:S(2)}, u32[]{:S(2)}) collective-permute-start(f32[456,128]{1,0:T(8,128)} %get-tuple-element.52), channel_id=1, source_target_pairs={{0,1},{1,0},{2,3},{3,2},{4,5},{5,4},{6,7},{7,6},{8,9},{9,8},{10,11... | collective-permute-start | bytes 700424 | tf_op jit(solution)/shard_map/ppermute | solution.py:592
  26.9 9.8 %collective-permute-start.14 = (f32[456,128]{1,0:T(8,128)S(1)}, f32[456,128]{1,0:T(8,128)S(1)}, u32[]{:S(2)}, u32[]{:S(2)}) collective-permute-start(f32[456,128]{1,0:T(8,128)S(1)} %get-tuple-element.53), channel_id=1, source_target_pairs={{0,7},{1,2},{2,1},{3,4},{4,3},{5,6},{6,5},{7,0},{8,15},{9,10},{10,... | collective-permute-start | bytes 700424 | tf_op jit(solution)/shard_map/ppermute | solution.py:592
  32.2 6.2 %collective-permute-start.11 = (f32[328,128]{1,0:T(8,128)}, f32[328,128]{1,0:T(8,128)S(1)}, u32[]{:S(2)}, u32[]{:S(2)}) collective-permute-start(f32[328,128]{1,0:T(8,128)} %get-tuple-element.58), channel_id=1, source_target_pairs={{0,1},{1,0},{2,3},{3,2},{4,5},{5,4},{6,7},{7,6},{8,9},{9,8},{10,11... | collective-permute-start | bytes 503816 | tf_op jit(solution)/shard_map/ppermute | solution.py:592
  32.2 8.3 %collective-permute-start.12 = (f32[328,128]{1,0:T(8,128)S(1)}, f32[328,128]{1,0:T(8,128)S(1)}, u32[]{:S(2)}, u32[]{:S(2)}) collective-permute-start(f32[328,128]{1,0:T(8,128)S(1)} %get-tuple-element.59), channel_id=1, source_target_pairs={{0,7},{1,2},{2,1},{3,4},{4,3},{5,6},{6,5},{7,0},{8,15},{9,10},{10,... | collective-permute-start | bytes 503816 | tf_op jit(solution)/shard_map/ppermute | solution.py:592
  50.0 6.1 %collective-permute-start.17 = (f32[104,128]{1,0:T(8,128)S(1)}, f32[104,128]{1,0:T(8,128)S(1)}, u32[]{:S(2)}, u32[]{:S(2)}) collective-permute-start(f32[104,128]{1,0:T(8,128)S(1)} %get-tuple-element.65.refs_0_), channel_id=1, source_target_pairs={{0,6},{1,7},{2,4},{3,5},{4,2},{5,3},{6,0},{7,1},{8,14},{9,15},{10,... | collective-permute-start | bytes 159752 | tf_op jit(solution)/shard_map/ppermute | solution.py:592
  50.3 5.8 %collective-permute-start.16 = (f32[104,128]{1,0:T(8,128)S(1)}, f32[104,128]{1,0:T(8,128)S(1)}, u32[]{:S(2)}, u32[]{:S(2)}) collective-permute-start(f32[104,128]{1,0:T(8,128)S(1)} %get-tuple-element.65.refs_0_), channel_id=1, source_target_pairs={{0,4},{1,5},{2,6},{3,7},{4,0},{5,1},{6,2},{7,3},{8,12},{9,13},{10,... | collective-permute-start | bytes 159752 | tf_op jit(solution)/shard_map/ppermute | solution.py:592
  50.3 7.3 %collective-permute-start.15 = (f32[104,128]{1,0:T(8,128)S(1)}, f32[104,128]{1,0:T(8,128)S(1)}, u32[]{:S(2)}, u32[]{:S(2)}) collective-permute-start(f32[104,128]{1,0:T(8,128)S(1)} %get-tuple-element.65.refs_0_), channel_id=1, source_target_pairs={{0,2},{1,3},{2,0},{3,1},{4,6},{5,7},{6,4},{7,5},{8,10},{9,11},{10,... | collective-permute-start | bytes 159752 | tf_op jit(solution)/shard_map/ppermute | solution.py:592
  54.5 3.6 %collective-permute-start.18 = (f32[104,128]{1,0:T(8,128)S(1)}, f32[104,128]{1,0:T(8,128)S(1)}, u32[]{:S(2)}, u32[]{:S(2)}) collective-permute-start(f32[104,128]{1,0:T(8,128)S(1)} %get-tuple-element.65.refs_0_), channel_id=1, source_target_pairs={{0,1},{1,0},{2,3},{3,2},{4,5},{5,4},{6,7},{7,6},{8,9},{9,8},{10,11... | collective-permute-start | bytes 159752 | tf_op jit(solution)/shard_map/ppermute | solution.py:592
  56.1 2.0 %collective-permute-start.21 = (f32[104,128]{1,0:T(8,128)S(1)}, f32[104,128]{1,0:T(8,128)S(1)}, u32[]{:S(2)}, u32[]{:S(2)}) collective-permute-start(f32[104,128]{1,0:T(8,128)S(1)} %collective-permute-done.17.refs_3_), channel_id=1, source_target_pairs={{0,1},{1,0},{2,3},{3,2},{4,5},{5,4},{6,7},{7,6},{8,9},{9,8},{10,11... | collective-permute-start | bytes 159752 | tf_op jit(solution)/shard_map/ppermute | solution.py:592
  56.1 2.0 %collective-permute-start.20 = (f32[104,128]{1,0:T(8,128)S(1)}, f32[104,128]{1,0:T(8,128)S(1)}, u32[]{:S(2)}, u32[]{:S(2)}) collective-permute-start(f32[104,128]{1,0:T(8,128)S(1)} %collective-permute-done.16.refs_2_), channel_id=1, source_target_pairs={{0,1},{1,0},{2,3},{3,2},{4,5},{5,4},{6,7},{7,6},{8,9},{9,8},{10,11... | collective-permute-start | bytes 159752 | tf_op jit(solution)/shard_map/ppermute | solution.py:592
  57.6 1.2 %collective-permute-start.19 = (f32[104,128]{1,0:T(8,128)S(1)}, f32[104,128]{1,0:T(8,128)S(1)}, u32[]{:S(2)}, u32[]{:S(2)}) collective-permute-start(f32[104,128]{1,0:T(8,128)S(1)} %collective-permute-done.15.refs_1_), channel_id=1, source_target_pairs={{0,1},{1,0},{2,3},{3,2},{4,5},{5,4},{6,7},{7,6},{8,9},{9,8},{10,11... | collective-permute-start | bytes 159752 | tf_op jit(solution)/shard_map/ppermute | solution.py:592
  61.2 6.8 %collective-permute-start.24 = (f32[208,128]{1,0:T(8,128)S(1)}, f32[208,128]{1,0:T(8,128)S(1)}, u32[]{:S(2)}, u32[]{:S(2)}) collective-permute-start(f32[208,128]{1,0:T(8,128)S(1)} %adjoint_next.2.message), channel_id=1, source_target_pairs={{0,24},{8,16},{16,8},{24,0},{1,25},{9,17},{17,9},{25,1},{2,26},{10... | collective-permute-start | bytes 319496 | tf_op jit(solution)/shard_map/ppermute | solution.py:592
  63.7 5.1 %collective-permute-start.23 = (f32[208,128]{1,0:T(8,128)S(1)}, f32[208,128]{1,0:T(8,128)S(1)}, u32[]{:S(2)}, u32[]{:S(2)}) collective-permute-start(f32[208,128]{1,0:T(8,128)S(1)} %adjoint_next.2.message), channel_id=1, source_target_pairs={{0,8},{8,0},{16,24},{24,16},{1,9},{9,1},{17,25},{25,17},{2,10},{10... | collective-permute-start | bytes 319496 | tf_op jit(solution)/shard_map/ppermute | solution.py:592
  63.7 7.8 %collective-permute-start.22 = (f32[16,128]{1,0:T(8,128)S(1)}, f32[16,128]{1,0:T(8,128)S(1)}, u32[]{:S(2)}, u32[]{:S(2)}) collective-permute-start(f32[16,128]{1,0:T(8,128)S(1)} %slice.81), channel_id=1, source_target_pairs={{0,16},{8,24},{16,0},{24,8},{1,17},{9,25},{17,1},{25,9},{2,18},{10... | collective-permute-start | bytes 24584 | tf_op jit(solution)/shard_map/ppermute | solution.py:592
  65.0 6.5 %collective-permute-start.25 = (f32[192,128]{1,0:T(8,128)S(1)}, f32[192,128]{1,0:T(8,128)S(1)}, u32[]{:S(2)}, u32[]{:S(2)}) collective-permute-start(f32[192,128]{1,0:T(8,128)S(1)} %get-tuple-element.71), channel_id=1, source_target_pairs={{0,1},{1,0},{2,3},{3,2},{4,5},{5,4},{6,7},{7,6},{8,9},{9,8},{10,11... | collective-permute-start | bytes 294920 | tf_op jit(solution)/shard_map/ppermute | solution.py:592
  65.1 6.5 %collective-permute-start.26 = (f32[192,128]{1,0:T(8,128)S(1)}, f32[192,128]{1,0:T(8,128)S(1)}, u32[]{:S(2)}, u32[]{:S(2)}) collective-permute-start(f32[192,128]{1,0:T(8,128)S(1)} %get-tuple-element.72), channel_id=1, source_target_pairs={{0,7},{1,2},{2,1},{3,4},{4,3},{5,6},{6,5},{7,0},{8,15},{9,10},{10,... | collective-permute-start | bytes 294920 | tf_op jit(solution)/shard_map/ppermute | solution.py:592
  69.2 2.4 %collective-permute-start.27 = (f32[136,128]{1,0:T(8,128)S(1)}, f32[136,128]{1,0:T(8,128)S(1)}, u32[]{:S(2)}, u32[]{:S(2)}) collective-permute-start(f32[136,128]{1,0:T(8,128)S(1)} %get-tuple-element.73), channel_id=1, source_target_pairs={{0,1},{1,0},{2,3},{3,2},{4,5},{5,4},{6,7},{7,6},{8,9},{9,8},{10,11... | collective-permute-start | bytes 208904 | tf_op jit(solution)/shard_map/ppermute | solution.py:592
  69.3 5.7 %collective-permute-start.28 = (f32[136,128]{1,0:T(8,128)S(1)}, f32[136,128]{1,0:T(8,128)S(1)}, u32[]{:S(2)}, u32[]{:S(2)}) collective-permute-start(f32[136,128]{1,0:T(8,128)S(1)} %get-tuple-element.74), channel_id=1, source_target_pairs={{0,7},{1,2},{2,1},{3,4},{4,3},{5,6},{6,5},{7,0},{8,15},{9,10},{10,... | collective-permute-start | bytes 208904 | tf_op jit(solution)/shard_map/ppermute | solution.py:592
  85.0 6.1 %collective-permute-start.31 = (f32[104,128]{1,0:T(8,128)S(1)}, f32[104,128]{1,0:T(8,128)S(1)}, u32[]{:S(2)}, u32[]{:S(2)}) collective-permute-start(f32[104,128]{1,0:T(8,128)S(1)} %get-tuple-element.77.refs_0_), channel_id=1, source_target_pairs={{0,6},{1,7},{2,4},{3,5},{4,2},{5,3},{6,0},{7,1},{8,14},{9,15},{10,... | collective-permute-start | bytes 159752 | tf_op jit(solution)/shard_map/ppermute | solution.py:592
  85.3 5.8 %collective-permute-start.30 = (f32[104,128]{1,0:T(8,128)S(1)}, f32[104,128]{1,0:T(8,128)S(1)}, u32[]{:S(2)}, u32[]{:S(2)}) collective-permute-start(f32[104,128]{1,0:T(8,128)S(1)} %get-tuple-element.77.refs_0_), channel_id=1, source_target_pairs={{0,4},{1,5},{2,6},{3,7},{4,0},{5,1},{6,2},{7,3},{8,12},{9,13},{10,... | collective-permute-start | bytes 159752 | tf_op jit(solution)/shard_map/ppermute | solution.py:592
  85.8 6.8 %collective-permute-start.29 = (f32[104,128]{1,0:T(8,128)S(1)}, f32[104,128]{1,0:T(8,128)S(1)}, u32[]{:S(2)}, u32[]{:S(2)}) collective-permute-start(f32[104,128]{1,0:T(8,128)S(1)} %get-tuple-element.77.refs_0_), channel_id=1, source_target_pairs={{0,2},{1,3},{2,0},{3,1},{4,6},{5,7},{6,4},{7,5},{8,10},{9,11},{10,... | collective-permute-start | bytes 159752 | tf_op jit(solution)/shard_map/ppermute | solution.py:592
  89.4 3.2 %collective-permute-start.32 = (f32[104,128]{1,0:T(8,128)S(1)}, f32[104,128]{1,0:T(8,128)S(1)}, u32[]{:S(2)}, u32[]{:S(2)}) collective-permute-start(f32[104,128]{1,0:T(8,128)S(1)} %get-tuple-element.77.refs_0_), channel_id=1, source_target_pairs={{0,1},{1,0},{2,3},{3,2},{4,5},{5,4},{6,7},{7,6},{8,9},{9,8},{10,11... | collective-permute-start | bytes 159752 | tf_op jit(solution)/shard_map/ppermute | solution.py:592
  91.1 1.5 %collective-permute-start.35 = (f32[104,128]{1,0:T(8,128)S(1)}, f32[104,128]{1,0:T(8,128)S(1)}, u32[]{:S(2)}, u32[]{:S(2)}) collective-permute-start(f32[104,128]{1,0:T(8,128)S(1)} %collective-permute-done.31.refs_3_), channel_id=1, source_target_pairs={{0,1},{1,0},{2,3},{3,2},{4,5},{5,4},{6,7},{7,6},{8,9},{9,8},{10,11... | collective-permute-start | bytes 159752 | tf_op jit(solution)/shard_map/ppermute | solution.py:592
  91.1 1.8 %collective-permute-start.34 = (f32[104,128]{1,0:T(8,128)S(1)}, f32[104,128]{1,0:T(8,128)S(1)}, u32[]{:S(2)}, u32[]{:S(2)}) collective-permute-start(f32[104,128]{1,0:T(8,128)S(1)} %collective-permute-done.30.refs_2_), channel_id=1, source_target_pairs={{0,1},{1,0},{2,3},{3,2},{4,5},{5,4},{6,7},{7,6},{8,9},{9,8},{10,11... | collective-permute-start | bytes 159752 | tf_op jit(solution)/shard_map/ppermute | solution.py:592
  92.6 1.2 %collective-permute-start.33 = (f32[104,128]{1,0:T(8,128)S(1)}, f32[104,128]{1,0:T(8,128)S(1)}, u32[]{:S(2)}, u32[]{:S(2)}) collective-permute-start(f32[104,128]{1,0:T(8,128)S(1)} %collective-permute-done.29.refs_1_), channel_id=1, source_target_pairs={{0,1},{1,0},{2,3},{3,2},{4,5},{5,4},{6,7},{7,6},{8,9},{9,8},{10,11... | collective-permute-start | bytes 159752 | tf_op jit(solution)/shard_map/ppermute | solution.py:592
  96.2 6.4 %collective-permute-start.38 = (f32[208,128]{1,0:T(8,128)S(1)}, f32[208,128]{1,0:T(8,128)S(1)}, u32[]{:S(2)}, u32[]{:S(2)}) collective-permute-start(f32[208,128]{1,0:T(8,128)S(1)} %adjoint_next.3.message), channel_id=1, source_target_pairs={{0,24},{8,16},{16,8},{24,0},{1,25},{9,17},{17,9},{25,1},{2,26},{10... | collective-permute-start | bytes 319496 | tf_op jit(solution)/shard_map/ppermute | solution.py:592
  97.9 6.2 %collective-permute-start.37 = (f32[208,128]{1,0:T(8,128)S(1)}, f32[208,128]{1,0:T(8,128)S(1)}, u32[]{:S(2)}, u32[]{:S(2)}) collective-permute-start(f32[208,128]{1,0:T(8,128)S(1)} %adjoint_next.3.message), channel_id=1, source_target_pairs={{0,8},{8,0},{16,24},{24,16},{1,9},{9,1},{17,25},{25,17},{2,10},{10... | collective-permute-start | bytes 319496 | tf_op jit(solution)/shard_map/ppermute | solution.py:592
  98.8 7.8 %collective-permute-start.36 = (f32[16,128]{1,0:T(8,128)S(1)}, f32[16,128]{1,0:T(8,128)S(1)}, u32[]{:S(2)}, u32[]{:S(2)}) collective-permute-start(f32[16,128]{1,0:T(8,128)S(1)} %slice.84), channel_id=1, source_target_pairs={{0,16},{8,24},{16,0},{24,8},{1,17},{9,25},{17,1},{25,9},{2,18},{10... | collective-permute-start | bytes 24584 | tf_op jit(solution)/shard_map/ppermute | solution.py:592
  100.1 7.6 %collective-permute-start.39 = (f32[96,128]{1,0:T(8,128)S(1)}, f32[96,128]{1,0:T(8,128)S(1)}, u32[]{:S(2)}, u32[]{:S(2)}) collective-permute-start(f32[96,128]{1,0:T(8,128)S(1)} %get-tuple-element.84), channel_id=1, source_target_pairs={{0,1},{1,0},{2,3},{3,2},{4,5},{5,4},{6,7},{7,6},{8,9},{9,8},{10,11... | collective-permute-start | bytes 147464 | tf_op jit(solution)/shard_map/ppermute | solution.py:592
  100.2 7.5 %collective-permute-start.40 = (f32[96,128]{1,0:T(8,128)S(1)}, f32[96,128]{1,0:T(8,128)S(1)}, u32[]{:S(2)}, u32[]{:S(2)}) collective-permute-start(f32[96,128]{1,0:T(8,128)S(1)} %get-tuple-element.85), channel_id=1, source_target_pairs={{0,7},{1,2},{2,1},{3,4},{4,3},{5,6},{6,5},{7,0},{8,15},{9,10},{10,... | collective-permute-start | bytes 147464 | tf_op jit(solution)/shard_map/ppermute | solution.py:592
  104.4 3.3 %collective-permute-start.41 = (f32[32,128]{1,0:T(8,128)S(1)}, f32[32,128]{1,0:T(8,128)S(1)}, u32[]{:S(2)}, u32[]{:S(2)}) collective-permute-start(f32[32,128]{1,0:T(8,128)S(1)} %get-tuple-element.86), channel_id=1, source_target_pairs={{0,1},{1,0},{2,3},{3,2},{4,5},{5,4},{6,7},{7,6},{8,9},{9,8},{10,11... | collective-permute-start | bytes 49160 | tf_op jit(solution)/shard_map/ppermute | solution.py:592
  104.5 5.0 %collective-permute-start.42 = (f32[32,128]{1,0:T(8,128)S(1)}, f32[32,128]{1,0:T(8,128)S(1)}, u32[]{:S(2)}, u32[]{:S(2)}) collective-permute-start(f32[32,128]{1,0:T(8,128)S(1)} %get-tuple-element.87), channel_id=1, source_target_pairs={{0,7},{1,2},{2,1},{3,4},{4,3},{5,6},{6,5},{7,0},{8,15},{9,10},{10,... | collective-permute-start | bytes 49160 | tf_op jit(solution)/shard_map/ppermute | solution.py:592
